TPU v7x, 32 devices: a whole 2x2x4 slice. The times are simulated.
32 devices in a mesh: groups: 2 (over y), points: 4 (over z), mp: 2 (over x), sub: 2 (over core).
Axes of the slice: x: 2, y: 2, z: 4, core: 2. Of those that a mesh axis runs over, the one named last changes fastest.
Arguments:
- points_in: bfloat16 [32768, 512], P(('groups', 'points', 'mp', 'sub')), parts along dimension 0, may hold values from -80 to 80
- cotangent: bfloat16 [32768, 512], P(('groups', 'points', 'mp', 'sub')), parts along dimension 0, may hold values from -9 to 9
- w_query: bfloat16 [512, 512], replicated, may hold values from -0.25 to 0.25
- w_key: bfloat16 [512, 512], replicated, may hold values from -1 to 1
- w_value: bfloat16 [512, 512], replicated, may hold values from -1 to 1
Outputs:
- grad_points: bfloat16 [32768, 512], P(('groups', 'points', 'mp', 'sub')), parts along dimension 0
- grad_query: float32 [1024, 512], P(('groups', 'points', 'sub'), 'mp'), parts along dimension 0
- grad_key: float32 [1024, 512], P(('groups', 'points', 'sub'), 'mp'), parts along dimension 0
- grad_value: float32 [1024, 512], P(('groups', 'points', 'sub'), 'mp'), parts along dimension 0
There are 2 independent parts, one for each index of `groups`. A program takes and returns all parts, laid end to end along the dimension named above; an argument that names none is the same for every part. Nothing has to cross between parts.
All inputs are finite; a program needn't handle non-finite values.
Results may differ from a plain program's by a relative error of at most 0.006.
Values sent between devices are 32-bit elements; how exact they have to be, the bound alone decides.
No kernel may reach another device: no remote copies, remote signals or barrier semaphores. Data moves between devices by JAX's collectives and lax.ppermute only.
A program may use at most 64 MiB of HBM per device.

v0:
```python
import jax
import jax.numpy as jnp
from jax import lax
from jax.sharding import PartitionSpec as P

HEADS = 16
HS = 32


def layer_norm(raw):
    mean_val = jnp.mean(raw, axis=-1, keepdims=True)
    centred = raw - mean_val
    spread = jnp.mean(centred * centred, axis=-1, keepdims=True)
    inverse = lax.rsqrt(spread + 1e-05)
    return (centred * inverse, inverse)


def norm_back(grad_norm, normed, inverse):
    first = jnp.mean(grad_norm, axis=-1, keepdims=True)
    second = jnp.mean(grad_norm * normed, axis=-1, keepdims=True)
    return (grad_norm - first - normed * second) * inverse


def local(points_in, cotangent, w_query, w_key, w_value):
    f32 = jnp.float32
    rows = points_in.shape[0]
    width = points_in.shape[1]
    total = rows * lax.axis_size(("points", "mp", "sub"))
    w_all = jnp.concatenate([w_query, w_key, w_value], axis=1)
    projected = jnp.dot(points_in, w_all, preferred_element_type=f32)
    query = projected[:, :width].astype(jnp.bfloat16).reshape(rows, HEADS, HS)
    key_norm, key_inv = layer_norm(projected[:, width : 2 * width].reshape(rows, HEADS, HS))
    value_norm, value_inv = layer_norm(projected[:, 2 * width :].reshape(rows, HEADS, HS))
    key_low = key_norm.astype(jnp.bfloat16)
    value_low = value_norm.astype(jnp.bfloat16)
    grad_out = cotangent.reshape(rows, HEADS, HS)
    state_part = jnp.einsum("nhi,nhj->hij", key_low, value_low, preferred_element_type=f32)
    grad_part = jnp.einsum("nhi,nhj->hij", query, grad_out, preferred_element_type=f32)
    state_total, grad_total = lax.psum((state_part, grad_part), ("points", "mp", "sub"))
    state = state_total / total
    grad_state = grad_total / total
    state_low = state.astype(jnp.bfloat16)
    grad_low = grad_state.astype(jnp.bfloat16)
    grad_q = jnp.einsum("nhj,hij->nhi", grad_out, state_low, preferred_element_type=f32)
    grad_kn = jnp.einsum("nhj,hij->nhi", value_low, grad_low, preferred_element_type=f32)
    grad_vn = jnp.einsum("nhi,hij->nhj", key_low, grad_low, preferred_element_type=f32)
    grad_k = norm_back(grad_kn, key_norm, key_inv)
    grad_v = norm_back(grad_vn, value_norm, value_inv)
    grad_cat = jnp.concatenate(
        [grad_q.reshape(rows, width), grad_k.reshape(rows, width), grad_v.reshape(rows, width)],
        axis=1,
    ).astype(jnp.bfloat16)
    point_count = lax.axis_size("points")
    sub_count = lax.axis_size("sub")
    row_block = width // (point_count * sub_count)
    row_part = lax.psum_scatter(
        lax.dot_general(points_in, grad_cat, (((0,), (0,)), ((), ())), preferred_element_type=f32)
        / total,
        ("points", "sub"),
        scatter_dimension=0,
        tiled=True,
    )
    grads = lax.psum_scatter(
        row_part.reshape(row_block, 3, width), "mp", scatter_dimension=2, tiled=True
    )
    grad_points = lax.dot_general(
        grad_cat, w_all, (((1,), (1,)), ((), ())), preferred_element_type=f32
    ).astype(jnp.bfloat16)
    grad_query = grads[:, 0, :]
    grad_key = grads[:, 1, :]
    grad_value = grads[:, 2, :]
    return (grad_points, grad_query, grad_key, grad_value)


def solution(mesh):
    return jax.shard_map(
        local,
        mesh=mesh,
        in_specs=(
            P(("groups", "points", "mp", "sub"), None),
            P(("groups", "points", "mp", "sub"), None),
            P(),
            P(),
            P(),
        ),
        out_specs=(
            P(("groups", "points", "mp", "sub"), None),
            P(("groups", "points", "sub"), "mp"),
            P(("groups", "points", "sub"), "mp"),
            P(("groups", "points", "sub"), "mp"),
        ),
        check_vma=False,
    )
```

profile of v0, /device:TPU:0, one launch (start us, length us, event | category | flops | bytes accessed | tf_op | source)
XLA Modules:
  0.0 198.8 jit_solution(16361809479786719109)
XLA Ops:
  7.2 0.0 copy-start
  7.2 0.0 all-reduce.3.cloned.1.call-start
  7.2 1.2 constant_dynamic-update-slice_fusion.2
  8.4 1.1 constant_dynamic-update-slice_fusion.1
  9.6 1.9 convolution_bitcast_fusion
  11.5 0.7 bitcast_reduce_fusion.2
  12.1 2.0 copy-done.1
  14.1 0.2 slice.57
  14.3 1.5 copy.16
  15.8 3.0 %multiply_reduce_fusion = (f32[1024,16]{0,1:T(8,128)S(1)}, f32[1024,16]{0,1:T(8,128)S(1)}) fusion(f32[1024,1536]{0,1:T(8,128)} %copy-done.1, f32[1024,16]{0,1:T(8,128)S(1)} %get-tuple-element.20, f32[1024,16]{0,1:T(8,128)S(1)} %get-tuple-element.21), kind=kLoop, calls=%fused_computation.23 | loop fusion | flops 3112960 | bytes 4456448 | tf_op jit(solution)/shard_map/reduce_sum | solution.py:13
  18.9 3.4 %fusion.22 = f32[16,32,32]{2,1,0:T(8,128)} fusion(f32[1024,1536]{0,1:T(8,128)} %copy-done.1, f32[1024,16]{0,1:T(8,128)S(1)} %add_rsqrt_fusion.1, f32[1024,16]{0,1:T(8,128)S(1)} %get-tuple-element.21, f32[1024,16]{0,1:T(8,128)S(1)} %add_rsqrt_fusion, f32[1024,16]{0,1:T(8,128)S(1)} %get-tuple-element.20), kind=kOutput, calls=%fused_computation.55 | convolution fusion | flops 36700160 | bytes 4521984 | tf_op jit(solution)/shard_map/nhi,nhj->hij/dot_general | solution.py:37
  22.3 1.1 fusion.26
  23.4 0.0 all-reduce.3.cloned.1.call-update
  23.5 0.0 reduce-scatter.7.cloned.1.call-start
  23.5 92.8 %all-reduce.3.cloned.1.call-done = (f32[16,32,32]{2,1,0:T(8,128)}, f32[16,32,32]{2,1,0:T(8,128)}) async-done(((f32[16,32,32]{2,1,0:T(8,128)}, f32[16,32,32]{2,1,0:T(8,128)}), (f32[16,32,32]{2,1,0:T(8,128)}, f32[16,32,32]{2,1,0:T(8,128)})) %all-reduce.3.cloned.1.call-update) | async-done | bytes 131088 | tf_op jit(solution)/shard_map/psum | solution.py:39
  116.3 1.4 convolution_convert_fusion.1
  117.7 2.2 %fusion.14 = f32[16,32,1024]{2,1,0:T(8,128)S(1)} fusion(f32[16,32,32]{2,1,0:T(8,128)S(1)} %copy-done.5, f32[1024,1536]{0,1:T(8,128)} %copy-done.1, f32[1024,16]{0,1:T(8,128)S(1)} %add_rsqrt_fusion.1, f32[1024,16]{0,1:T(8,128)S(1)} %get-tuple-element.21), kind=kOutput, calls=%fused_computation.39 | convolution fusion | flops 35160064 | bytes 4390912 | tf_op jit(solution)/shard_map/nhi,hij->nhj/dot_general | solution.py:46
  120.0 4.5 %fusion.8 = (f32[1024,16]{0,1:T(8,128)S(1)}, f32[1024,16]{0,1:T(8,128)S(1)}, f32[1024,16]{0,1:T(8,128)S(1)}, f32[1024,16]{0,1:T(8,128)S(1)}, f32[16,32,1024]{2,1,0:T(8,128)S(1)}) fusion(f32[1024,1536]{0,1:T(8,128)} %copy-done.1, f32[1024,16]{0,1:T(8,128)S(1)} %add_rsqrt_fusion.1, f32[1024,16]{0,1:T(8,128)S(1)} %get-tuple-element.21, ...), kind=kOutput, calls=%fused_computation.18 | convolution fusion | flops 40337408 | bytes 11403264 | tf_op jit(solution)/shard_map/nhj,hij->nhi/dot_general | solution.py:45
  124.6 2.0 fusion.7
  126.6 1.0 copy-done.2
  127.6 0.4 copy-done.3
  128.0 3.5 %fusion = f32[512,1536]{0,1:T(8,128)} fusion(bf16[1024,512]{1,0:T(8,128)(2,1)S(1)} %copy-done, bf16[1024,512]{0,1:T(8,128)(2,1)S(1)} %bitcast.92, bf16[1024,512]{0,1:T(8,128)(2,1)S(1)} %bitcast.90, bf16[1024,512]{0,1:T(8,128)(2,1)S(1)} %bitcast.88), kind=kOutput, calls=%fused_computation.2 | convolution fusion | flops 1620836352 | bytes 7340032 | tf_op jit(solution)/shard_map/dot_general | solution.py:57
  131.5 3.5 %copy.20 = f32[512,1536]{1,0:T(8,128)} copy(f32[512,1536]{0,1:T(8,128)} %fusion) | data formatting | bytes 6291456
  135.0 0.0 reduce-scatter.7.cloned.1.call-update
  135.1 0.0 reduce-scatter.5.cloned.1.call-start
  135.1 41.0 %reduce-scatter.7.cloned.1.call-done = f32[64,1536]{1,0:T(8,128)} async-done(((f32[512,1536]{1,0:T(8,128)}), f32[64,1536]{1,0:T(8,128)}) %reduce-scatter.7.cloned.1.call-update) | async-done | bytes 393232
  176.1 1.3 copy.21
  177.4 1.0 copy.18
  178.4 0.0 reduce-scatter.5.cloned.1.call-update
  178.4 4.9 %convolution_convert_fusion = bf16[1024,512]{1,0:T(8,128)(2,1)} fusion(bf16[512,1536]{1,0:T(8,128)(2,1)} %copy-done.6, bf16[1024,512]{0,1:T(8,128)(2,1)} %bitcast.93, bf16[1024,512]{0,1:T(8,128)(2,1)} %bitcast.91, bf16[1024,512]{0,1:T(8,128)(2,1)S(1)} %bitcast.89), kind=kOutput, calls=%fused_computation.27 | convolution fusion | flops 1620574208 | bytes 5767168 | tf_op jit(solution)/shard_map/dot_general | solution.py:66
  183.3 7.4 %reduce-scatter.5.cloned.1.call-done = f32[64,3,256]{2,0,1:T(8,128)} async-done(((f32[64,3,512]{2,0,1:T(8,128)}), f32[64,3,256]{2,0,1:T(8,128)}) %reduce-scatter.5.cloned.1.call-update) | async-done | bytes 196624 | tf_op jit(solution)/shard_map/reduce_scatter | solution.py:63
  190.7 1.6 slice_bitcast_fusion
  (23 shorter events, 0.1 us)
Async XLA Ops:
  7.2 2.4 %copy-start = (bf16[1024,512]{1,0:T(8,128)(2,1)S(1)}, bf16[1024,512]{1,0:T(8,128)(2,1)}, u32[]{:S(2)}) copy-start(bf16[1024,512]{1,0:T(8,128)(2,1)} %param.5) | copy-start | bytes 3145732
  7.2 2.3 %copy-start.4 = (bf16[512,512]{1,0:T(8,128)(2,1)S(1)}, bf16[512,512]{1,0:T(8,128)(2,1)}, u32[]{:S(2)}) copy-start(bf16[512,512]{1,0:T(8,128)(2,1)} %param.9) | copy-start | bytes 1572868
  7.2 109.1 %all-reduce.3.cloned.1.call-start = ((), (), s32[]{:S(2)}) async-start(), calls=%async_computation.4 | async-start | bytes 1048576 | tf_op jit(solution)/shard_map/psum | solution.py:39
  9.6 1.9 copy-start.6
  11.5 2.7 %copy-start.1 = (f32[1024,1536]{0,1:T(8,128)}, f32[1024,1536]{0,1:T(8,128)S(1)}, u32[]{:S(2)}) copy-start(f32[1024,1536]{0,1:T(8,128)S(1)} %convolution_bitcast_fusion) | copy-start | bytes 18874372
  23.5 152.7 %reduce-scatter.7.cloned.1.call-start = ((), (), s32[]{:S(2)}) async-start(), calls=%async_computation.3 | async-start | bytes 3538944
  116.3 1.4 copy-start.5
  117.7 6.9 %slice-start = ((s8[6291456]{0:T(1024)(128)(4,1)}), s8[4194304]{0:T(1024)(128)(4,1)S(1)}, s32[]{:S(2)}) async-start(s8[6291456]{0:T(1024)(128)(4,1)} %bitcast.82), calls=%async_computation.5 | async-start | bytes 8388608
  119.9 4.6 %slice-start.1 = ((s8[6291456]{0:T(1024)(128)(4,1)}), s8[2097152]{0:T(1024)(128)(4,1)S(1)}, s32[]{:S(2)}) async-start(s8[6291456]{0:T(1024)(128)(4,1)} %bitcast.82), calls=%async_computation.6 | async-start | bytes 4194304
  126.6 1.0 copy-start.2
  126.6 1.4 copy-start.3
  135.1 55.6 %reduce-scatter.5.cloned.1.call-start = ((), (), s32[]{:S(2)}) async-start(), calls=%async_computation.2 | async-start | bytes 589824 | tf_op jit(solution)/shard_map/reduce_scatter | solution.py:63
Sparse Core Ops, SparseCore 0:
  23.6 92.6 all-reduce.2
  135.2 40.8 reduce-scatter.6
  178.5 12.1 reduce-scatter.4
where the time goes:
time: 199 us
  waiting for transfers between devices  141 us (71%)
  matrix products  23 us (12%)
  local copies, waits for them, and re-layouts  14.7 us (7%)
  between operations  14 us (7%)
  other arithmetic  5.74 us (3%)
    psum x1, waiting for transfers between devices, local(): lax.psum((state_part, grad_part), ('points', 'mp', 'sub'))  92.8 us
    unnamed x4, waiting for transfers between devices  41.1 us
    unnamed x23, local copies, waits for them, and re-layouts  12 us
    reduce_scatter x1, waiting for transfers between devices, local(): lax.psum_scatter(row_part.reshape(row_block, 3, width), 'mp', scatter_dim...  7.44 us
    dot_general x1, matrix products, local(): lax.dot_general(grad_cat, w_all, (((1,), (1,)), ((), ())), preferred_elem...  4.86 us
    dot_general x1, matrix products, local(): jnp.einsum('nhj,hij->nhi', value_low, grad_low, preferred_element_type=f32)  4.54 us
  transfers between devices with their start and end apart: 3, of which 3 were waited for; matrix products, arithmetic and copies ran while one was open for 2% of the time, Pallas kernels for 0%

commit v1 on v0

v1 whole, which is shorter than its diff:
```python
import functools

import jax
import jax.numpy as jnp
from jax import lax
from jax.experimental import pallas as pl
from jax.experimental.pallas import tpu as pltpu
from jax.sharding import PartitionSpec as P

HS = 32
F32 = jnp.float32
BF16 = jnp.bfloat16
NT = (((1,), (1,)), ((), ()))
TN = (((0,), (0,)), ((), ()))
NN = (((1,), (0,)), ((), ()))
VMEM = pl.BlockSpec(memory_space=pltpu.VMEM)
PARAMS = pltpu.CompilerParams(vmem_limit_bytes=32 * 1024 * 1024)


def dot(a, b, dims):
    return lax.dot_general(a, b, dims, preferred_element_type=F32)


def split(x):
    high = x.astype(BF16)
    return high, (x - high.astype(F32)).astype(BF16)


def head_mask(size):
    rows = lax.broadcasted_iota(jnp.int32, (size, size), 0) // HS
    cols = lax.broadcasted_iota(jnp.int32, (size, size), 1) // HS
    return rows == cols


def averager(size):
    return jnp.where(head_mask(size), F32(1.0 / HS), F32(0.0)).astype(BF16)


def pack(full):
    size = full.shape[0]
    kept = jnp.where(head_mask(size), full, F32(0.0))
    total = kept[:HS]
    for i in range(1, size // HS):
        total = total + kept[i * HS : (i + 1) * HS]
    return total


def unpack(packed):
    size = packed.shape[1]
    tiled = jnp.concatenate([packed] * (size // HS), axis=0)
    return jnp.where(head_mask(size), tiled, F32(0.0))


def place(refs, value, x_first):
    z, x, s = lax.axis_index("points"), lax.axis_index("mp"), lax.axis_index("sub")
    nz, nx, ns = lax.axis_size("points"), lax.axis_size("mp"), lax.axis_size("sub")
    rb, cb = value.shape[0] // (nz * ns), value.shape[1] // nx
    for zb in range(nz):
        for sb in range(ns):
            row = (zb * ns + sb) * rb
            for xb in range(nx):
                block = value[row : row + rb, xb * cb : (xb + 1) * cb]
                first, second = (x ^ xb, z ^ zb) if x_first else (z ^ zb, x ^ xb)
                refs[s ^ sb, first, second] = block


def cross_kernel(p_ref, c_ref, wq_ref, m_ref, g_ref):
    width = p_ref.shape[1]
    ns = lax.axis_size("sub")
    s = lax.axis_index("sub")
    half = width // ns
    parts = []
    for g in range(ns):
        cols = slice(g * half, (g + 1) * half)
        cross = dot(p_ref[...], c_ref[:, cols], TN)
        high, low = split(cross)
        wq = wq_ref[:, cols]
        g_ref[s ^ g] = pack(dot(wq, high, TN) + dot(wq, low, TN))
        parts.append(cross)
    place(m_ref, jnp.concatenate(parts, axis=1), True)


def norm_kernel(p_ref, wk_ref, wv_ref, kn_ref, kr_ref, vn_ref, vr_ref, s_ref, wc_ref):
    rows, width = p_ref.shape
    ns = lax.axis_size("sub")
    s = lax.axis_index("sub")
    half = width // ns
    mean = averager(half)
    for w, w_ref in enumerate((wk_ref, wv_ref)):
        for g in range(ns):
            cols = slice(g * half, (g + 1) * half)
            raw = w_ref[:, cols]
            high, low = split(raw.astype(F32) - dot(raw, mean, NN))
            wc_ref[w, 0, :, cols] = high
            wc_ref[w, 1, :, cols] = low
    for g in range(ns):
        cols = slice(g * half, (g + 1) * half)
        for w, (n_ref, r_ref) in enumerate(((kn_ref, kr_ref), (vn_ref, vr_ref))):
            chunk = 256
            for r in range(rows // chunk):
                span = slice(r * chunk, (r + 1) * chunk)
                p = p_ref[span, :]
                centred = dot(p, wc_ref[w, 0, :, cols], NN) + dot(p, wc_ref[w, 1, :, cols], NN)
                high, low = split(centred * centred)
                inverse = lax.rsqrt(dot(high, mean, NN) + dot(low, mean, NN) + 1e-05)
                n_ref[span, cols] = centred * inverse
                r_ref[span, cols] = inverse
        s_ref[s ^ g] = pack(dot(kn_ref[:, cols].astype(BF16), vn_ref[:, cols].astype(BF16), TN))


def back_kernel(total, key, p_ref, n_ref, r_ref, o_ref, own_ref, got_ref, w_ref, gl_ref):
    rows, width = p_ref.shape
    ns = lax.axis_size("sub")
    s = lax.axis_index("sub")
    half = width // ns
    mean = averager(half)
    parts = []
    for g in range(ns):
        cols = slice(g * half, (g + 1) * half)
        packed = jnp.where(s == g, own_ref[...], got_ref[...])
        low = (packed / total).astype(BF16).astype(F32)
        full = unpack(low)
        if key:
            grouped = dot(mean, full.astype(BF16), NN)
            dims = NT
        else:
            grouped = dot(full.astype(BF16), mean, NN)
            dims = NN
        high, small = split(full - grouped)
        chunk = 256
        for r in range(rows // chunk):
            span = slice(r * chunk, (r + 1) * chunk)
            other = o_ref[span, cols].astype(BF16)
            grad = dot(other, high, dims) + dot(other, small, dims)
            normed = n_ref[span, cols]
            ph, pl_ = split(grad * normed)
            second = dot(ph, mean, NN) + dot(pl_, mean, NN)
            gl_ref[span, cols] = ((grad - normed * second) * r_ref[span, cols]).astype(BF16)
        parts.append(dot(p_ref[...], gl_ref[:, cols], TN))
    place(w_ref, jnp.concatenate(parts, axis=1), key)


def points_kernel(total, c_ref, gk_ref, gv_ref, wq_ref, wk_ref, wv_ref, own_ref, got_ref, m_ref, gp_ref, gq_ref, q_ref):
    rows, width = c_ref.shape
    ns, nx = lax.axis_size("sub"), lax.axis_size("mp")
    s, x = lax.axis_index("sub"), lax.axis_index("mp")
    half = width // ns
    lows = []
    for g in range(ns):
        cols = slice(g * half, (g + 1) * half)
        packed = jnp.where(s == g, own_ref[...], got_ref[...])
        low = (packed / total).astype(BF16).astype(F32)
        lows.append(low)
        q_ref[:, cols] = dot(c_ref[:, cols], unpack(low).astype(BF16), NT).astype(BF16)
    whole = jnp.concatenate(lows, axis=1)
    cb = width // nx
    high, rest = split(m_ref[...])
    third = (m_ref[...] - high.astype(F32) - rest.astype(F32)).astype(BF16)
    for xb in range(nx):

        @pl.when(x == xb)
        def _():
            state = unpack(whole[:, xb * cb : (xb + 1) * cb]).astype(BF16)
            gq_ref[...] = (dot(high, state, NT) + dot(rest, state, NT) + dot(third, state, NT)) / total

    chunk = 256
    for r in range(rows // chunk):
        span = slice(r * chunk, (r + 1) * chunk)
        acc = dot(gk_ref[span, :], wk_ref[...], NT) + dot(gv_ref[span, :], wv_ref[...], NT)
        gp_ref[span, :] = (acc + dot(q_ref[span, :], wq_ref[...], NT)).astype(BF16)


def pairs(size, bit):
    return [(i, i ^ bit) for i in range(size)]


def swap(value, axis, bit):
    return lax.ppermute(value, axis, pairs(lax.axis_size(axis), bit))


def bits(axis):
    bit = 1
    while bit < lax.axis_size(axis):
        yield bit
        bit *= 2


def sum_all(value):
    own = value[0] + swap(value[1], "sub", 1)
    for axis in ("mp", "points"):
        for bit in bits(axis):
            own = own + swap(own, axis, bit)
    return own, swap(own, "sub", 1)


def scatter(value, axes):
    got = swap(value[1], "sub", 1)
    kept = value[0]
    for place_, axis in enumerate(axes):
        for bit in bits(axis):
            shape = kept.shape
            if place_ == 0:
                view = lambda a, i: a.reshape((shape[0] // 2, 2) + shape[1:])[:, i]
            else:
                view = lambda a, i: a.reshape((shape[0] // 2, 2) + shape[1:])[:, i]
            send = view(kept, 1) + view(got, 1)
            kept = view(kept, 0) + view(got, 0)
            got = swap(send, axis, bit)
        kept, got = kept[0], got[0]
    return kept + got


def local(points_in, cotangent, w_query, w_key, w_value):
    rows, width = points_in.shape
    nz, nx, ns = lax.axis_size("points"), lax.axis_size("mp"), lax.axis_size("sub")
    total = rows * nz * nx * ns
    half = width // ns
    rb, cb = width // (nz * ns), width // nx
    by_x = jax.ShapeDtypeStruct((ns, nx, nz, rb, cb), F32)
    by_z = jax.ShapeDtypeStruct((ns, nz, nx, rb, cb), F32)
    state = jax.ShapeDtypeStruct((ns, HS, half), F32)
    wide = jax.ShapeDtypeStruct((rows, width), F32)
    low = jax.ShapeDtypeStruct((rows, width), BF16)

    cross, grad_part = pl.pallas_call(
        cross_kernel, out_shape=(by_x, state), in_specs=[VMEM] * 3, out_specs=(VMEM,) * 2, compiler_params=PARAMS, name="cross"
    )(points_in, cotangent, w_query)
    key_norm, key_inv, value_norm, value_inv, state_part = pl.pallas_call(
        norm_kernel,
        out_shape=(wide, wide, wide, wide, state),
        in_specs=[VMEM] * 3,
        out_specs=(VMEM,) * 5,
        scratch_shapes=[pltpu.VMEM((2, 2, width, width), BF16)],
        compiler_params=PARAMS,
        name="norm",
    )(points_in, w_key, w_value)
    g_own, g_got = sum_all(grad_part)
    s_own, s_got = sum_all(state_part)
    m_total = scatter(cross, ("mp", "points"))

    def back(key, normed, inverse, other):
        return pl.pallas_call(
            functools.partial(back_kernel, total, key),
            out_shape=(by_x if key else by_z, low),
            in_specs=[VMEM] * 6,
            out_specs=(VMEM,) * 2,
            compiler_params=PARAMS,
            name="back_key" if key else "back_value",
        )(points_in, normed, inverse, other, g_own, g_got)

    key_blocks, key_low = back(True, key_norm, key_inv, value_norm)
    value_blocks, value_low = back(False, value_norm, value_inv, key_norm)
    grad_key = scatter(key_blocks, ("mp", "points")) / total
    grad_value = scatter(value_blocks, ("points", "mp")) / total
    grad_points, grad_query = pl.pallas_call(
        functools.partial(points_kernel, total),
        out_shape=(low, jax.ShapeDtypeStruct((rb, cb), F32)),
        in_specs=[VMEM] * 9,
        out_specs=(VMEM,) * 2,
        scratch_shapes=[pltpu.VMEM((rows, width), BF16)],
        compiler_params=PARAMS,
        name="grad_points",
    )(cotangent, key_low, value_low, w_query, w_key, w_value, s_own, s_got, m_total)
    return grad_points, grad_query, grad_key, grad_value


def solution(mesh):
    whole = P(("groups", "points", "mp", "sub"), None)
    block = P(("groups", "points", "sub"), "mp")
    return jax.shard_map(
        local,
        mesh=mesh,
        in_specs=(whole, whole, P(), P(), P()),
        out_specs=(whole, block, block, block),
        check_vma=False,
    )
```

time: 199 us -> 73 us (0.37)
  waiting for transfers between devices: 141 us -> 25.3 us
  matrix products: 23 us -> 0 us
  starting transfers between devices: 0.12 us -> 22.8 us
  Pallas kernels: 0 us -> 18.5 us
  between operations: 14 us -> 0.86 us
  local copies, waits for them, and re-layouts: 14.7 us -> 3.67 us
  other arithmetic: 5.74 us -> 1.69 us
    psum x1 -> x0, waiting for transfers between devices: 92.8 us -> none  [local(): lax.psum((state_part, grad_part), ('points', 'mp', 'sub'))]
    unnamed x4 -> x0, waiting for transfers between devices: 41.1 us -> none
    ppermute x0 -> x22, waiting for transfers between devices: none -> 25.3 us  [swap(): return lax.ppermute(value, axis, pairs(lax.axis_size(axis), bit))]
    dot_general x8 -> x0, matrix products: 23 us -> none  [the longest x1 4.86 us: local(): lax.dot_general(grad_cat, w_all, (((1,), (1,)), ((), ())), preferred_elem...]
    ppermute x0 -> x22, starting transfers between devices: none -> 22.8 us  [swap(): return lax.ppermute(value, axis, pairs(lax.axis_size(axis), bit))]
    pallas_call x0 -> x5, Pallas kernels: none -> 18.5 us  [the longest x1 7.7 us: local(): pl.pallas_call(norm_kernel, out_shape=(wide, wide, wide, wide, state), in...]
    unnamed x23 -> x14, local copies, waits for them, and re-layouts: 12 us -> 3.5 us
    reduce_scatter x1 -> x0, waiting for transfers between devices: 7.44 us -> none  [local(): lax.psum_scatter(row_part.reshape(row_block, 3, width), 'mp', scatter_dim...]
  transfers between devices with their start and end apart: 3 -> 22, of which waited for: 3 -> 10; matrix products, arithmetic and copies ran while one was open for 2% -> 2% of each run, Pallas kernels for 0% -> 23%
where the time goes in v1:
time: 73 us; the launch traced here: 72.7 us
  waiting for transfers between devices  25.3 us (35%)
  starting transfers between devices  22.8 us (31%)
  Pallas kernels  18.5 us (25%)
  local copies, waits for them, and re-layouts  3.67 us (5%)
  other arithmetic  1.69 us (2%)
  between operations  0.86 us (1%)
    ppermute x22, waiting for transfers between devices, swap(): return lax.ppermute(value, axis, pairs(lax.axis_size(axis), bit))  25.3 us
    ppermute x22, starting transfers between devices, swap(): return lax.ppermute(value, axis, pairs(lax.axis_size(axis), bit))  22.8 us
    pallas_call x1, Pallas kernels, local(): pl.pallas_call(norm_kernel, out_shape=(wide, wide, wide, wide, state), in...  7.7 us
    pallas_call x2, Pallas kernels, back(): pl.pallas_call(functools.partial(back_kernel, total, key), out_shape=(by_...  5.35 us
    pallas_call x1, Pallas kernels, local(): pl.pallas_call(functools.partial(points_kernel, total), out_shape=(low, j...  3.53 us
    unnamed x14, local copies, waits for them, and re-layouts  3.5 us
    pallas_call x1, Pallas kernels, local(): pl.pallas_call(cross_kernel, out_shape=(by_x, state), in_specs=[VMEM] * 3...  1.9 us
  transfers between devices with their start and end apart: 22, of which 10 were waited for; matrix products, arithmetic and copies ran while one was open for 2% of the time, Pallas kernels for 23%

profile of v1, /device:TPU:0, one launch (start us, length us, event | category | flops | bytes accessed | tf_op | source)
XLA Modules:
  0.0 72.7 jit_solution(8567169549582248555)
XLA Ops:
  0.6 1.2 %copy-done = bf16[1024,512]{1,0:T(8,128)(2,1)S(1)} copy-done((bf16[1024,512]{1,0:T(8,128)(2,1)S(1)}, bf16[1024,512]{1,0:T(8,128)(2,1)}, u32[]{:S(2)}) %copy-start) | copy-done | bytes 1048600
  1.9 1.2 %copy-done.1 = bf16[1024,512]{1,0:T(8,128)(2,1)S(1)} copy-done((bf16[1024,512]{1,0:T(8,128)(2,1)S(1)}, bf16[1024,512]{1,0:T(8,128)(2,1)}, u32[]{:S(2)}) %copy-start.1) | copy-done | bytes 1048600
  3.1 1.0 %copy-done.3 = bf16[512,512]{1,0:T(8,128)(2,1)S(1)} copy-done((bf16[512,512]{1,0:T(8,128)(2,1)S(1)}, bf16[512,512]{1,0:T(8,128)(2,1)}, u32[]{:S(2)}) %copy-start.3) | copy-done | bytes 524312
  4.1 1.9 %cross.1 = (f32[2,2,4,64,256]{4,3,2,1,0:T(8,128)S(1)}, f32[2,32,256]{2,1,0:T(8,128)S(1)}) custom-call(bf16[1024,512]{1,0:T(8,128)(2,1)S(1)} %copy-done, bf16[1024,512]{1,0:T(8,128)(2,1)S(1)} %copy-done.1, bf16[512,512]{1,0:T(8,128)(2,1)S(1)} %copy-done.3), custom_call_target="tpu_custom_call" | custom-call | tf_op jit(solution)/shard_map/cross/pallas_call | solution.py:225
  6.6 0.9 %collective-permute-done = f32[32,256]{1,0:T(8,128)S(1)} collective-permute-done((f32[32,256]{1,0:T(8,128)S(1)}, f32[32,256]{1,0:T(8,128)S(1)}, u32[]{:S(2)}, u32[]{:S(2)}) %collective-permute-start) | collective-permute-done | bytes 32800 | tf_op jit(solution)/shard_map/ppermute | solution.py:178
  7.4 2.8 %collective-permute-start.1 = (f32[32,256]{1,0:T(8,128)S(1)}, f32[32,256]{1,0:T(8,128)S(1)}, u32[]{:S(2)}, u32[]{:S(2)}) collective-permute-start(f32[32,256]{1,0:T(8,128)S(1)} %bitcast_add_fusion.1), channel_id=1, source_target_pairs={{0,2},{2,0},{1,3},{3,1},{4,6},{6,4},{5,7},{7,5},{8,10},{10,8},{9,1... | collective-permute-start | bytes 98312 | tf_op jit(solution)/shard_map/ppermute | solution.py:178
  10.3 7.7 %norm.1 = (f32[1024,512]{1,0:T(8,128)S(1)}, f32[1024,512]{1,0:T(8,128)S(1)}, f32[1024,512]{1,0:T(8,128)S(1)}, f32[1024,512]{1,0:T(8,128)S(1)}, f32[2,32,256]{2,1,0:T(8,128)S(1)}) custom-call(bf16[1024,512]{1,0:T(8,128)(2,1)S(1)} %copy-done, bf16[512,512]{1,0:T(8,128)(2,1)S(1)} %copy-done.5, bf16[512,512]{1,0:T(8,128)(2,1)S(1)} %copy-done.6), custom_call_target="tpu_custom_call" | custom-call | tf_op jit(solution)/shard_map/norm/pallas_call | solution.py:228
  18.0 1.6 %collective-permute-start.2 = (f32[32,256]{1,0:T(8,128)S(1)}, f32[32,256]{1,0:T(8,128)S(1)}, u32[]{:S(2)}, u32[]{:S(2)}) collective-permute-start(f32[32,256]{1,0:T(8,128)S(1)} %add.234), channel_id=1, source_target_pairs={{0,4},{4,0},{8,12},{12,8},{1,5},{5,1},{9,13},{13,9},{2,6},{6,2},{1... | collective-permute-start | bytes 98312 | tf_op jit(solution)/shard_map/ppermute | solution.py:178
  19.6 2.3 %collective-permute-done.2 = f32[32,256]{1,0:T(8,128)S(1)} collective-permute-done((f32[32,256]{1,0:T(8,128)S(1)}, f32[32,256]{1,0:T(8,128)S(1)}, u32[]{:S(2)}, u32[]{:S(2)}) %collective-permute-start.2) | collective-permute-done | bytes 32800 | tf_op jit(solution)/shard_map/ppermute | solution.py:178
  22.0 2.6 %collective-permute-start.3 = (f32[32,256]{1,0:T(8,128)S(1)}, f32[32,256]{1,0:T(8,128)S(1)}, u32[]{:S(2)}, u32[]{:S(2)}) collective-permute-start(f32[32,256]{1,0:T(8,128)S(1)} %add.235), channel_id=1, source_target_pairs={{0,8},{4,12},{8,0},{12,4},{1,9},{5,13},{9,1},{13,5},{2,10},{6,14},... | collective-permute-start | bytes 98312 | tf_op jit(solution)/shard_map/ppermute | solution.py:178
  25.2 1.6 %collective-permute-done.3 = f32[32,256]{1,0:T(8,128)S(1)} collective-permute-done((f32[32,256]{1,0:T(8,128)S(1)}, f32[32,256]{1,0:T(8,128)S(1)}, u32[]{:S(2)}, u32[]{:S(2)}) %collective-permute-start.3) | collective-permute-done | bytes 32800 | tf_op jit(solution)/shard_map/ppermute | solution.py:178
  27.4 1.1 %collective-permute-done.6 = f32[32,256]{1,0:T(8,128)S(1)} collective-permute-done((f32[32,256]{1,0:T(8,128)S(1)}, f32[32,256]{1,0:T(8,128)S(1)}, u32[]{:S(2)}, u32[]{:S(2)}) %collective-permute-start.6) | collective-permute-done | bytes 32800 | tf_op jit(solution)/shard_map/ppermute | solution.py:178
  28.6 1.6 %collective-permute-start.7 = (f32[32,256]{1,0:T(8,128)S(1)}, f32[32,256]{1,0:T(8,128)S(1)}, u32[]{:S(2)}, u32[]{:S(2)}) collective-permute-start(f32[32,256]{1,0:T(8,128)S(1)} %add.238), channel_id=1, source_target_pairs={{0,4},{4,0},{8,12},{12,8},{1,5},{5,1},{9,13},{13,9},{2,6},{6,2},{1... | collective-permute-start | bytes 98312 | tf_op jit(solution)/shard_map/ppermute | solution.py:178
  30.1 2.8 %back_key.1 = (f32[2,2,4,64,256]{4,3,2,1,0:T(8,128)S(1)}, bf16[1024,512]{1,0:T(8,128)(2,1)S(1)}) custom-call(bf16[1024,512]{1,0:T(8,128)(2,1)S(1)} %copy-done, f32[1024,512]{1,0:T(8,128)S(1)} %get-tuple-element.17.n_ref.o_ref, f32[1024,512]{1,0:T(8,128)S(1)} %get-tuple-element.18.r_ref, f32[1024,512]{1,0:T(8,128)S(1)} %get-tuple-element.19.o_ref.n_ref, ...), custom_call_target="tpu_custom_call" | custom-call | tf_op jit(solution)/shard_map/back_key/pallas_call | solution.py:242
  33.1 1.8 %collective-permute-start.8 = (f32[32,256]{1,0:T(8,128)S(1)}, f32[32,256]{1,0:T(8,128)S(1)}, u32[]{:S(2)}, u32[]{:S(2)}) collective-permute-start(f32[32,256]{1,0:T(8,128)S(1)} %add.239), channel_id=1, source_target_pairs={{0,8},{4,12},{8,0},{12,4},{1,9},{5,13},{9,1},{13,5},{2,10},{6,14},... | collective-permute-start | bytes 98312 | tf_op jit(solution)/shard_map/ppermute | solution.py:178
  34.9 2.6 %back_value.1 = (f32[2,4,2,64,256]{4,3,2,1,0:T(8,128)S(1)}, bf16[1024,512]{1,0:T(8,128)(2,1)S(1)}) custom-call(bf16[1024,512]{1,0:T(8,128)(2,1)S(1)} %copy-done, f32[1024,512]{1,0:T(8,128)S(1)} %get-tuple-element.19.o_ref.n_ref, f32[1024,512]{1,0:T(8,128)S(1)} %get-tuple-element.22.r_ref, f32[1024,512]{1,0:T(8,128)S(1)} %get-tuple-element.17.n_ref.o_ref, ...), custom_call_target="tpu_custom_call" | custom-call | tf_op jit(solution)/shard_map/back_value/pallas_call | solution.py:242
  38.1 0.6 collective-permute-start.11
  38.9 1.5 %collective-permute-start.15 = (f32[1,4,64,256]{3,2,1,0:T(8,128)S(1)}, f32[1,4,64,256]{3,2,1,0:T(8,128)S(1)}, u32[]{:S(2)}, u32[]{:S(2)}) collective-permute-start(f32[1,4,64,256]{3,2,1,0:T(8,128)S(1)} %get-tuple-element.31), channel_id=1, source_target_pairs={{0,2},{2,0},{1,3},{3,1},{4,6},{6,4},{5,7},{7,5},{8,10},{10,8},{9,1... | collective-permute-start | bytes 786440 | tf_op jit(solution)/shard_map/ppermute | solution.py:178
  40.4 6.9 %collective-permute-done.11 = f32[1,4,64,256]{3,2,1,0:T(8,128)S(1)} collective-permute-done((f32[1,4,64,256]{3,2,1,0:T(8,128)S(1)}, f32[1,4,64,256]{3,2,1,0:T(8,128)S(1)}, u32[]{:S(2)}, u32[]{:S(2)}) %collective-permute-start.11) | collective-permute-done | bytes 262176 | tf_op jit(solution)/shard_map/ppermute | solution.py:178
  47.3 0.8 %collective-permute-start.12 = (f32[2,64,256]{2,1,0:T(8,128)S(1)}, f32[2,64,256]{2,1,0:T(8,128)S(1)}, u32[]{:S(2)}, u32[]{:S(2)}) collective-permute-start(f32[2,64,256]{2,1,0:T(8,128)S(1)} %get-tuple-element.43), channel_id=1, source_target_pairs={{0,4},{4,0},{8,12},{12,8},{1,5},{5,1},{9,13},{13,9},{2,6},{6,2},{1... | collective-permute-start | bytes 393224 | tf_op jit(solution)/shard_map/ppermute | solution.py:178
  48.2 1.3 %collective-permute-start.19 = (f32[2,2,64,256]{3,2,1,0:T(8,128)S(1)}, f32[2,2,64,256]{3,2,1,0:T(8,128)S(1)}, u32[]{:S(2)}, u32[]{:S(2)}) collective-permute-start(f32[2,2,64,256]{3,2,1,0:T(8,128)S(1)} %get-tuple-element.35), channel_id=1, source_target_pairs={{0,4},{4,0},{8,12},{12,8},{1,5},{5,1},{9,13},{13,9},{2,6},{6,2},{1... | collective-permute-start | bytes 786440 | tf_op jit(solution)/shard_map/ppermute | solution.py:178
  49.6 4.3 %collective-permute-done.12 = f32[2,64,256]{2,1,0:T(8,128)S(1)} collective-permute-done((f32[2,64,256]{2,1,0:T(8,128)S(1)}, f32[2,64,256]{2,1,0:T(8,128)S(1)}, u32[]{:S(2)}, u32[]{:S(2)}) %collective-permute-start.12) | collective-permute-done | bytes 131104 | tf_op jit(solution)/shard_map/ppermute | solution.py:178
  53.8 1.3 %collective-permute-start.13 = (f32[1,64,256]{2,1,0:T(8,128)S(1)}, f32[1,64,256]{2,1,0:T(8,128)S(1)}, u32[]{:S(2)}, u32[]{:S(2)}) collective-permute-start(f32[1,64,256]{2,1,0:T(8,128)S(1)} %fusion.24), channel_id=1, source_target_pairs={{0,8},{4,12},{8,0},{12,4},{1,9},{5,13},{9,1},{13,5},{2,10},{6,14},... | collective-permute-start | bytes 196616 | tf_op jit(solution)/shard_map/ppermute | solution.py:178
  55.1 0.8 %collective-permute-start.16 = (f32[2,64,256]{2,1,0:T(8,128)S(1)}, f32[2,64,256]{2,1,0:T(8,128)S(1)}, u32[]{:S(2)}, u32[]{:S(2)}) collective-permute-start(f32[2,64,256]{2,1,0:T(8,128)S(1)} %get-tuple-element.41), channel_id=1, source_target_pairs={{0,4},{4,0},{8,12},{12,8},{1,5},{5,1},{9,13},{13,9},{2,6},{6,2},{1... | collective-permute-start | bytes 393224 | tf_op jit(solution)/shard_map/ppermute | solution.py:178
  55.9 4.7 %collective-permute-done.19 = f32[2,2,64,256]{3,2,1,0:T(8,128)S(1)} collective-permute-done((f32[2,2,64,256]{3,2,1,0:T(8,128)S(1)}, f32[2,2,64,256]{3,2,1,0:T(8,128)S(1)}, u32[]{:S(2)}, u32[]{:S(2)}) %collective-permute-start.19) | collective-permute-done | bytes 262176 | tf_op jit(solution)/shard_map/ppermute | solution.py:178
  60.8 3.5 %grad_points.1 = (bf16[1024,512]{1,0:T(8,128)(2,1)}, f32[64,256]{1,0:T(8,128)}) custom-call(bf16[1024,512]{1,0:T(8,128)(2,1)S(1)} %copy-done.2, bf16[1024,512]{1,0:T(8,128)(2,1)S(1)} %get-tuple-element.21.gk_ref, bf16[1024,512]{1,0:T(8,128)(2,1)S(1)} %get-tuple-element.23.gv_ref, bf16[512,512]{1,0:T(8,128)(2,1)S(1)} %copy-done.4, ...), custom_call_target="tpu_custom_call" | custom-call | tf_op jit(solution)/shard_map/grad_points/pallas_call | solution.py:255
  64.4 3.0 %collective-permute-start.17 = (f32[1,64,256]{2,1,0:T(8,128)S(1)}, f32[1,64,256]{2,1,0:T(8,128)S(1)}, u32[]{:S(2)}, u32[]{:S(2)}) collective-permute-start(f32[1,64,256]{2,1,0:T(8,128)S(1)} %fusion.20), channel_id=1, source_target_pairs={{0,8},{4,12},{8,0},{12,4},{1,9},{5,13},{9,1},{13,5},{2,10},{6,14},... | collective-permute-start | bytes 196616 | tf_op jit(solution)/shard_map/ppermute | solution.py:178
  67.8 0.6 collective-permute-start.21
  68.4 1.2 %collective-permute-done.17 = f32[1,64,256]{2,1,0:T(8,128)S(1)} collective-permute-done((f32[1,64,256]{2,1,0:T(8,128)S(1)}, f32[1,64,256]{2,1,0:T(8,128)S(1)}, u32[]{:S(2)}, u32[]{:S(2)}) %collective-permute-start.17) | collective-permute-done | bytes 65568 | tf_op jit(solution)/shard_map/ppermute | solution.py:178
  69.6 0.6 fusion.23
  70.3 1.8 %collective-permute-done.21 = f32[1,64,256]{2,1,0:T(8,128)S(1)} collective-permute-done((f32[1,64,256]{2,1,0:T(8,128)S(1)}, f32[1,64,256]{2,1,0:T(8,128)S(1)}, u32[]{:S(2)}, u32[]{:S(2)}) %collective-permute-start.21) | collective-permute-done | bytes 65568 | tf_op jit(solution)/shard_map/ppermute | solution.py:178
  72.1 0.6 fusion.19
  (56 shorter events, 3.4 us)
Async XLA Ops:
  0.6 1.2 %copy-start = (bf16[1024,512]{1,0:T(8,128)(2,1)S(1)}, bf16[1024,512]{1,0:T(8,128)(2,1)}, u32[]{:S(2)}) copy-start(bf16[1024,512]{1,0:T(8,128)(2,1)} %p_ref.7) | copy-start | bytes 3145732
  1.9 1.2 %copy-start.1 = (bf16[1024,512]{1,0:T(8,128)(2,1)S(1)}, bf16[1024,512]{1,0:T(8,128)(2,1)}, u32[]{:S(2)}) copy-start(bf16[1024,512]{1,0:T(8,128)(2,1)} %c_ref.3) | copy-start | bytes 3145732
  3.1 1.0 %copy-start.3 = (bf16[512,512]{1,0:T(8,128)(2,1)S(1)}, bf16[512,512]{1,0:T(8,128)(2,1)}, u32[]{:S(2)}) copy-start(bf16[512,512]{1,0:T(8,128)(2,1)} %wq_ref.3) | copy-start | bytes 1572868
  4.1 6.1 %copy-start.5 = (bf16[512,512]{1,0:T(8,128)(2,1)S(1)}, bf16[512,512]{1,0:T(8,128)(2,1)}, u32[]{:S(2)}) copy-start(bf16[512,512]{1,0:T(8,128)(2,1)} %wk_ref.3) | copy-start | bytes 1572868
  4.1 6.1 %copy-start.6 = (bf16[512,512]{1,0:T(8,128)(2,1)S(1)}, bf16[512,512]{1,0:T(8,128)(2,1)}, u32[]{:S(2)}) copy-start(bf16[512,512]{1,0:T(8,128)(2,1)} %wv_ref.3) | copy-start | bytes 1572868
  6.0 1.4 %collective-permute-start = (f32[32,256]{1,0:T(8,128)S(1)}, f32[32,256]{1,0:T(8,128)S(1)}, u32[]{:S(2)}, u32[]{:S(2)}) collective-permute-start(f32[32,256]{1,0:T(8,128)S(1)} %slice_bitcast_fusion.16), channel_id=1, source_target_pairs={{0,1},{1,0},{2,3},{3,2},{4,5},{5,4},{6,7},{7,6},{8,9},{9,8},{10,11... | collective-permute-start | bytes 98312 | tf_op jit(solution)/shard_map/ppermute | solution.py:178
  7.4 10.5 %collective-permute-start.1 = (f32[32,256]{1,0:T(8,128)S(1)}, f32[32,256]{1,0:T(8,128)S(1)}, u32[]{:S(2)}, u32[]{:S(2)}) collective-permute-start(f32[32,256]{1,0:T(8,128)S(1)} %bitcast_add_fusion.1), channel_id=1, source_target_pairs={{0,2},{2,0},{1,3},{3,1},{4,6},{6,4},{5,7},{7,5},{8,10},{10,8},{9,1... | collective-permute-start | bytes 98312 | tf_op jit(solution)/shard_map/ppermute | solution.py:178
  18.0 4.0 %collective-permute-start.2 = (f32[32,256]{1,0:T(8,128)S(1)}, f32[32,256]{1,0:T(8,128)S(1)}, u32[]{:S(2)}, u32[]{:S(2)}) collective-permute-start(f32[32,256]{1,0:T(8,128)S(1)} %add.234), channel_id=1, source_target_pairs={{0,4},{4,0},{8,12},{12,8},{1,5},{5,1},{9,13},{13,9},{2,6},{6,2},{1... | collective-permute-start | bytes 98312 | tf_op jit(solution)/shard_map/ppermute | solution.py:178
  19.6 4.9 %collective-permute-start.5 = (f32[32,256]{1,0:T(8,128)S(1)}, f32[32,256]{1,0:T(8,128)S(1)}, u32[]{:S(2)}, u32[]{:S(2)}) collective-permute-start(f32[32,256]{1,0:T(8,128)S(1)} %slice_bitcast_fusion.15), channel_id=1, source_target_pairs={{0,1},{1,0},{2,3},{3,2},{4,5},{5,4},{6,7},{7,6},{8,9},{9,8},{10,11... | collective-permute-start | bytes 98312 | tf_op jit(solution)/shard_map/ppermute | solution.py:178
  22.0 4.8 %collective-permute-start.3 = (f32[32,256]{1,0:T(8,128)S(1)}, f32[32,256]{1,0:T(8,128)S(1)}, u32[]{:S(2)}, u32[]{:S(2)}) collective-permute-start(f32[32,256]{1,0:T(8,128)S(1)} %add.235), channel_id=1, source_target_pairs={{0,8},{4,12},{8,0},{12,4},{1,9},{5,13},{9,1},{13,5},{2,10},{6,14},... | collective-permute-start | bytes 98312 | tf_op jit(solution)/shard_map/ppermute | solution.py:178
  24.6 4.0 %collective-permute-start.6 = (f32[32,256]{1,0:T(8,128)S(1)}, f32[32,256]{1,0:T(8,128)S(1)}, u32[]{:S(2)}, u32[]{:S(2)}) collective-permute-start(f32[32,256]{1,0:T(8,128)S(1)} %bitcast_add_fusion), channel_id=1, source_target_pairs={{0,2},{2,0},{1,3},{3,1},{4,6},{6,4},{5,7},{7,5},{8,10},{10,8},{9,1... | collective-permute-start | bytes 98312 | tf_op jit(solution)/shard_map/ppermute | solution.py:178
  26.8 3.3 %collective-permute-start.4 = (f32[32,256]{1,0:T(8,128)S(1)}, f32[32,256]{1,0:T(8,128)S(1)}, u32[]{:S(2)}, u32[]{:S(2)}) collective-permute-start(f32[32,256]{1,0:T(8,128)S(1)} %add.236.own_ref), channel_id=1, source_target_pairs={{0,1},{1,0},{2,3},{3,2},{4,5},{5,4},{6,7},{7,6},{8,9},{9,8},{10,11... | collective-permute-start | bytes 98312 | tf_op jit(solution)/shard_map/ppermute | solution.py:178
  26.9 11.2 %collective-permute-start.10 = (f32[2,4,64,256]{3,2,1,0:T(8,128)S(1)}, f32[2,4,64,256]{3,2,1,0:T(8,128)S(1)}, u32[]{:S(2)}, u32[]{:S(2)}) collective-permute-start(f32[2,4,64,256]{3,2,1,0:T(8,128)S(1)} %slice_bitcast_fusion.2), channel_id=1, source_target_pairs={{0,1},{1,0},{2,3},{3,2},{4,5},{5,4},{6,7},{7,6},{8,9},{9,8},{10,11... | collective-permute-start | bytes 1572872 | tf_op jit(solution)/shard_map/ppermute | solution.py:178
  28.6 4.5 %collective-permute-start.7 = (f32[32,256]{1,0:T(8,128)S(1)}, f32[32,256]{1,0:T(8,128)S(1)}, u32[]{:S(2)}, u32[]{:S(2)}) collective-permute-start(f32[32,256]{1,0:T(8,128)S(1)} %add.238), channel_id=1, source_target_pairs={{0,4},{4,0},{8,12},{12,8},{1,5},{5,1},{9,13},{13,9},{2,6},{6,2},{1... | collective-permute-start | bytes 98312 | tf_op jit(solution)/shard_map/ppermute | solution.py:178
  32.9 5.9 %collective-permute-start.14 = (f32[2,4,64,256]{3,2,1,0:T(8,128)S(1)}, f32[2,4,64,256]{3,2,1,0:T(8,128)S(1)}, u32[]{:S(2)}, u32[]{:S(2)}) collective-permute-start(f32[2,4,64,256]{3,2,1,0:T(8,128)S(1)} %slice_bitcast_fusion.1), channel_id=1, source_target_pairs={{0,1},{1,0},{2,3},{3,2},{4,5},{5,4},{6,7},{7,6},{8,9},{9,8},{10,11... | collective-permute-start | bytes 1572872 | tf_op jit(solution)/shard_map/ppermute | solution.py:178
  33.1 5.6 %collective-permute-start.8 = (f32[32,256]{1,0:T(8,128)S(1)}, f32[32,256]{1,0:T(8,128)S(1)}, u32[]{:S(2)}, u32[]{:S(2)}) collective-permute-start(f32[32,256]{1,0:T(8,128)S(1)} %add.239), channel_id=1, source_target_pairs={{0,8},{4,12},{8,0},{12,4},{1,9},{5,13},{9,1},{13,5},{2,10},{6,14},... | collective-permute-start | bytes 98312 | tf_op jit(solution)/shard_map/ppermute | solution.py:178
  37.6 10.6 %collective-permute-start.18 = (f32[4,2,64,256]{3,2,1,0:T(8,128)S(1)}, f32[4,2,64,256]{3,2,1,0:T(8,128)S(1)}, u32[]{:S(2)}, u32[]{:S(2)}) collective-permute-start(f32[4,2,64,256]{3,2,1,0:T(8,128)S(1)} %get-tuple-element.37), channel_id=1, source_target_pairs={{0,1},{1,0},{2,3},{3,2},{4,5},{5,4},{6,7},{7,6},{8,9},{9,8},{10,11... | collective-permute-start | bytes 1572872 | tf_op jit(solution)/shard_map/ppermute | solution.py:178
  38.1 9.2 %collective-permute-start.11 = (f32[1,4,64,256]{3,2,1,0:T(8,128)S(1)}, f32[1,4,64,256]{3,2,1,0:T(8,128)S(1)}, u32[]{:S(2)}, u32[]{:S(2)}) collective-permute-start(f32[1,4,64,256]{3,2,1,0:T(8,128)S(1)} %get-tuple-element.33), channel_id=1, source_target_pairs={{0,2},{2,0},{1,3},{3,1},{4,6},{6,4},{5,7},{7,5},{8,10},{10,8},{9,1... | collective-permute-start | bytes 786440 | tf_op jit(solution)/shard_map/ppermute | solution.py:178
  38.7 22.1 %collective-permute-start.9 = (f32[32,256]{1,0:T(8,128)S(1)}, f32[32,256]{1,0:T(8,128)S(1)}, u32[]{:S(2)}, u32[]{:S(2)}) collective-permute-start(f32[32,256]{1,0:T(8,128)S(1)} %add.240.own_ref), channel_id=1, source_target_pairs={{0,1},{1,0},{2,3},{3,2},{4,5},{5,4},{6,7},{7,6},{8,9},{9,8},{10,11... | collective-permute-start | bytes 98312 | tf_op jit(solution)/shard_map/ppermute | solution.py:178
  38.9 16.2 %collective-permute-start.15 = (f32[1,4,64,256]{3,2,1,0:T(8,128)S(1)}, f32[1,4,64,256]{3,2,1,0:T(8,128)S(1)}, u32[]{:S(2)}, u32[]{:S(2)}) collective-permute-start(f32[1,4,64,256]{3,2,1,0:T(8,128)S(1)} %get-tuple-element.31), channel_id=1, source_target_pairs={{0,2},{2,0},{1,3},{3,1},{4,6},{6,4},{5,7},{7,5},{8,10},{10,8},{9,1... | collective-permute-start | bytes 786440 | tf_op jit(solution)/shard_map/ppermute | solution.py:178
  47.3 13.5 %copy-start.2 = (bf16[1024,512]{1,0:T(8,128)(2,1)S(1)}, bf16[1024,512]{1,0:T(8,128)(2,1)}, u32[]{:S(2)}) copy-start(bf16[1024,512]{1,0:T(8,128)(2,1)} %c_ref.3) | copy-start | bytes 3145732
  47.3 13.5 %copy-start.4 = (bf16[512,512]{1,0:T(8,128)(2,1)S(1)}, bf16[512,512]{1,0:T(8,128)(2,1)}, u32[]{:S(2)}) copy-start(bf16[512,512]{1,0:T(8,128)(2,1)} %wq_ref.3) | copy-start | bytes 1572868
  47.3 6.5 %collective-permute-start.12 = (f32[2,64,256]{2,1,0:T(8,128)S(1)}, f32[2,64,256]{2,1,0:T(8,128)S(1)}, u32[]{:S(2)}, u32[]{:S(2)}) collective-permute-start(f32[2,64,256]{2,1,0:T(8,128)S(1)} %get-tuple-element.43), channel_id=1, source_target_pairs={{0,4},{4,0},{8,12},{12,8},{1,5},{5,1},{9,13},{13,9},{2,6},{6,2},{1... | collective-permute-start | bytes 393224 | tf_op jit(solution)/shard_map/ppermute | solution.py:178
  48.2 12.4 %collective-permute-start.19 = (f32[2,2,64,256]{3,2,1,0:T(8,128)S(1)}, f32[2,2,64,256]{3,2,1,0:T(8,128)S(1)}, u32[]{:S(2)}, u32[]{:S(2)}) collective-permute-start(f32[2,2,64,256]{3,2,1,0:T(8,128)S(1)} %get-tuple-element.35), channel_id=1, source_target_pairs={{0,4},{4,0},{8,12},{12,8},{1,5},{5,1},{9,13},{13,9},{2,6},{6,2},{1... | collective-permute-start | bytes 786440 | tf_op jit(solution)/shard_map/ppermute | solution.py:178
  53.8 6.9 %collective-permute-start.13 = (f32[1,64,256]{2,1,0:T(8,128)S(1)}, f32[1,64,256]{2,1,0:T(8,128)S(1)}, u32[]{:S(2)}, u32[]{:S(2)}) collective-permute-start(f32[1,64,256]{2,1,0:T(8,128)S(1)} %fusion.24), channel_id=1, source_target_pairs={{0,8},{4,12},{8,0},{12,4},{1,9},{5,13},{9,1},{13,5},{2,10},{6,14},... | collective-permute-start | bytes 196616 | tf_op jit(solution)/shard_map/ppermute | solution.py:178
  55.1 9.2 %collective-permute-start.16 = (f32[2,64,256]{2,1,0:T(8,128)S(1)}, f32[2,64,256]{2,1,0:T(8,128)S(1)}, u32[]{:S(2)}, u32[]{:S(2)}) collective-permute-start(f32[2,64,256]{2,1,0:T(8,128)S(1)} %get-tuple-element.41), channel_id=1, source_target_pairs={{0,4},{4,0},{8,12},{12,8},{1,5},{5,1},{9,13},{13,9},{2,6},{6,2},{1... | collective-permute-start | bytes 393224 | tf_op jit(solution)/shard_map/ppermute | solution.py:178
  60.7 7.1 %collective-permute-start.20 = (f32[1,2,64,256]{3,2,1,0:T(8,128)S(1)}, f32[1,2,64,256]{3,2,1,0:T(8,128)S(1)}, u32[]{:S(2)}, u32[]{:S(2)}) collective-permute-start(f32[1,2,64,256]{3,2,1,0:T(8,128)S(1)} %get-tuple-element.39), channel_id=1, source_target_pairs={{0,8},{4,12},{8,0},{12,4},{1,9},{5,13},{9,1},{13,5},{2,10},{6,14},... | collective-permute-start | bytes 393224 | tf_op jit(solution)/shard_map/ppermute | solution.py:178
  64.4 5.2 %collective-permute-start.17 = (f32[1,64,256]{2,1,0:T(8,128)S(1)}, f32[1,64,256]{2,1,0:T(8,128)S(1)}, u32[]{:S(2)}, u32[]{:S(2)}) collective-permute-start(f32[1,64,256]{2,1,0:T(8,128)S(1)} %fusion.20), channel_id=1, source_target_pairs={{0,8},{4,12},{8,0},{12,4},{1,9},{5,13},{9,1},{13,5},{2,10},{6,14},... | collective-permute-start | bytes 196616 | tf_op jit(solution)/shard_map/ppermute | solution.py:178
  67.8 4.3 %collective-permute-start.21 = (f32[1,64,256]{2,1,0:T(8,128)S(1)}, f32[1,64,256]{2,1,0:T(8,128)S(1)}, u32[]{:S(2)}, u32[]{:S(2)}) collective-permute-start(f32[1,64,256]{2,1,0:T(8,128)S(1)} %fusion.16), channel_id=1, source_target_pairs={{0,2},{2,0},{1,3},{3,1},{4,6},{6,4},{5,7},{7,5},{8,10},{10,8},{9,1... | collective-permute-start | bytes 196616 | tf_op jit(solution)/shard_map/ppermute | solution.py:178

commit v2 on v1

v2 whole, which is shorter than its diff:
```python
import functools

import jax
import jax.numpy as jnp
from jax import lax
from jax.experimental import pallas as pl
from jax.experimental.pallas import tpu as pltpu
from jax.sharding import PartitionSpec as P

HS = 32
F32 = jnp.float32
BF16 = jnp.bfloat16
NT = (((1,), (1,)), ((), ()))
TN = (((0,), (0,)), ((), ()))
NN = (((1,), (0,)), ((), ()))
VMEM = pl.BlockSpec(memory_space=pltpu.VMEM)
HBM = pl.BlockSpec(memory_space=pltpu.HBM)
ANY = pl.BlockSpec(memory_space=pl.ANY)
CHUNKS = 4
QUERY_LAST = False
ORDER = "MKVPTKVKV"
US = {"add_key": 5.0, "back_key": 5.0, "back_value": 5.0}

PARAMS = pltpu.CompilerParams(vmem_limit_bytes=16 * 1024 * 1024)


def dot(a, b, dims):
    return lax.dot_general(a, b, dims, preferred_element_type=F32)


def split(x):
    high = x.astype(BF16)
    return high, (x - high.astype(F32)).astype(BF16)


def head_mask(size):
    rows = lax.broadcasted_iota(jnp.int32, (size, size), 0) // HS
    cols = lax.broadcasted_iota(jnp.int32, (size, size), 1) // HS
    return rows == cols


def averager(size):
    return jnp.where(head_mask(size), F32(1.0 / HS), F32(0.0)).astype(BF16)


def pack(full):
    size = full.shape[0]
    kept = jnp.where(head_mask(size), full, F32(0.0))
    total = kept[:HS]
    for i in range(1, size // HS):
        total = total + kept[i * HS : (i + 1) * HS]
    return total


def unpack(packed):
    size = packed.shape[1]
    tiled = jnp.concatenate([packed] * (size // HS), axis=0)
    return jnp.where(head_mask(size), tiled, F32(0.0))


def place(refs, value, x_first):
    z, x, s = lax.axis_index("points"), lax.axis_index("mp"), lax.axis_index("sub")
    nz, nx, ns = lax.axis_size("points"), lax.axis_size("mp"), lax.axis_size("sub")
    rb, cb = value.shape[0] // (nz * ns), value.shape[1] // nx
    for zb in range(nz):
        for sb in range(ns):
            row = (zb * ns + sb) * rb
            for xb in range(nx):
                block = value[row : row + rb, xb * cb : (xb + 1) * cb]
                first, second = (x ^ xb, z ^ zb) if x_first else (z ^ zb, x ^ xb)
                refs[s ^ sb, first, second] = block


def cross_kernel(p_hbm, c_hbm, wq_hbm, m_ref, g_ref, p_ref, pt_ref, c_ref, wq_ref, sums, sems):
    rows, width = p_hbm.shape
    ns = lax.axis_size("sub")
    s = lax.axis_index("sub")
    half = width // ns
    chunk = rows // CHUNKS
    spans = [slice(r * chunk, (r + 1) * chunk) for r in range(CHUNKS)]
    loads = []
    for r, span in enumerate(spans):
        for k, (src, dst) in enumerate(((p_hbm, p_ref), (c_hbm, c_ref))):
            loads.append(pltpu.make_async_copy(src.at[span, :], dst.at[span, :], sems.at[2 * r + k]))
    loads.append(pltpu.make_async_copy(wq_hbm, wq_ref, sems.at[2 * CHUNKS]))
    for load in loads:
        load.start()
    for r, span in enumerate(spans):
        loads[2 * r].wait()
        flipped = p_ref[span, :].T
        pt_ref[:, span] = flipped
        loads[2 * r + 1].wait()
        for g in range(ns):
            cols = slice(g * half, (g + 1) * half)
            part = dot(flipped, c_ref[span, cols], NN)
            sums[:, cols] = part if r == 0 else sums[:, cols] + part
    loads[-1].wait()
    for g in range(ns):
        cols = slice(g * half, (g + 1) * half)
        high, low = split(sums[:, cols])
        wq = wq_ref[:, cols]
        g_ref[s ^ g] = pack(dot(wq, high, TN) + dot(wq, low, TN))
    place(m_ref, sums[...], True)


def norm_kernel(g, p_ref, wk_ref, wv_ref, *rest):
    ns = lax.axis_size("sub")
    s = lax.axis_index("sub")
    kn_ref, kr_ref, vn_ref, vr_ref, s_ref, c_ref, sq_ref = rest[-7:]
    rows, width = p_ref.shape
    half = width // ns
    cols = slice(g * half, (g + 1) * half)
    mean = averager(half)
    chunk = rows // CHUNKS
    spans = [slice(r * chunk, (r + 1) * chunk) for r in range(CHUNKS)]
    for w, w_ref in enumerate((wk_ref, wv_ref)):
        raw = w_ref[:, cols]
        high, low = split(raw.astype(F32) - dot(raw, mean, NN))
        for span in spans:
            p = p_ref[span, :]
            centred = dot(p, high, NN) + dot(p, low, NN)
            c_ref[w, span, :] = centred
            sq_ref[w, span, :] = (centred * centred).astype(BF16)
    for w, (n_ref, r_ref) in enumerate(((kn_ref, kr_ref), (vn_ref, vr_ref))):
        for span in spans:
            inverse = lax.rsqrt(dot(sq_ref[w, span, :], mean, NN) + 1e-05)
            n_ref[span, :] = c_ref[w, span, :] * inverse
            r_ref[span, :] = inverse
    packed = pack(dot(kn_ref[...].astype(BF16), vn_ref[...].astype(BF16), TN))
    if g < ns - 1:
        s_ref[...] = packed
    else:
        s_ref[s ^ g] = packed
        for earlier in range(g):
            s_ref[s ^ earlier] = rest[earlier][...]


def back_kernel(total, key, pt_ref, own_ref, got_ref, *rest):
    w_ref, gl_ref, grad_ref, prod_ref = rest[-4:]
    rows, width = gl_ref.shape
    ns = lax.axis_size("sub")
    n_refs, r_refs, o_refs = rest[:ns], rest[ns : 2 * ns], rest[2 * ns : 3 * ns]
    s = lax.axis_index("sub")
    half = width // ns
    mean = averager(half)
    dims = NT if key else NN
    chunk = rows // CHUNKS
    spans = [slice(r * chunk, (r + 1) * chunk) for r in range(CHUNKS)]
    for g in range(ns):
        cols = slice(g * half, (g + 1) * half)
        packed = jnp.where(s == g, own_ref[...], got_ref[...])
        full = unpack((packed / total).astype(BF16).astype(F32))
        if key:
            grouped = dot(mean, full.astype(BF16), NN)
        else:
            grouped = dot(full.astype(BF16), mean, NN)
        high, small = split(full - grouped)
        for span in spans:
            other = o_refs[g][span, :].astype(BF16)
            grad = dot(other, high, dims) + dot(other, small, dims)
            grad_ref[span, cols] = grad
            prod_ref[span, cols] = (grad * n_refs[g][span, :]).astype(BF16)
    for g in range(ns):
        cols = slice(g * half, (g + 1) * half)
        for span in spans:
            second = dot(prod_ref[span, cols], mean, NN)
            gl_ref[span, cols] = ((grad_ref[span, cols] - n_refs[g][span, :] * second) * r_refs[g][span, :]).astype(BF16)
    parts = [dot(pt_ref[...], gl_ref[:, g * half : (g + 1) * half], NN) for g in range(ns)]
    place(w_ref, jnp.concatenate(parts, axis=1), not key)


def points_kernel(gk_ref, gv_ref, wk_ref, wv_ref, *rest):
    acc_ref = rest[-1]
    rows = acc_ref.shape[0]
    chunk = rows // CHUNKS
    for r in range(CHUNKS):
        span = slice(r * chunk, (r + 1) * chunk)
        acc_ref[span, :] = dot(gk_ref[span, :], wk_ref[...], NT) + dot(gv_ref[span, :], wv_ref[...], NT)


def query_kernel(total, acc_ref, c_ref, wq_ref, own_ref, got_ref, m_ref, *rest):
    gp_ref, gq_ref, q_ref = rest[-3:]
    rows, width = c_ref.shape
    ns, nx = lax.axis_size("sub"), lax.axis_size("mp")
    s, x = lax.axis_index("sub"), lax.axis_index("mp")
    half = width // ns
    lows = []
    for g in range(ns):
        cols = slice(g * half, (g + 1) * half)
        packed = jnp.where(s == g, own_ref[...], got_ref[...])
        low = (packed / total).astype(BF16).astype(F32)
        lows.append(low)
        q_ref[:, cols] = dot(c_ref[:, cols], unpack(low).astype(BF16), NT).astype(BF16)
    whole = jnp.concatenate(lows, axis=1)
    cb = width // nx
    high, rest_ = split(m_ref[...])
    third = (m_ref[...] - high.astype(F32) - rest_.astype(F32)).astype(BF16)
    for xb in range(nx):

        @pl.when(x == xb)
        def _():
            state = unpack(whole[:, xb * cb : (xb + 1) * cb]).astype(BF16)
            gq_ref[...] = (dot(high, state, NT) + dot(rest_, state, NT) + dot(third, state, NT)) / total

    chunk = rows // CHUNKS
    for r in range(CHUNKS):
        span = slice(r * chunk, (r + 1) * chunk)
        gp_ref[span, :] = (acc_ref[span, :] + dot(q_ref[span, :], wq_ref[...], NT)).astype(BF16)


def step_kernel(tailed, *refs):
    kept_ref, got_ref = refs[:2]
    send_ref, keep_ref = refs[-3 if tailed else -2 :][:2]
    count, size = keep_ref.shape[0], keep_ref.shape[1]
    for i in range(count):
        even, odd = 2 * i, 2 * i + 1
        keep_ref[i] = kept_ref[even] + got_ref[even * size : (even + 1) * size, :]
        send_ref[i * size : (i + 1) * size, :] = kept_ref[odd] + got_ref[odd * size : (odd + 1) * size, :]
    if tailed:
        refs[-1][...] = refs[2][...]
        joined = 2 * count * size
        if got_ref.shape[0] > joined:
            refs[-1][...] += got_ref[joined:, :]
        send_ref[count * size :, :] = refs[-1][...]


def pairs(size, bit):
    return [(i, i ^ bit) for i in range(size)]


def swap(value, axis, bit):
    return lax.ppermute(value, axis, pairs(lax.axis_size(axis), bit))


def bits(axis):
    bit = 1
    while bit < lax.axis_size(axis):
        yield bit
        bit *= 2


def call(kernel, name, out_shape, inputs, specs, after=(), scratch=(), us=1.0):
    us = US.get(name, us)
    inputs, specs = list(inputs) + list(after), list(specs) + [ANY] * len(after)
    return pl.pallas_call(
        kernel,
        out_shape=out_shape,
        in_specs=specs,
        out_specs=(VMEM,) * len(out_shape),
        scratch_shapes=scratch,
        compiler_params=PARAMS,
        cost_estimate=pl.CostEstimate(flops=int(us * 1.1e9), bytes_accessed=int(us * 1e5), transcendentals=0),
        name=name,
    )(*inputs)


def sum_kernel(a_ref, b_ref, *rest):
    rest[-1][...] = a_ref[...] + b_ref[...]


class Total:
    def __init__(self, parts, axes):
        self.value, self.got = parts[0], swap(parts[1], "sub", 1)
        self.todo = [(axis, bit) for axis in axes for bit in bits(axis)]

    def add(self, after=()):
        (self.value,) = call(
            sum_kernel,
            "sum",
            (jax.ShapeDtypeStruct(self.value.shape, F32),),
            (self.value, self.got),
            [VMEM] * 2,
            after=after,
            us=0.1,
        )
        self.sent = self.value
        if self.todo:
            self.got = swap(self.value, *self.todo.pop(0))
            return True
        self.got = swap(self.value, "sub", 1)
        return False


class Scatter:
    def __init__(self, blocks, axes, name):
        self.name = name
        self.sizes = blocks.shape
        self.kept = blocks[0]
        self.tail = None
        self.got = swap(blocks[1], "sub", 1)
        self.todo = [(axis, bit) for axis in axes for bit in bits(axis)]
        self.axes = axes

    def step(self, after=(), tail=None):
        axis, bit = self.todo.pop(0)
        rb, cb = self.sizes[-2:]
        inner = self.sizes[2] if axis == self.axes[0] else 1
        size = inner * rb
        kept = self.kept.reshape(-1, size, cb)
        got = self.got.reshape(-1, cb)
        count = kept.shape[0] // 2
        if tail is not None:
            self.tail = tail.reshape(-1, cb)
        tailed = self.tail is not None
        extra = self.tail.shape[0] if tailed else 0
        shape = jax.ShapeDtypeStruct
        outs = (shape((count * size + extra, cb), F32), shape((count, size, cb), F32))
        if tailed:
            outs += (shape((extra, cb), F32),)
        res = call(
            functools.partial(step_kernel, tailed),
            "add_" + self.name,
            outs,
            (kept, got) + ((self.tail,) if tailed else ()),
            [VMEM] * (3 if tailed else 2),
            after=after,
            us=0.2,
        )
        self.kept = res[1]
        if tailed:
            self.tail = res[2]
        self.sent = res[0]
        self.got = swap(res[0], axis, bit)

    def end(self, after=()):
        rb, cb = self.sizes[-2:]
        (total,) = call(
            sum_kernel,
            "end_" + self.name,
            (jax.ShapeDtypeStruct((rb, cb), F32),),
            (self.kept.reshape(rb, cb), self.got.reshape(rb, cb)),
            [VMEM] * 2,
            after=after,
            us=0.1,
        )
        return total

    def result(self):
        rb, cb = self.sizes[-2:]
        total = self.kept.reshape(rb, cb) + self.got.reshape(-1, cb)[:rb]
        if self.tail is None:
            return total
        return total, self.tail + self.got.reshape(-1, cb)[rb:]


def local(points_in, cotangent, w_query, w_key, w_value):
    rows, width = points_in.shape
    nz, nx, ns = lax.axis_size("points"), lax.axis_size("mp"), lax.axis_size("sub")
    total = rows * nz * nx * ns
    half = width // ns
    rb, cb = width // (nz * ns), width // nx
    shape = jax.ShapeDtypeStruct
    by_x = shape((ns, nx, nz, rb, cb), F32)
    by_z = shape((ns, nz, nx, rb, cb), F32)
    state = shape((ns, HS, half), F32)
    low = shape((rows, width), BF16)
    tall = shape((rows, half), F32)

    cross, grad_part, p_in, p_flip = call(
        cross_kernel,
        "cross",
        (by_x, state, low, shape((width, rows), BF16)),
        [pltpu.with_memory_space_constraint(a, pltpu.HBM) for a in (points_in, cotangent, w_query)],
        [HBM] * 3,
        scratch=[
            pltpu.VMEM((rows, width), BF16),
            pltpu.VMEM((width, width), BF16),
            pltpu.VMEM((width, width), F32),
            pltpu.SemaphoreType.DMA((2 * CHUNKS + 1,)),
        ],
        us=3.0,
    )
    cross_sum = Scatter(cross, ("mp", "points"), "query")
    g_sum = Total(grad_part, ("mp", "points"))
    norms, states = [], []
    g_sum.add()
    for g in range(ns):
        norms.append(
            call(
                functools.partial(norm_kernel, g),
                "norm",
                (tall, tall, tall, tall, state if g == ns - 1 else shape((HS, half), F32)),
                [p_in, w_key, w_value] + states,
                [VMEM] * (3 + g),
                after=(g_sum.sent,),
                scratch=[pltpu.VMEM((2, rows, half), F32), pltpu.VMEM((2, rows, half), BF16)],
                us=2.3,
            )
        )
        states.append(norms[-1][-1])
        g_sum.add(after=(states[-1],))
        if g == 0:
            cross_sum.step(after=(g_sum.sent,))
            g_sum.add(after=(cross_sum.sent,))
    while g_sum.todo:
        g_sum.add()
    g_own, g_got = g_sum.value, g_sum.got
    key_norm, key_inv, value_norm, value_inv, _ = zip(*norms)
    s_half = states[-1][0] + swap(states[-1][1], "sub", 1)
    cross_sum.step(after=(g_own,))

    def back(key, normed, inverse, other, after):
        return call(
            functools.partial(back_kernel, total, key),
            "back_key" if key else "back_value",
            (by_z if key else by_x, low),
            (p_flip, g_own, g_got) + normed + inverse + other,
            [VMEM] * (3 + 3 * ns),
            after=after,
            scratch=[pltpu.VMEM((rows, width), F32), pltpu.VMEM((rows, width), BF16)],
            us=2.1,
        )

    key_blocks, key_low = back(True, key_norm, key_inv, value_norm, (cross_sum.sent,))
    key_sum = Scatter(key_blocks, ("points", "mp"), "key")
    value_blocks, value_low = back(False, value_norm, value_inv, key_norm, (key_low,))
    value_sum = Scatter(value_blocks, ("mp", "points"), "value")
    last = value_low
    m_total = None
    for turn in ORDER:
        if turn == "P":
            (partial,) = call(
                points_kernel,
                "grad_points_part",
                (shape((rows, width), F32),),
                (key_low, value_low, w_key, w_value),
                [VMEM] * 4,
                after=(last,),
                us=1.3,
            )
            last = partial
            continue
        if turn == "T":
            if not cross_sum.todo:
                m_total = cross_sum.end(after=(last,))
                last = m_total
            continue
        one = {"M": cross_sum, "K": key_sum, "V": value_sum}[turn]
        one.step(after=(last,), tail=s_half if turn == "K" and one.tail is None else None)
        last = one.sent
    while cross_sum.todo or key_sum.todo or value_sum.todo:
        for turn in (cross_sum, key_sum, value_sum):
            if turn.todo:
                turn.step()
    if m_total is None:
        m_total = cross_sum.end()
    grad_value = value_sum.result()
    grad_key, s_own = key_sum.result()
    s_own = s_own.reshape(HS, half)
    s_got = swap(s_own, "sub", 1)
    grad_points, grad_query = call(
        functools.partial(query_kernel, total),
        "grad_points",
        (low, shape((rb, cb), F32)),
        (partial, cotangent, w_query, s_own, s_got, m_total),
        [VMEM] * 6,
        after=(last,) if QUERY_LAST else (),
        scratch=[pltpu.VMEM((rows, width), BF16)],
        us=1.5,
    )
    return grad_points, grad_query, grad_key / total, grad_value / total


def solution(mesh):
    whole = P(("groups", "points", "mp", "sub"), None)
    block = P(("groups", "points", "sub"), "mp")
    return jax.shard_map(
        local,
        mesh=mesh,
        in_specs=(whole, whole, P(), P(), P()),
        out_specs=(whole, block, block, block),
        check_vma=False,
    )
```

time: 73 us -> 58 us (0.79)
  waiting for transfers between devices: 25.3 us -> 18 us
  local copies, waits for them, and re-layouts: 3.67 us -> 0.3 us
  Pallas kernels: 18.5 us -> 15.8 us
  starting transfers between devices: 22.8 us -> 21.6 us
    ppermute x22 -> x19, waiting for transfers between devices: 25.3 us -> 18 us  [swap(): return lax.ppermute(value, axis, pairs(lax.axis_size(axis), bit))]
    unnamed x14 -> x8, local copies, waits for them, and re-layouts: 3.5 us -> 0.02 us
    pallas_call x5 -> x21, Pallas kernels: 18.5 us -> 15.8 us  [call(): pl.pallas_call(kernel, out_shape=out_shape, in_specs=specs, out_specs=(VM...]
    ppermute x22 -> x19, starting transfers between devices: 22.8 us -> 21.6 us  [swap(): return lax.ppermute(value, axis, pairs(lax.axis_size(axis), bit))]
  transfers between devices with their start and end apart: 22 -> 19, of which waited for: 10 -> 8; matrix products, arithmetic and copies ran while one was open for 2% -> 3% of each run, Pallas kernels for 23% -> 18%
where the time goes in v2:
time: 58 us; the launch traced here: 57.9 us
  starting transfers between devices  21.6 us (37%)
  waiting for transfers between devices  18 us (31%)
  Pallas kernels  15.8 us (27%)
  other arithmetic  1.29 us (2%)
  between operations  0.87 us (2%)
    ppermute x19, starting transfers between devices, swap(): return lax.ppermute(value, axis, pairs(lax.axis_size(axis), bit))  21.6 us
    ppermute x19, waiting for transfers between devices, swap(): return lax.ppermute(value, axis, pairs(lax.axis_size(axis), bit))  18 us
    pallas_call x21, Pallas kernels, call(): pl.pallas_call(kernel, out_shape=out_shape, in_specs=specs, out_specs=(VM...  15.8 us
    div x2, other arithmetic, local(): return (grad_points, grad_query, grad_key / total, grad_value / total)  1.28 us
  transfers between devices with their start and end apart: 19, of which 8 were waited for; matrix products, arithmetic and copies ran while one was open for 3% of the time, Pallas kernels for 18%

profile of v2, /device:TPU:0, one launch (start us, length us, event | category | flops | bytes accessed | tf_op | source)
XLA Modules:
  0.0 57.9 jit_solution(5527043329378762037)
XLA Ops:
  0.6 2.9 %cross.1 = (f32[2,2,4,64,256]{4,3,2,1,0:T(8,128)S(1)}, f32[2,32,256]{2,1,0:T(8,128)S(1)}, bf16[1024,512]{1,0:T(8,128)(2,1)S(1)}, bf16[512,1024]{1,0:T(8,128)(2,1)S(1)}) custom-call(bf16[1024,512]{1,0:T(8,128)(2,1)} %p_hbm.1, bf16[1024,512]{1,0:T(8,128)(2,1)} %c_ref.1, bf16[512,512]{1,0:T(8,128)(2,1)} %wq_ref.1), custom_call_target="tpu_custom_call" | custom-call | flops 3300000000 | bytes 300000 | tf_op jit(solution)/shard_map/cross/pallas_call | solution.py:245
  3.6 0.5 collective-permute-start.3
  4.3 1.5 %collective-permute-done.b_ref = f32[32,256]{1,0:T(8,128)S(1)} collective-permute-done((f32[32,256]{1,0:T(8,128)S(1)}, f32[32,256]{1,0:T(8,128)S(1)}, u32[]{:S(2)}, u32[]{:S(2)}) %collective-permute-start) | collective-permute-done | bytes 32800 | tf_op jit(solution)/shard_map/ppermute | solution.py:232
  5.8 2.8 %collective-permute-start.1 = (f32[32,256]{1,0:T(8,128)S(1)}, f32[32,256]{1,0:T(8,128)S(1)}, u32[]{:S(2)}, u32[]{:S(2)}) collective-permute-start(f32[32,256]{1,0:T(8,128)S(1)} %sum.4.rest_0_.a_ref), channel_id=1, source_target_pairs={{0,2},{2,0},{1,3},{3,1},{4,6},{6,4},{5,7},{7,5},{8,10},{10,8},{9,1... | collective-permute-start | bytes 98312 | tf_op jit(solution)/shard_map/ppermute | solution.py:232
  8.6 2.3 %norm.2 = (f32[1024,256]{1,0:T(8,128)S(1)}, f32[1024,256]{1,0:T(8,128)S(1)}, f32[1024,256]{1,0:T(8,128)S(1)}, f32[1024,256]{1,0:T(8,128)S(1)}, f32[32,256]{1,0:T(8,128)S(1)}) custom-call(bf16[1024,512]{1,0:T(8,128)(2,1)S(1)} %get-tuple-element.47.p_ref, bf16[512,512]{1,0:T(8,128)(2,1)S(1)} %copy-done, bf16[512,512]{1,0:T(8,128)(2,1)S(1)} %copy-done.1, ...), custom_call_target="tpu_custom_call" | custom-call | flops 2529999872 | bytes 229999 | tf_op jit(solution)/shard_map/norm/pallas_call | solution.py:245
  11.0 1.7 %collective-permute-start.2 = (f32[32,256]{1,0:T(8,128)S(1)}, f32[32,256]{1,0:T(8,128)S(1)}, u32[]{:S(2)}, u32[]{:S(2)}) collective-permute-start(f32[32,256]{1,0:T(8,128)S(1)} %sum.5.refs_2_.a_ref), channel_id=1, source_target_pairs={{0,4},{4,0},{8,12},{12,8},{1,5},{5,1},{9,13},{13,9},{2,6},{6,2},{1... | collective-permute-start | bytes 98312 | tf_op jit(solution)/shard_map/ppermute | solution.py:232
  12.7 1.6 %collective-permute-start.6 = (f32[256,256]{1,0:T(8,128)S(1)}, f32[256,256]{1,0:T(8,128)S(1)}, u32[]{:S(2)}, u32[]{:S(2)}) collective-permute-start(f32[256,256]{1,0:T(8,128)S(1)} %get-tuple-element.50.rest_0_), channel_id=1, source_target_pairs={{0,2},{2,0},{1,3},{3,1},{4,6},{6,4},{5,7},{7,5},{8,10},{10,8},{9,1... | collective-permute-start | bytes 786440 | tf_op jit(solution)/shard_map/ppermute | solution.py:232
  14.2 0.7 %collective-permute-done.2.b_ref = f32[32,256]{1,0:T(8,128)S(1)} collective-permute-done((f32[32,256]{1,0:T(8,128)S(1)}, f32[32,256]{1,0:T(8,128)S(1)}, u32[]{:S(2)}, u32[]{:S(2)}) %collective-permute-start.2) | collective-permute-done | bytes 32800 | tf_op jit(solution)/shard_map/ppermute | solution.py:232
  14.9 2.6 %collective-permute-start.4 = (f32[32,256]{1,0:T(8,128)S(1)}, f32[32,256]{1,0:T(8,128)S(1)}, u32[]{:S(2)}, u32[]{:S(2)}) collective-permute-start(f32[32,256]{1,0:T(8,128)S(1)} %sum.6.rest_1_.a_ref), channel_id=1, source_target_pairs={{0,8},{4,12},{8,0},{12,4},{1,9},{5,13},{9,1},{13,5},{2,10},{6,14},... | collective-permute-start | bytes 98312 | tf_op jit(solution)/shard_map/ppermute | solution.py:232
  17.6 2.3 %norm.3 = (f32[1024,256]{1,0:T(8,128)S(1)}, f32[1024,256]{1,0:T(8,128)S(1)}, f32[1024,256]{1,0:T(8,128)S(1)}, f32[1024,256]{1,0:T(8,128)S(1)}, f32[2,32,256]{2,1,0:T(8,128)S(1)}) custom-call(bf16[1024,512]{1,0:T(8,128)(2,1)S(1)} %get-tuple-element.47.p_ref, bf16[512,512]{1,0:T(8,128)(2,1)S(1)} %copy-done, bf16[512,512]{1,0:T(8,128)(2,1)S(1)} %copy-done.1, ...), custom_call_target="tpu_custom_call" | custom-call | flops 2529999872 | bytes 229999 | tf_op jit(solution)/shard_map/norm/pallas_call | solution.py:245
  20.0 0.5 collective-permute-start.5
  20.6 0.6 %collective-permute-done.9 = f32[32,256]{1,0:T(8,128)S(1)} collective-permute-done((f32[32,256]{1,0:T(8,128)S(1)}, f32[32,256]{1,0:T(8,128)S(1)}, u32[]{:S(2)}, u32[]{:S(2)}) %collective-permute-start.9) | collective-permute-done | bytes 32800 | tf_op jit(solution)/shard_map/ppermute | solution.py:232
  21.2 1.6 %collective-permute-start.10 = (f32[128,256]{1,0:T(8,128)S(1)}, f32[128,256]{1,0:T(8,128)S(1)}, u32[]{:S(2)}, u32[]{:S(2)}) collective-permute-start(f32[128,256]{1,0:T(8,128)S(1)} %get-tuple-element.59.rest_6_), channel_id=1, source_target_pairs={{0,4},{4,0},{8,12},{12,8},{1,5},{5,1},{9,13},{13,9},{2,6},{6,2},{1... | collective-permute-start | bytes 393224 | tf_op jit(solution)/shard_map/ppermute | solution.py:232
  22.9 2.1 %back_key.1 = (f32[2,4,2,64,256]{4,3,2,1,0:T(8,128)S(1)}, bf16[1024,512]{1,0:T(8,128)(2,1)S(1)}) custom-call(bf16[512,1024]{1,0:T(8,128)(2,1)S(1)} %get-tuple-element.45.pt_ref, f32[32,256]{1,0:T(8,128)S(1)} %sum.7.refs_2_.own_ref, f32[32,256]{1,0:T(8,128)S(1)} %collective-permute-done.5.got_ref, f32[1024,256]{1,0:T(8,128)S(1)} %get-tuple-element.52.rest_0_.rest_4_, ...), custom_call_target="tpu_custom_call" | custom-call | flops 5500000256 | bytes 500000 | tf_op jit(solution)/shard_map/back_key/pallas_call | solution.py:245
  25.2 2.1 %back_value.1 = (f32[2,2,4,64,256]{4,3,2,1,0:T(8,128)S(1)}, bf16[1024,512]{1,0:T(8,128)(2,1)S(1)}) custom-call(bf16[512,1024]{1,0:T(8,128)(2,1)S(1)} %get-tuple-element.45.pt_ref, f32[32,256]{1,0:T(8,128)S(1)} %sum.7.refs_2_.own_ref, f32[32,256]{1,0:T(8,128)S(1)} %collective-permute-done.5.got_ref, f32[1024,256]{1,0:T(8,128)S(1)} %get-tuple-element.56.rest_4_.rest_0_, ...), custom_call_target="tpu_custom_call" | custom-call | flops 5500000256 | bytes 500000 | tf_op jit(solution)/shard_map/back_value/pallas_call | solution.py:245
  27.3 0.6 collective-permute-start.7
  28.0 0.6 %collective-permute-start.11 = (f32[288,256]{1,0:T(8,128)S(1)}, f32[288,256]{1,0:T(8,128)S(1)}, u32[]{:S(2)}, u32[]{:S(2)}) collective-permute-start(f32[288,256]{1,0:T(8,128)S(1)} %get-tuple-element.68.refs_2_), channel_id=1, source_target_pairs={{0,4},{4,0},{8,12},{12,8},{1,5},{5,1},{9,13},{13,9},{2,6},{6,2},{1... | collective-permute-start | bytes 884744 | tf_op jit(solution)/shard_map/ppermute | solution.py:232
  28.6 2.0 %collective-permute-start.12 = (f32[64,256]{1,0:T(8,128)S(1)}, f32[64,256]{1,0:T(8,128)S(1)}, u32[]{:S(2)}, u32[]{:S(2)}) collective-permute-start(f32[64,256]{1,0:T(8,128)S(1)} %get-tuple-element.67.refs_3_), channel_id=1, source_target_pairs={{0,8},{4,12},{8,0},{12,4},{1,9},{5,13},{9,1},{13,5},{2,10},{6,14},... | collective-permute-start | bytes 196616 | tf_op jit(solution)/shard_map/ppermute | solution.py:232
  30.7 1.3 %grad_points_part.1.rest_0_.acc_ref = f32[1024,512]{1,0:T(8,128)S(1)} custom-call(bf16[1024,512]{1,0:T(8,128)(2,1)S(1)} %get-tuple-element.60.rest_6_.gk_ref, bf16[1024,512]{1,0:T(8,128)(2,1)S(1)} %get-tuple-element.63.refs_2_.gv_ref, bf16[512,512]{1,0:T(8,128)(2,1)S(1)} %copy-done, bf16[512,512]{1,0:T(8,128)(2,1)S(1)} %copy-done.1, ...), custom_call_target="tpu_custom_call" | custom-call | flops 1430000000 | bytes 130000 | tf_op jit(solution)/shard_map/grad_points_part/pallas_call | solution.py:245
  31.9 1.5 %collective-permute-start.14 = (f32[256,256]{1,0:T(8,128)S(1)}, f32[256,256]{1,0:T(8,128)S(1)}, u32[]{:S(2)}, u32[]{:S(2)}) collective-permute-start(f32[256,256]{1,0:T(8,128)S(1)} %get-tuple-element.69.rest_0_), channel_id=1, source_target_pairs={{0,2},{2,0},{1,3},{3,1},{4,6},{6,4},{5,7},{7,5},{8,10},{10,8},{9,1... | collective-permute-start | bytes 786440 | tf_op jit(solution)/shard_map/ppermute | solution.py:232
  33.5 2.9 %collective-permute-done.12.b_ref = f32[64,256]{1,0:T(8,128)S(1)} collective-permute-done((f32[64,256]{1,0:T(8,128)S(1)}, f32[64,256]{1,0:T(8,128)S(1)}, u32[]{:S(2)}, u32[]{:S(2)}) %collective-permute-start.12) | collective-permute-done | bytes 65568 | tf_op jit(solution)/shard_map/ppermute | solution.py:232
  36.4 2.0 %collective-permute-done.11.refs_1_ = f32[288,256]{1,0:T(8,128)S(1)} collective-permute-done((f32[288,256]{1,0:T(8,128)S(1)}, f32[288,256]{1,0:T(8,128)S(1)}, u32[]{:S(2)}, u32[]{:S(2)}) %collective-permute-start.11) | collective-permute-done | bytes 294944 | tf_op jit(solution)/shard_map/ppermute | solution.py:232
  38.4 1.4 %collective-permute-start.13 = (f32[160,256]{1,0:T(8,128)S(1)}, f32[160,256]{1,0:T(8,128)S(1)}, u32[]{:S(2)}, u32[]{:S(2)}) collective-permute-start(f32[160,256]{1,0:T(8,128)S(1)} %get-tuple-element.74.refs_2_), channel_id=1, source_target_pairs={{0,8},{4,12},{8,0},{12,4},{1,9},{5,13},{9,1},{13,5},{2,10},{6,14},... | collective-permute-start | bytes 491528 | tf_op jit(solution)/shard_map/ppermute | solution.py:232
  39.9 1.4 %collective-permute-start.17 = (f32[128,256]{1,0:T(8,128)S(1)}, f32[128,256]{1,0:T(8,128)S(1)}, u32[]{:S(2)}, u32[]{:S(2)}) collective-permute-start(f32[128,256]{1,0:T(8,128)S(1)} %get-tuple-element.77.refs_3_), channel_id=1, source_target_pairs={{0,4},{4,0},{8,12},{12,8},{1,5},{5,1},{9,13},{13,9},{2,6},{6,2},{1... | collective-permute-start | bytes 393224 | tf_op jit(solution)/shard_map/ppermute | solution.py:232
  41.3 6.9 %collective-permute-done.13.refs_1_ = f32[160,256]{1,0:T(8,128)S(1)} collective-permute-done((f32[160,256]{1,0:T(8,128)S(1)}, f32[160,256]{1,0:T(8,128)S(1)}, u32[]{:S(2)}, u32[]{:S(2)}) %collective-permute-start.13) | collective-permute-done | bytes 163872 | tf_op jit(solution)/shard_map/ppermute | solution.py:232
  48.3 0.9 %collective-permute-start.18 = (f32[64,256]{1,0:T(8,128)S(1)}, f32[64,256]{1,0:T(8,128)S(1)}, u32[]{:S(2)}, u32[]{:S(2)}) collective-permute-start(f32[64,256]{1,0:T(8,128)S(1)} %get-tuple-element.85), channel_id=1, source_target_pairs={{0,8},{4,12},{8,0},{12,4},{1,9},{5,13},{9,1},{13,5},{2,10},{6,14},... | collective-permute-start | bytes 196616 | tf_op jit(solution)/shard_map/ppermute | solution.py:232
  49.2 1.5 %collective-permute-start.15 = (f32[96,256]{1,0:T(8,128)S(1)}, f32[96,256]{1,0:T(8,128)S(1)}, u32[]{:S(2)}, u32[]{:S(2)}) collective-permute-start(f32[96,256]{1,0:T(8,128)S(1)} %get-tuple-element.79.refs_2_), channel_id=1, source_target_pairs={{0,2},{2,0},{1,3},{3,1},{4,6},{6,4},{5,7},{7,5},{8,10},{10,8},{9,1... | collective-permute-start | bytes 294920 | tf_op jit(solution)/shard_map/ppermute | solution.py:232
  50.7 2.8 %collective-permute-done.18 = f32[64,256]{1,0:T(8,128)S(1)} collective-permute-done((f32[64,256]{1,0:T(8,128)S(1)}, f32[64,256]{1,0:T(8,128)S(1)}, u32[]{:S(2)}, u32[]{:S(2)}) %collective-permute-start.18) | collective-permute-done | bytes 65568 | tf_op jit(solution)/shard_map/ppermute | solution.py:232
  53.5 0.6 %fusion.1 = f32[64,256]{1,0:T(8,128)} fusion(f32[64,256]{1,0:T(8,128)S(1)} %collective-permute-done.18, f32[1,64,256]{2,1,0:T(8,128)S(1)} %get-tuple-element.84), kind=kLoop, calls=%fused_computation.6 | loop fusion | flops 32768 | bytes 196608 | tf_op jit(solution)/shard_map/div | solution.py:461
  54.2 0.6 %fusion = f32[64,256]{1,0:T(8,128)} fusion(f32[96,256]{1,0:T(8,128)S(1)} %collective-permute-done.15, f32[1,64,256]{2,1,0:T(8,128)S(1)} %get-tuple-element.82), kind=kLoop, calls=%fused_computation.4 | loop fusion | flops 32768 | bytes 196608 | tf_op jit(solution)/shard_map/div | solution.py:461
  54.9 0.6 collective-permute-done.16.got_ref
  55.4 2.4 %grad_points.1 = (bf16[1024,512]{1,0:T(8,128)(2,1)}, f32[64,256]{1,0:T(8,128)}) custom-call(f32[1024,512]{1,0:T(8,128)S(1)} %grad_points_part.1.rest_0_.acc_ref, bf16[1024,512]{1,0:T(8,128)(2,1)S(1)} %copy-done.2, bf16[512,512]{1,0:T(8,128)(2,1)S(1)} %copy-done.3, f32[32,256]{1,0:T(8,128)S(1)} %slice_add_fusion.1.own_ref, ...), custom_call_target="tpu_custom_call" | custom-call | flops 1650000000 | bytes 150000 | tf_op jit(solution)/shard_map/grad_points/pallas_call | solution.py:245
  (44 shorter events, 1.0 us)
Async XLA Ops:
  3.5 5.1 %copy-start = (bf16[512,512]{1,0:T(8,128)(2,1)S(1)}, bf16[512,512]{1,0:T(8,128)(2,1)}, u32[]{:S(2)}) copy-start(bf16[512,512]{1,0:T(8,128)(2,1)} %wk_ref.5) | copy-start | bytes 1572868
  3.5 5.1 %copy-start.1 = (bf16[512,512]{1,0:T(8,128)(2,1)S(1)}, bf16[512,512]{1,0:T(8,128)(2,1)}, u32[]{:S(2)}) copy-start(bf16[512,512]{1,0:T(8,128)(2,1)} %wv_ref.5) | copy-start | bytes 1572868
  3.6 9.0 %collective-permute-start.3 = (f32[2,4,64,256]{3,2,1,0:T(8,128)S(1)}, f32[2,4,64,256]{3,2,1,0:T(8,128)S(1)}, u32[]{:S(2)}, u32[]{:S(2)}) collective-permute-start(f32[2,4,64,256]{3,2,1,0:T(8,128)S(1)} %get-tuple-element.90), channel_id=1, source_target_pairs={{0,1},{1,0},{2,3},{3,2},{4,5},{5,4},{6,7},{7,6},{8,9},{9,8},{10,11... | collective-permute-start | bytes 1572872 | tf_op jit(solution)/shard_map/ppermute | solution.py:232
  4.2 1.6 %collective-permute-start = (f32[32,256]{1,0:T(8,128)S(1)}, f32[32,256]{1,0:T(8,128)S(1)}, u32[]{:S(2)}, u32[]{:S(2)}) collective-permute-start(f32[32,256]{1,0:T(8,128)S(1)} %get-tuple-element.92), channel_id=1, source_target_pairs={{0,1},{1,0},{2,3},{3,2},{4,5},{5,4},{6,7},{7,6},{8,9},{9,8},{10,11... | collective-permute-start | bytes 98312 | tf_op jit(solution)/shard_map/ppermute | solution.py:232
  5.8 5.2 %collective-permute-start.1 = (f32[32,256]{1,0:T(8,128)S(1)}, f32[32,256]{1,0:T(8,128)S(1)}, u32[]{:S(2)}, u32[]{:S(2)}) collective-permute-start(f32[32,256]{1,0:T(8,128)S(1)} %sum.4.rest_0_.a_ref), channel_id=1, source_target_pairs={{0,2},{2,0},{1,3},{3,1},{4,6},{6,4},{5,7},{7,5},{8,10},{10,8},{9,1... | collective-permute-start | bytes 98312 | tf_op jit(solution)/shard_map/ppermute | solution.py:232
  11.0 4.0 %collective-permute-start.2 = (f32[32,256]{1,0:T(8,128)S(1)}, f32[32,256]{1,0:T(8,128)S(1)}, u32[]{:S(2)}, u32[]{:S(2)}) collective-permute-start(f32[32,256]{1,0:T(8,128)S(1)} %sum.5.refs_2_.a_ref), channel_id=1, source_target_pairs={{0,4},{4,0},{8,12},{12,8},{1,5},{5,1},{9,13},{13,9},{2,6},{6,2},{1... | collective-permute-start | bytes 98312 | tf_op jit(solution)/shard_map/ppermute | solution.py:232
  12.7 8.5 %collective-permute-start.6 = (f32[256,256]{1,0:T(8,128)S(1)}, f32[256,256]{1,0:T(8,128)S(1)}, u32[]{:S(2)}, u32[]{:S(2)}) collective-permute-start(f32[256,256]{1,0:T(8,128)S(1)} %get-tuple-element.50.rest_0_), channel_id=1, source_target_pairs={{0,2},{2,0},{1,3},{3,1},{4,6},{6,4},{5,7},{7,5},{8,10},{10,8},{9,1... | collective-permute-start | bytes 786440 | tf_op jit(solution)/shard_map/ppermute | solution.py:232
  14.9 5.0 %collective-permute-start.4 = (f32[32,256]{1,0:T(8,128)S(1)}, f32[32,256]{1,0:T(8,128)S(1)}, u32[]{:S(2)}, u32[]{:S(2)}) collective-permute-start(f32[32,256]{1,0:T(8,128)S(1)} %sum.6.rest_1_.a_ref), channel_id=1, source_target_pairs={{0,8},{4,12},{8,0},{12,4},{1,9},{5,13},{9,1},{13,5},{2,10},{6,14},... | collective-permute-start | bytes 98312 | tf_op jit(solution)/shard_map/ppermute | solution.py:232
  19.9 1.3 %collective-permute-start.9 = (f32[32,256]{1,0:T(8,128)S(1)}, f32[32,256]{1,0:T(8,128)S(1)}, u32[]{:S(2)}, u32[]{:S(2)}) collective-permute-start(f32[32,256]{1,0:T(8,128)S(1)} %slice_bitcast_fusion.3), channel_id=1, source_target_pairs={{0,1},{1,0},{2,3},{3,2},{4,5},{5,4},{6,7},{7,6},{8,9},{9,8},{10,11... | collective-permute-start | bytes 98312 | tf_op jit(solution)/shard_map/ppermute | solution.py:232
  20.0 2.9 %collective-permute-start.5 = (f32[32,256]{1,0:T(8,128)S(1)}, f32[32,256]{1,0:T(8,128)S(1)}, u32[]{:S(2)}, u32[]{:S(2)}) collective-permute-start(f32[32,256]{1,0:T(8,128)S(1)} %sum.7.refs_2_.own_ref), channel_id=1, source_target_pairs={{0,1},{1,0},{2,3},{3,2},{4,5},{5,4},{6,7},{7,6},{8,9},{9,8},{10,11... | collective-permute-start | bytes 98312 | tf_op jit(solution)/shard_map/ppermute | solution.py:232
  21.2 6.7 %collective-permute-start.10 = (f32[128,256]{1,0:T(8,128)S(1)}, f32[128,256]{1,0:T(8,128)S(1)}, u32[]{:S(2)}, u32[]{:S(2)}) collective-permute-start(f32[128,256]{1,0:T(8,128)S(1)} %get-tuple-element.59.rest_6_), channel_id=1, source_target_pairs={{0,4},{4,0},{8,12},{12,8},{1,5},{5,1},{9,13},{13,9},{2,6},{6,2},{1... | collective-permute-start | bytes 393224 | tf_op jit(solution)/shard_map/ppermute | solution.py:232
  25.1 2.8 %collective-permute-start.8 = (f32[4,2,64,256]{3,2,1,0:T(8,128)S(1)}, f32[4,2,64,256]{3,2,1,0:T(8,128)S(1)}, u32[]{:S(2)}, u32[]{:S(2)}) collective-permute-start(f32[4,2,64,256]{3,2,1,0:T(8,128)S(1)} %get-tuple-element.86), channel_id=1, source_target_pairs={{0,1},{1,0},{2,3},{3,2},{4,5},{5,4},{6,7},{7,6},{8,9},{9,8},{10,11... | collective-permute-start | bytes 1572872 | tf_op jit(solution)/shard_map/ppermute | solution.py:232
  27.3 3.3 %collective-permute-start.7 = (f32[2,4,64,256]{3,2,1,0:T(8,128)S(1)}, f32[2,4,64,256]{3,2,1,0:T(8,128)S(1)}, u32[]{:S(2)}, u32[]{:S(2)}) collective-permute-start(f32[2,4,64,256]{3,2,1,0:T(8,128)S(1)} %get-tuple-element.88), channel_id=1, source_target_pairs={{0,1},{1,0},{2,3},{3,2},{4,5},{5,4},{6,7},{7,6},{8,9},{9,8},{10,11... | collective-permute-start | bytes 1572872 | tf_op jit(solution)/shard_map/ppermute | solution.py:232
  28.0 10.4 %collective-permute-start.11 = (f32[288,256]{1,0:T(8,128)S(1)}, f32[288,256]{1,0:T(8,128)S(1)}, u32[]{:S(2)}, u32[]{:S(2)}) collective-permute-start(f32[288,256]{1,0:T(8,128)S(1)} %get-tuple-element.68.refs_2_), channel_id=1, source_target_pairs={{0,4},{4,0},{8,12},{12,8},{1,5},{5,1},{9,13},{13,9},{2,6},{6,2},{1... | collective-permute-start | bytes 884744 | tf_op jit(solution)/shard_map/ppermute | solution.py:232
  28.6 7.8 %collective-permute-start.12 = (f32[64,256]{1,0:T(8,128)S(1)}, f32[64,256]{1,0:T(8,128)S(1)}, u32[]{:S(2)}, u32[]{:S(2)}) collective-permute-start(f32[64,256]{1,0:T(8,128)S(1)} %get-tuple-element.67.refs_3_), channel_id=1, source_target_pairs={{0,8},{4,12},{8,0},{12,4},{1,9},{5,13},{9,1},{13,5},{2,10},{6,14},... | collective-permute-start | bytes 196616 | tf_op jit(solution)/shard_map/ppermute | solution.py:232
  31.9 7.9 %collective-permute-start.14 = (f32[256,256]{1,0:T(8,128)S(1)}, f32[256,256]{1,0:T(8,128)S(1)}, u32[]{:S(2)}, u32[]{:S(2)}) collective-permute-start(f32[256,256]{1,0:T(8,128)S(1)} %get-tuple-element.69.rest_0_), channel_id=1, source_target_pairs={{0,2},{2,0},{1,3},{3,1},{4,6},{6,4},{5,7},{7,5},{8,10},{10,8},{9,1... | collective-permute-start | bytes 786440 | tf_op jit(solution)/shard_map/ppermute | solution.py:232
  38.4 9.8 %collective-permute-start.13 = (f32[160,256]{1,0:T(8,128)S(1)}, f32[160,256]{1,0:T(8,128)S(1)}, u32[]{:S(2)}, u32[]{:S(2)}) collective-permute-start(f32[160,256]{1,0:T(8,128)S(1)} %get-tuple-element.74.refs_2_), channel_id=1, source_target_pairs={{0,8},{4,12},{8,0},{12,4},{1,9},{5,13},{9,1},{13,5},{2,10},{6,14},... | collective-permute-start | bytes 491528 | tf_op jit(solution)/shard_map/ppermute | solution.py:232
  39.9 8.3 %collective-permute-start.17 = (f32[128,256]{1,0:T(8,128)S(1)}, f32[128,256]{1,0:T(8,128)S(1)}, u32[]{:S(2)}, u32[]{:S(2)}) collective-permute-start(f32[128,256]{1,0:T(8,128)S(1)} %get-tuple-element.77.refs_3_), channel_id=1, source_target_pairs={{0,4},{4,0},{8,12},{12,8},{1,5},{5,1},{9,13},{13,9},{2,6},{6,2},{1... | collective-permute-start | bytes 393224 | tf_op jit(solution)/shard_map/ppermute | solution.py:232
  48.2 7.2 %copy-start.2 = (bf16[1024,512]{1,0:T(8,128)(2,1)S(1)}, bf16[1024,512]{1,0:T(8,128)(2,1)}, u32[]{:S(2)}) copy-start(bf16[1024,512]{1,0:T(8,128)(2,1)} %c_ref.1) | copy-start | bytes 3145732
  48.2 7.2 %copy-start.3 = (bf16[512,512]{1,0:T(8,128)(2,1)S(1)}, bf16[512,512]{1,0:T(8,128)(2,1)}, u32[]{:S(2)}) copy-start(bf16[512,512]{1,0:T(8,128)(2,1)} %wq_ref.1) | copy-start | bytes 1572868
  48.3 5.2 %collective-permute-start.18 = (f32[64,256]{1,0:T(8,128)S(1)}, f32[64,256]{1,0:T(8,128)S(1)}, u32[]{:S(2)}, u32[]{:S(2)}) collective-permute-start(f32[64,256]{1,0:T(8,128)S(1)} %get-tuple-element.85), channel_id=1, source_target_pairs={{0,8},{4,12},{8,0},{12,4},{1,9},{5,13},{9,1},{13,5},{2,10},{6,14},... | collective-permute-start | bytes 196616 | tf_op jit(solution)/shard_map/ppermute | solution.py:232
  49.2 4.9 %collective-permute-start.15 = (f32[96,256]{1,0:T(8,128)S(1)}, f32[96,256]{1,0:T(8,128)S(1)}, u32[]{:S(2)}, u32[]{:S(2)}) collective-permute-start(f32[96,256]{1,0:T(8,128)S(1)} %get-tuple-element.79.refs_2_), channel_id=1, source_target_pairs={{0,2},{2,0},{1,3},{3,1},{4,6},{6,4},{5,7},{7,5},{8,10},{10,8},{9,1... | collective-permute-start | bytes 294920 | tf_op jit(solution)/shard_map/ppermute | solution.py:232
  54.1 1.3 %collective-permute-start.16 = (f32[32,256]{1,0:T(8,128)S(1)}, f32[32,256]{1,0:T(8,128)S(1)}, u32[]{:S(2)}, u32[]{:S(2)}) collective-permute-start(f32[32,256]{1,0:T(8,128)S(1)} %slice_add_fusion.1.own_ref), channel_id=1, source_target_pairs={{0,1},{1,0},{2,3},{3,2},{4,5},{5,4},{6,7},{7,6},{8,9},{9,8},{10,11... | collective-permute-start | bytes 98312 | tf_op jit(solution)/shard_map/ppermute | solution.py:232

commit v3 on v2

--- a/solution.py
+++ b/solution.py
@@ -17,9 +17,8 @@
 HBM = pl.BlockSpec(memory_space=pltpu.HBM)
 ANY = pl.BlockSpec(memory_space=pl.ANY)
 CHUNKS = 4
-QUERY_LAST = False
-ORDER = "MKVPTKVKV"
-US = {"add_key": 5.0, "back_key": 5.0, "back_value": 5.0}
+ORDER = "MKVPKVTVK"
+US = {"add_key_0": 5.0, "sum_0": 5.0, "back_key": 5.0, "back_value": 5.0}
 
 PARAMS = pltpu.CompilerParams(vmem_limit_bytes=16 * 1024 * 1024)
 
@@ -71,7 +70,7 @@
                 refs[s ^ sb, first, second] = block
 
 
-def cross_kernel(p_hbm, c_hbm, wq_hbm, m_ref, g_ref, p_ref, pt_ref, c_ref, wq_ref, sums, sems):
+def cross_kernel(p_hbm, c_hbm, wq_hbm, sums, g_ref, p_ref, pt_ref, c_ref, wq_ref, sems):
     rows, width = p_hbm.shape
     ns = lax.axis_size("sub")
     s = lax.axis_index("sub")
@@ -100,7 +99,10 @@
         high, low = split(sums[:, cols])
         wq = wq_ref[:, cols]
         g_ref[s ^ g] = pack(dot(wq, high, TN) + dot(wq, low, TN))
-    place(m_ref, sums[...], True)
+
+
+def deal_kernel(sums_ref, *rest):
+    place(rest[-1], sums_ref[...], True)
 
 
 def norm_kernel(g, p_ref, wk_ref, wv_ref, *rest):
@@ -258,15 +260,29 @@
     rest[-1][...] = a_ref[...] + b_ref[...]
 
 
+def end_kernel(kept_ref, got_ref, *rest):
+    rb = kept_ref.shape[0]
+    if got_ref.shape[0] == rb:
+        rest[-1][...] = kept_ref[...] + got_ref[...]
+    else:
+        rest[-2][...] = kept_ref[...] + got_ref[:rb, :]
+        rest[-1][...] = rest[0][...] + got_ref[rb:, :]
+
+
+def scale_kernel(total, *refs):
+    for i in range(2):
+        refs[-2 + i][...] = (refs[2 * i][...] + refs[2 * i + 1][...]) / total
+
+
 class Total:
     def __init__(self, parts, axes):
-        self.value, self.got = parts[0], swap(parts[1], "sub", 1)
+        self.value, self.got, self.done = parts[0], swap(parts[1], "sub", 1), 0
         self.todo = [(axis, bit) for axis in axes for bit in bits(axis)]
 
     def add(self, after=()):
         (self.value,) = call(
             sum_kernel,
-            "sum",
+            "sum_%d" % self.done,
             (jax.ShapeDtypeStruct(self.value.shape, F32),),
             (self.value, self.got),
             [VMEM] * 2,
@@ -274,6 +290,7 @@
             us=0.1,
         )
         self.sent = self.value
+        self.done += 1
         if self.todo:
             self.got = swap(self.value, *self.todo.pop(0))
             return True
@@ -283,7 +300,7 @@
 
 class Scatter:
     def __init__(self, blocks, axes, name):
-        self.name = name
+        self.name, self.done = name, 0
         self.sizes = blocks.shape
         self.kept = blocks[0]
         self.tail = None
@@ -309,7 +326,7 @@
             outs += (shape((extra, cb), F32),)
         res = call(
             functools.partial(step_kernel, tailed),
-            "add_" + self.name,
+            "add_%s_%d" % (self.name, self.done),
             outs,
             (kept, got) + ((self.tail,) if tailed else ()),
             [VMEM] * (3 if tailed else 2),
@@ -321,26 +338,17 @@
             self.tail = res[2]
         self.sent = res[0]
         self.got = swap(res[0], axis, bit)
+        self.done += 1
 
     def end(self, after=()):
         rb, cb = self.sizes[-2:]
-        (total,) = call(
-            sum_kernel,
-            "end_" + self.name,
-            (jax.ShapeDtypeStruct((rb, cb), F32),),
-            (self.kept.reshape(rb, cb), self.got.reshape(rb, cb)),
-            [VMEM] * 2,
-            after=after,
-            us=0.1,
-        )
-        return total
-
-    def result(self):
-        rb, cb = self.sizes[-2:]
-        total = self.kept.reshape(rb, cb) + self.got.reshape(-1, cb)[:rb]
-        if self.tail is None:
-            return total
-        return total, self.tail + self.got.reshape(-1, cb)[rb:]
+        kept = self.kept.reshape(rb, cb)
+        shapes = [jax.ShapeDtypeStruct((rb, cb), F32)]
+        inputs = [kept, self.got]
+        if self.tail is not None:
+            shapes.append(jax.ShapeDtypeStruct(self.tail.shape, F32))
+            inputs.append(self.tail)
+        return call(end_kernel, "end_" + self.name, shapes, inputs, [VMEM] * len(inputs), after=after, us=0.1)
 
 
 def local(points_in, cotangent, w_query, w_key, w_value):
@@ -356,24 +364,26 @@
     low = shape((rows, width), BF16)
     tall = shape((rows, half), F32)
 
-    cross, grad_part, p_in, p_flip = call(
+    sums, grad_part, p_in, p_flip = call(
         cross_kernel,
         "cross",
-        (by_x, state, low, shape((width, rows), BF16)),
+        (shape((width, width), F32), state, low, shape((width, rows), BF16)),
         [pltpu.with_memory_space_constraint(a, pltpu.HBM) for a in (points_in, cotangent, w_query)],
         [HBM] * 3,
         scratch=[
             pltpu.VMEM((rows, width), BF16),
             pltpu.VMEM((width, width), BF16),
-            pltpu.VMEM((width, width), F32),
             pltpu.SemaphoreType.DMA((2 * CHUNKS + 1,)),
         ],
         us=3.0,
     )
+    g_sum = Total(grad_part, ("mp", "points"))
+    (cross,) = call(deal_kernel, "deal", (by_x,), (sums,), [VMEM], us=0.3)
     cross_sum = Scatter(cross, ("mp", "points"), "query")
-    g_sum = Total(grad_part, ("mp", "points"))
+    g_sum.add()
+    cross_sum.step(after=(g_sum.sent,))
+    g_sum.add(after=(cross_sum.sent,))
     norms, states = [], []
-    g_sum.add()
     for g in range(ns):
         norms.append(
             call(
@@ -389,15 +399,14 @@
         )
         states.append(norms[-1][-1])
         g_sum.add(after=(states[-1],))
-        if g == 0:
-            cross_sum.step(after=(g_sum.sent,))
-            g_sum.add(after=(cross_sum.sent,))
     while g_sum.todo:
         g_sum.add()
     g_own, g_got = g_sum.value, g_sum.got
     key_norm, key_inv, value_norm, value_inv, _ = zip(*norms)
     s_half = states[-1][0] + swap(states[-1][1], "sub", 1)
-    cross_sum.step(after=(g_own,))
+    while cross_sum.todo[0][0] == "mp":
+        cross_sum.step()
+    cross_sum.step(after=(g_own,), tail=s_half)
 
     def back(key, normed, inverse, other, after):
         return call(
@@ -432,21 +441,21 @@
             continue
         if turn == "T":
             if not cross_sum.todo:
-                m_total = cross_sum.end(after=(last,))
+                m_total, s_own = cross_sum.end(after=(last,))
                 last = m_total
             continue
         one = {"M": cross_sum, "K": key_sum, "V": value_sum}[turn]
-        one.step(after=(last,), tail=s_half if turn == "K" and one.tail is None else None)
+        one.step(after=(last,))
         last = one.sent
     while cross_sum.todo or key_sum.todo or value_sum.todo:
         for turn in (cross_sum, key_sum, value_sum):
             if turn.todo:
                 turn.step()
     if m_total is None:
-        m_total = cross_sum.end()
-    grad_value = value_sum.result()
-    grad_key, s_own = key_sum.result()
+        m_total, s_own = cross_sum.end()
     s_own = s_own.reshape(HS, half)
+    for bit in bits("mp"):
+        s_own = s_own + swap(s_own, "mp", bit)
     s_got = swap(s_own, "sub", 1)
     grad_points, grad_query = call(
         functools.partial(query_kernel, total),
@@ -454,11 +463,21 @@
         (low, shape((rb, cb), F32)),
         (partial, cotangent, w_query, s_own, s_got, m_total),
         [VMEM] * 6,
-        after=(last,) if QUERY_LAST else (),
         scratch=[pltpu.VMEM((rows, width), BF16)],
         us=1.5,
     )
-    return grad_points, grad_query, grad_key / total, grad_value / total
+    parts = []
+    for one in (key_sum, value_sum):
+        parts += [one.kept.reshape(rb, cb), one.got]
+    grad_key, grad_value = call(
+        functools.partial(scale_kernel, total),
+        "scale",
+        (shape((rb, cb), F32),) * 2,
+        parts,
+        [VMEM] * 4,
+        us=0.7,
+    )
+    return grad_points, grad_query, grad_key, grad_value
 
 
 def solution(mesh):

time: 58 us -> 52.2 us (0.900)
  waiting for transfers between devices: 18 us -> 11.4 us
  starting transfers between devices: 21.6 us -> 23 us
  other arithmetic: 1.29 us -> 0.01 us
  Pallas kernels: 15.8 us -> 16.5 us
    ppermute x19 -> x20, waiting for transfers between devices: 18 us -> 11.4 us  [swap(): return lax.ppermute(value, axis, pairs(lax.axis_size(axis), bit))]
    ppermute x19 -> x20, starting transfers between devices: 21.6 us -> 23 us  [swap(): return lax.ppermute(value, axis, pairs(lax.axis_size(axis), bit))]
    div x2 -> x0, other arithmetic: 1.28 us -> none  [local(): return (grad_points, grad_query, grad_key / total, grad_value / total)]
    pallas_call x21 -> x23, Pallas kernels: 15.8 us -> 16.5 us  [call(): pl.pallas_call(kernel, out_shape=out_shape, in_specs=specs, out_specs=(VM...]
  transfers between devices with their start and end apart: 19 -> 20, of which waited for: 8 -> 10; matrix products, arithmetic and copies ran while one was open for 3% -> 1% of each run, Pallas kernels for 18% -> 25%
where the time goes in v3:
time: 52.2 us; the launch traced here: 52.1 us
  starting transfers between devices  23 us (44%)
  Pallas kernels  16.5 us (32%)
  waiting for transfers between devices  11.4 us (22%)
  between operations  0.88 us (2%)
    ppermute x20, starting transfers between devices, swap(): return lax.ppermute(value, axis, pairs(lax.axis_size(axis), bit))  23 us
    pallas_call x23, Pallas kernels, call(): pl.pallas_call(kernel, out_shape=out_shape, in_specs=specs, out_specs=(VM...  16.5 us
    ppermute x20, waiting for transfers between devices, swap(): return lax.ppermute(value, axis, pairs(lax.axis_size(axis), bit))  11.4 us
  transfers between devices with their start and end apart: 20, of which 10 were waited for; matrix products, arithmetic and copies ran while one was open for 1% of the time, Pallas kernels for 25%

profile of v3, /device:TPU:0, one launch (start us, length us, event | category | flops | bytes accessed | tf_op | source)
XLA Modules:
  0.0 52.1 jit_solution(4372060157238212756)
XLA Ops:
  0.6 2.9 %cross.1 = (f32[512,512]{1,0:T(8,128)S(1)}, f32[2,32,256]{2,1,0:T(8,128)S(1)}, bf16[1024,512]{1,0:T(8,128)(2,1)S(1)}, bf16[512,1024]{1,0:T(8,128)(2,1)S(1)}) custom-call(bf16[1024,512]{1,0:T(8,128)(2,1)} %p_hbm.1, bf16[1024,512]{1,0:T(8,128)(2,1)} %c_ref.1, bf16[512,512]{1,0:T(8,128)(2,1)} %wq_ref.1), custom_call_target="tpu_custom_call" | custom-call | flops 3300000000 | bytes 300000 | tf_op jit(solution)/shard_map/cross/pallas_call | solution.py:247
  3.5 0.5 collective-permute-start
  4.4 0.6 %collective-permute-done.b_ref = f32[32,256]{1,0:T(8,128)S(1)} collective-permute-done((f32[32,256]{1,0:T(8,128)S(1)}, f32[32,256]{1,0:T(8,128)S(1)}, u32[]{:S(2)}, u32[]{:S(2)}) %collective-permute-start) | collective-permute-done | bytes 32800 | tf_op jit(solution)/shard_map/ppermute | solution.py:234
  4.9 2.9 %collective-permute-start.1 = (f32[32,256]{1,0:T(8,128)S(1)}, f32[32,256]{1,0:T(8,128)S(1)}, u32[]{:S(2)}, u32[]{:S(2)}) collective-permute-start(f32[32,256]{1,0:T(8,128)S(1)} %sum_0.1.refs_2_.a_ref), channel_id=1, source_target_pairs={{0,2},{2,0},{1,3},{3,1},{4,6},{6,4},{5,7},{7,5},{8,10},{10,8},{9,1... | collective-permute-start | bytes 98312 | tf_op jit(solution)/shard_map/ppermute | solution.py:234
  7.9 1.1 %collective-permute-start.6 = (f32[256,256]{1,0:T(8,128)S(1)}, f32[256,256]{1,0:T(8,128)S(1)}, u32[]{:S(2)}, u32[]{:S(2)}) collective-permute-start(f32[256,256]{1,0:T(8,128)S(1)} %get-tuple-element.51.rest_0_), channel_id=1, source_target_pairs={{0,2},{2,0},{1,3},{3,1},{4,6},{6,4},{5,7},{7,5},{8,10},{10,8},{9,1... | collective-permute-start | bytes 786440 | tf_op jit(solution)/shard_map/ppermute | solution.py:234
  9.0 0.7 %collective-permute-done.1.b_ref = f32[32,256]{1,0:T(8,128)S(1)} collective-permute-done((f32[32,256]{1,0:T(8,128)S(1)}, f32[32,256]{1,0:T(8,128)S(1)}, u32[]{:S(2)}, u32[]{:S(2)}) %collective-permute-start.1) | collective-permute-done | bytes 32800 | tf_op jit(solution)/shard_map/ppermute | solution.py:234
  9.7 2.1 %collective-permute-start.3 = (f32[32,256]{1,0:T(8,128)S(1)}, f32[32,256]{1,0:T(8,128)S(1)}, u32[]{:S(2)}, u32[]{:S(2)}) collective-permute-start(f32[32,256]{1,0:T(8,128)S(1)} %sum_1.1.rest_0_.a_ref), channel_id=1, source_target_pairs={{0,4},{4,0},{8,12},{12,8},{1,5},{5,1},{9,13},{13,9},{2,6},{6,2},{1... | collective-permute-start | bytes 98312 | tf_op jit(solution)/shard_map/ppermute | solution.py:234
  11.8 2.3 %norm.2 = (f32[1024,256]{1,0:T(8,128)S(1)}, f32[1024,256]{1,0:T(8,128)S(1)}, f32[1024,256]{1,0:T(8,128)S(1)}, f32[1024,256]{1,0:T(8,128)S(1)}, f32[32,256]{1,0:T(8,128)S(1)}) custom-call(bf16[1024,512]{1,0:T(8,128)(2,1)S(1)} %get-tuple-element.52.p_ref, bf16[512,512]{1,0:T(8,128)(2,1)S(1)} %copy-done, bf16[512,512]{1,0:T(8,128)(2,1)S(1)} %copy-done.1, ...), custom_call_target="tpu_custom_call" | custom-call | flops 2529999872 | bytes 229999 | tf_op jit(solution)/shard_map/norm/pallas_call | solution.py:247
  14.2 2.7 %collective-permute-start.4 = (f32[32,256]{1,0:T(8,128)S(1)}, f32[32,256]{1,0:T(8,128)S(1)}, u32[]{:S(2)}, u32[]{:S(2)}) collective-permute-start(f32[32,256]{1,0:T(8,128)S(1)} %sum_2.1.rest_1_.a_ref), channel_id=1, source_target_pairs={{0,8},{4,12},{8,0},{12,4},{1,9},{5,13},{9,1},{13,5},{2,10},{6,14},... | collective-permute-start | bytes 98312 | tf_op jit(solution)/shard_map/ppermute | solution.py:234
  16.9 2.3 %norm.3 = (f32[1024,256]{1,0:T(8,128)S(1)}, f32[1024,256]{1,0:T(8,128)S(1)}, f32[1024,256]{1,0:T(8,128)S(1)}, f32[1024,256]{1,0:T(8,128)S(1)}, f32[2,32,256]{2,1,0:T(8,128)S(1)}) custom-call(bf16[1024,512]{1,0:T(8,128)(2,1)S(1)} %get-tuple-element.52.p_ref, bf16[512,512]{1,0:T(8,128)(2,1)S(1)} %copy-done, bf16[512,512]{1,0:T(8,128)(2,1)S(1)} %copy-done.1, ...), custom_call_target="tpu_custom_call" | custom-call | flops 2529999872 | bytes 229999 | tf_op jit(solution)/shard_map/norm/pallas_call | solution.py:247
  19.3 0.5 %collective-permute-start.5 = (f32[32,256]{1,0:T(8,128)S(1)}, f32[32,256]{1,0:T(8,128)S(1)}, u32[]{:S(2)}, u32[]{:S(2)}) collective-permute-start(f32[32,256]{1,0:T(8,128)S(1)} %sum_3.1.refs_3_.own_ref), channel_id=1, source_target_pairs={{0,1},{1,0},{2,3},{3,2},{4,5},{5,4},{6,7},{7,6},{8,9},{9,8},{10,11... | collective-permute-start | bytes 98312 | tf_op jit(solution)/shard_map/ppermute | solution.py:234
  19.9 0.6 %collective-permute-done.7 = f32[32,256]{1,0:T(8,128)S(1)} collective-permute-done((f32[32,256]{1,0:T(8,128)S(1)}, f32[32,256]{1,0:T(8,128)S(1)}, u32[]{:S(2)}, u32[]{:S(2)}) %collective-permute-start.7) | collective-permute-done | bytes 32800 | tf_op jit(solution)/shard_map/ppermute | solution.py:234
  20.5 1.6 %collective-permute-start.10 = (f32[160,256]{1,0:T(8,128)S(1)}, f32[160,256]{1,0:T(8,128)S(1)}, u32[]{:S(2)}, u32[]{:S(2)}) collective-permute-start(f32[160,256]{1,0:T(8,128)S(1)} %get-tuple-element.62.rest_6_), channel_id=1, source_target_pairs={{0,4},{4,0},{8,12},{12,8},{1,5},{5,1},{9,13},{13,9},{2,6},{6,2},{1... | collective-permute-start | bytes 491528 | tf_op jit(solution)/shard_map/ppermute | solution.py:234
  22.1 2.1 %back_key.1 = (f32[2,4,2,64,256]{4,3,2,1,0:T(8,128)S(1)}, bf16[1024,512]{1,0:T(8,128)(2,1)S(1)}) custom-call(bf16[512,1024]{1,0:T(8,128)(2,1)S(1)} %get-tuple-element.48.pt_ref, f32[32,256]{1,0:T(8,128)S(1)} %sum_3.1.refs_3_.own_ref, f32[32,256]{1,0:T(8,128)S(1)} %collective-permute-done.5.got_ref, f32[1024,256]{1,0:T(8,128)S(1)} %get-tuple-element.55.rest_0_.rest_4_, ...), custom_call_target="tpu_custom_call" | custom-call | flops 5500000256 | bytes 500000 | tf_op jit(solution)/shard_map/back_key/pallas_call | solution.py:247
  24.4 2.1 %back_value.1 = (f32[2,2,4,64,256]{4,3,2,1,0:T(8,128)S(1)}, bf16[1024,512]{1,0:T(8,128)(2,1)S(1)}) custom-call(bf16[512,1024]{1,0:T(8,128)(2,1)S(1)} %get-tuple-element.48.pt_ref, f32[32,256]{1,0:T(8,128)S(1)} %sum_3.1.refs_3_.own_ref, f32[32,256]{1,0:T(8,128)S(1)} %collective-permute-done.5.got_ref, f32[1024,256]{1,0:T(8,128)S(1)} %get-tuple-element.59.rest_4_.rest_0_, ...), custom_call_target="tpu_custom_call" | custom-call | flops 5500000256 | bytes 500000 | tf_op jit(solution)/shard_map/back_value/pallas_call | solution.py:247
  26.6 0.6 %collective-permute-start.8 = (f32[2,4,64,256]{3,2,1,0:T(8,128)S(1)}, f32[2,4,64,256]{3,2,1,0:T(8,128)S(1)}, u32[]{:S(2)}, u32[]{:S(2)}) collective-permute-start(f32[2,4,64,256]{3,2,1,0:T(8,128)S(1)} %get-tuple-element.94), channel_id=1, source_target_pairs={{0,1},{1,0},{2,3},{3,2},{4,5},{5,4},{6,7},{7,6},{8,9},{9,8},{10,11... | collective-permute-start | bytes 1572872 | tf_op jit(solution)/shard_map/ppermute | solution.py:234
  27.2 1.3 %collective-permute-start.13 = (f32[256,256]{1,0:T(8,128)S(1)}, f32[256,256]{1,0:T(8,128)S(1)}, u32[]{:S(2)}, u32[]{:S(2)}) collective-permute-start(f32[256,256]{1,0:T(8,128)S(1)} %get-tuple-element.72.refs_2_), channel_id=1, source_target_pairs={{0,4},{4,0},{8,12},{12,8},{1,5},{5,1},{9,13},{13,9},{2,6},{6,2},{1... | collective-permute-start | bytes 786440 | tf_op jit(solution)/shard_map/ppermute | solution.py:234
  28.7 1.5 %collective-permute-start.12 = (f32[256,256]{1,0:T(8,128)S(1)}, f32[256,256]{1,0:T(8,128)S(1)}, u32[]{:S(2)}, u32[]{:S(2)}) collective-permute-start(f32[256,256]{1,0:T(8,128)S(1)} %get-tuple-element.73.rest_0_), channel_id=1, source_target_pairs={{0,2},{2,0},{1,3},{3,1},{4,6},{6,4},{5,7},{7,5},{8,10},{10,8},{9,1... | collective-permute-start | bytes 786440 | tf_op jit(solution)/shard_map/ppermute | solution.py:234
  30.3 1.7 %collective-permute-start.11 = (f32[96,256]{1,0:T(8,128)S(1)}, f32[96,256]{1,0:T(8,128)S(1)}, u32[]{:S(2)}, u32[]{:S(2)}) collective-permute-start(f32[96,256]{1,0:T(8,128)S(1)} %get-tuple-element.71.refs_2_), channel_id=1, source_target_pairs={{0,8},{4,12},{8,0},{12,4},{1,9},{5,13},{9,1},{13,5},{2,10},{6,14},... | collective-permute-start | bytes 294920 | tf_op jit(solution)/shard_map/ppermute | solution.py:234
  32.0 1.3 %grad_points_part.1.refs_2_.acc_ref = f32[1024,512]{1,0:T(8,128)S(1)} custom-call(bf16[1024,512]{1,0:T(8,128)(2,1)S(1)} %get-tuple-element.63.rest_6_.gk_ref, bf16[1024,512]{1,0:T(8,128)(2,1)S(1)} %get-tuple-element.66.refs_3_.gv_ref, bf16[512,512]{1,0:T(8,128)(2,1)S(1)} %copy-done, bf16[512,512]{1,0:T(8,128)(2,1)S(1)} %copy-done.1, ...), custom_call_target="tpu_custom_call" | custom-call | flops 1430000000 | bytes 130000 | tf_op jit(solution)/shard_map/grad_points_part/pallas_call | solution.py:247
  33.3 4.4 %collective-permute-done.13.refs_1_ = f32[256,256]{1,0:T(8,128)S(1)} collective-permute-done((f32[256,256]{1,0:T(8,128)S(1)}, f32[256,256]{1,0:T(8,128)S(1)}, u32[]{:S(2)}, u32[]{:S(2)}) %collective-permute-start.13) | collective-permute-done | bytes 262176 | tf_op jit(solution)/shard_map/ppermute | solution.py:234
  38.0 2.6 %collective-permute-start.16 = (f32[128,256]{1,0:T(8,128)S(1)}, f32[128,256]{1,0:T(8,128)S(1)}, u32[]{:S(2)}, u32[]{:S(2)}) collective-permute-start(f32[128,256]{1,0:T(8,128)S(1)} %get-tuple-element.78.refs_2_), channel_id=1, source_target_pairs={{0,8},{4,12},{8,0},{12,4},{1,9},{5,13},{9,1},{13,5},{2,10},{6,14},... | collective-permute-start | bytes 393224 | tf_op jit(solution)/shard_map/ppermute | solution.py:234
  40.6 1.5 %collective-permute-start.14 = (f32[32,256]{1,0:T(8,128)S(1)}, f32[32,256]{1,0:T(8,128)S(1)}, u32[]{:S(2)}, u32[]{:S(2)}) collective-permute-start(f32[32,256]{1,0:T(8,128)S(1)} %get-tuple-element.80), channel_id=1, source_target_pairs={{0,2},{2,0},{1,3},{3,1},{4,6},{6,4},{5,7},{7,5},{8,10},{10,8},{9,1... | collective-permute-start | bytes 98312 | tf_op jit(solution)/shard_map/ppermute | solution.py:234
  42.1 2.4 %collective-permute-done.14 = f32[32,256]{1,0:T(8,128)S(1)} collective-permute-done((f32[32,256]{1,0:T(8,128)S(1)}, f32[32,256]{1,0:T(8,128)S(1)}, u32[]{:S(2)}, u32[]{:S(2)}) %collective-permute-start.14) | collective-permute-done | bytes 32800 | tf_op jit(solution)/shard_map/ppermute | solution.py:234
  44.6 0.4 collective-permute-done.17.refs_1_
  45.0 0.3 collective-permute-start.19
  45.3 1.0 %collective-permute-done.16.refs_1_ = f32[128,256]{1,0:T(8,128)S(1)} collective-permute-done((f32[128,256]{1,0:T(8,128)S(1)}, f32[128,256]{1,0:T(8,128)S(1)}, u32[]{:S(2)}, u32[]{:S(2)}) %collective-permute-start.16) | collective-permute-done | bytes 131104 | tf_op jit(solution)/shard_map/ppermute | solution.py:234
  46.3 1.5 %collective-permute-start.18 = (f32[64,256]{1,0:T(8,128)S(1)}, f32[64,256]{1,0:T(8,128)S(1)}, u32[]{:S(2)}, u32[]{:S(2)}) collective-permute-start(f32[64,256]{1,0:T(8,128)S(1)} %get-tuple-element.88), channel_id=1, source_target_pairs={{0,2},{2,0},{1,3},{3,1},{4,6},{6,4},{5,7},{7,5},{8,10},{10,8},{9,1... | collective-permute-start | bytes 196616 | tf_op jit(solution)/shard_map/ppermute | solution.py:234
  47.9 2.4 %grad_points.1 = (bf16[1024,512]{1,0:T(8,128)(2,1)}, f32[64,256]{1,0:T(8,128)}) custom-call(f32[1024,512]{1,0:T(8,128)S(1)} %grad_points_part.1.refs_2_.acc_ref, bf16[1024,512]{1,0:T(8,128)(2,1)S(1)} %copy-done.2, bf16[512,512]{1,0:T(8,128)(2,1)S(1)} %copy-done.3, f32[32,256]{1,0:T(8,128)S(1)} %add.7.own_ref, f32[32,256]{1,0:T(8,128)S(1)} %collective-permute-done.15.got_ref, ...), custom_call_target="tpu_custom_call" | custom-call | flops 1650000000 | bytes 150000 | tf_op jit(solution)/shard_map/grad_points/pallas_call | solution.py:247
  50.3 0.4 collective-permute-done.18.refs_1_
  50.6 0.7 %collective-permute-done.19.refs_3_ = f32[64,256]{1,0:T(8,128)S(1)} collective-permute-done((f32[64,256]{1,0:T(8,128)S(1)}, f32[64,256]{1,0:T(8,128)S(1)}, u32[]{:S(2)}, u32[]{:S(2)}) %collective-permute-start.19) | collective-permute-done | bytes 65568 | tf_op jit(solution)/shard_map/ppermute | solution.py:234
  51.4 0.7 %scale.1 = (f32[64,256]{1,0:T(8,128)}, f32[64,256]{1,0:T(8,128)}) custom-call(f32[64,256]{1,0:T(8,128)S(1)} %bitcast.37, f32[64,256]{1,0:T(8,128)S(1)} %collective-permute-done.18.refs_1_, f32[64,256]{1,0:T(8,128)S(1)} %bitcast.36, f32[64,256]{1,0:T(8,128)S(1)} %collective-permute-done.19.refs_3_), custom_call_target="tpu_custom_call" | custom-call | flops 770000000 | bytes 70000 | tf_op jit(solution)/shard_map/scale/pallas_call | solution.py:247
  (46 shorter events, 1.4 us)
Async XLA Ops:
  3.5 1.4 %collective-permute-start = (f32[32,256]{1,0:T(8,128)S(1)}, f32[32,256]{1,0:T(8,128)S(1)}, u32[]{:S(2)}, u32[]{:S(2)}) collective-permute-start(f32[32,256]{1,0:T(8,128)S(1)} %get-tuple-element.98), channel_id=1, source_target_pairs={{0,1},{1,0},{2,3},{3,2},{4,5},{5,4},{6,7},{7,6},{8,9},{9,8},{10,11... | collective-permute-start | bytes 98312 | tf_op jit(solution)/shard_map/ppermute | solution.py:234
  4.2 3.6 %collective-permute-start.2 = (f32[2,4,64,256]{3,2,1,0:T(8,128)S(1)}, f32[2,4,64,256]{3,2,1,0:T(8,128)S(1)}, u32[]{:S(2)}, u32[]{:S(2)}) collective-permute-start(f32[2,4,64,256]{3,2,1,0:T(8,128)S(1)} %get-tuple-element.96), channel_id=1, source_target_pairs={{0,1},{1,0},{2,3},{3,2},{4,5},{5,4},{6,7},{7,6},{8,9},{9,8},{10,11... | collective-permute-start | bytes 1572872 | tf_op jit(solution)/shard_map/ppermute | solution.py:234
  4.9 6.9 %copy-start = (bf16[512,512]{1,0:T(8,128)(2,1)S(1)}, bf16[512,512]{1,0:T(8,128)(2,1)}, u32[]{:S(2)}) copy-start(bf16[512,512]{1,0:T(8,128)(2,1)} %wk_ref.5) | copy-start | bytes 1572868
  4.9 6.9 %copy-start.1 = (bf16[512,512]{1,0:T(8,128)(2,1)S(1)}, bf16[512,512]{1,0:T(8,128)(2,1)}, u32[]{:S(2)}) copy-start(bf16[512,512]{1,0:T(8,128)(2,1)} %wv_ref.5) | copy-start | bytes 1572868
  4.9 4.8 %collective-permute-start.1 = (f32[32,256]{1,0:T(8,128)S(1)}, f32[32,256]{1,0:T(8,128)S(1)}, u32[]{:S(2)}, u32[]{:S(2)}) collective-permute-start(f32[32,256]{1,0:T(8,128)S(1)} %sum_0.1.refs_2_.a_ref), channel_id=1, source_target_pairs={{0,2},{2,0},{1,3},{3,1},{4,6},{6,4},{5,7},{7,5},{8,10},{10,8},{9,1... | collective-permute-start | bytes 98312 | tf_op jit(solution)/shard_map/ppermute | solution.py:234
  7.9 12.6 %collective-permute-start.6 = (f32[256,256]{1,0:T(8,128)S(1)}, f32[256,256]{1,0:T(8,128)S(1)}, u32[]{:S(2)}, u32[]{:S(2)}) collective-permute-start(f32[256,256]{1,0:T(8,128)S(1)} %get-tuple-element.51.rest_0_), channel_id=1, source_target_pairs={{0,2},{2,0},{1,3},{3,1},{4,6},{6,4},{5,7},{7,5},{8,10},{10,8},{9,1... | collective-permute-start | bytes 786440 | tf_op jit(solution)/shard_map/ppermute | solution.py:234
  9.7 4.4 %collective-permute-start.3 = (f32[32,256]{1,0:T(8,128)S(1)}, f32[32,256]{1,0:T(8,128)S(1)}, u32[]{:S(2)}, u32[]{:S(2)}) collective-permute-start(f32[32,256]{1,0:T(8,128)S(1)} %sum_1.1.rest_0_.a_ref), channel_id=1, source_target_pairs={{0,4},{4,0},{8,12},{12,8},{1,5},{5,1},{9,13},{13,9},{2,6},{6,2},{1... | collective-permute-start | bytes 98312 | tf_op jit(solution)/shard_map/ppermute | solution.py:234
  14.2 5.1 %collective-permute-start.4 = (f32[32,256]{1,0:T(8,128)S(1)}, f32[32,256]{1,0:T(8,128)S(1)}, u32[]{:S(2)}, u32[]{:S(2)}) collective-permute-start(f32[32,256]{1,0:T(8,128)S(1)} %sum_2.1.rest_1_.a_ref), channel_id=1, source_target_pairs={{0,8},{4,12},{8,0},{12,4},{1,9},{5,13},{9,1},{13,5},{2,10},{6,14},... | collective-permute-start | bytes 98312 | tf_op jit(solution)/shard_map/ppermute | solution.py:234
  19.2 1.3 %collective-permute-start.7 = (f32[32,256]{1,0:T(8,128)S(1)}, f32[32,256]{1,0:T(8,128)S(1)}, u32[]{:S(2)}, u32[]{:S(2)}) collective-permute-start(f32[32,256]{1,0:T(8,128)S(1)} %slice_bitcast_fusion.3), channel_id=1, source_target_pairs={{0,1},{1,0},{2,3},{3,2},{4,5},{5,4},{6,7},{7,6},{8,9},{9,8},{10,11... | collective-permute-start | bytes 98312 | tf_op jit(solution)/shard_map/ppermute | solution.py:234
  19.3 2.8 %collective-permute-start.5 = (f32[32,256]{1,0:T(8,128)S(1)}, f32[32,256]{1,0:T(8,128)S(1)}, u32[]{:S(2)}, u32[]{:S(2)}) collective-permute-start(f32[32,256]{1,0:T(8,128)S(1)} %sum_3.1.refs_3_.own_ref), channel_id=1, source_target_pairs={{0,1},{1,0},{2,3},{3,2},{4,5},{5,4},{6,7},{7,6},{8,9},{9,8},{10,11... | collective-permute-start | bytes 98312 | tf_op jit(solution)/shard_map/ppermute | solution.py:234
  20.5 6.6 %collective-permute-start.10 = (f32[160,256]{1,0:T(8,128)S(1)}, f32[160,256]{1,0:T(8,128)S(1)}, u32[]{:S(2)}, u32[]{:S(2)}) collective-permute-start(f32[160,256]{1,0:T(8,128)S(1)} %get-tuple-element.62.rest_6_), channel_id=1, source_target_pairs={{0,4},{4,0},{8,12},{12,8},{1,5},{5,1},{9,13},{13,9},{2,6},{6,2},{1... | collective-permute-start | bytes 491528 | tf_op jit(solution)/shard_map/ppermute | solution.py:234
  24.3 2.8 %collective-permute-start.9 = (f32[4,2,64,256]{3,2,1,0:T(8,128)S(1)}, f32[4,2,64,256]{3,2,1,0:T(8,128)S(1)}, u32[]{:S(2)}, u32[]{:S(2)}) collective-permute-start(f32[4,2,64,256]{3,2,1,0:T(8,128)S(1)} %get-tuple-element.92), channel_id=1, source_target_pairs={{0,1},{1,0},{2,3},{3,2},{4,5},{5,4},{6,7},{7,6},{8,9},{9,8},{10,11... | collective-permute-start | bytes 1572872 | tf_op jit(solution)/shard_map/ppermute | solution.py:234
  26.6 2.1 %collective-permute-start.8 = (f32[2,4,64,256]{3,2,1,0:T(8,128)S(1)}, f32[2,4,64,256]{3,2,1,0:T(8,128)S(1)}, u32[]{:S(2)}, u32[]{:S(2)}) collective-permute-start(f32[2,4,64,256]{3,2,1,0:T(8,128)S(1)} %get-tuple-element.94), channel_id=1, source_target_pairs={{0,1},{1,0},{2,3},{3,2},{4,5},{5,4},{6,7},{7,6},{8,9},{9,8},{10,11... | collective-permute-start | bytes 1572872 | tf_op jit(solution)/shard_map/ppermute | solution.py:234
  27.2 10.4 %collective-permute-start.13 = (f32[256,256]{1,0:T(8,128)S(1)}, f32[256,256]{1,0:T(8,128)S(1)}, u32[]{:S(2)}, u32[]{:S(2)}) collective-permute-start(f32[256,256]{1,0:T(8,128)S(1)} %get-tuple-element.72.refs_2_), channel_id=1, source_target_pairs={{0,4},{4,0},{8,12},{12,8},{1,5},{5,1},{9,13},{13,9},{2,6},{6,2},{1... | collective-permute-start | bytes 786440 | tf_op jit(solution)/shard_map/ppermute | solution.py:234
  28.7 9.0 %collective-permute-start.12 = (f32[256,256]{1,0:T(8,128)S(1)}, f32[256,256]{1,0:T(8,128)S(1)}, u32[]{:S(2)}, u32[]{:S(2)}) collective-permute-start(f32[256,256]{1,0:T(8,128)S(1)} %get-tuple-element.73.rest_0_), channel_id=1, source_target_pairs={{0,2},{2,0},{1,3},{3,1},{4,6},{6,4},{5,7},{7,5},{8,10},{10,8},{9,1... | collective-permute-start | bytes 786440 | tf_op jit(solution)/shard_map/ppermute | solution.py:234
  30.3 10.3 %collective-permute-start.11 = (f32[96,256]{1,0:T(8,128)S(1)}, f32[96,256]{1,0:T(8,128)S(1)}, u32[]{:S(2)}, u32[]{:S(2)}) collective-permute-start(f32[96,256]{1,0:T(8,128)S(1)} %get-tuple-element.71.refs_2_), channel_id=1, source_target_pairs={{0,8},{4,12},{8,0},{12,4},{1,9},{5,13},{9,1},{13,5},{2,10},{6,14},... | collective-permute-start | bytes 294920 | tf_op jit(solution)/shard_map/ppermute | solution.py:234
  37.7 10.2 %copy-start.2 = (bf16[1024,512]{1,0:T(8,128)(2,1)S(1)}, bf16[1024,512]{1,0:T(8,128)(2,1)}, u32[]{:S(2)}) copy-start(bf16[1024,512]{1,0:T(8,128)(2,1)} %c_ref.1) | copy-start | bytes 3145732
  37.7 10.2 %copy-start.3 = (bf16[512,512]{1,0:T(8,128)(2,1)S(1)}, bf16[512,512]{1,0:T(8,128)(2,1)}, u32[]{:S(2)}) copy-start(bf16[512,512]{1,0:T(8,128)(2,1)} %wq_ref.1) | copy-start | bytes 1572868
  37.7 7.2 %collective-permute-start.17 = (f32[128,256]{1,0:T(8,128)S(1)}, f32[128,256]{1,0:T(8,128)S(1)}, u32[]{:S(2)}, u32[]{:S(2)}) collective-permute-start(f32[128,256]{1,0:T(8,128)S(1)} %get-tuple-element.79.rest_1_), channel_id=1, source_target_pairs={{0,4},{4,0},{8,12},{12,8},{1,5},{5,1},{9,13},{13,9},{2,6},{6,2},{1... | collective-permute-start | bytes 393224 | tf_op jit(solution)/shard_map/ppermute | solution.py:234
  38.0 8.3 %collective-permute-start.16 = (f32[128,256]{1,0:T(8,128)S(1)}, f32[128,256]{1,0:T(8,128)S(1)}, u32[]{:S(2)}, u32[]{:S(2)}) collective-permute-start(f32[128,256]{1,0:T(8,128)S(1)} %get-tuple-element.78.refs_2_), channel_id=1, source_target_pairs={{0,8},{4,12},{8,0},{12,4},{1,9},{5,13},{9,1},{13,5},{2,10},{6,14},... | collective-permute-start | bytes 393224 | tf_op jit(solution)/shard_map/ppermute | solution.py:234
  40.6 4.0 %collective-permute-start.14 = (f32[32,256]{1,0:T(8,128)S(1)}, f32[32,256]{1,0:T(8,128)S(1)}, u32[]{:S(2)}, u32[]{:S(2)}) collective-permute-start(f32[32,256]{1,0:T(8,128)S(1)} %get-tuple-element.80), channel_id=1, source_target_pairs={{0,2},{2,0},{1,3},{3,1},{4,6},{6,4},{5,7},{7,5},{8,10},{10,8},{9,1... | collective-permute-start | bytes 98312 | tf_op jit(solution)/shard_map/ppermute | solution.py:234
  44.6 3.2 %collective-permute-start.15 = (f32[32,256]{1,0:T(8,128)S(1)}, f32[32,256]{1,0:T(8,128)S(1)}, u32[]{:S(2)}, u32[]{:S(2)}) collective-permute-start(f32[32,256]{1,0:T(8,128)S(1)} %add.7.own_ref), channel_id=1, source_target_pairs={{0,1},{1,0},{2,3},{3,2},{4,5},{5,4},{6,7},{7,6},{8,9},{9,8},{10,11... | collective-permute-start | bytes 98312 | tf_op jit(solution)/shard_map/ppermute | solution.py:234
  45.0 6.4 %collective-permute-start.19 = (f32[64,256]{1,0:T(8,128)S(1)}, f32[64,256]{1,0:T(8,128)S(1)}, u32[]{:S(2)}, u32[]{:S(2)}) collective-permute-start(f32[64,256]{1,0:T(8,128)S(1)} %get-tuple-element.86.refs_2_), channel_id=1, source_target_pairs={{0,8},{4,12},{8,0},{12,4},{1,9},{5,13},{9,1},{13,5},{2,10},{6,14},... | collective-permute-start | bytes 196616 | tf_op jit(solution)/shard_map/ppermute | solution.py:234
  46.3 4.3 %collective-permute-start.18 = (f32[64,256]{1,0:T(8,128)S(1)}, f32[64,256]{1,0:T(8,128)S(1)}, u32[]{:S(2)}, u32[]{:S(2)}) collective-permute-start(f32[64,256]{1,0:T(8,128)S(1)} %get-tuple-element.88), channel_id=1, source_target_pairs={{0,2},{2,0},{1,3},{3,1},{4,6},{6,4},{5,7},{7,5},{8,10},{10,8},{9,1... | collective-permute-start | bytes 196616 | tf_op jit(solution)/shard_map/ppermute | solution.py:234

commit v4 on v2

v4 whole, which is shorter than its diff:
```python
import functools

import jax
import jax.numpy as jnp
from jax import lax
from jax.experimental import pallas as pl
from jax.experimental.pallas import tpu as pltpu
from jax.sharding import PartitionSpec as P

HS = 32
F32 = jnp.float32
BF16 = jnp.bfloat16
NT = (((1,), (1,)), ((), ()))
TN = (((0,), (0,)), ((), ()))
NN = (((1,), (0,)), ((), ()))
VMEM = pl.BlockSpec(memory_space=pltpu.VMEM)
HBM = pl.BlockSpec(memory_space=pltpu.HBM)
ANY = pl.BlockSpec(memory_space=pl.ANY)
CHUNKS = 2
BLOCKS = 4
NORM_BLOCKS = 1
ORDER = "kVMPkVTkVS"
US = {"end_query": 2.0, "grad_points": 0.01, "back_own": 0.01, "add_key_0": 5.0, "sum_0": 5.0, "back_key": 5.0, "back_value": 5.0}

PARAMS = pltpu.CompilerParams(vmem_limit_bytes=16 * 1024 * 1024)


def dot(a, b, dims):
    return lax.dot_general(a, b, dims, preferred_element_type=F32)


def split(x):
    high = x.astype(BF16)
    return high, (x - high.astype(F32)).astype(BF16)


def head_mask(size):
    rows = lax.broadcasted_iota(jnp.int32, (size, size), 0) // HS
    cols = lax.broadcasted_iota(jnp.int32, (size, size), 1) // HS
    return rows == cols


def averager(size):
    return jnp.where(head_mask(size), F32(1.0 / HS), F32(0.0)).astype(BF16)


def pack(full):
    size = full.shape[0]
    kept = jnp.where(head_mask(size), full, F32(0.0))
    total = kept[:HS]
    for i in range(1, size // HS):
        total = total + kept[i * HS : (i + 1) * HS]
    return total


def unpack(packed):
    size = packed.shape[1]
    tiled = jnp.concatenate([packed] * (size // HS), axis=0)
    return jnp.where(head_mask(size), tiled, F32(0.0))


def bits(axis):
    bit = 1
    while bit < lax.axis_size(axis):
        yield axis, bit
        bit *= 2


def routes(name):
    x, z = list(bits("mp")), list(bits("points"))
    if name == "state":
        return x + z, z + x
    return x + z, z[:1] + x + z[1:]


def place(refs, value, g, name):
    z, x, s = lax.axis_index("points"), lax.axis_index("mp"), lax.axis_index("sub")
    nz, nx, ns = lax.axis_size("points"), lax.axis_size("mp"), lax.axis_size("sub")
    rb, cb = refs.shape[-2:]
    count = value.shape[1] // cb
    for zb in range(nz):
        for sb in range(ns):
            row = (zb * ns + sb) * rb
            for j in range(count):
                away = {"points": z ^ zb, "mp": x ^ (g * count + j)}
                spot = 0
                for t, (axis, bit) in enumerate(routes(name)[sb]):
                    spot = spot + jnp.where((away[axis] & bit) != 0, 1 << t, 0)
                refs[s ^ sb, spot] = value[row : row + rb, j * cb : (j + 1) * cb]


def half_columns(g, width):
    half = width // lax.axis_size("sub")
    return pl.ds(pl.multiple_of(g * half, half), half)


def cross_kernel(p_hbm, c_hbm, wq_hbm, sums, g_ref, p_ref, pt_ref, c_ref, wq_ref, sems):
    rows, width = p_hbm.shape
    ns = lax.axis_size("sub")
    s = lax.axis_index("sub")
    half = width // ns
    chunk = rows // CHUNKS
    spans = [slice(r * chunk, (r + 1) * chunk) for r in range(CHUNKS)]
    loads = []
    for r, span in enumerate(spans):
        for k, (src, dst) in enumerate(((p_hbm, p_ref), (c_hbm, c_ref))):
            loads.append(pltpu.make_async_copy(src.at[span, :], dst.at[span, :], sems.at[2 * r + k]))
    loads.append(pltpu.make_async_copy(wq_hbm, wq_ref, sems.at[2 * CHUNKS]))
    for load in loads:
        load.start()
    for r, span in enumerate(spans):
        loads[2 * r].wait()
        flipped = p_ref[span, :].T
        pt_ref[:, span] = flipped
        loads[2 * r + 1].wait()
        for g in range(ns):
            cols = slice(g * half, (g + 1) * half)
            part = dot(flipped, c_ref[span, cols], NN)
            sums[:, cols] = part if r == 0 else sums[:, cols] + part
    loads[-1].wait()
    for g in range(ns):
        cols = slice(g * half, (g + 1) * half)
        high, low = split(sums[:, cols])
        wq = wq_ref[:, cols]
        g_ref[s ^ g] = pack(dot(wq, high, TN) + dot(wq, low, TN))


def deal_kernel(sums_ref, *rest):
    half = sums_ref.shape[1] // lax.axis_size("sub")
    for g in range(lax.axis_size("sub")):
        place(rest[-1], sums_ref[:, g * half : (g + 1) * half], g, "query")


def norm_kernel(other, p_ref, wk_ref, wv_ref, *rest):
    kn_ref, kr_ref, vn_ref, vr_ref, s_ref, c_ref, sq_ref = rest[-7:]
    rows, width = p_ref.shape
    cols = half_columns(lax.axis_index("sub") ^ other, width)
    mean = averager(width // lax.axis_size("sub"))
    chunk = rows // NORM_BLOCKS
    spans = [slice(r * chunk, (r + 1) * chunk) for r in range(NORM_BLOCKS)]
    for w, w_ref in enumerate((wk_ref, wv_ref)):
        raw = w_ref[:, cols]
        high, low = split(raw.astype(F32) - dot(raw, mean, NN))
        for span in spans:
            p = p_ref[span, :]
            centred = dot(p, high, NN) + dot(p, low, NN)
            c_ref[w, span, :] = centred
            sq_ref[w, span, :] = (centred * centred).astype(BF16)
    for w, (n_ref, r_ref) in enumerate(((kn_ref, kr_ref), (vn_ref, vr_ref))):
        for span in spans:
            inverse = lax.rsqrt(dot(sq_ref[w, span, :], mean, NN) + 1e-05)
            n_ref[span, :] = c_ref[w, span, :] * inverse
            r_ref[span, :] = inverse
    s_ref[...] = pack(dot(kn_ref[...].astype(BF16), vn_ref[...].astype(BF16), TN))


def back_centre(total, key, g_ref):
    full = unpack((g_ref[...] / total).astype(BF16).astype(F32))
    mean = averager(full.shape[0])
    grouped = dot(mean, full.astype(BF16), NN) if key else dot(full.astype(BF16), mean, NN)
    return split(full - grouped)


def back_halves(total, keys, g_ref, sets, gl_refs, grad_refs, prod_refs):
    rows, half = gl_refs[0].shape
    mean = averager(half)
    chunk = rows // BLOCKS
    spans = [slice(r * chunk, (r + 1) * chunk) for r in range(BLOCKS)]
    centred = [back_centre(total, key, g_ref) for key in keys]
    for key, (high, small), (n_ref, r_ref, o_ref), grad_ref, prod_ref in zip(keys, centred, sets, grad_refs, prod_refs):
        dims = NT if key else NN
        for span in spans:
            low = o_ref[span, :].astype(BF16)
            grad = dot(low, high, dims) + dot(low, small, dims)
            grad_ref[span, :] = grad
            prod_ref[span, :] = (grad * n_ref[span, :]).astype(BF16)
    for (n_ref, r_ref, o_ref), gl_ref, grad_ref, prod_ref in zip(sets, gl_refs, grad_refs, prod_refs):
        for span in spans:
            second = dot(prod_ref[span, :], mean, NN)
            gl_ref[span, :] = ((grad_ref[span, :] - n_ref[span, :] * second) * r_ref[span, :]).astype(BF16)


def own_kernel(total, pt_ref, g_ref, kn_ref, kr_ref, vn_ref, vr_ref, *rest):
    gk_ref, gv_ref, wk_ref, wv_ref, kgrad_ref, vgrad_ref, kprod_ref, vprod_ref = rest[-8:]
    sets = ((kn_ref, kr_ref, vn_ref), (vn_ref, vr_ref, kn_ref))
    back_halves(total, (True, False), g_ref, sets, (gk_ref, gv_ref), (kgrad_ref, vgrad_ref), (kprod_ref, vprod_ref))
    wk_ref[...] = dot(pt_ref[...], gk_ref[...], NN)
    wv_ref[...] = dot(pt_ref[...], gv_ref[...], NN)


def other_kernel(total, key, pt_ref, own_ref, g_ref, n_ref, r_ref, o_ref, *rest):
    gl_ref, w_ref, grad_ref, prod_ref = rest[-4:]
    s = lax.axis_index("sub")
    back_halves(total, (key,), g_ref, ((n_ref, r_ref, o_ref),), (gl_ref,), (grad_ref,), (prod_ref,))
    place(w_ref, own_ref[...], s, "key")
    place(w_ref, dot(pt_ref[...], gl_ref[...], NN), 1 - s, "key")


def points_kernel(*refs):
    acc_ref = refs[-1]
    rows, width = acc_ref.shape
    s = lax.axis_index("sub")
    chunk = rows // BLOCKS
    for r in range(BLOCKS):
        span = slice(r * chunk, (r + 1) * chunk)
        total = None
        for w_ref, halves in ((refs[4], refs[:2]), (refs[5], refs[2:4])):
            for other, gl_ref in enumerate(halves):
                part = dot(gl_ref[span, :], w_ref[:, half_columns(s ^ other, width)], NT)
                total = part if total is None else total + part
        acc_ref[span, :] = total


def state_low(total, ref):
    return (ref[...] / total).astype(BF16).astype(F32)


def query_own_kernel(total, acc_ref, c_ref, wq_ref, own_ref, *rest):
    out_ref, q_ref = rest[-2:]
    rows, width = c_ref.shape
    cols = half_columns(lax.axis_index("sub"), width)
    q_ref[...] = dot(c_ref[:, cols], unpack(state_low(total, own_ref)).astype(BF16), NT).astype(BF16)
    chunk = rows // BLOCKS
    for r in range(BLOCKS):
        span = slice(r * chunk, (r + 1) * chunk)
        out_ref[span, :] = acc_ref[span, :] + dot(q_ref[span, :], wq_ref[:, cols], NT)


def last_kernel(total, acc_ref, c_ref, wq_ref, own_ref, got_ref, m_ref, *rest):
    parts, outs, (q_ref, gp_ref, g_ref, sems) = rest[:4], rest[-8:-4], rest[-4:]
    rows, width = c_ref.shape
    rb, cb = m_ref.shape
    ns, nx = lax.axis_size("sub"), lax.axis_size("mp")
    s, x = lax.axis_index("sub"), lax.axis_index("mp")
    other = 1 - s
    cols = half_columns(other, width)
    low_own, low_got = state_low(total, own_ref), state_low(total, got_ref)
    q_ref[...] = dot(c_ref[:, cols], unpack(low_got).astype(BF16), NT).astype(BF16)
    copies = []
    for i in range(2):
        kept_ref, got_part = parts[2 * i], parts[2 * i + 1]
        g_ref[1 + i] = (kept_ref[...] + got_part[:rb, :]) / total
        copies.append(pltpu.make_async_copy(g_ref.at[1 + i], outs[2 + i], sems.at[1 + i]))
        copies[-1].start()
    chunk = rows // BLOCKS
    for r in range(BLOCKS):
        span = slice(r * chunk, (r + 1) * chunk)
        gp_ref[span, :] = (acc_ref[span, :] + dot(q_ref[span, :], wq_ref[:, cols], NT)).astype(BF16)
        copies.append(pltpu.make_async_copy(gp_ref.at[span, :], outs[0].at[span, :], sems.at[3 + r]))
        copies[-1].start()
    whole = jnp.concatenate([jnp.where(s == g, low_own, low_got) for g in range(ns)], axis=1)
    high, rest_ = split(m_ref[...])
    third = (m_ref[...] - high.astype(F32) - rest_.astype(F32)).astype(BF16)
    for xb in range(nx):

        @pl.when(x == xb)
        def _():
            state = unpack(whole[:, xb * cb : (xb + 1) * cb]).astype(BF16)
            g_ref[0] = (dot(high, state, NT) + dot(rest_, state, NT) + dot(third, state, NT)) / total

    copies.append(pltpu.make_async_copy(g_ref.at[0], outs[1], sems.at[0]))
    copies[-1].start()
    for copy in copies:
        copy.wait()


def step_kernel(arrived, tailed, *refs):
    kept_ref, send_ref, keep_ref = refs[0], refs[-2], refs[-1]
    count, size = keep_ref.shape[0], keep_ref.shape[1]

    def block(i):
        return kept_ref[i] + refs[1][i * size : (i + 1) * size, :] if arrived else kept_ref[i]

    for i in range(count):
        keep_ref[i] = block(2 * i)
        send_ref[i * size : (i + 1) * size, :] = block(2 * i + 1)
    if tailed:
        send_ref[count * size :, :] = refs[1 + arrived][...]


def call(kernel, name, out_shape, inputs, specs, after=(), scratch=(), us=1.0, outs=None):
    us = US.get(name, us)
    inputs, specs = list(inputs) + list(after), list(specs) + [ANY] * len(after)
    return pl.pallas_call(
        kernel,
        out_shape=out_shape,
        in_specs=specs,
        out_specs=outs or (VMEM,) * len(out_shape),
        scratch_shapes=scratch,
        compiler_params=PARAMS,
        cost_estimate=pl.CostEstimate(flops=int(us * 1.1e9), bytes_accessed=int(us * 1e5), transcendentals=0),
        name=name,
    )(*inputs)


def swap_cores(value):
    return lax.ppermute(value, "sub", [(i, i ^ 1) for i in range(lax.axis_size("sub"))])


def swap(value, exchanges):
    nz, nx, ns = lax.axis_size("points"), lax.axis_size("mp"), lax.axis_size("sub")
    pairs = []
    for z in range(nz):
        for x in range(nx):
            for s, (axis, bit) in enumerate(exchanges):
                to = (z ^ bit, x) if axis == "points" else (z, x ^ bit)
                pairs.append(((z * nx + x) * ns + s, (to[0] * nx + to[1]) * ns + s))
    return lax.ppermute(value, ("points", "mp", "sub"), pairs)


def sum_kernel(a_ref, b_ref, *rest):
    rest[-1][...] = a_ref[...] + b_ref[: a_ref.shape[0], :]


class Total:
    def __init__(self, parts):
        self.value, self.got, self.done = parts[0], swap_cores(parts[1]), 0
        self.todo = list(zip(*routes("state")))

    def add(self, after=()):
        (self.value,) = call(
            sum_kernel,
            "sum_%d" % self.done,
            (jax.ShapeDtypeStruct(self.value.shape, F32),),
            (self.value, self.got),
            [VMEM] * 2,
            after=after,
            us=0.1,
        )
        self.sent = self.value
        self.done += 1
        if self.todo:
            self.got = swap(self.value, self.todo.pop(0))
            return True
        self.got = swap_cores(self.value)
        return False


class Tail:
    def __init__(self, value):
        self.value, self.got = value, None
        self.todo = [list(route) for route in routes("state")]

    def takes(self, exchanges):
        return all(one in todo for one, todo in zip(exchanges, self.todo))

    def add(self, after=()):
        if self.got is not None:
            (self.value,) = call(
                sum_kernel,
                "sum_state",
                (jax.ShapeDtypeStruct(self.value.shape, F32),),
                (self.value, self.got.reshape(self.value.shape)),
                [VMEM] * 2,
                after=after,
                us=0.1,
            )
        return self.value

    def sent(self, exchanges, got):
        self.got = got
        for one, todo in zip(exchanges, self.todo):
            todo.remove(one)

    def step(self, after=()):
        self.add(after)
        exchanges = [todo[0] for todo in self.todo]
        self.sent(exchanges, swap(self.value, exchanges))


class Scatter:
    def __init__(self, blocks, name):
        self.name, self.done = name, 0
        self.kept, self.got = blocks[0], swap_cores(blocks[1])
        self.todo = list(zip(*routes(name)))

    def step(self, after=(), tail=None):
        exchanges = self.todo.pop(0)
        blocks, rb, cb = self.kept.shape
        got = () if self.got is None else (self.got.reshape(-1, cb),)
        count = blocks // 2
        tailed = tail is not None and tail.takes(exchanges)
        extra = (tail.add().reshape(-1, cb),) if tailed else ()
        rows = count * rb
        shape = jax.ShapeDtypeStruct
        self.sent, self.kept = call(
            functools.partial(step_kernel, len(got), tailed),
            "add_%s_%d" % (self.name, self.done),
            (shape((rows + (extra[0].shape[0] if tailed else 0), cb), F32), shape((count, rb, cb), F32)),
            (self.kept,) + got + extra,
            [VMEM] * (1 + len(got) + tailed),
            after=after,
            us=0.2,
        )
        self.got = swap(self.sent, exchanges)
        if tailed:
            tail.sent(exchanges, self.got[rows:])
        self.done += 1

    def settle(self):
        blocks, rb, cb = self.kept.shape
        (summed,) = call(
            sum_kernel,
            "settle_" + self.name,
            (jax.ShapeDtypeStruct((blocks * rb, cb), F32),),
            (self.kept.reshape(blocks * rb, cb), self.got.reshape(-1, cb)),
            [VMEM] * 2,
            us=0.1,
        )
        self.kept, self.got = summed.reshape(blocks, rb, cb), None
        self.sent = summed

    def end(self, after=()):
        _, rb, cb = self.kept.shape
        (total,) = call(
            sum_kernel,
            "end_" + self.name,
            (jax.ShapeDtypeStruct((rb, cb), F32),),
            (self.kept.reshape(rb, cb), self.got),
            [VMEM] * 2,
            after=after,
            us=0.1,
        )
        return total


def local(points_in, cotangent, w_query, w_key, w_value):
    rows, width = points_in.shape
    nz, nx, ns = lax.axis_size("points"), lax.axis_size("mp"), lax.axis_size("sub")
    total = rows * nz * nx * ns
    half = width // ns
    rb, cb = width // (nz * ns), width // nx
    shape = jax.ShapeDtypeStruct
    dealt = shape((ns, nz * nx, rb, cb), F32)
    state = shape((ns, HS, half), F32)
    low = shape((rows, width), BF16)
    tall = shape((rows, half), F32)

    sums, grad_part, p_in, p_flip = call(
        cross_kernel,
        "cross",
        (shape((width, width), F32), state, low, shape((width, rows), BF16)),
        [pltpu.with_memory_space_constraint(a, pltpu.HBM) for a in (points_in, cotangent, w_query)],
        [HBM] * 3,
        scratch=[
            pltpu.VMEM((rows, width), BF16),
            pltpu.VMEM((width, width), BF16),
            pltpu.SemaphoreType.DMA((2 * CHUNKS + 1,)),
        ],
        us=3.0,
    )
    g_sum = Total(grad_part)
    (cross,) = call(deal_kernel, "deal", (dealt,), (sums,), [VMEM], us=0.3)
    cross_sum = Scatter(cross, "query")
    g_sum.add()
    cross_sum.step(after=(g_sum.sent,))
    g_sum.add(after=(cross_sum.sent,))
    norms, states = [], []
    for other in range(ns):
        norms.append(
            call(
                functools.partial(norm_kernel, other),
                "norm",
                (tall, tall, tall, tall, shape((HS, half), F32)),
                [p_in, w_key, w_value],
                [VMEM] * 3,
                after=(g_sum.sent, cross_sum.sent),
                scratch=[pltpu.VMEM((2, rows, half), F32), pltpu.VMEM((2, rows, half), BF16)],
                us=2.3,
            )
        )
        states.append(norms[-1][-1])
        g_sum.add(after=(states[-1],))
        if other == 0:
            cross_sum.step(after=(g_sum.sent,))
    while g_sum.todo:
        g_sum.add()
    g_own, g_got = g_sum.value, g_sum.got
    key_norm, key_inv, value_norm, value_inv, _ = zip(*norms)
    tail = Tail(states[0] + swap_cores(states[1]))
    cross_sum.settle()

    scratch = [pltpu.VMEM((rows, half), F32), pltpu.VMEM((rows, half), BF16)]

    scratch = [pltpu.VMEM((rows, half), F32), pltpu.VMEM((rows, half), BF16)]
    short, column = shape((rows, half), BF16), shape((width, half), F32)
    k_own, v_own, wk_own, wv_own = call(
        functools.partial(own_kernel, total),
        "back_own",
        (short, short, column, column),
        (p_flip, g_own, key_norm[0], key_inv[0], value_norm[0], value_inv[0]),
        [VMEM] * 6,
        scratch=[scratch[0]] * 2 + [scratch[1]] * 2,
        us=1.8,
    )

    def back(key, part, after):
        return call(
            functools.partial(other_kernel, total, key),
            "back_key" if key else "back_value",
            (short, dealt),
            (p_flip, part, g_got) + ((key_norm[1], key_inv[1], value_norm[1]) if key else (value_norm[1], value_inv[1], key_norm[1])),
            [VMEM] * 6,
            after=after,
            scratch=scratch,
            us=1.0,
        )

    k_other, key_blocks = back(True, wk_own, (cross_sum.sent,))
    key_sum = Scatter(key_blocks, "key")
    v_other, value_blocks = back(False, wv_own, (k_other,))
    value_sum = Scatter(value_blocks, "value")
    key_low, value_low = (k_own, k_other), (v_own, v_other)
    last = v_other
    m_total, s_own = None, None
    for turn in ORDER:
        if turn == "P":
            (partial,) = call(
                points_kernel,
                "grad_points_part",
                (shape((rows, width), F32),),
                key_low + value_low + (w_key, w_value),
                [VMEM] * 6,
                after=(last,),
                us=1.3,
            )
            last = partial
        elif turn == "T":
            if not cross_sum.todo:
                m_total = last = cross_sum.end(after=(last,))
        elif turn == "S":
            if tail.todo[0]:
                tail.step(after=(last,))
            else:
                s_own = tail.add(after=(last,))
            last = tail.value
        else:
            one = {"M": cross_sum, "K": key_sum, "V": value_sum}[turn.upper()]
            one.step(after=(last,), tail=tail if turn.islower() else None)
            last = one.sent
    while cross_sum.todo or key_sum.todo or value_sum.todo:
        for turn in (cross_sum, key_sum, value_sum):
            if turn.todo:
                turn.step()
    if m_total is None:
        m_total = cross_sum.end()
    while tail.todo[0]:
        tail.step()
    if s_own is None:
        s_own = tail.add()
    s_got = swap_cores(s_own)
    (partial,) = call(
        functools.partial(query_own_kernel, total),
        "grad_points_own",
        (shape((rows, width), F32),),
        (partial, cotangent, w_query, s_own),
        [VMEM] * 4,
        scratch=[pltpu.VMEM((rows, half), BF16)],
        us=1.0,
    )
    parts = []
    for one in (key_sum, value_sum):
        parts += [one.kept.reshape(rb, cb), one.got]
    block = shape((rb, cb), F32)
    return call(
        functools.partial(last_kernel, total),
        "outputs",
        (low, block, block, block),
        [partial, cotangent, w_query, s_own, s_got, m_total] + parts,
        [VMEM] * 10,
        scratch=[
            pltpu.VMEM((rows, half), BF16),
            pltpu.VMEM((rows, width), BF16),
            pltpu.VMEM((3, rb, cb), F32),
            pltpu.SemaphoreType.DMA((3 + BLOCKS,)),
        ],
        us=0.01,
        outs=(HBM,) * 4,
    )


def solution(mesh):
    whole = P(("groups", "points", "mp", "sub"), None)
    block = P(("groups", "points", "sub"), "mp")
    return jax.shard_map(
        local,
        mesh=mesh,
        in_specs=(whole, whole, P(), P(), P()),
        out_specs=(whole, block, block, block),
        check_vma=False,
    )
```

time: 58 us -> 50.2 us (0.87)
  waiting for transfers between devices: 18 us -> 13.8 us
  starting transfers between devices: 21.6 us -> 19.8 us
  other arithmetic: 1.29 us -> 0.01 us
  Pallas kernels: 15.8 us -> 15.2 us
    ppermute x19, waiting for transfers between devices: 18 us -> 13.8 us  [the longest x12 13.2 us: swap(): return lax.ppermute(value, ('points', 'mp', 'sub'), pairs)]
    ppermute x19, starting transfers between devices: 21.6 us -> 19.8 us  [the longest x12 17.8 us: swap(): return lax.ppermute(value, ('points', 'mp', 'sub'), pairs)]
    div x2 -> x0, other arithmetic: 1.28 us -> none  [local(): return (grad_points, grad_query, grad_key / total, grad_value / total)]
    pallas_call x21 -> x28, Pallas kernels: 15.8 us -> 15.2 us  [call(): pl.pallas_call(kernel, out_shape=out_shape, in_specs=specs, out_specs=out...]
  transfers between devices with their start and end apart: 19 -> 19, of which waited for: 8 -> 9; matrix products, arithmetic and copies ran while one was open for 3% -> 0% of each run, Pallas kernels for 18% -> 19%
where the time goes in v4:
time: 50.2 us; the launch traced here: 50 us
  starting transfers between devices  19.8 us (39%)
  Pallas kernels  15.2 us (30%)
  waiting for transfers between devices  13.8 us (27%)
  between operations  0.9 us (2%)
    ppermute x12, starting transfers between devices, swap(): return lax.ppermute(value, ('points', 'mp', 'sub'), pairs)  17.8 us
    pallas_call x28, Pallas kernels, call(): pl.pallas_call(kernel, out_shape=out_shape, in_specs=specs, out_specs=out...  15.2 us
    ppermute x12, waiting for transfers between devices, swap(): return lax.ppermute(value, ('points', 'mp', 'sub'), pairs)  13.2 us
    ppermute x7, starting transfers between devices, swap_cores(): lax.ppermute(value, 'sub', [(i, i ^ 1) for i in range(lax.axis_size('sub'...  1.96 us
  transfers between devices with their start and end apart: 19, of which 9 were waited for; matrix products, arithmetic and copies ran while one was open for 0% of the time, Pallas kernels for 19%

profile of v4, /device:TPU:0, one launch (start us, length us, event | category | flops | bytes accessed | tf_op | source)
XLA Modules:
  0.0 50.0 jit_solution(7275064617361596293)
XLA Ops:
  0.6 2.7 %cross.1 = (f32[512,512]{1,0:T(8,128)S(1)}, f32[2,32,256]{2,1,0:T(8,128)S(1)}, bf16[1024,512]{1,0:T(8,128)(2,1)S(1)}, bf16[512,1024]{1,0:T(8,128)(2,1)S(1)}) custom-call(bf16[1024,512]{1,0:T(8,128)(2,1)} %p_hbm.1, bf16[1024,512]{1,0:T(8,128)(2,1)} %c_ref.3, bf16[512,512]{1,0:T(8,128)(2,1)} %wq_ref.3), custom_call_target="tpu_custom_call" | custom-call | flops 3300000000 | bytes 300000 | tf_op jit(solution)/shard_map/cross/pallas_call | solution.py:284
  3.4 0.5 %collective-permute-start = (f32[32,256]{1,0:T(8,128)S(1)}, f32[32,256]{1,0:T(8,128)S(1)}, u32[]{:S(2)}, u32[]{:S(2)}) collective-permute-start(f32[32,256]{1,0:T(8,128)S(1)} %get-tuple-element.90), channel_id=1, source_target_pairs={{0,1},{1,0},{2,3},{3,2},{4,5},{5,4},{6,7},{7,6},{8,9},{9,8},{10,11... | collective-permute-start | bytes 98312 | tf_op jit(solution)/shard_map/ppermute | solution.py:297
  4.2 0.5 %collective-permute-done.b_ref = f32[32,256]{1,0:T(8,128)S(1)} collective-permute-done((f32[32,256]{1,0:T(8,128)S(1)}, f32[32,256]{1,0:T(8,128)S(1)}, u32[]{:S(2)}, u32[]{:S(2)}) %collective-permute-start) | collective-permute-done | bytes 32800 | tf_op jit(solution)/shard_map/ppermute | solution.py:297
  4.8 2.9 %collective-permute-start.1 = (f32[32,256]{1,0:T(8,128)S(1)}, f32[32,256]{1,0:T(8,128)S(1)}, u32[]{:S(2)}, u32[]{:S(2)}) collective-permute-start(f32[32,256]{1,0:T(8,128)S(1)} %sum_0.1.refs_2_.a_ref), channel_id=1, source_target_pairs={{0,2},{1,5},{2,0},{3,7},{4,6},{5,1},{6,4},{7,3},{8,10},{9,13},{10,... | collective-permute-start | bytes 98312 | tf_op jit(solution)/shard_map/ppermute | solution.py:308
  7.8 1.1 %collective-permute-start.5 = (f32[256,256]{1,0:T(8,128)S(1)}, f32[256,256]{1,0:T(8,128)S(1)}, u32[]{:S(2)}, u32[]{:S(2)}) collective-permute-start(f32[256,256]{1,0:T(8,128)S(1)} %get-tuple-element.47.rest_0_.rest_1_), channel_id=1, source_target_pairs={{0,2},{1,5},{2,0},{3,7},{4,6},{5,1},{6,4},{7,3},{8,10},{9,13},{10,... | collective-permute-start | bytes 786440 | tf_op jit(solution)/shard_map/ppermute | solution.py:308
  8.8 0.8 %collective-permute-done.1.b_ref = f32[32,256]{1,0:T(8,128)S(1)} collective-permute-done((f32[32,256]{1,0:T(8,128)S(1)}, f32[32,256]{1,0:T(8,128)S(1)}, u32[]{:S(2)}, u32[]{:S(2)}) %collective-permute-start.1) | collective-permute-done | bytes 32800 | tf_op jit(solution)/shard_map/ppermute | solution.py:308
  9.6 2.1 %collective-permute-start.3 = (f32[32,256]{1,0:T(8,128)S(1)}, f32[32,256]{1,0:T(8,128)S(1)}, u32[]{:S(2)}, u32[]{:S(2)}) collective-permute-start(f32[32,256]{1,0:T(8,128)S(1)} %sum_1.1.rest_0_.a_ref), channel_id=1, source_target_pairs={{0,4},{1,9},{2,6},{3,11},{4,0},{5,13},{6,2},{7,15},{8,12},{9,1},{1... | collective-permute-start | bytes 98312 | tf_op jit(solution)/shard_map/ppermute | solution.py:308
  11.7 2.0 %norm.2 = (f32[1024,256]{1,0:T(8,128)S(1)}, f32[1024,256]{1,0:T(8,128)S(1)}, f32[1024,256]{1,0:T(8,128)S(1)}, f32[1024,256]{1,0:T(8,128)S(1)}, f32[32,256]{1,0:T(8,128)S(1)}) custom-call(bf16[1024,512]{1,0:T(8,128)(2,1)S(1)} %get-tuple-element.48.p_ref, bf16[512,512]{1,0:T(8,128)(2,1)S(1)} %copy-done.2, bf16[512,512]{1,0:T(8,128)(2,1)S(1)} %copy-done.3, ...), custom_call_target="tpu_custom_call" | custom-call | flops 2529999872 | bytes 229999 | tf_op jit(solution)/shard_map/norm/pallas_call | solution.py:284
  13.9 2.7 %collective-permute-start.4 = (f32[32,256]{1,0:T(8,128)S(1)}, f32[32,256]{1,0:T(8,128)S(1)}, u32[]{:S(2)}, u32[]{:S(2)}) collective-permute-start(f32[32,256]{1,0:T(8,128)S(1)} %sum_2.1.refs_2_.rest_0_.a_ref), channel_id=1, source_target_pairs={{0,8},{1,3},{2,10},{3,1},{4,12},{5,7},{6,14},{7,5},{8,0},{9,11},{1... | collective-permute-start | bytes 98312 | tf_op jit(solution)/shard_map/ppermute | solution.py:308
  16.7 1.6 %collective-permute-start.7 = (f32[128,256]{1,0:T(8,128)S(1)}, f32[128,256]{1,0:T(8,128)S(1)}, u32[]{:S(2)}, u32[]{:S(2)}) collective-permute-start(f32[128,256]{1,0:T(8,128)S(1)} %get-tuple-element.51.rest_1_), channel_id=1, source_target_pairs={{0,4},{1,3},{2,6},{3,1},{4,0},{5,7},{6,2},{7,5},{8,12},{9,11},{10,... | collective-permute-start | bytes 393224 | tf_op jit(solution)/shard_map/ppermute | solution.py:308
  18.3 2.0 %norm.3 = (f32[1024,256]{1,0:T(8,128)S(1)}, f32[1024,256]{1,0:T(8,128)S(1)}, f32[1024,256]{1,0:T(8,128)S(1)}, f32[1024,256]{1,0:T(8,128)S(1)}, f32[32,256]{1,0:T(8,128)S(1)}) custom-call(bf16[1024,512]{1,0:T(8,128)(2,1)S(1)} %get-tuple-element.48.p_ref, bf16[512,512]{1,0:T(8,128)(2,1)S(1)} %copy-done.2, bf16[512,512]{1,0:T(8,128)(2,1)S(1)} %copy-done.3, ...), custom_call_target="tpu_custom_call" | custom-call | flops 2529999872 | bytes 229999 | tf_op jit(solution)/shard_map/norm/pallas_call | solution.py:284
  20.5 0.5 %collective-permute-start.6 = (f32[32,256]{1,0:T(8,128)S(1)}, f32[32,256]{1,0:T(8,128)S(1)}, u32[]{:S(2)}, u32[]{:S(2)}) collective-permute-start(f32[32,256]{1,0:T(8,128)S(1)} %sum_3.1.g_ref), channel_id=1, source_target_pairs={{0,1},{1,0},{2,3},{3,2},{4,5},{5,4},{6,7},{7,6},{8,9},{9,8},{10,11... | collective-permute-start | bytes 98312 | tf_op jit(solution)/shard_map/ppermute | solution.py:297
  21.0 1.9 %back_own.1 = (bf16[1024,256]{1,0:T(8,128)(2,1)S(1)}, bf16[1024,256]{1,0:T(8,128)(2,1)S(1)}, f32[512,256]{1,0:T(8,128)S(1)}, f32[512,256]{1,0:T(8,128)S(1)}) custom-call(bf16[512,1024]{1,0:T(8,128)(2,1)S(1)} %get-tuple-element.44.pt_ref, f32[32,256]{1,0:T(8,128)S(1)} %sum_3.1.g_ref, f32[1024,256]{1,0:T(8,128)S(1)} %get-tuple-element.53.kn_ref, ...), custom_call_target="tpu_custom_call" | custom-call | flops 11000000 | bytes 1000 | tf_op jit(solution)/shard_map/back_own/pallas_call | solution.py:284
  23.0 1.2 %back_key.1 = (bf16[1024,256]{1,0:T(8,128)(2,1)S(1)}, f32[2,8,64,256]{3,2,1,0:T(8,128)S(1)}) custom-call(bf16[512,1024]{1,0:T(8,128)(2,1)S(1)} %get-tuple-element.44.pt_ref, f32[512,256]{1,0:T(8,128)S(1)} %get-tuple-element.58.own_ref, f32[32,256]{1,0:T(8,128)S(1)} %collective-permute-done.6.g_ref, f32[1024,256]{1,0:T(8,128)S(1)} %get-tuple-element.59.n_ref.o_ref, ...), custom_call_target="tpu_custom_call" | custom-call | flops 5500000256 | bytes 500000 | tf_op jit(solution)/shard_map/back_key/pallas_call | solution.py:284
  24.4 1.2 %back_value.1 = (bf16[1024,256]{1,0:T(8,128)(2,1)S(1)}, f32[2,8,64,256]{3,2,1,0:T(8,128)S(1)}) custom-call(bf16[512,1024]{1,0:T(8,128)(2,1)S(1)} %get-tuple-element.44.pt_ref, f32[512,256]{1,0:T(8,128)S(1)} %get-tuple-element.65.own_ref, f32[32,256]{1,0:T(8,128)S(1)} %collective-permute-done.6.g_ref, f32[1024,256]{1,0:T(8,128)S(1)} %get-tuple-element.61.o_ref.n_ref, ...), custom_call_target="tpu_custom_call" | custom-call | flops 5500000256 | bytes 500000 | tf_op jit(solution)/shard_map/back_value/pallas_call | solution.py:284
  25.7 0.5 %collective-permute-start.8 = (f32[8,64,256]{2,1,0:T(8,128)S(1)}, f32[8,64,256]{2,1,0:T(8,128)S(1)}, u32[]{:S(2)}, u32[]{:S(2)}) collective-permute-start(f32[8,64,256]{2,1,0:T(8,128)S(1)} %get-tuple-element.86), channel_id=1, source_target_pairs={{0,1},{1,0},{2,3},{3,2},{4,5},{5,4},{6,7},{7,6},{8,9},{9,8},{10,11... | collective-permute-start | bytes 1572872 | tf_op jit(solution)/shard_map/ppermute | solution.py:297
  26.3 1.6 %collective-permute-start.11 = (f32[288,256]{1,0:T(8,128)S(1)}, f32[288,256]{1,0:T(8,128)S(1)}, u32[]{:S(2)}, u32[]{:S(2)}) collective-permute-start(f32[288,256]{1,0:T(8,128)S(1)} %get-tuple-element.70.refs_2_), channel_id=1, source_target_pairs={{0,2},{1,5},{2,0},{3,7},{4,6},{5,1},{6,4},{7,3},{8,10},{9,13},{10,... | collective-permute-start | bytes 884744 | tf_op jit(solution)/shard_map/ppermute | solution.py:308
  27.9 1.4 %collective-permute-start.14 = (f32[256,256]{1,0:T(8,128)S(1)}, f32[256,256]{1,0:T(8,128)S(1)}, u32[]{:S(2)}, u32[]{:S(2)}) collective-permute-start(f32[256,256]{1,0:T(8,128)S(1)} %get-tuple-element.71.refs_1_), channel_id=1, source_target_pairs={{0,2},{1,5},{2,0},{3,7},{4,6},{5,1},{6,4},{7,3},{8,10},{9,13},{10,... | collective-permute-start | bytes 786440 | tf_op jit(solution)/shard_map/ppermute | solution.py:308
  29.4 0.9 %collective-permute-start.13 = (f32[64,256]{1,0:T(8,128)S(1)}, f32[64,256]{1,0:T(8,128)S(1)}, u32[]{:S(2)}, u32[]{:S(2)}) collective-permute-start(f32[64,256]{1,0:T(8,128)S(1)} %get-tuple-element.72.refs_6_), channel_id=1, source_target_pairs={{0,8},{1,9},{2,10},{3,11},{4,12},{5,13},{6,14},{7,15},{8,0},{9,1},... | collective-permute-start | bytes 196616 | tf_op jit(solution)/shard_map/ppermute | solution.py:308
  30.3 1.3 %grad_points_part.1.refs_3_.acc_ref = f32[1024,512]{1,0:T(8,128)S(1)} custom-call(bf16[1024,256]{1,0:T(8,128)(2,1)S(1)} %get-tuple-element.57.refs_0_, bf16[1024,256]{1,0:T(8,128)(2,1)S(1)} %get-tuple-element.63.rest_0_.refs_1_, bf16[1024,256]{1,0:T(8,128)(2,1)S(1)} %get-tuple-element.64.refs_2_, bf16[1024,256]{1,0:T(8,128)(2,1)S(1)} %get-tuple-element.67.refs_3_, ...), custom_call_target="tpu_custom_call" | custom-call | flops 1430000000 | bytes 130000 | tf_op jit(solution)/shard_map/grad_points_part/pallas_call | solution.py:284
  31.5 1.5 %collective-permute-done.11.refs_1_ = f32[288,256]{1,0:T(8,128)S(1)} collective-permute-done((f32[288,256]{1,0:T(8,128)S(1)}, f32[288,256]{1,0:T(8,128)S(1)}, u32[]{:S(2)}, u32[]{:S(2)}) %collective-permute-start.11) | collective-permute-done | bytes 294944 | tf_op jit(solution)/shard_map/ppermute | solution.py:308
  33.1 0.5 %collective-permute-start.12 = (f32[160,256]{1,0:T(8,128)S(1)}, f32[160,256]{1,0:T(8,128)S(1)}, u32[]{:S(2)}, u32[]{:S(2)}) collective-permute-start(f32[160,256]{1,0:T(8,128)S(1)} %get-tuple-element.74.refs_2_), channel_id=1, source_target_pairs={{0,4},{1,3},{2,6},{3,1},{4,0},{5,7},{6,2},{7,5},{8,12},{9,11},{10,... | collective-permute-start | bytes 491528 | tf_op jit(solution)/shard_map/ppermute | solution.py:308
  33.7 2.3 %collective-permute-done.14.refs_1_ = f32[256,256]{1,0:T(8,128)S(1)} collective-permute-done((f32[256,256]{1,0:T(8,128)S(1)}, f32[256,256]{1,0:T(8,128)S(1)}, u32[]{:S(2)}, u32[]{:S(2)}) %collective-permute-start.14) | collective-permute-done | bytes 262176 | tf_op jit(solution)/shard_map/ppermute | solution.py:308
  36.0 1.2 %collective-permute-start.16 = (f32[128,256]{1,0:T(8,128)S(1)}, f32[128,256]{1,0:T(8,128)S(1)}, u32[]{:S(2)}, u32[]{:S(2)}) collective-permute-start(f32[128,256]{1,0:T(8,128)S(1)} %get-tuple-element.78.rest_0_), channel_id=1, source_target_pairs={{0,4},{1,3},{2,6},{3,1},{4,0},{5,7},{6,2},{7,5},{8,12},{9,11},{10,... | collective-permute-start | bytes 393224 | tf_op jit(solution)/shard_map/ppermute | solution.py:308
  37.2 1.3 %collective-permute-done.12.refs_1_ = f32[160,256]{1,0:T(8,128)S(1)} collective-permute-done((f32[160,256]{1,0:T(8,128)S(1)}, f32[160,256]{1,0:T(8,128)S(1)}, u32[]{:S(2)}, u32[]{:S(2)}) %collective-permute-start.12) | collective-permute-done | bytes 163872 | tf_op jit(solution)/shard_map/ppermute | solution.py:308
  38.6 0.8 %collective-permute-start.15 = (f32[96,256]{1,0:T(8,128)S(1)}, f32[96,256]{1,0:T(8,128)S(1)}, u32[]{:S(2)}, u32[]{:S(2)}) collective-permute-start(f32[96,256]{1,0:T(8,128)S(1)} %get-tuple-element.79.refs_2_), channel_id=1, source_target_pairs={{0,8},{1,9},{2,10},{3,11},{4,12},{5,13},{6,14},{7,15},{8,0},{9,1},... | collective-permute-start | bytes 294920 | tf_op jit(solution)/shard_map/ppermute | solution.py:308
  39.3 1.7 %collective-permute-done.16.refs_1_ = f32[128,256]{1,0:T(8,128)S(1)} collective-permute-done((f32[128,256]{1,0:T(8,128)S(1)}, f32[128,256]{1,0:T(8,128)S(1)}, u32[]{:S(2)}, u32[]{:S(2)}) %collective-permute-start.16) | collective-permute-done | bytes 131104 | tf_op jit(solution)/shard_map/ppermute | solution.py:308
  41.0 1.0 %collective-permute-start.18 = (f32[64,256]{1,0:T(8,128)S(1)}, f32[64,256]{1,0:T(8,128)S(1)}, u32[]{:S(2)}, u32[]{:S(2)}) collective-permute-start(f32[64,256]{1,0:T(8,128)S(1)} %get-tuple-element.81.rest_0_), channel_id=1, source_target_pairs={{0,8},{1,9},{2,10},{3,11},{4,12},{5,13},{6,14},{7,15},{8,0},{9,1},... | collective-permute-start | bytes 196616 | tf_op jit(solution)/shard_map/ppermute | solution.py:308
  42.0 5.0 %collective-permute-done.15.rest_1_ = f32[96,256]{1,0:T(8,128)S(1)} collective-permute-done((f32[96,256]{1,0:T(8,128)S(1)}, f32[96,256]{1,0:T(8,128)S(1)}, u32[]{:S(2)}, u32[]{:S(2)}) %collective-permute-start.15) | collective-permute-done | bytes 98336 | tf_op jit(solution)/shard_map/ppermute | solution.py:308
  47.1 0.7 %grad_points_own.1.acc_ref = f32[1024,512]{1,0:T(8,128)S(1)} custom-call(f32[1024,512]{1,0:T(8,128)S(1)} %grad_points_part.1.refs_3_.acc_ref, bf16[1024,512]{1,0:T(8,128)(2,1)S(1)} %copy-done, bf16[512,512]{1,0:T(8,128)(2,1)S(1)} %copy-done.1, f32[32,256]{1,0:T(8,128)S(1)} %sum_state.5.own_ref), custom_call_target="tpu_custom_call" | custom-call | flops 1100000000 | bytes 100000 | tf_op jit(solution)/shard_map/grad_points_own/pallas_call | solution.py:284
  47.8 0.6 %collective-permute-done.18.rest_3_ = f32[64,256]{1,0:T(8,128)S(1)} collective-permute-done((f32[64,256]{1,0:T(8,128)S(1)}, f32[64,256]{1,0:T(8,128)S(1)}, u32[]{:S(2)}, u32[]{:S(2)}) %collective-permute-start.18) | collective-permute-done | bytes 65568 | tf_op jit(solution)/shard_map/ppermute | solution.py:308
  48.4 1.7 %outputs.1 = (bf16[1024,512]{1,0:T(8,128)(2,1)}, f32[64,256]{1,0:T(8,128)}, f32[64,256]{1,0:T(8,128)}, f32[64,256]{1,0:T(8,128)}) custom-call(f32[1024,512]{1,0:T(8,128)S(1)} %grad_points_own.1.acc_ref, bf16[1024,512]{1,0:T(8,128)(2,1)S(1)} %copy-done, bf16[512,512]{1,0:T(8,128)(2,1)S(1)} %copy-done.1, f32[32,256]{1,0:T(8,128)S(1)} %sum_state.5.own_ref, ...), custom_call_target="tpu_custom_call" | custom-call | flops 11000000 | bytes 1000 | tf_op jit(solution)/shard_map/outputs/pallas_call | solution.py:284
  (50 shorter events, 1.3 us)
Async XLA Ops:
  3.4 1.4 %collective-permute-start = (f32[32,256]{1,0:T(8,128)S(1)}, f32[32,256]{1,0:T(8,128)S(1)}, u32[]{:S(2)}, u32[]{:S(2)}) collective-permute-start(f32[32,256]{1,0:T(8,128)S(1)} %get-tuple-element.90), channel_id=1, source_target_pairs={{0,1},{1,0},{2,3},{3,2},{4,5},{5,4},{6,7},{7,6},{8,9},{9,8},{10,11... | collective-permute-start | bytes 98312 | tf_op jit(solution)/shard_map/ppermute | solution.py:297
  4.1 3.6 %collective-permute-start.2 = (f32[8,64,256]{2,1,0:T(8,128)S(1)}, f32[8,64,256]{2,1,0:T(8,128)S(1)}, u32[]{:S(2)}, u32[]{:S(2)}) collective-permute-start(f32[8,64,256]{2,1,0:T(8,128)S(1)} %get-tuple-element.88), channel_id=1, source_target_pairs={{0,1},{1,0},{2,3},{3,2},{4,5},{5,4},{6,7},{7,6},{8,9},{9,8},{10,11... | collective-permute-start | bytes 1572872 | tf_op jit(solution)/shard_map/ppermute | solution.py:297
  4.8 6.9 %copy-start.2 = (bf16[512,512]{1,0:T(8,128)(2,1)S(1)}, bf16[512,512]{1,0:T(8,128)(2,1)}, u32[]{:S(2)}) copy-start(bf16[512,512]{1,0:T(8,128)(2,1)} %refs_4_.1) | copy-start | bytes 1572868
  4.8 6.9 %copy-start.3 = (bf16[512,512]{1,0:T(8,128)(2,1)S(1)}, bf16[512,512]{1,0:T(8,128)(2,1)}, u32[]{:S(2)}) copy-start(bf16[512,512]{1,0:T(8,128)(2,1)} %refs_5_.1) | copy-start | bytes 1572868
  4.8 4.8 %collective-permute-start.1 = (f32[32,256]{1,0:T(8,128)S(1)}, f32[32,256]{1,0:T(8,128)S(1)}, u32[]{:S(2)}, u32[]{:S(2)}) collective-permute-start(f32[32,256]{1,0:T(8,128)S(1)} %sum_0.1.refs_2_.a_ref), channel_id=1, source_target_pairs={{0,2},{1,5},{2,0},{3,7},{4,6},{5,1},{6,4},{7,3},{8,10},{9,13},{10,... | collective-permute-start | bytes 98312 | tf_op jit(solution)/shard_map/ppermute | solution.py:308
  7.8 8.9 %collective-permute-start.5 = (f32[256,256]{1,0:T(8,128)S(1)}, f32[256,256]{1,0:T(8,128)S(1)}, u32[]{:S(2)}, u32[]{:S(2)}) collective-permute-start(f32[256,256]{1,0:T(8,128)S(1)} %get-tuple-element.47.rest_0_.rest_1_), channel_id=1, source_target_pairs={{0,2},{1,5},{2,0},{3,7},{4,6},{5,1},{6,4},{7,3},{8,10},{9,13},{10,... | collective-permute-start | bytes 786440 | tf_op jit(solution)/shard_map/ppermute | solution.py:308
  9.6 4.3 %collective-permute-start.3 = (f32[32,256]{1,0:T(8,128)S(1)}, f32[32,256]{1,0:T(8,128)S(1)}, u32[]{:S(2)}, u32[]{:S(2)}) collective-permute-start(f32[32,256]{1,0:T(8,128)S(1)} %sum_1.1.rest_0_.a_ref), channel_id=1, source_target_pairs={{0,4},{1,9},{2,6},{3,11},{4,0},{5,13},{6,2},{7,15},{8,12},{9,1},{1... | collective-permute-start | bytes 98312 | tf_op jit(solution)/shard_map/ppermute | solution.py:308
  13.9 6.5 %collective-permute-start.4 = (f32[32,256]{1,0:T(8,128)S(1)}, f32[32,256]{1,0:T(8,128)S(1)}, u32[]{:S(2)}, u32[]{:S(2)}) collective-permute-start(f32[32,256]{1,0:T(8,128)S(1)} %sum_2.1.refs_2_.rest_0_.a_ref), channel_id=1, source_target_pairs={{0,8},{1,3},{2,10},{3,1},{4,12},{5,7},{6,14},{7,5},{8,0},{9,11},{1... | collective-permute-start | bytes 98312 | tf_op jit(solution)/shard_map/ppermute | solution.py:308
  16.7 6.3 %collective-permute-start.7 = (f32[128,256]{1,0:T(8,128)S(1)}, f32[128,256]{1,0:T(8,128)S(1)}, u32[]{:S(2)}, u32[]{:S(2)}) collective-permute-start(f32[128,256]{1,0:T(8,128)S(1)} %get-tuple-element.51.rest_1_), channel_id=1, source_target_pairs={{0,4},{1,3},{2,6},{3,1},{4,0},{5,7},{6,2},{7,5},{8,12},{9,11},{10,... | collective-permute-start | bytes 393224 | tf_op jit(solution)/shard_map/ppermute | solution.py:308
  20.4 2.6 %collective-permute-start.10 = (f32[32,256]{1,0:T(8,128)S(1)}, f32[32,256]{1,0:T(8,128)S(1)}, u32[]{:S(2)}, u32[]{:S(2)}) collective-permute-start(f32[32,256]{1,0:T(8,128)S(1)} %get-tuple-element.52.rest_0_), channel_id=1, source_target_pairs={{0,1},{1,0},{2,3},{3,2},{4,5},{5,4},{6,7},{7,6},{8,9},{9,8},{10,11... | collective-permute-start | bytes 98312 | tf_op jit(solution)/shard_map/ppermute | solution.py:297
  20.5 2.5 %collective-permute-start.6 = (f32[32,256]{1,0:T(8,128)S(1)}, f32[32,256]{1,0:T(8,128)S(1)}, u32[]{:S(2)}, u32[]{:S(2)}) collective-permute-start(f32[32,256]{1,0:T(8,128)S(1)} %sum_3.1.g_ref), channel_id=1, source_target_pairs={{0,1},{1,0},{2,3},{3,2},{4,5},{5,4},{6,7},{7,6},{8,9},{9,8},{10,11... | collective-permute-start | bytes 98312 | tf_op jit(solution)/shard_map/ppermute | solution.py:297
  24.3 2.0 %collective-permute-start.9 = (f32[8,64,256]{2,1,0:T(8,128)S(1)}, f32[8,64,256]{2,1,0:T(8,128)S(1)}, u32[]{:S(2)}, u32[]{:S(2)}) collective-permute-start(f32[8,64,256]{2,1,0:T(8,128)S(1)} %get-tuple-element.84), channel_id=1, source_target_pairs={{0,1},{1,0},{2,3},{3,2},{4,5},{5,4},{6,7},{7,6},{8,9},{9,8},{10,11... | collective-permute-start | bytes 1572872 | tf_op jit(solution)/shard_map/ppermute | solution.py:297
  25.7 2.2 %collective-permute-start.8 = (f32[8,64,256]{2,1,0:T(8,128)S(1)}, f32[8,64,256]{2,1,0:T(8,128)S(1)}, u32[]{:S(2)}, u32[]{:S(2)}) collective-permute-start(f32[8,64,256]{2,1,0:T(8,128)S(1)} %get-tuple-element.86), channel_id=1, source_target_pairs={{0,1},{1,0},{2,3},{3,2},{4,5},{5,4},{6,7},{7,6},{8,9},{9,8},{10,11... | collective-permute-start | bytes 1572872 | tf_op jit(solution)/shard_map/ppermute | solution.py:297
  26.3 6.8 %collective-permute-start.11 = (f32[288,256]{1,0:T(8,128)S(1)}, f32[288,256]{1,0:T(8,128)S(1)}, u32[]{:S(2)}, u32[]{:S(2)}) collective-permute-start(f32[288,256]{1,0:T(8,128)S(1)} %get-tuple-element.70.refs_2_), channel_id=1, source_target_pairs={{0,2},{1,5},{2,0},{3,7},{4,6},{5,1},{6,4},{7,3},{8,10},{9,13},{10,... | collective-permute-start | bytes 884744 | tf_op jit(solution)/shard_map/ppermute | solution.py:308
  27.9 8.0 %collective-permute-start.14 = (f32[256,256]{1,0:T(8,128)S(1)}, f32[256,256]{1,0:T(8,128)S(1)}, u32[]{:S(2)}, u32[]{:S(2)}) collective-permute-start(f32[256,256]{1,0:T(8,128)S(1)} %get-tuple-element.71.refs_1_), channel_id=1, source_target_pairs={{0,2},{1,5},{2,0},{3,7},{4,6},{5,1},{6,4},{7,3},{8,10},{9,13},{10,... | collective-permute-start | bytes 786440 | tf_op jit(solution)/shard_map/ppermute | solution.py:308
  29.4 7.8 %collective-permute-start.13 = (f32[64,256]{1,0:T(8,128)S(1)}, f32[64,256]{1,0:T(8,128)S(1)}, u32[]{:S(2)}, u32[]{:S(2)}) collective-permute-start(f32[64,256]{1,0:T(8,128)S(1)} %get-tuple-element.72.refs_6_), channel_id=1, source_target_pairs={{0,8},{1,9},{2,10},{3,11},{4,12},{5,13},{6,14},{7,15},{8,0},{9,1},... | collective-permute-start | bytes 196616 | tf_op jit(solution)/shard_map/ppermute | solution.py:308
  33.1 5.4 %collective-permute-start.12 = (f32[160,256]{1,0:T(8,128)S(1)}, f32[160,256]{1,0:T(8,128)S(1)}, u32[]{:S(2)}, u32[]{:S(2)}) collective-permute-start(f32[160,256]{1,0:T(8,128)S(1)} %get-tuple-element.74.refs_2_), channel_id=1, source_target_pairs={{0,4},{1,3},{2,6},{3,1},{4,0},{5,7},{6,2},{7,5},{8,12},{9,11},{10,... | collective-permute-start | bytes 491528 | tf_op jit(solution)/shard_map/ppermute | solution.py:308
  36.0 5.0 %collective-permute-start.16 = (f32[128,256]{1,0:T(8,128)S(1)}, f32[128,256]{1,0:T(8,128)S(1)}, u32[]{:S(2)}, u32[]{:S(2)}) collective-permute-start(f32[128,256]{1,0:T(8,128)S(1)} %get-tuple-element.78.rest_0_), channel_id=1, source_target_pairs={{0,4},{1,3},{2,6},{3,1},{4,0},{5,7},{6,2},{7,5},{8,12},{9,11},{10,... | collective-permute-start | bytes 393224 | tf_op jit(solution)/shard_map/ppermute | solution.py:308
  37.2 9.8 %copy-start = (bf16[1024,512]{1,0:T(8,128)(2,1)S(1)}, bf16[1024,512]{1,0:T(8,128)(2,1)}, u32[]{:S(2)}) copy-start(bf16[1024,512]{1,0:T(8,128)(2,1)} %c_ref.3) | copy-start | bytes 3145732
  37.2 9.8 %copy-start.1 = (bf16[512,512]{1,0:T(8,128)(2,1)S(1)}, bf16[512,512]{1,0:T(8,128)(2,1)}, u32[]{:S(2)}) copy-start(bf16[512,512]{1,0:T(8,128)(2,1)} %wq_ref.3) | copy-start | bytes 1572868
  38.6 8.4 %collective-permute-start.15 = (f32[96,256]{1,0:T(8,128)S(1)}, f32[96,256]{1,0:T(8,128)S(1)}, u32[]{:S(2)}, u32[]{:S(2)}) collective-permute-start(f32[96,256]{1,0:T(8,128)S(1)} %get-tuple-element.79.refs_2_), channel_id=1, source_target_pairs={{0,8},{1,9},{2,10},{3,11},{4,12},{5,13},{6,14},{7,15},{8,0},{9,1},... | collective-permute-start | bytes 294920 | tf_op jit(solution)/shard_map/ppermute | solution.py:308
  41.0 7.3 %collective-permute-start.18 = (f32[64,256]{1,0:T(8,128)S(1)}, f32[64,256]{1,0:T(8,128)S(1)}, u32[]{:S(2)}, u32[]{:S(2)}) collective-permute-start(f32[64,256]{1,0:T(8,128)S(1)} %get-tuple-element.81.rest_0_), channel_id=1, source_target_pairs={{0,8},{1,9},{2,10},{3,11},{4,12},{5,13},{6,14},{7,15},{8,0},{9,1},... | collective-permute-start | bytes 196616 | tf_op jit(solution)/shard_map/ppermute | solution.py:308
  47.0 1.4 %collective-permute-start.17 = (f32[32,256]{1,0:T(8,128)S(1)}, f32[32,256]{1,0:T(8,128)S(1)}, u32[]{:S(2)}, u32[]{:S(2)}) collective-permute-start(f32[32,256]{1,0:T(8,128)S(1)} %sum_state.5.own_ref), channel_id=1, source_target_pairs={{0,1},{1,0},{2,3},{3,2},{4,5},{5,4},{6,7},{7,6},{8,9},{9,8},{10,11... | collective-permute-start | bytes 98312 | tf_op jit(solution)/shard_map/ppermute | solution.py:297

commit v5 on v4

--- a/solution.py
+++ b/solution.py
@@ -19,7 +19,8 @@
 CHUNKS = 2
 BLOCKS = 4
 NORM_BLOCKS = 1
-ORDER = "kVMPkVTkVS"
+EARLY_Z = ("state", "value")
+ORDER = "kVMPkVTKSVS"
 US = {"end_query": 2.0, "grad_points": 0.01, "back_own": 0.01, "add_key_0": 5.0, "sum_0": 5.0, "back_key": 5.0, "back_value": 5.0}
 
 PARAMS = pltpu.CompilerParams(vmem_limit_bytes=16 * 1024 * 1024)
@@ -68,7 +69,7 @@
 
 def routes(name):
     x, z = list(bits("mp")), list(bits("points"))
-    if name == "state":
+    if name in EARLY_Z:
         return x + z, z + x
     return x + z, z[:1] + x + z[1:]
 
@@ -192,8 +193,9 @@
     gl_ref, w_ref, grad_ref, prod_ref = rest[-4:]
     s = lax.axis_index("sub")
     back_halves(total, (key,), g_ref, ((n_ref, r_ref, o_ref),), (gl_ref,), (grad_ref,), (prod_ref,))
-    place(w_ref, own_ref[...], s, "key")
-    place(w_ref, dot(pt_ref[...], gl_ref[...], NN), 1 - s, "key")
+    name = "key" if key else "value"
+    place(w_ref, own_ref[...], s, name)
+    place(w_ref, dot(pt_ref[...], gl_ref[...], NN), 1 - s, name)
 
 
 def points_kernel(*refs):
@@ -227,7 +229,7 @@
 
 
 def last_kernel(total, acc_ref, c_ref, wq_ref, own_ref, got_ref, m_ref, *rest):
-    parts, outs, (q_ref, gp_ref, g_ref, sems) = rest[:4], rest[-8:-4], rest[-4:]
+    kept_ref, got_part, outs, (q_ref, gp_ref, g_ref, sems) = rest[0], rest[1], rest[-7:-4], rest[-4:]
     rows, width = c_ref.shape
     rb, cb = m_ref.shape
     ns, nx = lax.axis_size("sub"), lax.axis_size("mp")
@@ -236,28 +238,23 @@
     cols = half_columns(other, width)
     low_own, low_got = state_low(total, own_ref), state_low(total, got_ref)
     q_ref[...] = dot(c_ref[:, cols], unpack(low_got).astype(BF16), NT).astype(BF16)
-    copies = []
-    for i in range(2):
-        kept_ref, got_part = parts[2 * i], parts[2 * i + 1]
-        g_ref[1 + i] = (kept_ref[...] + got_part[:rb, :]) / total
-        copies.append(pltpu.make_async_copy(g_ref.at[1 + i], outs[2 + i], sems.at[1 + i]))
-        copies[-1].start()
+    g_ref[1] = (kept_ref[...] + got_part[:rb, :]) / total
+    copies = [pltpu.make_async_copy(g_ref.at[1], outs[2], sems.at[1])]
+    copies[0].start()
     chunk = rows // BLOCKS
     for r in range(BLOCKS):
         span = slice(r * chunk, (r + 1) * chunk)
         gp_ref[span, :] = (acc_ref[span, :] + dot(q_ref[span, :], wq_ref[:, cols], NT)).astype(BF16)
-        copies.append(pltpu.make_async_copy(gp_ref.at[span, :], outs[0].at[span, :], sems.at[3 + r]))
+        copies.append(pltpu.make_async_copy(gp_ref.at[span, :], outs[0].at[span, :], sems.at[2 + r]))
         copies[-1].start()
     whole = jnp.concatenate([jnp.where(s == g, low_own, low_got) for g in range(ns)], axis=1)
     high, rest_ = split(m_ref[...])
     third = (m_ref[...] - high.astype(F32) - rest_.astype(F32)).astype(BF16)
-    for xb in range(nx):
-
-        @pl.when(x == xb)
-        def _():
-            state = unpack(whole[:, xb * cb : (xb + 1) * cb]).astype(BF16)
-            g_ref[0] = (dot(high, state, NT) + dot(rest_, state, NT) + dot(third, state, NT)) / total
-
+    mine = whole[:, :cb]
+    for xb in range(1, nx):
+        mine = jnp.where(x == xb, whole[:, xb * cb : (xb + 1) * cb], mine)
+    state = unpack(mine).astype(BF16)
+    g_ref[0] = (dot(high, state, NT) + dot(rest_, state, NT) + dot(third, state, NT)) / total
     copies.append(pltpu.make_async_copy(g_ref.at[0], outs[1], sems.at[0]))
     copies[-1].start()
     for copy in copies:
@@ -310,6 +307,10 @@
 
 def sum_kernel(a_ref, b_ref, *rest):
     rest[-1][...] = a_ref[...] + b_ref[: a_ref.shape[0], :]
+
+
+def value_out_kernel(total, kept_ref, got_ref, *rest):
+    rest[-1][...] = (kept_ref[...] + got_ref[...]) / total
 
 
 class Total:
@@ -558,25 +559,31 @@
         scratch=[pltpu.VMEM((rows, half), BF16)],
         us=1.0,
     )
-    parts = []
-    for one in (key_sum, value_sum):
-        parts += [one.kept.reshape(rb, cb), one.got]
     block = shape((rb, cb), F32)
-    return call(
+    grad_points, grad_query, grad_key = call(
         functools.partial(last_kernel, total),
         "outputs",
-        (low, block, block, block),
-        [partial, cotangent, w_query, s_own, s_got, m_total] + parts,
-        [VMEM] * 10,
+        (low, block, block),
+        [partial, cotangent, w_query, s_own, s_got, m_total, key_sum.kept.reshape(rb, cb), key_sum.got],
+        [VMEM] * 8,
         scratch=[
             pltpu.VMEM((rows, half), BF16),
             pltpu.VMEM((rows, width), BF16),
-            pltpu.VMEM((3, rb, cb), F32),
-            pltpu.SemaphoreType.DMA((3 + BLOCKS,)),
+            pltpu.VMEM((2, rb, cb), F32),
+            pltpu.SemaphoreType.DMA((2 + BLOCKS,)),
         ],
         us=0.01,
-        outs=(HBM,) * 4,
+        outs=(HBM,) * 3,
     )
+    (grad_value,) = call(
+        functools.partial(value_out_kernel, total),
+        "value_out",
+        (block,),
+        (value_sum.kept.reshape(rb, cb), value_sum.got, pltpu.with_memory_space_constraint(grad_query, pltpu.HBM)),
+        [VMEM, VMEM, HBM],
+        us=0.01,
+    )
+    return grad_points, grad_query, grad_key, grad_value
 
 
 def solution(mesh):

time: 50.2 us -> 48.9 us (0.974)
  waiting for transfers between devices: 13.8 us -> 10.1 us
  starting transfers between devices: 19.8 us -> 21.7 us
  Pallas kernels: 15.2 us -> 15.8 us
    ppermute x12 -> x13, waiting for transfers between devices: 13.2 us -> 9.05 us  [swap(): return lax.ppermute(value, ('points', 'mp', 'sub'), pairs)]
    ppermute x12 -> x13, starting transfers between devices: 17.8 us -> 19.8 us  [swap(): return lax.ppermute(value, ('points', 'mp', 'sub'), pairs)]
    pallas_call x28 -> x29, Pallas kernels: 15.2 us -> 15.8 us  [call(): pl.pallas_call(kernel, out_shape=out_shape, in_specs=specs, out_specs=out...]
  transfers between devices with their start and end apart: 19 -> 20, of which waited for: 9 -> 11; matrix products, arithmetic and copies ran while one was open for 0% -> 0% of each run, Pallas kernels for 19% -> 23%
where the time goes in v5:
time: 48.9 us; the launch traced here: 48.8 us
  starting transfers between devices  21.7 us (44%)
  Pallas kernels  15.8 us (32%)
  waiting for transfers between devices  10.1 us (21%)
  between operations  0.9 us (2%)
    ppermute x13, starting transfers between devices, swap(): return lax.ppermute(value, ('points', 'mp', 'sub'), pairs)  19.8 us
    pallas_call x29, Pallas kernels, call(): pl.pallas_call(kernel, out_shape=out_shape, in_specs=specs, out_specs=out...  15.8 us
    ppermute x13, waiting for transfers between devices, swap(): return lax.ppermute(value, ('points', 'mp', 'sub'), pairs)  9.05 us
    ppermute x7, starting transfers between devices, swap_cores(): lax.ppermute(value, 'sub', [(i, i ^ 1) for i in range(lax.axis_size('sub'...  1.89 us
    ppermute x7, waiting for transfers between devices, swap_cores(): lax.ppermute(value, 'sub', [(i, i ^ 1) for i in range(lax.axis_size('sub'...  1.05 us
  transfers between devices with their start and end apart: 20, of which 11 were waited for; matrix products, arithmetic and copies ran while one was open for 0% of the time, Pallas kernels for 23%

profile of v5, /device:TPU:0, one launch (start us, length us, event | category | flops | bytes accessed | tf_op | source)
XLA Modules:
  0.0 48.8 jit_solution(11072218197379248347)
XLA Ops:
  0.6 2.7 %cross.1 = (f32[512,512]{1,0:T(8,128)S(1)}, f32[2,32,256]{2,1,0:T(8,128)S(1)}, bf16[1024,512]{1,0:T(8,128)(2,1)S(1)}, bf16[512,1024]{1,0:T(8,128)(2,1)S(1)}) custom-call(bf16[1024,512]{1,0:T(8,128)(2,1)} %p_hbm.1, bf16[1024,512]{1,0:T(8,128)(2,1)} %c_ref.3, bf16[512,512]{1,0:T(8,128)(2,1)} %wq_ref.3), custom_call_target="tpu_custom_call" | custom-call | flops 3300000000 | bytes 300000 | tf_op jit(solution)/shard_map/cross/pallas_call | solution.py:281
  4.2 0.5 %collective-permute-done.b_ref = f32[32,256]{1,0:T(8,128)S(1)} collective-permute-done((f32[32,256]{1,0:T(8,128)S(1)}, f32[32,256]{1,0:T(8,128)S(1)}, u32[]{:S(2)}, u32[]{:S(2)}) %collective-permute-start) | collective-permute-done | bytes 32800 | tf_op jit(solution)/shard_map/ppermute | solution.py:294
  4.8 2.9 %collective-permute-start.1 = (f32[32,256]{1,0:T(8,128)S(1)}, f32[32,256]{1,0:T(8,128)S(1)}, u32[]{:S(2)}, u32[]{:S(2)}) collective-permute-start(f32[32,256]{1,0:T(8,128)S(1)} %sum_0.1.refs_2_.a_ref), channel_id=1, source_target_pairs={{0,2},{1,5},{2,0},{3,7},{4,6},{5,1},{6,4},{7,3},{8,10},{9,13},{10,... | collective-permute-start | bytes 98312 | tf_op jit(solution)/shard_map/ppermute | solution.py:305
  7.8 1.1 %collective-permute-start.5 = (f32[256,256]{1,0:T(8,128)S(1)}, f32[256,256]{1,0:T(8,128)S(1)}, u32[]{:S(2)}, u32[]{:S(2)}) collective-permute-start(f32[256,256]{1,0:T(8,128)S(1)} %get-tuple-element.50.rest_0_.rest_1_), channel_id=1, source_target_pairs={{0,2},{1,5},{2,0},{3,7},{4,6},{5,1},{6,4},{7,3},{8,10},{9,13},{10,... | collective-permute-start | bytes 786440 | tf_op jit(solution)/shard_map/ppermute | solution.py:305
  8.8 0.8 %collective-permute-done.1.b_ref = f32[32,256]{1,0:T(8,128)S(1)} collective-permute-done((f32[32,256]{1,0:T(8,128)S(1)}, f32[32,256]{1,0:T(8,128)S(1)}, u32[]{:S(2)}, u32[]{:S(2)}) %collective-permute-start.1) | collective-permute-done | bytes 32800 | tf_op jit(solution)/shard_map/ppermute | solution.py:305
  9.6 2.1 %collective-permute-start.3 = (f32[32,256]{1,0:T(8,128)S(1)}, f32[32,256]{1,0:T(8,128)S(1)}, u32[]{:S(2)}, u32[]{:S(2)}) collective-permute-start(f32[32,256]{1,0:T(8,128)S(1)} %sum_1.1.rest_0_.a_ref), channel_id=1, source_target_pairs={{0,4},{1,9},{2,6},{3,11},{4,0},{5,13},{6,2},{7,15},{8,12},{9,1},{1... | collective-permute-start | bytes 98312 | tf_op jit(solution)/shard_map/ppermute | solution.py:305
  11.7 2.0 %norm.2 = (f32[1024,256]{1,0:T(8,128)S(1)}, f32[1024,256]{1,0:T(8,128)S(1)}, f32[1024,256]{1,0:T(8,128)S(1)}, f32[1024,256]{1,0:T(8,128)S(1)}, f32[32,256]{1,0:T(8,128)S(1)}) custom-call(bf16[1024,512]{1,0:T(8,128)(2,1)S(1)} %get-tuple-element.51.p_ref, bf16[512,512]{1,0:T(8,128)(2,1)S(1)} %copy-done.2, bf16[512,512]{1,0:T(8,128)(2,1)S(1)} %copy-done.3, ...), custom_call_target="tpu_custom_call" | custom-call | flops 2529999872 | bytes 229999 | tf_op jit(solution)/shard_map/norm/pallas_call | solution.py:281
  13.9 2.7 %collective-permute-start.4 = (f32[32,256]{1,0:T(8,128)S(1)}, f32[32,256]{1,0:T(8,128)S(1)}, u32[]{:S(2)}, u32[]{:S(2)}) collective-permute-start(f32[32,256]{1,0:T(8,128)S(1)} %sum_2.1.refs_2_.rest_0_.a_ref), channel_id=1, source_target_pairs={{0,8},{1,3},{2,10},{3,1},{4,12},{5,7},{6,14},{7,5},{8,0},{9,11},{1... | collective-permute-start | bytes 98312 | tf_op jit(solution)/shard_map/ppermute | solution.py:305
  16.7 1.6 %collective-permute-start.7 = (f32[128,256]{1,0:T(8,128)S(1)}, f32[128,256]{1,0:T(8,128)S(1)}, u32[]{:S(2)}, u32[]{:S(2)}) collective-permute-start(f32[128,256]{1,0:T(8,128)S(1)} %get-tuple-element.54.rest_1_), channel_id=1, source_target_pairs={{0,4},{1,3},{2,6},{3,1},{4,0},{5,7},{6,2},{7,5},{8,12},{9,11},{10,... | collective-permute-start | bytes 393224 | tf_op jit(solution)/shard_map/ppermute | solution.py:305
  18.3 2.0 %norm.3 = (f32[1024,256]{1,0:T(8,128)S(1)}, f32[1024,256]{1,0:T(8,128)S(1)}, f32[1024,256]{1,0:T(8,128)S(1)}, f32[1024,256]{1,0:T(8,128)S(1)}, f32[32,256]{1,0:T(8,128)S(1)}) custom-call(bf16[1024,512]{1,0:T(8,128)(2,1)S(1)} %get-tuple-element.51.p_ref, bf16[512,512]{1,0:T(8,128)(2,1)S(1)} %copy-done.2, bf16[512,512]{1,0:T(8,128)(2,1)S(1)} %copy-done.3, ...), custom_call_target="tpu_custom_call" | custom-call | flops 2529999872 | bytes 229999 | tf_op jit(solution)/shard_map/norm/pallas_call | solution.py:281
  20.5 0.5 %collective-permute-start.6 = (f32[32,256]{1,0:T(8,128)S(1)}, f32[32,256]{1,0:T(8,128)S(1)}, u32[]{:S(2)}, u32[]{:S(2)}) collective-permute-start(f32[32,256]{1,0:T(8,128)S(1)} %sum_3.1.g_ref), channel_id=1, source_target_pairs={{0,1},{1,0},{2,3},{3,2},{4,5},{5,4},{6,7},{7,6},{8,9},{9,8},{10,11... | collective-permute-start | bytes 98312 | tf_op jit(solution)/shard_map/ppermute | solution.py:294
  21.0 1.9 %back_own.1 = (bf16[1024,256]{1,0:T(8,128)(2,1)S(1)}, bf16[1024,256]{1,0:T(8,128)(2,1)S(1)}, f32[512,256]{1,0:T(8,128)S(1)}, f32[512,256]{1,0:T(8,128)S(1)}) custom-call(bf16[512,1024]{1,0:T(8,128)(2,1)S(1)} %get-tuple-element.47.pt_ref, f32[32,256]{1,0:T(8,128)S(1)} %sum_3.1.g_ref, f32[1024,256]{1,0:T(8,128)S(1)} %get-tuple-element.56.kn_ref, ...), custom_call_target="tpu_custom_call" | custom-call | flops 11000000 | bytes 1000 | tf_op jit(solution)/shard_map/back_own/pallas_call | solution.py:281
  23.0 1.2 %back_key.1 = (bf16[1024,256]{1,0:T(8,128)(2,1)S(1)}, f32[2,8,64,256]{3,2,1,0:T(8,128)S(1)}) custom-call(bf16[512,1024]{1,0:T(8,128)(2,1)S(1)} %get-tuple-element.47.pt_ref, f32[512,256]{1,0:T(8,128)S(1)} %get-tuple-element.61.own_ref, f32[32,256]{1,0:T(8,128)S(1)} %collective-permute-done.6.g_ref, f32[1024,256]{1,0:T(8,128)S(1)} %get-tuple-element.62.n_ref.o_ref, ...), custom_call_target="tpu_custom_call" | custom-call | flops 5500000256 | bytes 500000 | tf_op jit(solution)/shard_map/back_key/pallas_call | solution.py:281
  24.4 1.2 %back_value.1 = (bf16[1024,256]{1,0:T(8,128)(2,1)S(1)}, f32[2,8,64,256]{3,2,1,0:T(8,128)S(1)}) custom-call(bf16[512,1024]{1,0:T(8,128)(2,1)S(1)} %get-tuple-element.47.pt_ref, f32[512,256]{1,0:T(8,128)S(1)} %get-tuple-element.68.own_ref, f32[32,256]{1,0:T(8,128)S(1)} %collective-permute-done.6.g_ref, f32[1024,256]{1,0:T(8,128)S(1)} %get-tuple-element.64.o_ref.n_ref, ...), custom_call_target="tpu_custom_call" | custom-call | flops 5500000256 | bytes 500000 | tf_op jit(solution)/shard_map/back_value/pallas_call | solution.py:281
  25.7 0.5 %collective-permute-start.8 = (f32[8,64,256]{2,1,0:T(8,128)S(1)}, f32[8,64,256]{2,1,0:T(8,128)S(1)}, u32[]{:S(2)}, u32[]{:S(2)}) collective-permute-start(f32[8,64,256]{2,1,0:T(8,128)S(1)} %get-tuple-element.92), channel_id=1, source_target_pairs={{0,1},{1,0},{2,3},{3,2},{4,5},{5,4},{6,7},{7,6},{8,9},{9,8},{10,11... | collective-permute-start | bytes 1572872 | tf_op jit(solution)/shard_map/ppermute | solution.py:294
  26.3 1.6 %collective-permute-start.11 = (f32[288,256]{1,0:T(8,128)S(1)}, f32[288,256]{1,0:T(8,128)S(1)}, u32[]{:S(2)}, u32[]{:S(2)}) collective-permute-start(f32[288,256]{1,0:T(8,128)S(1)} %get-tuple-element.73.refs_2_), channel_id=1, source_target_pairs={{0,2},{1,5},{2,0},{3,7},{4,6},{5,1},{6,4},{7,3},{8,10},{9,13},{10,... | collective-permute-start | bytes 884744 | tf_op jit(solution)/shard_map/ppermute | solution.py:305
  27.9 1.4 %collective-permute-start.14 = (f32[256,256]{1,0:T(8,128)S(1)}, f32[256,256]{1,0:T(8,128)S(1)}, u32[]{:S(2)}, u32[]{:S(2)}) collective-permute-start(f32[256,256]{1,0:T(8,128)S(1)} %get-tuple-element.74.refs_1_), channel_id=1, source_target_pairs={{0,2},{1,5},{2,0},{3,7},{4,6},{5,1},{6,4},{7,3},{8,10},{9,13},{10,... | collective-permute-start | bytes 786440 | tf_op jit(solution)/shard_map/ppermute | solution.py:305
  29.4 0.9 %collective-permute-start.13 = (f32[64,256]{1,0:T(8,128)S(1)}, f32[64,256]{1,0:T(8,128)S(1)}, u32[]{:S(2)}, u32[]{:S(2)}) collective-permute-start(f32[64,256]{1,0:T(8,128)S(1)} %get-tuple-element.75.refs_6_), channel_id=1, source_target_pairs={{0,8},{1,9},{2,10},{3,11},{4,12},{5,13},{6,14},{7,15},{8,0},{9,1},... | collective-permute-start | bytes 196616 | tf_op jit(solution)/shard_map/ppermute | solution.py:305
  30.3 1.3 %grad_points_part.1.refs_3_.acc_ref = f32[1024,512]{1,0:T(8,128)S(1)} custom-call(bf16[1024,256]{1,0:T(8,128)(2,1)S(1)} %get-tuple-element.60.refs_0_, bf16[1024,256]{1,0:T(8,128)(2,1)S(1)} %get-tuple-element.66.rest_0_.refs_1_, bf16[1024,256]{1,0:T(8,128)(2,1)S(1)} %get-tuple-element.67.refs_2_, bf16[1024,256]{1,0:T(8,128)(2,1)S(1)} %get-tuple-element.70.refs_3_, ...), custom_call_target="tpu_custom_call" | custom-call | flops 1430000000 | bytes 130000 | tf_op jit(solution)/shard_map/grad_points_part/pallas_call | solution.py:281
  31.5 1.6 %collective-permute-done.11.refs_1_ = f32[288,256]{1,0:T(8,128)S(1)} collective-permute-done((f32[288,256]{1,0:T(8,128)S(1)}, f32[288,256]{1,0:T(8,128)S(1)}, u32[]{:S(2)}, u32[]{:S(2)}) %collective-permute-start.11) | collective-permute-done | bytes 294944 | tf_op jit(solution)/shard_map/ppermute | solution.py:305
  33.1 0.5 %collective-permute-start.12 = (f32[160,256]{1,0:T(8,128)S(1)}, f32[160,256]{1,0:T(8,128)S(1)}, u32[]{:S(2)}, u32[]{:S(2)}) collective-permute-start(f32[160,256]{1,0:T(8,128)S(1)} %get-tuple-element.77.refs_2_), channel_id=1, source_target_pairs={{0,4},{1,3},{2,6},{3,1},{4,0},{5,7},{6,2},{7,5},{8,12},{9,11},{10,... | collective-permute-start | bytes 491528 | tf_op jit(solution)/shard_map/ppermute | solution.py:305
  33.7 2.3 %collective-permute-done.14.refs_1_ = f32[256,256]{1,0:T(8,128)S(1)} collective-permute-done((f32[256,256]{1,0:T(8,128)S(1)}, f32[256,256]{1,0:T(8,128)S(1)}, u32[]{:S(2)}, u32[]{:S(2)}) %collective-permute-start.14) | collective-permute-done | bytes 262176 | tf_op jit(solution)/shard_map/ppermute | solution.py:305
  36.0 1.2 %collective-permute-start.16 = (f32[128,256]{1,0:T(8,128)S(1)}, f32[128,256]{1,0:T(8,128)S(1)}, u32[]{:S(2)}, u32[]{:S(2)}) collective-permute-start(f32[128,256]{1,0:T(8,128)S(1)} %get-tuple-element.81.rest_0_), channel_id=1, source_target_pairs={{0,4},{1,9},{2,6},{3,11},{4,0},{5,13},{6,2},{7,15},{8,12},{9,1},{1... | collective-permute-start | bytes 393224 | tf_op jit(solution)/shard_map/ppermute | solution.py:305
  37.2 1.3 %collective-permute-done.12.refs_1_ = f32[160,256]{1,0:T(8,128)S(1)} collective-permute-done((f32[160,256]{1,0:T(8,128)S(1)}, f32[160,256]{1,0:T(8,128)S(1)}, u32[]{:S(2)}, u32[]{:S(2)}) %collective-permute-start.12) | collective-permute-done | bytes 163872 | tf_op jit(solution)/shard_map/ppermute | solution.py:305
  38.6 0.8 %collective-permute-start.15 = (f32[32,256]{1,0:T(8,128)S(1)}, f32[32,256]{1,0:T(8,128)S(1)}, u32[]{:S(2)}, u32[]{:S(2)}) collective-permute-start(f32[32,256]{1,0:T(8,128)S(1)} %sum_state.4.refs_2_.a_ref), channel_id=1, source_target_pairs={{0,8},{1,9},{2,10},{3,11},{4,12},{5,13},{6,14},{7,15},{8,0},{9,1},... | collective-permute-start | bytes 98312 | tf_op jit(solution)/shard_map/ppermute | solution.py:305
  39.3 2.2 %collective-permute-start.18 = (f32[64,256]{1,0:T(8,128)S(1)}, f32[64,256]{1,0:T(8,128)S(1)}, u32[]{:S(2)}, u32[]{:S(2)}) collective-permute-start(f32[64,256]{1,0:T(8,128)S(1)} %get-tuple-element.82.rest_0_), channel_id=1, source_target_pairs={{0,8},{1,9},{2,10},{3,11},{4,12},{5,13},{6,14},{7,15},{8,0},{9,1},... | collective-permute-start | bytes 196616 | tf_op jit(solution)/shard_map/ppermute | solution.py:305
  41.6 0.8 %collective-permute-done.16.refs_1_ = f32[128,256]{1,0:T(8,128)S(1)} collective-permute-done((f32[128,256]{1,0:T(8,128)S(1)}, f32[128,256]{1,0:T(8,128)S(1)}, u32[]{:S(2)}, u32[]{:S(2)}) %collective-permute-start.16) | collective-permute-done | bytes 131104 | tf_op jit(solution)/shard_map/ppermute | solution.py:305
  42.4 0.7 %collective-permute-start.19 = (f32[64,256]{1,0:T(8,128)S(1)}, f32[64,256]{1,0:T(8,128)S(1)}, u32[]{:S(2)}, u32[]{:S(2)}) collective-permute-start(f32[64,256]{1,0:T(8,128)S(1)} %get-tuple-element.84.rest_0_), channel_id=1, source_target_pairs={{0,8},{1,3},{2,10},{3,1},{4,12},{5,7},{6,14},{7,5},{8,0},{9,11},{1... | collective-permute-start | bytes 196616 | tf_op jit(solution)/shard_map/ppermute | solution.py:305
  43.1 1.7 %collective-permute-done.15.b_ref = f32[32,256]{1,0:T(8,128)S(1)} collective-permute-done((f32[32,256]{1,0:T(8,128)S(1)}, f32[32,256]{1,0:T(8,128)S(1)}, u32[]{:S(2)}, u32[]{:S(2)}) %collective-permute-start.15) | collective-permute-done | bytes 32800 | tf_op jit(solution)/shard_map/ppermute | solution.py:305
  44.8 0.7 %grad_points_own.1.acc_ref = f32[1024,512]{1,0:T(8,128)S(1)} custom-call(f32[1024,512]{1,0:T(8,128)S(1)} %grad_points_part.1.refs_3_.acc_ref, bf16[1024,512]{1,0:T(8,128)(2,1)S(1)} %copy-done, bf16[512,512]{1,0:T(8,128)(2,1)S(1)} %copy-done.1, f32[32,256]{1,0:T(8,128)S(1)} %sum_state.5.own_ref), custom_call_target="tpu_custom_call" | custom-call | flops 1100000000 | bytes 100000 | tf_op jit(solution)/shard_map/grad_points_own/pallas_call | solution.py:281
  46.4 1.6 %outputs.1 = (bf16[1024,512]{1,0:T(8,128)(2,1)}, f32[64,256]{1,0:T(8,128)}, f32[64,256]{1,0:T(8,128)}) custom-call(f32[1024,512]{1,0:T(8,128)S(1)} %grad_points_own.1.acc_ref, bf16[1024,512]{1,0:T(8,128)(2,1)S(1)} %copy-done, bf16[512,512]{1,0:T(8,128)(2,1)S(1)} %copy-done.1, f32[32,256]{1,0:T(8,128)S(1)} %sum_state.5.own_ref, ...), custom_call_target="tpu_custom_call" | custom-call | flops 11000000 | bytes 1000 | tf_op jit(solution)/shard_map/outputs/pallas_call | solution.py:281
  48.1 0.6 %value_out.1 = f32[64,256]{1,0:T(8,128)} custom-call(f32[64,256]{1,0:T(8,128)S(1)} %bitcast.27, f32[64,256]{1,0:T(8,128)S(1)} %collective-permute-done.19.got_ref, f32[64,256]{1,0:T(8,128)} %get-tuple-element.44.rest_0_), custom_call_target="tpu_custom_call" | custom-call | flops 11000000 | bytes 1000 | tf_op jit(solution)/shard_map/value_out/pallas_call | solution.py:281
  (52 shorter events, 2.7 us)
Async XLA Ops:
  3.4 1.4 %collective-permute-start = (f32[32,256]{1,0:T(8,128)S(1)}, f32[32,256]{1,0:T(8,128)S(1)}, u32[]{:S(2)}, u32[]{:S(2)}) collective-permute-start(f32[32,256]{1,0:T(8,128)S(1)} %get-tuple-element.96), channel_id=1, source_target_pairs={{0,1},{1,0},{2,3},{3,2},{4,5},{5,4},{6,7},{7,6},{8,9},{9,8},{10,11... | collective-permute-start | bytes 98312 | tf_op jit(solution)/shard_map/ppermute | solution.py:294
  4.1 3.6 %collective-permute-start.2 = (f32[8,64,256]{2,1,0:T(8,128)S(1)}, f32[8,64,256]{2,1,0:T(8,128)S(1)}, u32[]{:S(2)}, u32[]{:S(2)}) collective-permute-start(f32[8,64,256]{2,1,0:T(8,128)S(1)} %get-tuple-element.94), channel_id=1, source_target_pairs={{0,1},{1,0},{2,3},{3,2},{4,5},{5,4},{6,7},{7,6},{8,9},{9,8},{10,11... | collective-permute-start | bytes 1572872 | tf_op jit(solution)/shard_map/ppermute | solution.py:294
  4.8 6.9 %copy-start.2 = (bf16[512,512]{1,0:T(8,128)(2,1)S(1)}, bf16[512,512]{1,0:T(8,128)(2,1)}, u32[]{:S(2)}) copy-start(bf16[512,512]{1,0:T(8,128)(2,1)} %refs_4_.1) | copy-start | bytes 1572868
  4.8 6.9 %copy-start.3 = (bf16[512,512]{1,0:T(8,128)(2,1)S(1)}, bf16[512,512]{1,0:T(8,128)(2,1)}, u32[]{:S(2)}) copy-start(bf16[512,512]{1,0:T(8,128)(2,1)} %refs_5_.1) | copy-start | bytes 1572868
  4.8 4.8 %collective-permute-start.1 = (f32[32,256]{1,0:T(8,128)S(1)}, f32[32,256]{1,0:T(8,128)S(1)}, u32[]{:S(2)}, u32[]{:S(2)}) collective-permute-start(f32[32,256]{1,0:T(8,128)S(1)} %sum_0.1.refs_2_.a_ref), channel_id=1, source_target_pairs={{0,2},{1,5},{2,0},{3,7},{4,6},{5,1},{6,4},{7,3},{8,10},{9,13},{10,... | collective-permute-start | bytes 98312 | tf_op jit(solution)/shard_map/ppermute | solution.py:305
  7.8 8.9 %collective-permute-start.5 = (f32[256,256]{1,0:T(8,128)S(1)}, f32[256,256]{1,0:T(8,128)S(1)}, u32[]{:S(2)}, u32[]{:S(2)}) collective-permute-start(f32[256,256]{1,0:T(8,128)S(1)} %get-tuple-element.50.rest_0_.rest_1_), channel_id=1, source_target_pairs={{0,2},{1,5},{2,0},{3,7},{4,6},{5,1},{6,4},{7,3},{8,10},{9,13},{10,... | collective-permute-start | bytes 786440 | tf_op jit(solution)/shard_map/ppermute | solution.py:305
  9.6 4.3 %collective-permute-start.3 = (f32[32,256]{1,0:T(8,128)S(1)}, f32[32,256]{1,0:T(8,128)S(1)}, u32[]{:S(2)}, u32[]{:S(2)}) collective-permute-start(f32[32,256]{1,0:T(8,128)S(1)} %sum_1.1.rest_0_.a_ref), channel_id=1, source_target_pairs={{0,4},{1,9},{2,6},{3,11},{4,0},{5,13},{6,2},{7,15},{8,12},{9,1},{1... | collective-permute-start | bytes 98312 | tf_op jit(solution)/shard_map/ppermute | solution.py:305
  13.9 6.5 %collective-permute-start.4 = (f32[32,256]{1,0:T(8,128)S(1)}, f32[32,256]{1,0:T(8,128)S(1)}, u32[]{:S(2)}, u32[]{:S(2)}) collective-permute-start(f32[32,256]{1,0:T(8,128)S(1)} %sum_2.1.refs_2_.rest_0_.a_ref), channel_id=1, source_target_pairs={{0,8},{1,3},{2,10},{3,1},{4,12},{5,7},{6,14},{7,5},{8,0},{9,11},{1... | collective-permute-start | bytes 98312 | tf_op jit(solution)/shard_map/ppermute | solution.py:305
  16.7 6.3 %collective-permute-start.7 = (f32[128,256]{1,0:T(8,128)S(1)}, f32[128,256]{1,0:T(8,128)S(1)}, u32[]{:S(2)}, u32[]{:S(2)}) collective-permute-start(f32[128,256]{1,0:T(8,128)S(1)} %get-tuple-element.54.rest_1_), channel_id=1, source_target_pairs={{0,4},{1,3},{2,6},{3,1},{4,0},{5,7},{6,2},{7,5},{8,12},{9,11},{10,... | collective-permute-start | bytes 393224 | tf_op jit(solution)/shard_map/ppermute | solution.py:305
  20.4 2.6 %collective-permute-start.10 = (f32[32,256]{1,0:T(8,128)S(1)}, f32[32,256]{1,0:T(8,128)S(1)}, u32[]{:S(2)}, u32[]{:S(2)}) collective-permute-start(f32[32,256]{1,0:T(8,128)S(1)} %get-tuple-element.55.rest_0_), channel_id=1, source_target_pairs={{0,1},{1,0},{2,3},{3,2},{4,5},{5,4},{6,7},{7,6},{8,9},{9,8},{10,11... | collective-permute-start | bytes 98312 | tf_op jit(solution)/shard_map/ppermute | solution.py:294
  20.5 2.5 %collective-permute-start.6 = (f32[32,256]{1,0:T(8,128)S(1)}, f32[32,256]{1,0:T(8,128)S(1)}, u32[]{:S(2)}, u32[]{:S(2)}) collective-permute-start(f32[32,256]{1,0:T(8,128)S(1)} %sum_3.1.g_ref), channel_id=1, source_target_pairs={{0,1},{1,0},{2,3},{3,2},{4,5},{5,4},{6,7},{7,6},{8,9},{9,8},{10,11... | collective-permute-start | bytes 98312 | tf_op jit(solution)/shard_map/ppermute | solution.py:294
  24.3 2.0 %collective-permute-start.9 = (f32[8,64,256]{2,1,0:T(8,128)S(1)}, f32[8,64,256]{2,1,0:T(8,128)S(1)}, u32[]{:S(2)}, u32[]{:S(2)}) collective-permute-start(f32[8,64,256]{2,1,0:T(8,128)S(1)} %get-tuple-element.90), channel_id=1, source_target_pairs={{0,1},{1,0},{2,3},{3,2},{4,5},{5,4},{6,7},{7,6},{8,9},{9,8},{10,11... | collective-permute-start | bytes 1572872 | tf_op jit(solution)/shard_map/ppermute | solution.py:294
  25.7 2.2 %collective-permute-start.8 = (f32[8,64,256]{2,1,0:T(8,128)S(1)}, f32[8,64,256]{2,1,0:T(8,128)S(1)}, u32[]{:S(2)}, u32[]{:S(2)}) collective-permute-start(f32[8,64,256]{2,1,0:T(8,128)S(1)} %get-tuple-element.92), channel_id=1, source_target_pairs={{0,1},{1,0},{2,3},{3,2},{4,5},{5,4},{6,7},{7,6},{8,9},{9,8},{10,11... | collective-permute-start | bytes 1572872 | tf_op jit(solution)/shard_map/ppermute | solution.py:294
  26.3 6.8 %collective-permute-start.11 = (f32[288,256]{1,0:T(8,128)S(1)}, f32[288,256]{1,0:T(8,128)S(1)}, u32[]{:S(2)}, u32[]{:S(2)}) collective-permute-start(f32[288,256]{1,0:T(8,128)S(1)} %get-tuple-element.73.refs_2_), channel_id=1, source_target_pairs={{0,2},{1,5},{2,0},{3,7},{4,6},{5,1},{6,4},{7,3},{8,10},{9,13},{10,... | collective-permute-start | bytes 884744 | tf_op jit(solution)/shard_map/ppermute | solution.py:305
  27.9 8.0 %collective-permute-start.14 = (f32[256,256]{1,0:T(8,128)S(1)}, f32[256,256]{1,0:T(8,128)S(1)}, u32[]{:S(2)}, u32[]{:S(2)}) collective-permute-start(f32[256,256]{1,0:T(8,128)S(1)} %get-tuple-element.74.refs_1_), channel_id=1, source_target_pairs={{0,2},{1,5},{2,0},{3,7},{4,6},{5,1},{6,4},{7,3},{8,10},{9,13},{10,... | collective-permute-start | bytes 786440 | tf_op jit(solution)/shard_map/ppermute | solution.py:305
  29.4 7.8 %collective-permute-start.13 = (f32[64,256]{1,0:T(8,128)S(1)}, f32[64,256]{1,0:T(8,128)S(1)}, u32[]{:S(2)}, u32[]{:S(2)}) collective-permute-start(f32[64,256]{1,0:T(8,128)S(1)} %get-tuple-element.75.refs_6_), channel_id=1, source_target_pairs={{0,8},{1,9},{2,10},{3,11},{4,12},{5,13},{6,14},{7,15},{8,0},{9,1},... | collective-permute-start | bytes 196616 | tf_op jit(solution)/shard_map/ppermute | solution.py:305
  33.1 5.4 %collective-permute-start.12 = (f32[160,256]{1,0:T(8,128)S(1)}, f32[160,256]{1,0:T(8,128)S(1)}, u32[]{:S(2)}, u32[]{:S(2)}) collective-permute-start(f32[160,256]{1,0:T(8,128)S(1)} %get-tuple-element.77.refs_2_), channel_id=1, source_target_pairs={{0,4},{1,3},{2,6},{3,1},{4,0},{5,7},{6,2},{7,5},{8,12},{9,11},{10,... | collective-permute-start | bytes 491528 | tf_op jit(solution)/shard_map/ppermute | solution.py:305
  36.0 6.4 %collective-permute-start.16 = (f32[128,256]{1,0:T(8,128)S(1)}, f32[128,256]{1,0:T(8,128)S(1)}, u32[]{:S(2)}, u32[]{:S(2)}) collective-permute-start(f32[128,256]{1,0:T(8,128)S(1)} %get-tuple-element.81.rest_0_), channel_id=1, source_target_pairs={{0,4},{1,9},{2,6},{3,11},{4,0},{5,13},{6,2},{7,15},{8,12},{9,1},{1... | collective-permute-start | bytes 393224 | tf_op jit(solution)/shard_map/ppermute | solution.py:305
  37.2 7.6 %copy-start = (bf16[1024,512]{1,0:T(8,128)(2,1)S(1)}, bf16[1024,512]{1,0:T(8,128)(2,1)}, u32[]{:S(2)}) copy-start(bf16[1024,512]{1,0:T(8,128)(2,1)} %c_ref.3) | copy-start | bytes 3145732
  37.2 7.6 %copy-start.1 = (bf16[512,512]{1,0:T(8,128)(2,1)S(1)}, bf16[512,512]{1,0:T(8,128)(2,1)}, u32[]{:S(2)}) copy-start(bf16[512,512]{1,0:T(8,128)(2,1)} %wq_ref.3) | copy-start | bytes 1572868
  38.6 6.2 %collective-permute-start.15 = (f32[32,256]{1,0:T(8,128)S(1)}, f32[32,256]{1,0:T(8,128)S(1)}, u32[]{:S(2)}, u32[]{:S(2)}) collective-permute-start(f32[32,256]{1,0:T(8,128)S(1)} %sum_state.4.refs_2_.a_ref), channel_id=1, source_target_pairs={{0,8},{1,9},{2,10},{3,11},{4,12},{5,13},{6,14},{7,15},{8,0},{9,1},... | collective-permute-start | bytes 98312 | tf_op jit(solution)/shard_map/ppermute | solution.py:305
  39.3 7.1 %collective-permute-start.18 = (f32[64,256]{1,0:T(8,128)S(1)}, f32[64,256]{1,0:T(8,128)S(1)}, u32[]{:S(2)}, u32[]{:S(2)}) collective-permute-start(f32[64,256]{1,0:T(8,128)S(1)} %get-tuple-element.82.rest_0_), channel_id=1, source_target_pairs={{0,8},{1,9},{2,10},{3,11},{4,12},{5,13},{6,14},{7,15},{8,0},{9,1},... | collective-permute-start | bytes 196616 | tf_op jit(solution)/shard_map/ppermute | solution.py:305
  42.4 5.7 %collective-permute-start.19 = (f32[64,256]{1,0:T(8,128)S(1)}, f32[64,256]{1,0:T(8,128)S(1)}, u32[]{:S(2)}, u32[]{:S(2)}) collective-permute-start(f32[64,256]{1,0:T(8,128)S(1)} %get-tuple-element.84.rest_0_), channel_id=1, source_target_pairs={{0,8},{1,3},{2,10},{3,1},{4,12},{5,7},{6,14},{7,5},{8,0},{9,11},{1... | collective-permute-start | bytes 196616 | tf_op jit(solution)/shard_map/ppermute | solution.py:305
  44.8 1.2 %collective-permute-start.17 = (f32[32,256]{1,0:T(8,128)S(1)}, f32[32,256]{1,0:T(8,128)S(1)}, u32[]{:S(2)}, u32[]{:S(2)}) collective-permute-start(f32[32,256]{1,0:T(8,128)S(1)} %sum_state.5.own_ref), channel_id=1, source_target_pairs={{0,1},{1,0},{2,3},{3,2},{4,5},{5,4},{6,7},{7,6},{8,9},{9,8},{10,11... | collective-permute-start | bytes 98312 | tf_op jit(solution)/shard_map/ppermute | solution.py:294

commit v6 on v5

--- a/solution.py
+++ b/solution.py
@@ -18,7 +18,6 @@
 ANY = pl.BlockSpec(memory_space=pl.ANY)
 CHUNKS = 2
 BLOCKS = 4
-NORM_BLOCKS = 1
 EARLY_Z = ("state", "value")
 ORDER = "kVMPkVTKSVS"
 US = {"end_query": 2.0, "grad_points": 0.01, "back_own": 0.01, "add_key_0": 5.0, "sum_0": 5.0, "back_key": 5.0, "back_value": 5.0}
@@ -132,27 +131,36 @@
         place(rest[-1], sums_ref[:, g * half : (g + 1) * half], g, "query")
 
 
-def norm_kernel(other, p_ref, wk_ref, wv_ref, *rest):
-    kn_ref, kr_ref, vn_ref, vr_ref, s_ref, c_ref, sq_ref = rest[-7:]
+def centre_weights(raw):
+    return split(raw.astype(F32) - dot(raw, averager(raw.shape[1]), NN))
+
+
+def norm_kernel(other, p_ref, *rest):
     rows, width = p_ref.shape
-    cols = half_columns(lax.axis_index("sub") ^ other, width)
-    mean = averager(width // lax.axis_size("sub"))
-    chunk = rows // NORM_BLOCKS
-    spans = [slice(r * chunk, (r + 1) * chunk) for r in range(NORM_BLOCKS)]
-    for w, w_ref in enumerate((wk_ref, wv_ref)):
-        raw = w_ref[:, cols]
-        high, low = split(raw.astype(F32) - dot(raw, mean, NN))
-        for span in spans:
-            p = p_ref[span, :]
-            centred = dot(p, high, NN) + dot(p, low, NN)
-            c_ref[w, span, :] = centred
-            sq_ref[w, span, :] = (centred * centred).astype(BF16)
+    half = width // lax.axis_size("sub")
+    mean = averager(half)
+    c_ref, sq_ref = rest[-2:]
+    if other:
+        w_ref = rest[0]
+        kn_ref, kr_ref, vn_ref, vr_ref, s_ref = rest[-7:-2]
+        weights = [(w_ref[2 * w], w_ref[2 * w + 1]) for w in range(2)]
+    else:
+        kn_ref, kr_ref, vn_ref, vr_ref, s_ref, w_ref = rest[-8:-2]
+        s = lax.axis_index("sub")
+        weights = [centre_weights(ref[:, half_columns(s, width)]) for ref in rest[:2]]
+    for w, (high, low) in enumerate(weights):
+        p = p_ref[...]
+        centred = dot(p, high, NN) + dot(p, low, NN)
+        c_ref[w] = centred
+        sq_ref[w] = (centred * centred).astype(BF16)
     for w, (n_ref, r_ref) in enumerate(((kn_ref, kr_ref), (vn_ref, vr_ref))):
-        for span in spans:
-            inverse = lax.rsqrt(dot(sq_ref[w, span, :], mean, NN) + 1e-05)
-            n_ref[span, :] = c_ref[w, span, :] * inverse
-            r_ref[span, :] = inverse
+        inverse = lax.rsqrt(dot(sq_ref[w], mean, NN) + 1e-05)
+        n_ref[...] = c_ref[w] * inverse
+        r_ref[...] = inverse
     s_ref[...] = pack(dot(kn_ref[...].astype(BF16), vn_ref[...].astype(BF16), TN))
+    if not other:
+        for w, ref in enumerate(rest[:2]):
+            w_ref[2 * w], w_ref[2 * w + 1] = centre_weights(ref[:, half_columns(1 - s, width)])
 
 
 def back_centre(total, key, g_ref):
@@ -315,7 +323,7 @@
 
 class Total:
     def __init__(self, parts):
-        self.value, self.got, self.done = parts[0], swap_cores(parts[1]), 0
+        self.value, self.got, self.done, self.over = parts[0], swap_cores(parts[1]), 0, False
         self.todo = list(zip(*routes("state")))
 
     def add(self, after=()):
@@ -332,9 +340,8 @@
         self.done += 1
         if self.todo:
             self.got = swap(self.value, self.todo.pop(0))
-            return True
-        self.got = swap_cores(self.value)
-        return False
+        else:
+            self.got, self.over = swap_cores(self.value), True
 
 
 class Tail:
@@ -356,6 +363,7 @@
                 after=after,
                 us=0.1,
             )
+            self.got = None
         return self.value
 
     def sent(self, exchanges, got):
@@ -457,31 +465,31 @@
     cross_sum.step(after=(g_sum.sent,))
     g_sum.add(after=(cross_sum.sent,))
     norms, states = [], []
+    weights = (w_key, w_value)
     for other in range(ns):
-        norms.append(
-            call(
-                functools.partial(norm_kernel, other),
-                "norm",
-                (tall, tall, tall, tall, shape((HS, half), F32)),
-                [p_in, w_key, w_value],
-                [VMEM] * 3,
-                after=(g_sum.sent, cross_sum.sent),
-                scratch=[pltpu.VMEM((2, rows, half), F32), pltpu.VMEM((2, rows, half), BF16)],
-                us=2.3,
-            )
+        first = other == 0
+        res = call(
+            functools.partial(norm_kernel, other),
+            "norm",
+            (tall, tall, tall, tall, shape((HS, half), F32)) + ((shape((4, width, half), BF16),) if first else ()),
+            (p_in,) + weights,
+            [VMEM] * (1 + len(weights)),
+            after=(g_sum.sent, cross_sum.sent),
+            scratch=[pltpu.VMEM((2, rows, half), F32), pltpu.VMEM((2, rows, half), BF16)],
+            us=2.3,
         )
-        states.append(norms[-1][-1])
+        norms.append(res[:5])
+        states.append(res[4])
         g_sum.add(after=(states[-1],))
-        if other == 0:
+        if first:
+            weights = (res[5],)
             cross_sum.step(after=(g_sum.sent,))
-    while g_sum.todo:
+    while not g_sum.over:
         g_sum.add()
     g_own, g_got = g_sum.value, g_sum.got
     key_norm, key_inv, value_norm, value_inv, _ = zip(*norms)
     tail = Tail(states[0] + swap_cores(states[1]))
     cross_sum.settle()
-
-    scratch = [pltpu.VMEM((rows, half), F32), pltpu.VMEM((rows, half), BF16)]
 
     scratch = [pltpu.VMEM((rows, half), F32), pltpu.VMEM((rows, half), BF16)]
     short, column = shape((rows, half), BF16), shape((width, half), F32)

time: 48.9 us -> 48.8 us (level)
  starting transfers between devices: 21.7 us -> 22.5 us
  waiting for transfers between devices: 10.1 us -> 9.3 us
    ppermute x13, starting transfers between devices: 19.8 us -> 20.6 us  [swap(): return lax.ppermute(value, ('points', 'mp', 'sub'), pairs)]
    ppermute x13, waiting for transfers between devices: 9.05 us -> 8.24 us  [swap(): return lax.ppermute(value, ('points', 'mp', 'sub'), pairs)]
  transfers between devices with their start and end apart: 20 -> 20, of which waited for: 11 -> 10; matrix products, arithmetic and copies ran while one was open for 0% -> 0% of each run, Pallas kernels for 23% -> 23%
where the time goes in v6:
time: 48.8 us; the launch traced here: 48.7 us
  starting transfers between devices  22.5 us (46%)
  Pallas kernels  15.6 us (32%)
  waiting for transfers between devices  9.3 us (19%)
  between operations  0.91 us (2%)
    ppermute x13, starting transfers between devices, swap(): return lax.ppermute(value, ('points', 'mp', 'sub'), pairs)  20.6 us
    pallas_call x29, Pallas kernels, call(): pl.pallas_call(kernel, out_shape=out_shape, in_specs=specs, out_specs=out...  15.6 us
    ppermute x13, waiting for transfers between devices, swap(): return lax.ppermute(value, ('points', 'mp', 'sub'), pairs)  8.24 us
    ppermute x7, starting transfers between devices, swap_cores(): lax.ppermute(value, 'sub', [(i, i ^ 1) for i in range(lax.axis_size('sub'...  1.9 us
    ppermute x7, waiting for transfers between devices, swap_cores(): lax.ppermute(value, 'sub', [(i, i ^ 1) for i in range(lax.axis_size('sub'...  1.05 us
  transfers between devices with their start and end apart: 20, of which 10 were waited for; matrix products, arithmetic and copies ran while one was open for 0% of the time, Pallas kernels for 23%

profile of v6, /device:TPU:0, one launch (start us, length us, event | category | flops | bytes accessed | tf_op | source)
XLA Modules:
  0.0 48.7 jit_solution(5464839880787962334)
XLA Ops:
  0.6 2.7 %cross.1 = (f32[512,512]{1,0:T(8,128)S(1)}, f32[2,32,256]{2,1,0:T(8,128)S(1)}, bf16[1024,512]{1,0:T(8,128)(2,1)S(1)}, bf16[512,1024]{1,0:T(8,128)(2,1)S(1)}) custom-call(bf16[1024,512]{1,0:T(8,128)(2,1)} %p_hbm.1, bf16[1024,512]{1,0:T(8,128)(2,1)} %c_ref.3, bf16[512,512]{1,0:T(8,128)(2,1)} %wq_ref.3), custom_call_target="tpu_custom_call" | custom-call | flops 3300000000 | bytes 300000 | tf_op jit(solution)/shard_map/cross/pallas_call | solution.py:289
  3.4 0.5 %collective-permute-start = (f32[32,256]{1,0:T(8,128)S(1)}, f32[32,256]{1,0:T(8,128)S(1)}, u32[]{:S(2)}, u32[]{:S(2)}) collective-permute-start(f32[32,256]{1,0:T(8,128)S(1)} %get-tuple-element.98), channel_id=1, source_target_pairs={{0,1},{1,0},{2,3},{3,2},{4,5},{5,4},{6,7},{7,6},{8,9},{9,8},{10,11... | collective-permute-start | bytes 98312 | tf_op jit(solution)/shard_map/ppermute | solution.py:302
  4.2 0.5 %collective-permute-done.b_ref = f32[32,256]{1,0:T(8,128)S(1)} collective-permute-done((f32[32,256]{1,0:T(8,128)S(1)}, f32[32,256]{1,0:T(8,128)S(1)}, u32[]{:S(2)}, u32[]{:S(2)}) %collective-permute-start) | collective-permute-done | bytes 32800 | tf_op jit(solution)/shard_map/ppermute | solution.py:302
  4.8 2.9 %collective-permute-start.1 = (f32[32,256]{1,0:T(8,128)S(1)}, f32[32,256]{1,0:T(8,128)S(1)}, u32[]{:S(2)}, u32[]{:S(2)}) collective-permute-start(f32[32,256]{1,0:T(8,128)S(1)} %sum_0.1.refs_2_.a_ref), channel_id=1, source_target_pairs={{0,2},{1,5},{2,0},{3,7},{4,6},{5,1},{6,4},{7,3},{8,10},{9,13},{10,... | collective-permute-start | bytes 98312 | tf_op jit(solution)/shard_map/ppermute | solution.py:313
  7.8 1.1 %collective-permute-start.5 = (f32[256,256]{1,0:T(8,128)S(1)}, f32[256,256]{1,0:T(8,128)S(1)}, u32[]{:S(2)}, u32[]{:S(2)}) collective-permute-start(f32[256,256]{1,0:T(8,128)S(1)} %get-tuple-element.51.rest_0_.rest_3_), channel_id=1, source_target_pairs={{0,2},{1,5},{2,0},{3,7},{4,6},{5,1},{6,4},{7,3},{8,10},{9,13},{10,... | collective-permute-start | bytes 786440 | tf_op jit(solution)/shard_map/ppermute | solution.py:313
  8.8 0.8 %collective-permute-done.1.b_ref = f32[32,256]{1,0:T(8,128)S(1)} collective-permute-done((f32[32,256]{1,0:T(8,128)S(1)}, f32[32,256]{1,0:T(8,128)S(1)}, u32[]{:S(2)}, u32[]{:S(2)}) %collective-permute-start.1) | collective-permute-done | bytes 32800 | tf_op jit(solution)/shard_map/ppermute | solution.py:313
  9.6 2.1 %collective-permute-start.3 = (f32[32,256]{1,0:T(8,128)S(1)}, f32[32,256]{1,0:T(8,128)S(1)}, u32[]{:S(2)}, u32[]{:S(2)}) collective-permute-start(f32[32,256]{1,0:T(8,128)S(1)} %sum_1.1.rest_2_.a_ref), channel_id=1, source_target_pairs={{0,4},{1,9},{2,6},{3,11},{4,0},{5,13},{6,2},{7,15},{8,12},{9,1},{1... | collective-permute-start | bytes 98312 | tf_op jit(solution)/shard_map/ppermute | solution.py:313
  11.7 2.1 %norm.2 = (f32[1024,256]{1,0:T(8,128)S(1)}, f32[1024,256]{1,0:T(8,128)S(1)}, f32[1024,256]{1,0:T(8,128)S(1)}, f32[1024,256]{1,0:T(8,128)S(1)}, f32[32,256]{1,0:T(8,128)S(1)}, /*index=5*/bf16[4,512,256]{2,1,0:T(8,128)(2,1)S(1)}) custom-call(bf16[1024,512]{1,0:T(8,128)(2,1)S(1)} %get-tuple-element.52.p_ref, bf16[512,512]{1,0:T(8,128)(2,1)S(1)} %copy-done.2, ...), custom_call_target="tpu_custom_call" | custom-call | flops 2529999872 | bytes 229999 | tf_op jit(solution)/shard_map/norm/pallas_call | solution.py:289
  13.9 2.7 %collective-permute-start.4 = (f32[32,256]{1,0:T(8,128)S(1)}, f32[32,256]{1,0:T(8,128)S(1)}, u32[]{:S(2)}, u32[]{:S(2)}) collective-permute-start(f32[32,256]{1,0:T(8,128)S(1)} %sum_2.1.refs_2_.rest_1_.a_ref), channel_id=1, source_target_pairs={{0,8},{1,3},{2,10},{3,1},{4,12},{5,7},{6,14},{7,5},{8,0},{9,11},{1... | collective-permute-start | bytes 98312 | tf_op jit(solution)/shard_map/ppermute | solution.py:313
  16.7 1.6 %collective-permute-start.7 = (f32[128,256]{1,0:T(8,128)S(1)}, f32[128,256]{1,0:T(8,128)S(1)}, u32[]{:S(2)}, u32[]{:S(2)}) collective-permute-start(f32[128,256]{1,0:T(8,128)S(1)} %get-tuple-element.56.rest_2_), channel_id=1, source_target_pairs={{0,4},{1,3},{2,6},{3,1},{4,0},{5,7},{6,2},{7,5},{8,12},{9,11},{10,... | collective-permute-start | bytes 393224 | tf_op jit(solution)/shard_map/ppermute | solution.py:313
  18.3 1.9 %norm.3 = (f32[1024,256]{1,0:T(8,128)S(1)}, f32[1024,256]{1,0:T(8,128)S(1)}, f32[1024,256]{1,0:T(8,128)S(1)}, f32[1024,256]{1,0:T(8,128)S(1)}, f32[32,256]{1,0:T(8,128)S(1)}) custom-call(bf16[1024,512]{1,0:T(8,128)(2,1)S(1)} %get-tuple-element.52.p_ref, bf16[4,512,256]{2,1,0:T(8,128)(2,1)S(1)} %get-tuple-element.54.rest_0_, ...), custom_call_target="tpu_custom_call" | custom-call | flops 2529999872 | bytes 229999 | tf_op jit(solution)/shard_map/norm/pallas_call | solution.py:289
  20.3 0.5 %collective-permute-start.6 = (f32[32,256]{1,0:T(8,128)S(1)}, f32[32,256]{1,0:T(8,128)S(1)}, u32[]{:S(2)}, u32[]{:S(2)}) collective-permute-start(f32[32,256]{1,0:T(8,128)S(1)} %sum_3.1.g_ref), channel_id=1, source_target_pairs={{0,1},{1,0},{2,3},{3,2},{4,5},{5,4},{6,7},{7,6},{8,9},{9,8},{10,11... | collective-permute-start | bytes 98312 | tf_op jit(solution)/shard_map/ppermute | solution.py:302
  20.8 1.9 %back_own.1 = (bf16[1024,256]{1,0:T(8,128)(2,1)S(1)}, bf16[1024,256]{1,0:T(8,128)(2,1)S(1)}, f32[512,256]{1,0:T(8,128)S(1)}, f32[512,256]{1,0:T(8,128)S(1)}) custom-call(bf16[512,1024]{1,0:T(8,128)(2,1)S(1)} %get-tuple-element.48.pt_ref, f32[32,256]{1,0:T(8,128)S(1)} %sum_3.1.g_ref, f32[1024,256]{1,0:T(8,128)S(1)} %get-tuple-element.58.kn_ref, ...), custom_call_target="tpu_custom_call" | custom-call | flops 11000000 | bytes 1000 | tf_op jit(solution)/shard_map/back_own/pallas_call | solution.py:289
  22.8 1.2 %back_key.1 = (bf16[1024,256]{1,0:T(8,128)(2,1)S(1)}, f32[2,8,64,256]{3,2,1,0:T(8,128)S(1)}) custom-call(bf16[512,1024]{1,0:T(8,128)(2,1)S(1)} %get-tuple-element.48.pt_ref, f32[512,256]{1,0:T(8,128)S(1)} %get-tuple-element.63.own_ref, f32[32,256]{1,0:T(8,128)S(1)} %collective-permute-done.6.g_ref, f32[1024,256]{1,0:T(8,128)S(1)} %get-tuple-element.64.n_ref.o_ref, ...), custom_call_target="tpu_custom_call" | custom-call | flops 5500000256 | bytes 500000 | tf_op jit(solution)/shard_map/back_key/pallas_call | solution.py:289
  24.2 1.2 %back_value.1 = (bf16[1024,256]{1,0:T(8,128)(2,1)S(1)}, f32[2,8,64,256]{3,2,1,0:T(8,128)S(1)}) custom-call(bf16[512,1024]{1,0:T(8,128)(2,1)S(1)} %get-tuple-element.48.pt_ref, f32[512,256]{1,0:T(8,128)S(1)} %get-tuple-element.70.own_ref, f32[32,256]{1,0:T(8,128)S(1)} %collective-permute-done.6.g_ref, f32[1024,256]{1,0:T(8,128)S(1)} %get-tuple-element.66.o_ref.n_ref, ...), custom_call_target="tpu_custom_call" | custom-call | flops 5500000256 | bytes 500000 | tf_op jit(solution)/shard_map/back_value/pallas_call | solution.py:289
  25.5 0.6 %collective-permute-start.8 = (f32[8,64,256]{2,1,0:T(8,128)S(1)}, f32[8,64,256]{2,1,0:T(8,128)S(1)}, u32[]{:S(2)}, u32[]{:S(2)}) collective-permute-start(f32[8,64,256]{2,1,0:T(8,128)S(1)} %get-tuple-element.94), channel_id=1, source_target_pairs={{0,1},{1,0},{2,3},{3,2},{4,5},{5,4},{6,7},{7,6},{8,9},{9,8},{10,11... | collective-permute-start | bytes 1572872 | tf_op jit(solution)/shard_map/ppermute | solution.py:302
  26.1 1.6 %collective-permute-start.11 = (f32[288,256]{1,0:T(8,128)S(1)}, f32[288,256]{1,0:T(8,128)S(1)}, u32[]{:S(2)}, u32[]{:S(2)}) collective-permute-start(f32[288,256]{1,0:T(8,128)S(1)} %get-tuple-element.75.refs_2_), channel_id=1, source_target_pairs={{0,2},{1,5},{2,0},{3,7},{4,6},{5,1},{6,4},{7,3},{8,10},{9,13},{10,... | collective-permute-start | bytes 884744 | tf_op jit(solution)/shard_map/ppermute | solution.py:313
  27.7 1.4 %collective-permute-start.14 = (f32[256,256]{1,0:T(8,128)S(1)}, f32[256,256]{1,0:T(8,128)S(1)}, u32[]{:S(2)}, u32[]{:S(2)}) collective-permute-start(f32[256,256]{1,0:T(8,128)S(1)} %get-tuple-element.76.refs_1_), channel_id=1, source_target_pairs={{0,2},{1,5},{2,0},{3,7},{4,6},{5,1},{6,4},{7,3},{8,10},{9,13},{10,... | collective-permute-start | bytes 786440 | tf_op jit(solution)/shard_map/ppermute | solution.py:313
  29.2 1.1 %collective-permute-start.13 = (f32[64,256]{1,0:T(8,128)S(1)}, f32[64,256]{1,0:T(8,128)S(1)}, u32[]{:S(2)}, u32[]{:S(2)}) collective-permute-start(f32[64,256]{1,0:T(8,128)S(1)} %get-tuple-element.77.refs_6_), channel_id=1, source_target_pairs={{0,8},{1,9},{2,10},{3,11},{4,12},{5,13},{6,14},{7,15},{8,0},{9,1},... | collective-permute-start | bytes 196616 | tf_op jit(solution)/shard_map/ppermute | solution.py:313
  30.3 1.3 %grad_points_part.1.refs_3_.acc_ref = f32[1024,512]{1,0:T(8,128)S(1)} custom-call(bf16[1024,256]{1,0:T(8,128)(2,1)S(1)} %get-tuple-element.62.refs_0_, bf16[1024,256]{1,0:T(8,128)(2,1)S(1)} %get-tuple-element.68.rest_0_.refs_1_, bf16[1024,256]{1,0:T(8,128)(2,1)S(1)} %get-tuple-element.69.refs_2_, bf16[1024,256]{1,0:T(8,128)(2,1)S(1)} %get-tuple-element.72.refs_3_, ...), custom_call_target="tpu_custom_call" | custom-call | flops 1430000000 | bytes 130000 | tf_op jit(solution)/shard_map/grad_points_part/pallas_call | solution.py:289
  31.5 1.4 %collective-permute-done.11.refs_1_ = f32[288,256]{1,0:T(8,128)S(1)} collective-permute-done((f32[288,256]{1,0:T(8,128)S(1)}, f32[288,256]{1,0:T(8,128)S(1)}, u32[]{:S(2)}, u32[]{:S(2)}) %collective-permute-start.11) | collective-permute-done | bytes 294944 | tf_op jit(solution)/shard_map/ppermute | solution.py:313
  33.0 0.6 %collective-permute-start.12 = (f32[160,256]{1,0:T(8,128)S(1)}, f32[160,256]{1,0:T(8,128)S(1)}, u32[]{:S(2)}, u32[]{:S(2)}) collective-permute-start(f32[160,256]{1,0:T(8,128)S(1)} %get-tuple-element.79.refs_2_), channel_id=1, source_target_pairs={{0,4},{1,3},{2,6},{3,1},{4,0},{5,7},{6,2},{7,5},{8,12},{9,11},{10,... | collective-permute-start | bytes 491528 | tf_op jit(solution)/shard_map/ppermute | solution.py:313
  33.6 2.2 %collective-permute-done.14.refs_1_ = f32[256,256]{1,0:T(8,128)S(1)} collective-permute-done((f32[256,256]{1,0:T(8,128)S(1)}, f32[256,256]{1,0:T(8,128)S(1)}, u32[]{:S(2)}, u32[]{:S(2)}) %collective-permute-start.14) | collective-permute-done | bytes 262176 | tf_op jit(solution)/shard_map/ppermute | solution.py:313
  35.8 1.3 %collective-permute-start.16 = (f32[128,256]{1,0:T(8,128)S(1)}, f32[128,256]{1,0:T(8,128)S(1)}, u32[]{:S(2)}, u32[]{:S(2)}) collective-permute-start(f32[128,256]{1,0:T(8,128)S(1)} %get-tuple-element.83.rest_0_), channel_id=1, source_target_pairs={{0,4},{1,9},{2,6},{3,11},{4,0},{5,13},{6,2},{7,15},{8,12},{9,1},{1... | collective-permute-start | bytes 393224 | tf_op jit(solution)/shard_map/ppermute | solution.py:313
  37.1 1.2 %collective-permute-done.12.refs_1_ = f32[160,256]{1,0:T(8,128)S(1)} collective-permute-done((f32[160,256]{1,0:T(8,128)S(1)}, f32[160,256]{1,0:T(8,128)S(1)}, u32[]{:S(2)}, u32[]{:S(2)}) %collective-permute-start.12) | collective-permute-done | bytes 163872 | tf_op jit(solution)/shard_map/ppermute | solution.py:313
  38.4 0.9 %collective-permute-start.15 = (f32[32,256]{1,0:T(8,128)S(1)}, f32[32,256]{1,0:T(8,128)S(1)}, u32[]{:S(2)}, u32[]{:S(2)}) collective-permute-start(f32[32,256]{1,0:T(8,128)S(1)} %sum_state.4.refs_2_.a_ref), channel_id=1, source_target_pairs={{0,8},{1,9},{2,10},{3,11},{4,12},{5,13},{6,14},{7,15},{8,0},{9,1},... | collective-permute-start | bytes 98312 | tf_op jit(solution)/shard_map/ppermute | solution.py:313
  39.3 2.0 %collective-permute-start.18 = (f32[64,256]{1,0:T(8,128)S(1)}, f32[64,256]{1,0:T(8,128)S(1)}, u32[]{:S(2)}, u32[]{:S(2)}) collective-permute-start(f32[64,256]{1,0:T(8,128)S(1)} %get-tuple-element.84.rest_0_), channel_id=1, source_target_pairs={{0,8},{1,9},{2,10},{3,11},{4,12},{5,13},{6,14},{7,15},{8,0},{9,1},... | collective-permute-start | bytes 196616 | tf_op jit(solution)/shard_map/ppermute | solution.py:313
  41.9 1.2 %collective-permute-start.19 = (f32[64,256]{1,0:T(8,128)S(1)}, f32[64,256]{1,0:T(8,128)S(1)}, u32[]{:S(2)}, u32[]{:S(2)}) collective-permute-start(f32[64,256]{1,0:T(8,128)S(1)} %get-tuple-element.86.rest_0_), channel_id=1, source_target_pairs={{0,8},{1,3},{2,10},{3,1},{4,12},{5,7},{6,14},{7,5},{8,0},{9,11},{1... | collective-permute-start | bytes 196616 | tf_op jit(solution)/shard_map/ppermute | solution.py:313
  43.1 1.6 %collective-permute-done.15.b_ref = f32[32,256]{1,0:T(8,128)S(1)} collective-permute-done((f32[32,256]{1,0:T(8,128)S(1)}, f32[32,256]{1,0:T(8,128)S(1)}, u32[]{:S(2)}, u32[]{:S(2)}) %collective-permute-start.15) | collective-permute-done | bytes 32800 | tf_op jit(solution)/shard_map/ppermute | solution.py:313
  44.8 0.7 %grad_points_own.1.acc_ref = f32[1024,512]{1,0:T(8,128)S(1)} custom-call(f32[1024,512]{1,0:T(8,128)S(1)} %grad_points_part.1.refs_3_.acc_ref, bf16[1024,512]{1,0:T(8,128)(2,1)S(1)} %copy-done, bf16[512,512]{1,0:T(8,128)(2,1)S(1)} %copy-done.1, f32[32,256]{1,0:T(8,128)S(1)} %sum_state.5.own_ref), custom_call_target="tpu_custom_call" | custom-call | flops 1100000000 | bytes 100000 | tf_op jit(solution)/shard_map/grad_points_own/pallas_call | solution.py:289
  46.4 1.6 %outputs.1 = (bf16[1024,512]{1,0:T(8,128)(2,1)}, f32[64,256]{1,0:T(8,128)}, f32[64,256]{1,0:T(8,128)}) custom-call(f32[1024,512]{1,0:T(8,128)S(1)} %grad_points_own.1.acc_ref, bf16[1024,512]{1,0:T(8,128)(2,1)S(1)} %copy-done, bf16[512,512]{1,0:T(8,128)(2,1)S(1)} %copy-done.1, f32[32,256]{1,0:T(8,128)S(1)} %sum_state.5.own_ref, ...), custom_call_target="tpu_custom_call" | custom-call | flops 11000000 | bytes 1000 | tf_op jit(solution)/shard_map/outputs/pallas_call | solution.py:289
  48.0 0.6 %value_out.1 = f32[64,256]{1,0:T(8,128)} custom-call(f32[64,256]{1,0:T(8,128)S(1)} %bitcast.27, f32[64,256]{1,0:T(8,128)S(1)} %collective-permute-done.19.got_ref, f32[64,256]{1,0:T(8,128)} %get-tuple-element.45.rest_0_), custom_call_target="tpu_custom_call" | custom-call | flops 11000000 | bytes 1000 | tf_op jit(solution)/shard_map/value_out/pallas_call | solution.py:289
  (52 shorter events, 2.6 us)
Async XLA Ops:
  3.4 1.4 %collective-permute-start = (f32[32,256]{1,0:T(8,128)S(1)}, f32[32,256]{1,0:T(8,128)S(1)}, u32[]{:S(2)}, u32[]{:S(2)}) collective-permute-start(f32[32,256]{1,0:T(8,128)S(1)} %get-tuple-element.98), channel_id=1, source_target_pairs={{0,1},{1,0},{2,3},{3,2},{4,5},{5,4},{6,7},{7,6},{8,9},{9,8},{10,11... | collective-permute-start | bytes 98312 | tf_op jit(solution)/shard_map/ppermute | solution.py:302
  4.1 3.6 %collective-permute-start.2 = (f32[8,64,256]{2,1,0:T(8,128)S(1)}, f32[8,64,256]{2,1,0:T(8,128)S(1)}, u32[]{:S(2)}, u32[]{:S(2)}) collective-permute-start(f32[8,64,256]{2,1,0:T(8,128)S(1)} %get-tuple-element.96), channel_id=1, source_target_pairs={{0,1},{1,0},{2,3},{3,2},{4,5},{5,4},{6,7},{7,6},{8,9},{9,8},{10,11... | collective-permute-start | bytes 1572872 | tf_op jit(solution)/shard_map/ppermute | solution.py:302
  4.8 6.9 %copy-start.2 = (bf16[512,512]{1,0:T(8,128)(2,1)S(1)}, bf16[512,512]{1,0:T(8,128)(2,1)}, u32[]{:S(2)}) copy-start(bf16[512,512]{1,0:T(8,128)(2,1)} %refs_4_.1) | copy-start | bytes 1572868
  4.8 6.9 %copy-start.3 = (bf16[512,512]{1,0:T(8,128)(2,1)S(1)}, bf16[512,512]{1,0:T(8,128)(2,1)}, u32[]{:S(2)}) copy-start(bf16[512,512]{1,0:T(8,128)(2,1)} %refs_5_.1) | copy-start | bytes 1572868
  4.8 4.8 %collective-permute-start.1 = (f32[32,256]{1,0:T(8,128)S(1)}, f32[32,256]{1,0:T(8,128)S(1)}, u32[]{:S(2)}, u32[]{:S(2)}) collective-permute-start(f32[32,256]{1,0:T(8,128)S(1)} %sum_0.1.refs_2_.a_ref), channel_id=1, source_target_pairs={{0,2},{1,5},{2,0},{3,7},{4,6},{5,1},{6,4},{7,3},{8,10},{9,13},{10,... | collective-permute-start | bytes 98312 | tf_op jit(solution)/shard_map/ppermute | solution.py:313
  7.8 8.9 %collective-permute-start.5 = (f32[256,256]{1,0:T(8,128)S(1)}, f32[256,256]{1,0:T(8,128)S(1)}, u32[]{:S(2)}, u32[]{:S(2)}) collective-permute-start(f32[256,256]{1,0:T(8,128)S(1)} %get-tuple-element.51.rest_0_.rest_3_), channel_id=1, source_target_pairs={{0,2},{1,5},{2,0},{3,7},{4,6},{5,1},{6,4},{7,3},{8,10},{9,13},{10,... | collective-permute-start | bytes 786440 | tf_op jit(solution)/shard_map/ppermute | solution.py:313
  9.6 4.3 %collective-permute-start.3 = (f32[32,256]{1,0:T(8,128)S(1)}, f32[32,256]{1,0:T(8,128)S(1)}, u32[]{:S(2)}, u32[]{:S(2)}) collective-permute-start(f32[32,256]{1,0:T(8,128)S(1)} %sum_1.1.rest_2_.a_ref), channel_id=1, source_target_pairs={{0,4},{1,9},{2,6},{3,11},{4,0},{5,13},{6,2},{7,15},{8,12},{9,1},{1... | collective-permute-start | bytes 98312 | tf_op jit(solution)/shard_map/ppermute | solution.py:313
  13.9 6.4 %collective-permute-start.4 = (f32[32,256]{1,0:T(8,128)S(1)}, f32[32,256]{1,0:T(8,128)S(1)}, u32[]{:S(2)}, u32[]{:S(2)}) collective-permute-start(f32[32,256]{1,0:T(8,128)S(1)} %sum_2.1.refs_2_.rest_1_.a_ref), channel_id=1, source_target_pairs={{0,8},{1,3},{2,10},{3,1},{4,12},{5,7},{6,14},{7,5},{8,0},{9,11},{1... | collective-permute-start | bytes 98312 | tf_op jit(solution)/shard_map/ppermute | solution.py:313
  16.7 6.1 %collective-permute-start.7 = (f32[128,256]{1,0:T(8,128)S(1)}, f32[128,256]{1,0:T(8,128)S(1)}, u32[]{:S(2)}, u32[]{:S(2)}) collective-permute-start(f32[128,256]{1,0:T(8,128)S(1)} %get-tuple-element.56.rest_2_), channel_id=1, source_target_pairs={{0,4},{1,3},{2,6},{3,1},{4,0},{5,7},{6,2},{7,5},{8,12},{9,11},{10,... | collective-permute-start | bytes 393224 | tf_op jit(solution)/shard_map/ppermute | solution.py:313
  20.2 2.6 %collective-permute-start.10 = (f32[32,256]{1,0:T(8,128)S(1)}, f32[32,256]{1,0:T(8,128)S(1)}, u32[]{:S(2)}, u32[]{:S(2)}) collective-permute-start(f32[32,256]{1,0:T(8,128)S(1)} %get-tuple-element.57.rest_0_), channel_id=1, source_target_pairs={{0,1},{1,0},{2,3},{3,2},{4,5},{5,4},{6,7},{7,6},{8,9},{9,8},{10,11... | collective-permute-start | bytes 98312 | tf_op jit(solution)/shard_map/ppermute | solution.py:302
  20.3 2.5 %collective-permute-start.6 = (f32[32,256]{1,0:T(8,128)S(1)}, f32[32,256]{1,0:T(8,128)S(1)}, u32[]{:S(2)}, u32[]{:S(2)}) collective-permute-start(f32[32,256]{1,0:T(8,128)S(1)} %sum_3.1.g_ref), channel_id=1, source_target_pairs={{0,1},{1,0},{2,3},{3,2},{4,5},{5,4},{6,7},{7,6},{8,9},{9,8},{10,11... | collective-permute-start | bytes 98312 | tf_op jit(solution)/shard_map/ppermute | solution.py:302
  24.1 2.0 %collective-permute-start.9 = (f32[8,64,256]{2,1,0:T(8,128)S(1)}, f32[8,64,256]{2,1,0:T(8,128)S(1)}, u32[]{:S(2)}, u32[]{:S(2)}) collective-permute-start(f32[8,64,256]{2,1,0:T(8,128)S(1)} %get-tuple-element.92), channel_id=1, source_target_pairs={{0,1},{1,0},{2,3},{3,2},{4,5},{5,4},{6,7},{7,6},{8,9},{9,8},{10,11... | collective-permute-start | bytes 1572872 | tf_op jit(solution)/shard_map/ppermute | solution.py:302
  25.5 2.2 %collective-permute-start.8 = (f32[8,64,256]{2,1,0:T(8,128)S(1)}, f32[8,64,256]{2,1,0:T(8,128)S(1)}, u32[]{:S(2)}, u32[]{:S(2)}) collective-permute-start(f32[8,64,256]{2,1,0:T(8,128)S(1)} %get-tuple-element.94), channel_id=1, source_target_pairs={{0,1},{1,0},{2,3},{3,2},{4,5},{5,4},{6,7},{7,6},{8,9},{9,8},{10,11... | collective-permute-start | bytes 1572872 | tf_op jit(solution)/shard_map/ppermute | solution.py:302
  26.1 6.8 %collective-permute-start.11 = (f32[288,256]{1,0:T(8,128)S(1)}, f32[288,256]{1,0:T(8,128)S(1)}, u32[]{:S(2)}, u32[]{:S(2)}) collective-permute-start(f32[288,256]{1,0:T(8,128)S(1)} %get-tuple-element.75.refs_2_), channel_id=1, source_target_pairs={{0,2},{1,5},{2,0},{3,7},{4,6},{5,1},{6,4},{7,3},{8,10},{9,13},{10,... | collective-permute-start | bytes 884744 | tf_op jit(solution)/shard_map/ppermute | solution.py:313
  27.7 8.0 %collective-permute-start.14 = (f32[256,256]{1,0:T(8,128)S(1)}, f32[256,256]{1,0:T(8,128)S(1)}, u32[]{:S(2)}, u32[]{:S(2)}) collective-permute-start(f32[256,256]{1,0:T(8,128)S(1)} %get-tuple-element.76.refs_1_), channel_id=1, source_target_pairs={{0,2},{1,5},{2,0},{3,7},{4,6},{5,1},{6,4},{7,3},{8,10},{9,13},{10,... | collective-permute-start | bytes 786440 | tf_op jit(solution)/shard_map/ppermute | solution.py:313
  29.2 7.9 %collective-permute-start.13 = (f32[64,256]{1,0:T(8,128)S(1)}, f32[64,256]{1,0:T(8,128)S(1)}, u32[]{:S(2)}, u32[]{:S(2)}) collective-permute-start(f32[64,256]{1,0:T(8,128)S(1)} %get-tuple-element.77.refs_6_), channel_id=1, source_target_pairs={{0,8},{1,9},{2,10},{3,11},{4,12},{5,13},{6,14},{7,15},{8,0},{9,1},... | collective-permute-start | bytes 196616 | tf_op jit(solution)/shard_map/ppermute | solution.py:313
  33.0 5.4 %collective-permute-start.12 = (f32[160,256]{1,0:T(8,128)S(1)}, f32[160,256]{1,0:T(8,128)S(1)}, u32[]{:S(2)}, u32[]{:S(2)}) collective-permute-start(f32[160,256]{1,0:T(8,128)S(1)} %get-tuple-element.79.refs_2_), channel_id=1, source_target_pairs={{0,4},{1,3},{2,6},{3,1},{4,0},{5,7},{6,2},{7,5},{8,12},{9,11},{10,... | collective-permute-start | bytes 491528 | tf_op jit(solution)/shard_map/ppermute | solution.py:313
  35.8 6.0 %collective-permute-start.16 = (f32[128,256]{1,0:T(8,128)S(1)}, f32[128,256]{1,0:T(8,128)S(1)}, u32[]{:S(2)}, u32[]{:S(2)}) collective-permute-start(f32[128,256]{1,0:T(8,128)S(1)} %get-tuple-element.83.rest_0_), channel_id=1, source_target_pairs={{0,4},{1,9},{2,6},{3,11},{4,0},{5,13},{6,2},{7,15},{8,12},{9,1},{1... | collective-permute-start | bytes 393224 | tf_op jit(solution)/shard_map/ppermute | solution.py:313
  37.1 7.7 %copy-start = (bf16[1024,512]{1,0:T(8,128)(2,1)S(1)}, bf16[1024,512]{1,0:T(8,128)(2,1)}, u32[]{:S(2)}) copy-start(bf16[1024,512]{1,0:T(8,128)(2,1)} %c_ref.3) | copy-start | bytes 3145732
  37.1 7.7 %copy-start.1 = (bf16[512,512]{1,0:T(8,128)(2,1)S(1)}, bf16[512,512]{1,0:T(8,128)(2,1)}, u32[]{:S(2)}) copy-start(bf16[512,512]{1,0:T(8,128)(2,1)} %wq_ref.3) | copy-start | bytes 1572868
  38.4 6.3 %collective-permute-start.15 = (f32[32,256]{1,0:T(8,128)S(1)}, f32[32,256]{1,0:T(8,128)S(1)}, u32[]{:S(2)}, u32[]{:S(2)}) collective-permute-start(f32[32,256]{1,0:T(8,128)S(1)} %sum_state.4.refs_2_.a_ref), channel_id=1, source_target_pairs={{0,8},{1,9},{2,10},{3,11},{4,12},{5,13},{6,14},{7,15},{8,0},{9,1},... | collective-permute-start | bytes 98312 | tf_op jit(solution)/shard_map/ppermute | solution.py:313
  39.3 7.1 %collective-permute-start.18 = (f32[64,256]{1,0:T(8,128)S(1)}, f32[64,256]{1,0:T(8,128)S(1)}, u32[]{:S(2)}, u32[]{:S(2)}) collective-permute-start(f32[64,256]{1,0:T(8,128)S(1)} %get-tuple-element.84.rest_0_), channel_id=1, source_target_pairs={{0,8},{1,9},{2,10},{3,11},{4,12},{5,13},{6,14},{7,15},{8,0},{9,1},... | collective-permute-start | bytes 196616 | tf_op jit(solution)/shard_map/ppermute | solution.py:313
  41.9 6.2 %collective-permute-start.19 = (f32[64,256]{1,0:T(8,128)S(1)}, f32[64,256]{1,0:T(8,128)S(1)}, u32[]{:S(2)}, u32[]{:S(2)}) collective-permute-start(f32[64,256]{1,0:T(8,128)S(1)} %get-tuple-element.86.rest_0_), channel_id=1, source_target_pairs={{0,8},{1,3},{2,10},{3,1},{4,12},{5,7},{6,14},{7,5},{8,0},{9,11},{1... | collective-permute-start | bytes 196616 | tf_op jit(solution)/shard_map/ppermute | solution.py:313
  44.7 1.2 %collective-permute-start.17 = (f32[32,256]{1,0:T(8,128)S(1)}, f32[32,256]{1,0:T(8,128)S(1)}, u32[]{:S(2)}, u32[]{:S(2)}) collective-permute-start(f32[32,256]{1,0:T(8,128)S(1)} %sum_state.5.own_ref), channel_id=1, source_target_pairs={{0,1},{1,0},{2,3},{3,2},{4,5},{5,4},{6,7},{7,6},{8,9},{9,8},{10,11... | collective-permute-start | bytes 98312 | tf_op jit(solution)/shard_map/ppermute | solution.py:302

commit v7 on v6

--- a/solution.py
+++ b/solution.py
@@ -73,20 +73,24 @@
     return x + z, z[:1] + x + z[1:]
 
 
-def place(refs, value, g, name):
+def place(send_ref, keep_ref, ref, first, g, name):
     z, x, s = lax.axis_index("points"), lax.axis_index("mp"), lax.axis_index("sub")
-    nz, nx, ns = lax.axis_size("points"), lax.axis_size("mp"), lax.axis_size("sub")
-    rb, cb = refs.shape[-2:]
-    count = value.shape[1] // cb
+    nz, ns = lax.axis_size("points"), lax.axis_size("sub")
+    _, rb, cb = keep_ref.shape
+    count = ref.shape[0] // ns // cb
     for zb in range(nz):
-        for sb in range(ns):
-            row = (zb * ns + sb) * rb
-            for j in range(count):
-                away = {"points": z ^ zb, "mp": x ^ (g * count + j)}
+        for j in range(count):
+            away = {"points": z ^ zb, "mp": x ^ (g * count + j)}
+            spots = []
+            for route in routes(name):
                 spot = 0
-                for t, (axis, bit) in enumerate(routes(name)[sb]):
+                for t, (axis, bit) in enumerate(route):
                     spot = spot + jnp.where((away[axis] & bit) != 0, 1 << t, 0)
-                refs[s ^ sb, spot] = value[row : row + rb, j * cb : (j + 1) * cb]
+                spots.append(spot)
+            cols = slice(first + j * cb, first + (j + 1) * cb)
+            for out_ref, core in ((send_ref, 1 - s), (keep_ref, s)):
+                rows = pl.ds(pl.multiple_of((zb * ns + core) * rb, rb), rb)
+                out_ref[jnp.where(core == 0, spots[0], spots[1])] = ref[rows, cols]
 
 
 def half_columns(g, width):
@@ -128,7 +132,7 @@
 def deal_kernel(sums_ref, *rest):
     half = sums_ref.shape[1] // lax.axis_size("sub")
     for g in range(lax.axis_size("sub")):
-        place(rest[-1], sums_ref[:, g * half : (g + 1) * half], g, "query")
+        place(rest[-2], rest[-1], sums_ref, g * half, g, "query")
 
 
 def centre_weights(raw):
@@ -198,12 +202,13 @@
 
 
 def other_kernel(total, key, pt_ref, own_ref, g_ref, n_ref, r_ref, o_ref, *rest):
-    gl_ref, w_ref, grad_ref, prod_ref = rest[-4:]
+    gl_ref, send_ref, keep_ref, w_ref, grad_ref, prod_ref = rest[-6:]
     s = lax.axis_index("sub")
     back_halves(total, (key,), g_ref, ((n_ref, r_ref, o_ref),), (gl_ref,), (grad_ref,), (prod_ref,))
     name = "key" if key else "value"
-    place(w_ref, own_ref[...], s, name)
-    place(w_ref, dot(pt_ref[...], gl_ref[...], NN), 1 - s, name)
+    w_ref[...] = dot(pt_ref[...], gl_ref[...], NN)
+    place(send_ref, keep_ref, own_ref, 0, s, name)
+    place(send_ref, keep_ref, w_ref, 0, 1 - s, name)
 
 
 def points_kernel(*refs):
@@ -380,7 +385,7 @@
 class Scatter:
     def __init__(self, blocks, name):
         self.name, self.done = name, 0
-        self.kept, self.got = blocks[0], swap_cores(blocks[1])
+        self.kept, self.got = blocks[1], swap_cores(blocks[0])
         self.todo = list(zip(*routes(name)))
 
     def step(self, after=(), tail=None):
@@ -440,7 +445,7 @@
     half = width // ns
     rb, cb = width // (nz * ns), width // nx
     shape = jax.ShapeDtypeStruct
-    dealt = shape((ns, nz * nx, rb, cb), F32)
+    dealt = shape((nz * nx, rb, cb), F32)
     state = shape((ns, HS, half), F32)
     low = shape((rows, width), BF16)
     tall = shape((rows, half), F32)
@@ -459,7 +464,7 @@
         us=3.0,
     )
     g_sum = Total(grad_part)
-    (cross,) = call(deal_kernel, "deal", (dealt,), (sums,), [VMEM], us=0.3)
+    cross = call(deal_kernel, "deal", (dealt, dealt), (sums,), [VMEM], us=0.3)
     cross_sum = Scatter(cross, "query")
     g_sum.add()
     cross_sum.step(after=(g_sum.sent,))
@@ -507,17 +512,17 @@
         return call(
             functools.partial(other_kernel, total, key),
             "back_key" if key else "back_value",
-            (short, dealt),
+            (short, dealt, dealt),
             (p_flip, part, g_got) + ((key_norm[1], key_inv[1], value_norm[1]) if key else (value_norm[1], value_inv[1], key_norm[1])),
             [VMEM] * 6,
             after=after,
-            scratch=scratch,
+            scratch=[pltpu.VMEM((width, half), F32)] + scratch,
             us=1.0,
         )
 
-    k_other, key_blocks = back(True, wk_own, (cross_sum.sent,))
+    k_other, *key_blocks = back(True, wk_own, (cross_sum.sent,))
     key_sum = Scatter(key_blocks, "key")
-    v_other, value_blocks = back(False, wv_own, (k_other,))
+    v_other, *value_blocks = back(False, wv_own, (k_other,))
     value_sum = Scatter(value_blocks, "value")
     key_low, value_low = (k_own, k_other), (v_own, v_other)
     last = v_other

time: 48.8 us -> 48.9 us (level)
  starting transfers between devices: 22.5 us -> 23.5 us
  waiting for transfers between devices: 9.3 us -> 8.62 us
    ppermute x13, starting transfers between devices: 20.6 us -> 21.6 us  [swap(): return lax.ppermute(value, ('points', 'mp', 'sub'), pairs)]
    ppermute x13, waiting for transfers between devices: 8.24 us -> 7.45 us  [swap(): return lax.ppermute(value, ('points', 'mp', 'sub'), pairs)]
  transfers between devices with their start and end apart: 20 -> 20, of which waited for: 10 -> 9; matrix products, arithmetic and copies ran while one was open for 0% -> 0% of each run, Pallas kernels for 23% -> 25%
where the time goes in v7:
time: 48.9 us; the launch traced here: 48.7 us
  starting transfers between devices  23.5 us (48%)
  Pallas kernels  15.8 us (32%)
  waiting for transfers between devices  8.62 us (18%)
  between operations  0.86 us (2%)
    ppermute x13, starting transfers between devices, swap(): return lax.ppermute(value, ('points', 'mp', 'sub'), pairs)  21.6 us
    pallas_call x29, Pallas kernels, call(): pl.pallas_call(kernel, out_shape=out_shape, in_specs=specs, out_specs=out...  15.8 us
    ppermute x13, waiting for transfers between devices, swap(): return lax.ppermute(value, ('points', 'mp', 'sub'), pairs)  7.45 us
    ppermute x7, starting transfers between devices, swap_cores(): lax.ppermute(value, 'sub', [(i, i ^ 1) for i in range(lax.axis_size('sub'...  1.85 us
    ppermute x7, waiting for transfers between devices, swap_cores(): lax.ppermute(value, 'sub', [(i, i ^ 1) for i in range(lax.axis_size('sub'...  1.17 us
  transfers between devices with their start and end apart: 20, of which 9 were waited for; matrix products, arithmetic and copies ran while one was open for 0% of the time, Pallas kernels for 25%

profile of v7, /device:TPU:0, one launch (start us, length us, event | category | flops | bytes accessed | tf_op | source)
XLA Modules:
  0.0 48.7 jit_solution(13918401092060227533)
XLA Ops:
  0.6 2.7 %cross.1 = (f32[512,512]{1,0:T(8,128)S(1)}, f32[2,32,256]{2,1,0:T(8,128)S(1)}, bf16[1024,512]{1,0:T(8,128)(2,1)S(1)}, bf16[512,1024]{1,0:T(8,128)(2,1)S(1)}) custom-call(bf16[1024,512]{1,0:T(8,128)(2,1)} %p_hbm.1, bf16[1024,512]{1,0:T(8,128)(2,1)} %c_ref.3, bf16[512,512]{1,0:T(8,128)(2,1)} %wq_ref.3), custom_call_target="tpu_custom_call" | custom-call | flops 3300000000 | bytes 300000 | tf_op jit(solution)/shard_map/cross/pallas_call | solution.py:294
  3.4 0.5 %collective-permute-start = (f32[32,256]{1,0:T(8,128)S(1)}, f32[32,256]{1,0:T(8,128)S(1)}, u32[]{:S(2)}, u32[]{:S(2)}) collective-permute-start(f32[32,256]{1,0:T(8,128)S(1)} %get-tuple-element.100), channel_id=1, source_target_pairs={{0,1},{1,0},{2,3},{3,2},{4,5},{5,4},{6,7},{7,6},{8,9},{9,8},{10,11... | collective-permute-start | bytes 98312 | tf_op jit(solution)/shard_map/ppermute | solution.py:307
  4.1 0.7 %collective-permute-done.b_ref = f32[32,256]{1,0:T(8,128)S(1)} collective-permute-done((f32[32,256]{1,0:T(8,128)S(1)}, f32[32,256]{1,0:T(8,128)S(1)}, u32[]{:S(2)}, u32[]{:S(2)}) %collective-permute-start) | collective-permute-done | bytes 32800 | tf_op jit(solution)/shard_map/ppermute | solution.py:307
  4.8 2.9 %collective-permute-start.1 = (f32[32,256]{1,0:T(8,128)S(1)}, f32[32,256]{1,0:T(8,128)S(1)}, u32[]{:S(2)}, u32[]{:S(2)}) collective-permute-start(f32[32,256]{1,0:T(8,128)S(1)} %sum_0.1.refs_2_.a_ref), channel_id=1, source_target_pairs={{0,2},{1,5},{2,0},{3,7},{4,6},{5,1},{6,4},{7,3},{8,10},{9,13},{10,... | collective-permute-start | bytes 98312 | tf_op jit(solution)/shard_map/ppermute | solution.py:318
  7.8 1.0 %collective-permute-start.5 = (f32[256,256]{1,0:T(8,128)S(1)}, f32[256,256]{1,0:T(8,128)S(1)}, u32[]{:S(2)}, u32[]{:S(2)}) collective-permute-start(f32[256,256]{1,0:T(8,128)S(1)} %get-tuple-element.57.rest_0_.rest_3_), channel_id=1, source_target_pairs={{0,2},{1,5},{2,0},{3,7},{4,6},{5,1},{6,4},{7,3},{8,10},{9,13},{10,... | collective-permute-start | bytes 786440 | tf_op jit(solution)/shard_map/ppermute | solution.py:318
  8.7 0.9 %collective-permute-done.1.b_ref = f32[32,256]{1,0:T(8,128)S(1)} collective-permute-done((f32[32,256]{1,0:T(8,128)S(1)}, f32[32,256]{1,0:T(8,128)S(1)}, u32[]{:S(2)}, u32[]{:S(2)}) %collective-permute-start.1) | collective-permute-done | bytes 32800 | tf_op jit(solution)/shard_map/ppermute | solution.py:318
  9.6 2.1 %collective-permute-start.3 = (f32[32,256]{1,0:T(8,128)S(1)}, f32[32,256]{1,0:T(8,128)S(1)}, u32[]{:S(2)}, u32[]{:S(2)}) collective-permute-start(f32[32,256]{1,0:T(8,128)S(1)} %sum_1.1.rest_2_.a_ref), channel_id=1, source_target_pairs={{0,4},{1,9},{2,6},{3,11},{4,0},{5,13},{6,2},{7,15},{8,12},{9,1},{1... | collective-permute-start | bytes 98312 | tf_op jit(solution)/shard_map/ppermute | solution.py:318
  11.7 2.1 %norm.2 = (f32[1024,256]{1,0:T(8,128)S(1)}, f32[1024,256]{1,0:T(8,128)S(1)}, f32[1024,256]{1,0:T(8,128)S(1)}, f32[1024,256]{1,0:T(8,128)S(1)}, f32[32,256]{1,0:T(8,128)S(1)}, /*index=5*/bf16[4,512,256]{2,1,0:T(8,128)(2,1)S(1)}) custom-call(bf16[1024,512]{1,0:T(8,128)(2,1)S(1)} %get-tuple-element.58.p_ref, bf16[512,512]{1,0:T(8,128)(2,1)S(1)} %copy-done.2, ...), custom_call_target="tpu_custom_call" | custom-call | flops 2529999872 | bytes 229999 | tf_op jit(solution)/shard_map/norm/pallas_call | solution.py:294
  13.9 2.7 %collective-permute-start.4 = (f32[32,256]{1,0:T(8,128)S(1)}, f32[32,256]{1,0:T(8,128)S(1)}, u32[]{:S(2)}, u32[]{:S(2)}) collective-permute-start(f32[32,256]{1,0:T(8,128)S(1)} %sum_2.1.refs_2_.rest_1_.a_ref), channel_id=1, source_target_pairs={{0,8},{1,3},{2,10},{3,1},{4,12},{5,7},{6,14},{7,5},{8,0},{9,11},{1... | collective-permute-start | bytes 98312 | tf_op jit(solution)/shard_map/ppermute | solution.py:318
  16.7 1.6 %collective-permute-start.7 = (f32[128,256]{1,0:T(8,128)S(1)}, f32[128,256]{1,0:T(8,128)S(1)}, u32[]{:S(2)}, u32[]{:S(2)}) collective-permute-start(f32[128,256]{1,0:T(8,128)S(1)} %get-tuple-element.62.rest_2_), channel_id=1, source_target_pairs={{0,4},{1,3},{2,6},{3,1},{4,0},{5,7},{6,2},{7,5},{8,12},{9,11},{10,... | collective-permute-start | bytes 393224 | tf_op jit(solution)/shard_map/ppermute | solution.py:318
  18.3 1.9 %norm.3 = (f32[1024,256]{1,0:T(8,128)S(1)}, f32[1024,256]{1,0:T(8,128)S(1)}, f32[1024,256]{1,0:T(8,128)S(1)}, f32[1024,256]{1,0:T(8,128)S(1)}, f32[32,256]{1,0:T(8,128)S(1)}) custom-call(bf16[1024,512]{1,0:T(8,128)(2,1)S(1)} %get-tuple-element.58.p_ref, bf16[4,512,256]{2,1,0:T(8,128)(2,1)S(1)} %get-tuple-element.60.rest_0_, ...), custom_call_target="tpu_custom_call" | custom-call | flops 2529999872 | bytes 229999 | tf_op jit(solution)/shard_map/norm/pallas_call | solution.py:294
  20.8 1.9 %back_own.1 = (bf16[1024,256]{1,0:T(8,128)(2,1)S(1)}, bf16[1024,256]{1,0:T(8,128)(2,1)S(1)}, f32[512,256]{1,0:T(8,128)S(1)}, f32[512,256]{1,0:T(8,128)S(1)}) custom-call(bf16[512,1024]{1,0:T(8,128)(2,1)S(1)} %get-tuple-element.52.pt_ref, f32[32,256]{1,0:T(8,128)S(1)} %sum_3.1.g_ref, f32[1024,256]{1,0:T(8,128)S(1)} %get-tuple-element.64.kn_ref, ...), custom_call_target="tpu_custom_call" | custom-call | flops 11000000 | bytes 1000 | tf_op jit(solution)/shard_map/back_own/pallas_call | solution.py:294
  22.7 1.2 %back_key.1 = (bf16[1024,256]{1,0:T(8,128)(2,1)S(1)}, f32[8,64,256]{2,1,0:T(8,128)S(1)}, f32[8,64,256]{2,1,0:T(8,128)S(1)}) custom-call(bf16[512,1024]{1,0:T(8,128)(2,1)S(1)} %get-tuple-element.52.pt_ref, f32[512,256]{1,0:T(8,128)S(1)} %get-tuple-element.69.own_ref, f32[32,256]{1,0:T(8,128)S(1)} %collective-permute-done.6.g_ref, ...), custom_call_target="tpu_custom_call" | custom-call | flops 5500000256 | bytes 500000 | tf_op jit(solution)/shard_map/back_key/pallas_call | solution.py:294
  24.1 1.3 %back_value.1 = (bf16[1024,256]{1,0:T(8,128)(2,1)S(1)}, f32[8,64,256]{2,1,0:T(8,128)S(1)}, f32[8,64,256]{2,1,0:T(8,128)S(1)}) custom-call(bf16[512,1024]{1,0:T(8,128)(2,1)S(1)} %get-tuple-element.52.pt_ref, f32[512,256]{1,0:T(8,128)S(1)} %get-tuple-element.76.own_ref, f32[32,256]{1,0:T(8,128)S(1)} %collective-permute-done.6.g_ref, ...), custom_call_target="tpu_custom_call" | custom-call | flops 5500000256 | bytes 500000 | tf_op jit(solution)/shard_map/back_value/pallas_call | solution.py:294
  25.4 0.5 %collective-permute-start.8 = (f32[8,64,256]{2,1,0:T(8,128)S(1)}, f32[8,64,256]{2,1,0:T(8,128)S(1)}, u32[]{:S(2)}, u32[]{:S(2)}) collective-permute-start(f32[8,64,256]{2,1,0:T(8,128)S(1)} %get-tuple-element.80), channel_id=1, source_target_pairs={{0,1},{1,0},{2,3},{3,2},{4,5},{5,4},{6,7},{7,6},{8,9},{9,8},{10,11... | collective-permute-start | bytes 1572872 | tf_op jit(solution)/shard_map/ppermute | solution.py:307
  26.0 1.6 %collective-permute-start.11 = (f32[288,256]{1,0:T(8,128)S(1)}, f32[288,256]{1,0:T(8,128)S(1)}, u32[]{:S(2)}, u32[]{:S(2)}) collective-permute-start(f32[288,256]{1,0:T(8,128)S(1)} %get-tuple-element.83.refs_2_), channel_id=1, source_target_pairs={{0,2},{1,5},{2,0},{3,7},{4,6},{5,1},{6,4},{7,3},{8,10},{9,13},{10,... | collective-permute-start | bytes 884744 | tf_op jit(solution)/shard_map/ppermute | solution.py:318
  27.6 1.4 %collective-permute-start.14 = (f32[256,256]{1,0:T(8,128)S(1)}, f32[256,256]{1,0:T(8,128)S(1)}, u32[]{:S(2)}, u32[]{:S(2)}) collective-permute-start(f32[256,256]{1,0:T(8,128)S(1)} %get-tuple-element.84.refs_1_), channel_id=1, source_target_pairs={{0,2},{1,5},{2,0},{3,7},{4,6},{5,1},{6,4},{7,3},{8,10},{9,13},{10,... | collective-permute-start | bytes 786440 | tf_op jit(solution)/shard_map/ppermute | solution.py:318
  29.1 1.3 %collective-permute-start.13 = (f32[64,256]{1,0:T(8,128)S(1)}, f32[64,256]{1,0:T(8,128)S(1)}, u32[]{:S(2)}, u32[]{:S(2)}) collective-permute-start(f32[64,256]{1,0:T(8,128)S(1)} %get-tuple-element.85.refs_6_), channel_id=1, source_target_pairs={{0,8},{1,9},{2,10},{3,11},{4,12},{5,13},{6,14},{7,15},{8,0},{9,1},... | collective-permute-start | bytes 196616 | tf_op jit(solution)/shard_map/ppermute | solution.py:318
  30.3 1.3 %grad_points_part.1.refs_3_.acc_ref = f32[1024,512]{1,0:T(8,128)S(1)} custom-call(bf16[1024,256]{1,0:T(8,128)(2,1)S(1)} %get-tuple-element.68.refs_0_, bf16[1024,256]{1,0:T(8,128)(2,1)S(1)} %get-tuple-element.74.rest_0_.refs_1_, bf16[1024,256]{1,0:T(8,128)(2,1)S(1)} %get-tuple-element.75.refs_2_, bf16[1024,256]{1,0:T(8,128)(2,1)S(1)} %get-tuple-element.78.refs_3_, ...), custom_call_target="tpu_custom_call" | custom-call | flops 1430000000 | bytes 130000 | tf_op jit(solution)/shard_map/grad_points_part/pallas_call | solution.py:294
  31.6 1.2 %collective-permute-done.11.refs_1_ = f32[288,256]{1,0:T(8,128)S(1)} collective-permute-done((f32[288,256]{1,0:T(8,128)S(1)}, f32[288,256]{1,0:T(8,128)S(1)}, u32[]{:S(2)}, u32[]{:S(2)}) %collective-permute-start.11) | collective-permute-done | bytes 294944 | tf_op jit(solution)/shard_map/ppermute | solution.py:318
  32.8 0.8 %collective-permute-start.12 = (f32[160,256]{1,0:T(8,128)S(1)}, f32[160,256]{1,0:T(8,128)S(1)}, u32[]{:S(2)}, u32[]{:S(2)}) collective-permute-start(f32[160,256]{1,0:T(8,128)S(1)} %get-tuple-element.87.refs_2_), channel_id=1, source_target_pairs={{0,4},{1,3},{2,6},{3,1},{4,0},{5,7},{6,2},{7,5},{8,12},{9,11},{10,... | collective-permute-start | bytes 491528 | tf_op jit(solution)/shard_map/ppermute | solution.py:318
  33.6 2.0 %collective-permute-done.14.refs_1_ = f32[256,256]{1,0:T(8,128)S(1)} collective-permute-done((f32[256,256]{1,0:T(8,128)S(1)}, f32[256,256]{1,0:T(8,128)S(1)}, u32[]{:S(2)}, u32[]{:S(2)}) %collective-permute-start.14) | collective-permute-done | bytes 262176 | tf_op jit(solution)/shard_map/ppermute | solution.py:318
  35.7 1.3 %collective-permute-start.16 = (f32[128,256]{1,0:T(8,128)S(1)}, f32[128,256]{1,0:T(8,128)S(1)}, u32[]{:S(2)}, u32[]{:S(2)}) collective-permute-start(f32[128,256]{1,0:T(8,128)S(1)} %get-tuple-element.91.rest_0_), channel_id=1, source_target_pairs={{0,4},{1,9},{2,6},{3,11},{4,0},{5,13},{6,2},{7,15},{8,12},{9,1},{1... | collective-permute-start | bytes 393224 | tf_op jit(solution)/shard_map/ppermute | solution.py:318
  37.1 1.2 %collective-permute-done.12.refs_1_ = f32[160,256]{1,0:T(8,128)S(1)} collective-permute-done((f32[160,256]{1,0:T(8,128)S(1)}, f32[160,256]{1,0:T(8,128)S(1)}, u32[]{:S(2)}, u32[]{:S(2)}) %collective-permute-start.12) | collective-permute-done | bytes 163872 | tf_op jit(solution)/shard_map/ppermute | solution.py:318
  38.3 1.3 %collective-permute-start.15 = (f32[32,256]{1,0:T(8,128)S(1)}, f32[32,256]{1,0:T(8,128)S(1)}, u32[]{:S(2)}, u32[]{:S(2)}) collective-permute-start(f32[32,256]{1,0:T(8,128)S(1)} %sum_state.4.refs_2_.a_ref), channel_id=1, source_target_pairs={{0,8},{1,9},{2,10},{3,11},{4,12},{5,13},{6,14},{7,15},{8,0},{9,1},... | collective-permute-start | bytes 98312 | tf_op jit(solution)/shard_map/ppermute | solution.py:318
  39.5 1.7 %collective-permute-start.18 = (f32[64,256]{1,0:T(8,128)S(1)}, f32[64,256]{1,0:T(8,128)S(1)}, u32[]{:S(2)}, u32[]{:S(2)}) collective-permute-start(f32[64,256]{1,0:T(8,128)S(1)} %get-tuple-element.92.rest_0_), channel_id=1, source_target_pairs={{0,8},{1,9},{2,10},{3,11},{4,12},{5,13},{6,14},{7,15},{8,0},{9,1},... | collective-permute-start | bytes 196616 | tf_op jit(solution)/shard_map/ppermute | solution.py:318
  41.3 1.9 %collective-permute-start.19 = (f32[64,256]{1,0:T(8,128)S(1)}, f32[64,256]{1,0:T(8,128)S(1)}, u32[]{:S(2)}, u32[]{:S(2)}) collective-permute-start(f32[64,256]{1,0:T(8,128)S(1)} %get-tuple-element.94.rest_0_), channel_id=1, source_target_pairs={{0,8},{1,3},{2,10},{3,1},{4,12},{5,7},{6,14},{7,5},{8,0},{9,11},{1... | collective-permute-start | bytes 196616 | tf_op jit(solution)/shard_map/ppermute | solution.py:318
  43.1 1.5 %collective-permute-done.15.b_ref = f32[32,256]{1,0:T(8,128)S(1)} collective-permute-done((f32[32,256]{1,0:T(8,128)S(1)}, f32[32,256]{1,0:T(8,128)S(1)}, u32[]{:S(2)}, u32[]{:S(2)}) %collective-permute-start.15) | collective-permute-done | bytes 32800 | tf_op jit(solution)/shard_map/ppermute | solution.py:318
  44.6 0.7 %grad_points_own.1.acc_ref = f32[1024,512]{1,0:T(8,128)S(1)} custom-call(f32[1024,512]{1,0:T(8,128)S(1)} %grad_points_part.1.refs_3_.acc_ref, bf16[1024,512]{1,0:T(8,128)(2,1)S(1)} %copy-done, bf16[512,512]{1,0:T(8,128)(2,1)S(1)} %copy-done.1, f32[32,256]{1,0:T(8,128)S(1)} %sum_state.5.own_ref), custom_call_target="tpu_custom_call" | custom-call | flops 1100000000 | bytes 100000 | tf_op jit(solution)/shard_map/grad_points_own/pallas_call | solution.py:294
  45.8 0.7 %collective-permute-done.18.rest_1_ = f32[64,256]{1,0:T(8,128)S(1)} collective-permute-done((f32[64,256]{1,0:T(8,128)S(1)}, f32[64,256]{1,0:T(8,128)S(1)}, u32[]{:S(2)}, u32[]{:S(2)}) %collective-permute-start.18) | collective-permute-done | bytes 65568 | tf_op jit(solution)/shard_map/ppermute | solution.py:318
  46.5 1.6 %outputs.1 = (bf16[1024,512]{1,0:T(8,128)(2,1)}, f32[64,256]{1,0:T(8,128)}, f32[64,256]{1,0:T(8,128)}) custom-call(f32[1024,512]{1,0:T(8,128)S(1)} %grad_points_own.1.acc_ref, bf16[1024,512]{1,0:T(8,128)(2,1)S(1)} %copy-done, bf16[512,512]{1,0:T(8,128)(2,1)S(1)} %copy-done.1, f32[32,256]{1,0:T(8,128)S(1)} %sum_state.5.own_ref, ...), custom_call_target="tpu_custom_call" | custom-call | flops 11000000 | bytes 1000 | tf_op jit(solution)/shard_map/outputs/pallas_call | solution.py:294
  48.1 0.6 %value_out.1 = f32[64,256]{1,0:T(8,128)} custom-call(f32[64,256]{1,0:T(8,128)S(1)} %bitcast.15, f32[64,256]{1,0:T(8,128)S(1)} %collective-permute-done.19.got_ref, f32[64,256]{1,0:T(8,128)} %get-tuple-element.49.rest_0_), custom_call_target="tpu_custom_call" | custom-call | flops 11000000 | bytes 1000 | tf_op jit(solution)/shard_map/value_out/pallas_call | solution.py:294
  (49 shorter events, 1.9 us)
Async XLA Ops:
  3.4 1.4 %collective-permute-start = (f32[32,256]{1,0:T(8,128)S(1)}, f32[32,256]{1,0:T(8,128)S(1)}, u32[]{:S(2)}, u32[]{:S(2)}) collective-permute-start(f32[32,256]{1,0:T(8,128)S(1)} %get-tuple-element.100), channel_id=1, source_target_pairs={{0,1},{1,0},{2,3},{3,2},{4,5},{5,4},{6,7},{7,6},{8,9},{9,8},{10,11... | collective-permute-start | bytes 98312 | tf_op jit(solution)/shard_map/ppermute | solution.py:307
  4.0 3.7 %collective-permute-start.2 = (f32[8,64,256]{2,1,0:T(8,128)S(1)}, f32[8,64,256]{2,1,0:T(8,128)S(1)}, u32[]{:S(2)}, u32[]{:S(2)}) collective-permute-start(f32[8,64,256]{2,1,0:T(8,128)S(1)} %get-tuple-element.56), channel_id=1, source_target_pairs={{0,1},{1,0},{2,3},{3,2},{4,5},{5,4},{6,7},{7,6},{8,9},{9,8},{10,11... | collective-permute-start | bytes 1572872 | tf_op jit(solution)/shard_map/ppermute | solution.py:307
  4.8 6.9 %copy-start.2 = (bf16[512,512]{1,0:T(8,128)(2,1)S(1)}, bf16[512,512]{1,0:T(8,128)(2,1)}, u32[]{:S(2)}) copy-start(bf16[512,512]{1,0:T(8,128)(2,1)} %refs_4_.1) | copy-start | bytes 1572868
  4.8 6.9 %copy-start.3 = (bf16[512,512]{1,0:T(8,128)(2,1)S(1)}, bf16[512,512]{1,0:T(8,128)(2,1)}, u32[]{:S(2)}) copy-start(bf16[512,512]{1,0:T(8,128)(2,1)} %refs_5_.1) | copy-start | bytes 1572868
  4.8 4.8 %collective-permute-start.1 = (f32[32,256]{1,0:T(8,128)S(1)}, f32[32,256]{1,0:T(8,128)S(1)}, u32[]{:S(2)}, u32[]{:S(2)}) collective-permute-start(f32[32,256]{1,0:T(8,128)S(1)} %sum_0.1.refs_2_.a_ref), channel_id=1, source_target_pairs={{0,2},{1,5},{2,0},{3,7},{4,6},{5,1},{6,4},{7,3},{8,10},{9,13},{10,... | collective-permute-start | bytes 98312 | tf_op jit(solution)/shard_map/ppermute | solution.py:318
  7.8 8.9 %collective-permute-start.5 = (f32[256,256]{1,0:T(8,128)S(1)}, f32[256,256]{1,0:T(8,128)S(1)}, u32[]{:S(2)}, u32[]{:S(2)}) collective-permute-start(f32[256,256]{1,0:T(8,128)S(1)} %get-tuple-element.57.rest_0_.rest_3_), channel_id=1, source_target_pairs={{0,2},{1,5},{2,0},{3,7},{4,6},{5,1},{6,4},{7,3},{8,10},{9,13},{10,... | collective-permute-start | bytes 786440 | tf_op jit(solution)/shard_map/ppermute | solution.py:318
  9.6 4.3 %collective-permute-start.3 = (f32[32,256]{1,0:T(8,128)S(1)}, f32[32,256]{1,0:T(8,128)S(1)}, u32[]{:S(2)}, u32[]{:S(2)}) collective-permute-start(f32[32,256]{1,0:T(8,128)S(1)} %sum_1.1.rest_2_.a_ref), channel_id=1, source_target_pairs={{0,4},{1,9},{2,6},{3,11},{4,0},{5,13},{6,2},{7,15},{8,12},{9,1},{1... | collective-permute-start | bytes 98312 | tf_op jit(solution)/shard_map/ppermute | solution.py:318
  13.9 6.3 %collective-permute-start.4 = (f32[32,256]{1,0:T(8,128)S(1)}, f32[32,256]{1,0:T(8,128)S(1)}, u32[]{:S(2)}, u32[]{:S(2)}) collective-permute-start(f32[32,256]{1,0:T(8,128)S(1)} %sum_2.1.refs_2_.rest_1_.a_ref), channel_id=1, source_target_pairs={{0,8},{1,3},{2,10},{3,1},{4,12},{5,7},{6,14},{7,5},{8,0},{9,11},{1... | collective-permute-start | bytes 98312 | tf_op jit(solution)/shard_map/ppermute | solution.py:318
  16.7 6.0 %collective-permute-start.7 = (f32[128,256]{1,0:T(8,128)S(1)}, f32[128,256]{1,0:T(8,128)S(1)}, u32[]{:S(2)}, u32[]{:S(2)}) collective-permute-start(f32[128,256]{1,0:T(8,128)S(1)} %get-tuple-element.62.rest_2_), channel_id=1, source_target_pairs={{0,4},{1,3},{2,6},{3,1},{4,0},{5,7},{6,2},{7,5},{8,12},{9,11},{10,... | collective-permute-start | bytes 393224 | tf_op jit(solution)/shard_map/ppermute | solution.py:318
  20.2 2.5 %collective-permute-start.6 = (f32[32,256]{1,0:T(8,128)S(1)}, f32[32,256]{1,0:T(8,128)S(1)}, u32[]{:S(2)}, u32[]{:S(2)}) collective-permute-start(f32[32,256]{1,0:T(8,128)S(1)} %sum_3.1.g_ref), channel_id=1, source_target_pairs={{0,1},{1,0},{2,3},{3,2},{4,5},{5,4},{6,7},{7,6},{8,9},{9,8},{10,11... | collective-permute-start | bytes 98312 | tf_op jit(solution)/shard_map/ppermute | solution.py:307
  20.3 3.8 %collective-permute-start.10 = (f32[32,256]{1,0:T(8,128)S(1)}, f32[32,256]{1,0:T(8,128)S(1)}, u32[]{:S(2)}, u32[]{:S(2)}) collective-permute-start(f32[32,256]{1,0:T(8,128)S(1)} %get-tuple-element.63.rest_0_), channel_id=1, source_target_pairs={{0,1},{1,0},{2,3},{3,2},{4,5},{5,4},{6,7},{7,6},{8,9},{9,8},{10,11... | collective-permute-start | bytes 98312 | tf_op jit(solution)/shard_map/ppermute | solution.py:307
  24.0 2.0 %collective-permute-start.9 = (f32[8,64,256]{2,1,0:T(8,128)S(1)}, f32[8,64,256]{2,1,0:T(8,128)S(1)}, u32[]{:S(2)}, u32[]{:S(2)}) collective-permute-start(f32[8,64,256]{2,1,0:T(8,128)S(1)} %get-tuple-element.82), channel_id=1, source_target_pairs={{0,1},{1,0},{2,3},{3,2},{4,5},{5,4},{6,7},{7,6},{8,9},{9,8},{10,11... | collective-permute-start | bytes 1572872 | tf_op jit(solution)/shard_map/ppermute | solution.py:307
  25.4 2.2 %collective-permute-start.8 = (f32[8,64,256]{2,1,0:T(8,128)S(1)}, f32[8,64,256]{2,1,0:T(8,128)S(1)}, u32[]{:S(2)}, u32[]{:S(2)}) collective-permute-start(f32[8,64,256]{2,1,0:T(8,128)S(1)} %get-tuple-element.80), channel_id=1, source_target_pairs={{0,1},{1,0},{2,3},{3,2},{4,5},{5,4},{6,7},{7,6},{8,9},{9,8},{10,11... | collective-permute-start | bytes 1572872 | tf_op jit(solution)/shard_map/ppermute | solution.py:307
  26.0 6.8 %collective-permute-start.11 = (f32[288,256]{1,0:T(8,128)S(1)}, f32[288,256]{1,0:T(8,128)S(1)}, u32[]{:S(2)}, u32[]{:S(2)}) collective-permute-start(f32[288,256]{1,0:T(8,128)S(1)} %get-tuple-element.83.refs_2_), channel_id=1, source_target_pairs={{0,2},{1,5},{2,0},{3,7},{4,6},{5,1},{6,4},{7,3},{8,10},{9,13},{10,... | collective-permute-start | bytes 884744 | tf_op jit(solution)/shard_map/ppermute | solution.py:318
  27.6 8.0 %collective-permute-start.14 = (f32[256,256]{1,0:T(8,128)S(1)}, f32[256,256]{1,0:T(8,128)S(1)}, u32[]{:S(2)}, u32[]{:S(2)}) collective-permute-start(f32[256,256]{1,0:T(8,128)S(1)} %get-tuple-element.84.refs_1_), channel_id=1, source_target_pairs={{0,2},{1,5},{2,0},{3,7},{4,6},{5,1},{6,4},{7,3},{8,10},{9,13},{10,... | collective-permute-start | bytes 786440 | tf_op jit(solution)/shard_map/ppermute | solution.py:318
  29.1 8.0 %collective-permute-start.13 = (f32[64,256]{1,0:T(8,128)S(1)}, f32[64,256]{1,0:T(8,128)S(1)}, u32[]{:S(2)}, u32[]{:S(2)}) collective-permute-start(f32[64,256]{1,0:T(8,128)S(1)} %get-tuple-element.85.refs_6_), channel_id=1, source_target_pairs={{0,8},{1,9},{2,10},{3,11},{4,12},{5,13},{6,14},{7,15},{8,0},{9,1},... | collective-permute-start | bytes 196616 | tf_op jit(solution)/shard_map/ppermute | solution.py:318
  32.8 5.4 %collective-permute-start.12 = (f32[160,256]{1,0:T(8,128)S(1)}, f32[160,256]{1,0:T(8,128)S(1)}, u32[]{:S(2)}, u32[]{:S(2)}) collective-permute-start(f32[160,256]{1,0:T(8,128)S(1)} %get-tuple-element.87.refs_2_), channel_id=1, source_target_pairs={{0,4},{1,3},{2,6},{3,1},{4,0},{5,7},{6,2},{7,5},{8,12},{9,11},{10,... | collective-permute-start | bytes 491528 | tf_op jit(solution)/shard_map/ppermute | solution.py:318
  35.7 5.6 %collective-permute-start.16 = (f32[128,256]{1,0:T(8,128)S(1)}, f32[128,256]{1,0:T(8,128)S(1)}, u32[]{:S(2)}, u32[]{:S(2)}) collective-permute-start(f32[128,256]{1,0:T(8,128)S(1)} %get-tuple-element.91.rest_0_), channel_id=1, source_target_pairs={{0,4},{1,9},{2,6},{3,11},{4,0},{5,13},{6,2},{7,15},{8,12},{9,1},{1... | collective-permute-start | bytes 393224 | tf_op jit(solution)/shard_map/ppermute | solution.py:318
  37.0 7.6 %copy-start = (bf16[1024,512]{1,0:T(8,128)(2,1)S(1)}, bf16[1024,512]{1,0:T(8,128)(2,1)}, u32[]{:S(2)}) copy-start(bf16[1024,512]{1,0:T(8,128)(2,1)} %c_ref.3) | copy-start | bytes 3145732
  37.0 7.6 %copy-start.1 = (bf16[512,512]{1,0:T(8,128)(2,1)S(1)}, bf16[512,512]{1,0:T(8,128)(2,1)}, u32[]{:S(2)}) copy-start(bf16[512,512]{1,0:T(8,128)(2,1)} %wq_ref.3) | copy-start | bytes 1572868
  38.3 6.3 %collective-permute-start.15 = (f32[32,256]{1,0:T(8,128)S(1)}, f32[32,256]{1,0:T(8,128)S(1)}, u32[]{:S(2)}, u32[]{:S(2)}) collective-permute-start(f32[32,256]{1,0:T(8,128)S(1)} %sum_state.4.refs_2_.a_ref), channel_id=1, source_target_pairs={{0,8},{1,9},{2,10},{3,11},{4,12},{5,13},{6,14},{7,15},{8,0},{9,1},... | collective-permute-start | bytes 98312 | tf_op jit(solution)/shard_map/ppermute | solution.py:318
  39.5 7.0 %collective-permute-start.18 = (f32[64,256]{1,0:T(8,128)S(1)}, f32[64,256]{1,0:T(8,128)S(1)}, u32[]{:S(2)}, u32[]{:S(2)}) collective-permute-start(f32[64,256]{1,0:T(8,128)S(1)} %get-tuple-element.92.rest_0_), channel_id=1, source_target_pairs={{0,8},{1,9},{2,10},{3,11},{4,12},{5,13},{6,14},{7,15},{8,0},{9,1},... | collective-permute-start | bytes 196616 | tf_op jit(solution)/shard_map/ppermute | solution.py:318
  41.3 6.8 %collective-permute-start.19 = (f32[64,256]{1,0:T(8,128)S(1)}, f32[64,256]{1,0:T(8,128)S(1)}, u32[]{:S(2)}, u32[]{:S(2)}) collective-permute-start(f32[64,256]{1,0:T(8,128)S(1)} %get-tuple-element.94.rest_0_), channel_id=1, source_target_pairs={{0,8},{1,3},{2,10},{3,1},{4,12},{5,7},{6,14},{7,5},{8,0},{9,11},{1... | collective-permute-start | bytes 196616 | tf_op jit(solution)/shard_map/ppermute | solution.py:318
  44.6 1.2 %collective-permute-start.17 = (f32[32,256]{1,0:T(8,128)S(1)}, f32[32,256]{1,0:T(8,128)S(1)}, u32[]{:S(2)}, u32[]{:S(2)}) collective-permute-start(f32[32,256]{1,0:T(8,128)S(1)} %sum_state.5.own_ref), channel_id=1, source_target_pairs={{0,1},{1,0},{2,3},{3,2},{4,5},{5,4},{6,7},{7,6},{8,9},{9,8},{10,11... | collective-permute-start | bytes 98312 | tf_op jit(solution)/shard_map/ppermute | solution.py:307

commit v8 on v7

--- a/solution.py
+++ b/solution.py
@@ -242,7 +242,7 @@
 
 
 def last_kernel(total, acc_ref, c_ref, wq_ref, own_ref, got_ref, m_ref, *rest):
-    kept_ref, got_part, outs, (q_ref, gp_ref, g_ref, sems) = rest[0], rest[1], rest[-7:-4], rest[-4:]
+    outs, (q_ref, gp_ref, g_ref, sems) = rest[-6:-4], rest[-4:]
     rows, width = c_ref.shape
     rb, cb = m_ref.shape
     ns, nx = lax.axis_size("sub"), lax.axis_size("mp")
@@ -251,14 +251,12 @@
     cols = half_columns(other, width)
     low_own, low_got = state_low(total, own_ref), state_low(total, got_ref)
     q_ref[...] = dot(c_ref[:, cols], unpack(low_got).astype(BF16), NT).astype(BF16)
-    g_ref[1] = (kept_ref[...] + got_part[:rb, :]) / total
-    copies = [pltpu.make_async_copy(g_ref.at[1], outs[2], sems.at[1])]
-    copies[0].start()
+    copies = []
     chunk = rows // BLOCKS
     for r in range(BLOCKS):
         span = slice(r * chunk, (r + 1) * chunk)
         gp_ref[span, :] = (acc_ref[span, :] + dot(q_ref[span, :], wq_ref[:, cols], NT)).astype(BF16)
-        copies.append(pltpu.make_async_copy(gp_ref.at[span, :], outs[0].at[span, :], sems.at[2 + r]))
+        copies.append(pltpu.make_async_copy(gp_ref.at[span, :], outs[0].at[span, :], sems.at[1 + r]))
         copies[-1].start()
     whole = jnp.concatenate([jnp.where(s == g, low_own, low_got) for g in range(ns)], axis=1)
     high, rest_ = split(m_ref[...])
@@ -267,8 +265,8 @@
     for xb in range(1, nx):
         mine = jnp.where(x == xb, whole[:, xb * cb : (xb + 1) * cb], mine)
     state = unpack(mine).astype(BF16)
-    g_ref[0] = (dot(high, state, NT) + dot(rest_, state, NT) + dot(third, state, NT)) / total
-    copies.append(pltpu.make_async_copy(g_ref.at[0], outs[1], sems.at[0]))
+    g_ref[...] = (dot(high, state, NT) + dot(rest_, state, NT) + dot(third, state, NT)) / total
+    copies.append(pltpu.make_async_copy(g_ref, outs[1], sems.at[0]))
     copies[-1].start()
     for copy in copies:
         copy.wait()
@@ -322,8 +320,10 @@
     rest[-1][...] = a_ref[...] + b_ref[: a_ref.shape[0], :]
 
 
-def value_out_kernel(total, kept_ref, got_ref, *rest):
-    rest[-1][...] = (kept_ref[...] + got_ref[...]) / total
+def sums_out_kernel(total, *refs):
+    for i in range(2):
+        kept_ref, got_ref = refs[2 * i : 2 * i + 2]
+        refs[-2 + i][...] = (kept_ref[...] + got_ref[: kept_ref.shape[0], :]) / total
 
 
 class Total:
@@ -573,27 +573,30 @@
         us=1.0,
     )
     block = shape((rb, cb), F32)
-    grad_points, grad_query, grad_key = call(
+    grad_points, grad_query = call(
         functools.partial(last_kernel, total),
         "outputs",
-        (low, block, block),
-        [partial, cotangent, w_query, s_own, s_got, m_total, key_sum.kept.reshape(rb, cb), key_sum.got],
-        [VMEM] * 8,
+        (low, block),
+        (partial, cotangent, w_query, s_own, s_got, m_total),
+        [VMEM] * 6,
         scratch=[
             pltpu.VMEM((rows, half), BF16),
             pltpu.VMEM((rows, width), BF16),
-            pltpu.VMEM((2, rb, cb), F32),
-            pltpu.SemaphoreType.DMA((2 + BLOCKS,)),
+            pltpu.VMEM((rb, cb), F32),
+            pltpu.SemaphoreType.DMA((1 + BLOCKS,)),
         ],
         us=0.01,
-        outs=(HBM,) * 3,
+        outs=(HBM,) * 2,
     )
-    (grad_value,) = call(
-        functools.partial(value_out_kernel, total),
-        "value_out",
-        (block,),
-        (value_sum.kept.reshape(rb, cb), value_sum.got, pltpu.with_memory_space_constraint(grad_query, pltpu.HBM)),
-        [VMEM, VMEM, HBM],
+    parts = []
+    for one in (key_sum, value_sum):
+        parts += [one.kept.reshape(rb, cb), one.got]
+    grad_key, grad_value = call(
+        functools.partial(sums_out_kernel, total),
+        "sums_out",
+        (block, block),
+        parts + [pltpu.with_memory_space_constraint(grad_query, pltpu.HBM)],
+        [VMEM] * 4 + [HBM],
         us=0.01,
     )
     return grad_points, grad_query, grad_key, grad_value

time: 48.9 us -> 48.7 us (level)
  no operation moved by 1% of the time
where the time goes in v8:
time: 48.7 us; the launch traced here: 48.6 us
  starting transfers between devices  23.5 us (48%)
  Pallas kernels  15.8 us (32%)
  waiting for transfers between devices  8.45 us (17%)
  between operations  0.85 us (2%)
    ppermute x13, starting transfers between devices, swap(): return lax.ppermute(value, ('points', 'mp', 'sub'), pairs)  21.6 us
    pallas_call x29, Pallas kernels, call(): pl.pallas_call(kernel, out_shape=out_shape, in_specs=specs, out_specs=out...  15.8 us
    ppermute x13, waiting for transfers between devices, swap(): return lax.ppermute(value, ('points', 'mp', 'sub'), pairs)  7.28 us
    ppermute x7, starting transfers between devices, swap_cores(): lax.ppermute(value, 'sub', [(i, i ^ 1) for i in range(lax.axis_size('sub'...  1.85 us
    ppermute x7, waiting for transfers between devices, swap_cores(): lax.ppermute(value, 'sub', [(i, i ^ 1) for i in range(lax.axis_size('sub'...  1.17 us
  transfers between devices with their start and end apart: 20, of which 9 were waited for; matrix products, arithmetic and copies ran while one was open for 0% of the time, Pallas kernels for 25%

profile of v8, /device:TPU:0, one launch (start us, length us, event | category | flops | bytes accessed | tf_op | source)
XLA Modules:
  0.0 48.6 jit_solution(17456943963736888721)
XLA Ops:
  0.6 2.7 %cross.1 = (f32[512,512]{1,0:T(8,128)S(1)}, f32[2,32,256]{2,1,0:T(8,128)S(1)}, bf16[1024,512]{1,0:T(8,128)(2,1)S(1)}, bf16[512,1024]{1,0:T(8,128)(2,1)S(1)}) custom-call(bf16[1024,512]{1,0:T(8,128)(2,1)} %p_hbm.1, bf16[1024,512]{1,0:T(8,128)(2,1)} %c_ref.3, bf16[512,512]{1,0:T(8,128)(2,1)} %wq_ref.3), custom_call_target="tpu_custom_call" | custom-call | flops 3300000000 | bytes 300000 | tf_op jit(solution)/shard_map/cross/pallas_call | solution.py:292
  3.4 0.5 %collective-permute-start = (f32[32,256]{1,0:T(8,128)S(1)}, f32[32,256]{1,0:T(8,128)S(1)}, u32[]{:S(2)}, u32[]{:S(2)}) collective-permute-start(f32[32,256]{1,0:T(8,128)S(1)} %get-tuple-element.102), channel_id=1, source_target_pairs={{0,1},{1,0},{2,3},{3,2},{4,5},{5,4},{6,7},{7,6},{8,9},{9,8},{10,11... | collective-permute-start | bytes 98312 | tf_op jit(solution)/shard_map/ppermute | solution.py:305
  4.1 0.7 %collective-permute-done.b_ref = f32[32,256]{1,0:T(8,128)S(1)} collective-permute-done((f32[32,256]{1,0:T(8,128)S(1)}, f32[32,256]{1,0:T(8,128)S(1)}, u32[]{:S(2)}, u32[]{:S(2)}) %collective-permute-start) | collective-permute-done | bytes 32800 | tf_op jit(solution)/shard_map/ppermute | solution.py:305
  4.8 2.9 %collective-permute-start.1 = (f32[32,256]{1,0:T(8,128)S(1)}, f32[32,256]{1,0:T(8,128)S(1)}, u32[]{:S(2)}, u32[]{:S(2)}) collective-permute-start(f32[32,256]{1,0:T(8,128)S(1)} %sum_0.1.refs_2_.a_ref), channel_id=1, source_target_pairs={{0,2},{1,5},{2,0},{3,7},{4,6},{5,1},{6,4},{7,3},{8,10},{9,13},{10,... | collective-permute-start | bytes 98312 | tf_op jit(solution)/shard_map/ppermute | solution.py:316
  7.8 1.0 %collective-permute-start.5 = (f32[256,256]{1,0:T(8,128)S(1)}, f32[256,256]{1,0:T(8,128)S(1)}, u32[]{:S(2)}, u32[]{:S(2)}) collective-permute-start(f32[256,256]{1,0:T(8,128)S(1)} %get-tuple-element.58.rest_0_.rest_3_), channel_id=1, source_target_pairs={{0,2},{1,5},{2,0},{3,7},{4,6},{5,1},{6,4},{7,3},{8,10},{9,13},{10,... | collective-permute-start | bytes 786440 | tf_op jit(solution)/shard_map/ppermute | solution.py:316
  8.7 0.9 %collective-permute-done.1.b_ref = f32[32,256]{1,0:T(8,128)S(1)} collective-permute-done((f32[32,256]{1,0:T(8,128)S(1)}, f32[32,256]{1,0:T(8,128)S(1)}, u32[]{:S(2)}, u32[]{:S(2)}) %collective-permute-start.1) | collective-permute-done | bytes 32800 | tf_op jit(solution)/shard_map/ppermute | solution.py:316
  9.6 2.1 %collective-permute-start.3 = (f32[32,256]{1,0:T(8,128)S(1)}, f32[32,256]{1,0:T(8,128)S(1)}, u32[]{:S(2)}, u32[]{:S(2)}) collective-permute-start(f32[32,256]{1,0:T(8,128)S(1)} %sum_1.1.rest_2_.a_ref), channel_id=1, source_target_pairs={{0,4},{1,9},{2,6},{3,11},{4,0},{5,13},{6,2},{7,15},{8,12},{9,1},{1... | collective-permute-start | bytes 98312 | tf_op jit(solution)/shard_map/ppermute | solution.py:316
  11.7 2.1 %norm.2 = (f32[1024,256]{1,0:T(8,128)S(1)}, f32[1024,256]{1,0:T(8,128)S(1)}, f32[1024,256]{1,0:T(8,128)S(1)}, f32[1024,256]{1,0:T(8,128)S(1)}, f32[32,256]{1,0:T(8,128)S(1)}, /*index=5*/bf16[4,512,256]{2,1,0:T(8,128)(2,1)S(1)}) custom-call(bf16[1024,512]{1,0:T(8,128)(2,1)S(1)} %get-tuple-element.59.p_ref, bf16[512,512]{1,0:T(8,128)(2,1)S(1)} %copy-done.2, ...), custom_call_target="tpu_custom_call" | custom-call | flops 2529999872 | bytes 229999 | tf_op jit(solution)/shard_map/norm/pallas_call | solution.py:292
  13.9 2.7 %collective-permute-start.4 = (f32[32,256]{1,0:T(8,128)S(1)}, f32[32,256]{1,0:T(8,128)S(1)}, u32[]{:S(2)}, u32[]{:S(2)}) collective-permute-start(f32[32,256]{1,0:T(8,128)S(1)} %sum_2.1.refs_2_.rest_1_.a_ref), channel_id=1, source_target_pairs={{0,8},{1,3},{2,10},{3,1},{4,12},{5,7},{6,14},{7,5},{8,0},{9,11},{1... | collective-permute-start | bytes 98312 | tf_op jit(solution)/shard_map/ppermute | solution.py:316
  16.7 1.6 %collective-permute-start.7 = (f32[128,256]{1,0:T(8,128)S(1)}, f32[128,256]{1,0:T(8,128)S(1)}, u32[]{:S(2)}, u32[]{:S(2)}) collective-permute-start(f32[128,256]{1,0:T(8,128)S(1)} %get-tuple-element.63.rest_2_), channel_id=1, source_target_pairs={{0,4},{1,3},{2,6},{3,1},{4,0},{5,7},{6,2},{7,5},{8,12},{9,11},{10,... | collective-permute-start | bytes 393224 | tf_op jit(solution)/shard_map/ppermute | solution.py:316
  18.3 1.9 %norm.3 = (f32[1024,256]{1,0:T(8,128)S(1)}, f32[1024,256]{1,0:T(8,128)S(1)}, f32[1024,256]{1,0:T(8,128)S(1)}, f32[1024,256]{1,0:T(8,128)S(1)}, f32[32,256]{1,0:T(8,128)S(1)}) custom-call(bf16[1024,512]{1,0:T(8,128)(2,1)S(1)} %get-tuple-element.59.p_ref, bf16[4,512,256]{2,1,0:T(8,128)(2,1)S(1)} %get-tuple-element.61.rest_0_, ...), custom_call_target="tpu_custom_call" | custom-call | flops 2529999872 | bytes 229999 | tf_op jit(solution)/shard_map/norm/pallas_call | solution.py:292
  20.8 1.9 %back_own.1 = (bf16[1024,256]{1,0:T(8,128)(2,1)S(1)}, bf16[1024,256]{1,0:T(8,128)(2,1)S(1)}, f32[512,256]{1,0:T(8,128)S(1)}, f32[512,256]{1,0:T(8,128)S(1)}) custom-call(bf16[512,1024]{1,0:T(8,128)(2,1)S(1)} %get-tuple-element.53.pt_ref, f32[32,256]{1,0:T(8,128)S(1)} %sum_3.1.g_ref, f32[1024,256]{1,0:T(8,128)S(1)} %get-tuple-element.65.kn_ref, ...), custom_call_target="tpu_custom_call" | custom-call | flops 11000000 | bytes 1000 | tf_op jit(solution)/shard_map/back_own/pallas_call | solution.py:292
  22.7 1.2 %back_key.1 = (bf16[1024,256]{1,0:T(8,128)(2,1)S(1)}, f32[8,64,256]{2,1,0:T(8,128)S(1)}, f32[8,64,256]{2,1,0:T(8,128)S(1)}) custom-call(bf16[512,1024]{1,0:T(8,128)(2,1)S(1)} %get-tuple-element.53.pt_ref, f32[512,256]{1,0:T(8,128)S(1)} %get-tuple-element.70.own_ref, f32[32,256]{1,0:T(8,128)S(1)} %collective-permute-done.6.g_ref, ...), custom_call_target="tpu_custom_call" | custom-call | flops 5500000256 | bytes 500000 | tf_op jit(solution)/shard_map/back_key/pallas_call | solution.py:292
  24.1 1.3 %back_value.1 = (bf16[1024,256]{1,0:T(8,128)(2,1)S(1)}, f32[8,64,256]{2,1,0:T(8,128)S(1)}, f32[8,64,256]{2,1,0:T(8,128)S(1)}) custom-call(bf16[512,1024]{1,0:T(8,128)(2,1)S(1)} %get-tuple-element.53.pt_ref, f32[512,256]{1,0:T(8,128)S(1)} %get-tuple-element.77.own_ref, f32[32,256]{1,0:T(8,128)S(1)} %collective-permute-done.6.g_ref, ...), custom_call_target="tpu_custom_call" | custom-call | flops 5500000256 | bytes 500000 | tf_op jit(solution)/shard_map/back_value/pallas_call | solution.py:292
  25.4 0.5 %collective-permute-start.8 = (f32[8,64,256]{2,1,0:T(8,128)S(1)}, f32[8,64,256]{2,1,0:T(8,128)S(1)}, u32[]{:S(2)}, u32[]{:S(2)}) collective-permute-start(f32[8,64,256]{2,1,0:T(8,128)S(1)} %get-tuple-element.81), channel_id=1, source_target_pairs={{0,1},{1,0},{2,3},{3,2},{4,5},{5,4},{6,7},{7,6},{8,9},{9,8},{10,11... | collective-permute-start | bytes 1572872 | tf_op jit(solution)/shard_map/ppermute | solution.py:305
  26.0 1.6 %collective-permute-start.11 = (f32[288,256]{1,0:T(8,128)S(1)}, f32[288,256]{1,0:T(8,128)S(1)}, u32[]{:S(2)}, u32[]{:S(2)}) collective-permute-start(f32[288,256]{1,0:T(8,128)S(1)} %get-tuple-element.84.refs_2_), channel_id=1, source_target_pairs={{0,2},{1,5},{2,0},{3,7},{4,6},{5,1},{6,4},{7,3},{8,10},{9,13},{10,... | collective-permute-start | bytes 884744 | tf_op jit(solution)/shard_map/ppermute | solution.py:316
  27.6 1.4 %collective-permute-start.14 = (f32[256,256]{1,0:T(8,128)S(1)}, f32[256,256]{1,0:T(8,128)S(1)}, u32[]{:S(2)}, u32[]{:S(2)}) collective-permute-start(f32[256,256]{1,0:T(8,128)S(1)} %get-tuple-element.85.refs_1_), channel_id=1, source_target_pairs={{0,2},{1,5},{2,0},{3,7},{4,6},{5,1},{6,4},{7,3},{8,10},{9,13},{10,... | collective-permute-start | bytes 786440 | tf_op jit(solution)/shard_map/ppermute | solution.py:316
  29.1 1.3 %collective-permute-start.13 = (f32[64,256]{1,0:T(8,128)S(1)}, f32[64,256]{1,0:T(8,128)S(1)}, u32[]{:S(2)}, u32[]{:S(2)}) collective-permute-start(f32[64,256]{1,0:T(8,128)S(1)} %get-tuple-element.86.refs_6_), channel_id=1, source_target_pairs={{0,8},{1,9},{2,10},{3,11},{4,12},{5,13},{6,14},{7,15},{8,0},{9,1},... | collective-permute-start | bytes 196616 | tf_op jit(solution)/shard_map/ppermute | solution.py:316
  30.3 1.3 %grad_points_part.1.refs_3_.acc_ref = f32[1024,512]{1,0:T(8,128)S(1)} custom-call(bf16[1024,256]{1,0:T(8,128)(2,1)S(1)} %get-tuple-element.69.refs_0_, bf16[1024,256]{1,0:T(8,128)(2,1)S(1)} %get-tuple-element.75.rest_0_.refs_1_, bf16[1024,256]{1,0:T(8,128)(2,1)S(1)} %get-tuple-element.76.refs_2_, bf16[1024,256]{1,0:T(8,128)(2,1)S(1)} %get-tuple-element.79.refs_3_, ...), custom_call_target="tpu_custom_call" | custom-call | flops 1430000000 | bytes 130000 | tf_op jit(solution)/shard_map/grad_points_part/pallas_call | solution.py:292
  31.6 1.2 %collective-permute-done.11.refs_1_ = f32[288,256]{1,0:T(8,128)S(1)} collective-permute-done((f32[288,256]{1,0:T(8,128)S(1)}, f32[288,256]{1,0:T(8,128)S(1)}, u32[]{:S(2)}, u32[]{:S(2)}) %collective-permute-start.11) | collective-permute-done | bytes 294944 | tf_op jit(solution)/shard_map/ppermute | solution.py:316
  32.8 0.8 %collective-permute-start.12 = (f32[160,256]{1,0:T(8,128)S(1)}, f32[160,256]{1,0:T(8,128)S(1)}, u32[]{:S(2)}, u32[]{:S(2)}) collective-permute-start(f32[160,256]{1,0:T(8,128)S(1)} %get-tuple-element.88.refs_2_), channel_id=1, source_target_pairs={{0,4},{1,3},{2,6},{3,1},{4,0},{5,7},{6,2},{7,5},{8,12},{9,11},{10,... | collective-permute-start | bytes 491528 | tf_op jit(solution)/shard_map/ppermute | solution.py:316
  33.6 2.0 %collective-permute-done.14.refs_1_ = f32[256,256]{1,0:T(8,128)S(1)} collective-permute-done((f32[256,256]{1,0:T(8,128)S(1)}, f32[256,256]{1,0:T(8,128)S(1)}, u32[]{:S(2)}, u32[]{:S(2)}) %collective-permute-start.14) | collective-permute-done | bytes 262176 | tf_op jit(solution)/shard_map/ppermute | solution.py:316
  35.7 1.3 %collective-permute-start.16 = (f32[128,256]{1,0:T(8,128)S(1)}, f32[128,256]{1,0:T(8,128)S(1)}, u32[]{:S(2)}, u32[]{:S(2)}) collective-permute-start(f32[128,256]{1,0:T(8,128)S(1)} %get-tuple-element.92.rest_0_), channel_id=1, source_target_pairs={{0,4},{1,9},{2,6},{3,11},{4,0},{5,13},{6,2},{7,15},{8,12},{9,1},{1... | collective-permute-start | bytes 393224 | tf_op jit(solution)/shard_map/ppermute | solution.py:316
  37.1 1.2 %collective-permute-done.12.refs_1_ = f32[160,256]{1,0:T(8,128)S(1)} collective-permute-done((f32[160,256]{1,0:T(8,128)S(1)}, f32[160,256]{1,0:T(8,128)S(1)}, u32[]{:S(2)}, u32[]{:S(2)}) %collective-permute-start.12) | collective-permute-done | bytes 163872 | tf_op jit(solution)/shard_map/ppermute | solution.py:316
  38.3 1.3 %collective-permute-start.15 = (f32[32,256]{1,0:T(8,128)S(1)}, f32[32,256]{1,0:T(8,128)S(1)}, u32[]{:S(2)}, u32[]{:S(2)}) collective-permute-start(f32[32,256]{1,0:T(8,128)S(1)} %sum_state.4.refs_2_.a_ref), channel_id=1, source_target_pairs={{0,8},{1,9},{2,10},{3,11},{4,12},{5,13},{6,14},{7,15},{8,0},{9,1},... | collective-permute-start | bytes 98312 | tf_op jit(solution)/shard_map/ppermute | solution.py:316
  39.5 1.7 %collective-permute-start.18 = (f32[64,256]{1,0:T(8,128)S(1)}, f32[64,256]{1,0:T(8,128)S(1)}, u32[]{:S(2)}, u32[]{:S(2)}) collective-permute-start(f32[64,256]{1,0:T(8,128)S(1)} %get-tuple-element.93.rest_0_), channel_id=1, source_target_pairs={{0,8},{1,9},{2,10},{3,11},{4,12},{5,13},{6,14},{7,15},{8,0},{9,1},... | collective-permute-start | bytes 196616 | tf_op jit(solution)/shard_map/ppermute | solution.py:316
  41.3 1.9 %collective-permute-start.19 = (f32[64,256]{1,0:T(8,128)S(1)}, f32[64,256]{1,0:T(8,128)S(1)}, u32[]{:S(2)}, u32[]{:S(2)}) collective-permute-start(f32[64,256]{1,0:T(8,128)S(1)} %get-tuple-element.95.rest_0_), channel_id=1, source_target_pairs={{0,8},{1,3},{2,10},{3,1},{4,12},{5,7},{6,14},{7,5},{8,0},{9,11},{1... | collective-permute-start | bytes 196616 | tf_op jit(solution)/shard_map/ppermute | solution.py:316
  43.1 1.5 %collective-permute-done.15.b_ref = f32[32,256]{1,0:T(8,128)S(1)} collective-permute-done((f32[32,256]{1,0:T(8,128)S(1)}, f32[32,256]{1,0:T(8,128)S(1)}, u32[]{:S(2)}, u32[]{:S(2)}) %collective-permute-start.15) | collective-permute-done | bytes 32800 | tf_op jit(solution)/shard_map/ppermute | solution.py:316
  44.6 0.7 %grad_points_own.1.acc_ref = f32[1024,512]{1,0:T(8,128)S(1)} custom-call(f32[1024,512]{1,0:T(8,128)S(1)} %grad_points_part.1.refs_3_.acc_ref, bf16[1024,512]{1,0:T(8,128)(2,1)S(1)} %copy-done, bf16[512,512]{1,0:T(8,128)(2,1)S(1)} %copy-done.1, f32[32,256]{1,0:T(8,128)S(1)} %sum_state.5.own_ref), custom_call_target="tpu_custom_call" | custom-call | flops 1100000000 | bytes 100000 | tf_op jit(solution)/shard_map/grad_points_own/pallas_call | solution.py:292
  45.8 1.6 %outputs.1 = (bf16[1024,512]{1,0:T(8,128)(2,1)}, f32[64,256]{1,0:T(8,128)}) custom-call(f32[1024,512]{1,0:T(8,128)S(1)} %grad_points_own.1.acc_ref, bf16[1024,512]{1,0:T(8,128)(2,1)S(1)} %copy-done, bf16[512,512]{1,0:T(8,128)(2,1)S(1)} %copy-done.1, f32[32,256]{1,0:T(8,128)S(1)} %sum_state.5.own_ref, f32[32,256]{1,0:T(8,128)S(1)} %collective-permute-done.17.got_ref, ...), custom_call_target="tpu_custom_call" | custom-call | flops 11000000 | bytes 1000 | tf_op jit(solution)/shard_map/outputs/pallas_call | solution.py:292
  47.4 0.5 %collective-permute-done.19.refs_3_ = f32[64,256]{1,0:T(8,128)S(1)} collective-permute-done((f32[64,256]{1,0:T(8,128)S(1)}, f32[64,256]{1,0:T(8,128)S(1)}, u32[]{:S(2)}, u32[]{:S(2)}) %collective-permute-start.19) | collective-permute-done | bytes 65568 | tf_op jit(solution)/shard_map/ppermute | solution.py:316
  47.9 0.7 %sums_out.1 = (f32[64,256]{1,0:T(8,128)}, f32[64,256]{1,0:T(8,128)}) custom-call(f32[64,256]{1,0:T(8,128)S(1)} %bitcast.14, f32[64,256]{1,0:T(8,128)S(1)} %collective-permute-done.18.refs_1_, f32[64,256]{1,0:T(8,128)S(1)} %bitcast.15, f32[64,256]{1,0:T(8,128)S(1)} %collective-permute-done.19.refs_3_, f32[64,256]{1,0:T(8,128)} %get-tuple-element.50.refs_4_), custom_call_target="tpu_custom_call" | custom-call | flops 11000000 | bytes 1000 | tf_op jit(solution)/shard_map/sums_out/pallas_call | solution.py:292
  (49 shorter events, 1.9 us)
Async XLA Ops:
  3.4 1.4 %collective-permute-start = (f32[32,256]{1,0:T(8,128)S(1)}, f32[32,256]{1,0:T(8,128)S(1)}, u32[]{:S(2)}, u32[]{:S(2)}) collective-permute-start(f32[32,256]{1,0:T(8,128)S(1)} %get-tuple-element.102), channel_id=1, source_target_pairs={{0,1},{1,0},{2,3},{3,2},{4,5},{5,4},{6,7},{7,6},{8,9},{9,8},{10,11... | collective-permute-start | bytes 98312 | tf_op jit(solution)/shard_map/ppermute | solution.py:305
  4.0 3.7 %collective-permute-start.2 = (f32[8,64,256]{2,1,0:T(8,128)S(1)}, f32[8,64,256]{2,1,0:T(8,128)S(1)}, u32[]{:S(2)}, u32[]{:S(2)}) collective-permute-start(f32[8,64,256]{2,1,0:T(8,128)S(1)} %get-tuple-element.57), channel_id=1, source_target_pairs={{0,1},{1,0},{2,3},{3,2},{4,5},{5,4},{6,7},{7,6},{8,9},{9,8},{10,11... | collective-permute-start | bytes 1572872 | tf_op jit(solution)/shard_map/ppermute | solution.py:305
  4.8 6.9 %copy-start.2 = (bf16[512,512]{1,0:T(8,128)(2,1)S(1)}, bf16[512,512]{1,0:T(8,128)(2,1)}, u32[]{:S(2)}) copy-start(bf16[512,512]{1,0:T(8,128)(2,1)} %refs_4_.1) | copy-start | bytes 1572868
  4.8 6.9 %copy-start.3 = (bf16[512,512]{1,0:T(8,128)(2,1)S(1)}, bf16[512,512]{1,0:T(8,128)(2,1)}, u32[]{:S(2)}) copy-start(bf16[512,512]{1,0:T(8,128)(2,1)} %refs_5_.1) | copy-start | bytes 1572868
  4.8 4.8 %collective-permute-start.1 = (f32[32,256]{1,0:T(8,128)S(1)}, f32[32,256]{1,0:T(8,128)S(1)}, u32[]{:S(2)}, u32[]{:S(2)}) collective-permute-start(f32[32,256]{1,0:T(8,128)S(1)} %sum_0.1.refs_2_.a_ref), channel_id=1, source_target_pairs={{0,2},{1,5},{2,0},{3,7},{4,6},{5,1},{6,4},{7,3},{8,10},{9,13},{10,... | collective-permute-start | bytes 98312 | tf_op jit(solution)/shard_map/ppermute | solution.py:316
  7.8 8.9 %collective-permute-start.5 = (f32[256,256]{1,0:T(8,128)S(1)}, f32[256,256]{1,0:T(8,128)S(1)}, u32[]{:S(2)}, u32[]{:S(2)}) collective-permute-start(f32[256,256]{1,0:T(8,128)S(1)} %get-tuple-element.58.rest_0_.rest_3_), channel_id=1, source_target_pairs={{0,2},{1,5},{2,0},{3,7},{4,6},{5,1},{6,4},{7,3},{8,10},{9,13},{10,... | collective-permute-start | bytes 786440 | tf_op jit(solution)/shard_map/ppermute | solution.py:316
  9.6 4.3 %collective-permute-start.3 = (f32[32,256]{1,0:T(8,128)S(1)}, f32[32,256]{1,0:T(8,128)S(1)}, u32[]{:S(2)}, u32[]{:S(2)}) collective-permute-start(f32[32,256]{1,0:T(8,128)S(1)} %sum_1.1.rest_2_.a_ref), channel_id=1, source_target_pairs={{0,4},{1,9},{2,6},{3,11},{4,0},{5,13},{6,2},{7,15},{8,12},{9,1},{1... | collective-permute-start | bytes 98312 | tf_op jit(solution)/shard_map/ppermute | solution.py:316
  13.9 6.3 %collective-permute-start.4 = (f32[32,256]{1,0:T(8,128)S(1)}, f32[32,256]{1,0:T(8,128)S(1)}, u32[]{:S(2)}, u32[]{:S(2)}) collective-permute-start(f32[32,256]{1,0:T(8,128)S(1)} %sum_2.1.refs_2_.rest_1_.a_ref), channel_id=1, source_target_pairs={{0,8},{1,3},{2,10},{3,1},{4,12},{5,7},{6,14},{7,5},{8,0},{9,11},{1... | collective-permute-start | bytes 98312 | tf_op jit(solution)/shard_map/ppermute | solution.py:316
  16.7 6.0 %collective-permute-start.7 = (f32[128,256]{1,0:T(8,128)S(1)}, f32[128,256]{1,0:T(8,128)S(1)}, u32[]{:S(2)}, u32[]{:S(2)}) collective-permute-start(f32[128,256]{1,0:T(8,128)S(1)} %get-tuple-element.63.rest_2_), channel_id=1, source_target_pairs={{0,4},{1,3},{2,6},{3,1},{4,0},{5,7},{6,2},{7,5},{8,12},{9,11},{10,... | collective-permute-start | bytes 393224 | tf_op jit(solution)/shard_map/ppermute | solution.py:316
  20.2 2.5 %collective-permute-start.6 = (f32[32,256]{1,0:T(8,128)S(1)}, f32[32,256]{1,0:T(8,128)S(1)}, u32[]{:S(2)}, u32[]{:S(2)}) collective-permute-start(f32[32,256]{1,0:T(8,128)S(1)} %sum_3.1.g_ref), channel_id=1, source_target_pairs={{0,1},{1,0},{2,3},{3,2},{4,5},{5,4},{6,7},{7,6},{8,9},{9,8},{10,11... | collective-permute-start | bytes 98312 | tf_op jit(solution)/shard_map/ppermute | solution.py:305
  20.3 3.8 %collective-permute-start.10 = (f32[32,256]{1,0:T(8,128)S(1)}, f32[32,256]{1,0:T(8,128)S(1)}, u32[]{:S(2)}, u32[]{:S(2)}) collective-permute-start(f32[32,256]{1,0:T(8,128)S(1)} %get-tuple-element.64.rest_0_), channel_id=1, source_target_pairs={{0,1},{1,0},{2,3},{3,2},{4,5},{5,4},{6,7},{7,6},{8,9},{9,8},{10,11... | collective-permute-start | bytes 98312 | tf_op jit(solution)/shard_map/ppermute | solution.py:305
  24.0 2.0 %collective-permute-start.9 = (f32[8,64,256]{2,1,0:T(8,128)S(1)}, f32[8,64,256]{2,1,0:T(8,128)S(1)}, u32[]{:S(2)}, u32[]{:S(2)}) collective-permute-start(f32[8,64,256]{2,1,0:T(8,128)S(1)} %get-tuple-element.83), channel_id=1, source_target_pairs={{0,1},{1,0},{2,3},{3,2},{4,5},{5,4},{6,7},{7,6},{8,9},{9,8},{10,11... | collective-permute-start | bytes 1572872 | tf_op jit(solution)/shard_map/ppermute | solution.py:305
  25.4 2.2 %collective-permute-start.8 = (f32[8,64,256]{2,1,0:T(8,128)S(1)}, f32[8,64,256]{2,1,0:T(8,128)S(1)}, u32[]{:S(2)}, u32[]{:S(2)}) collective-permute-start(f32[8,64,256]{2,1,0:T(8,128)S(1)} %get-tuple-element.81), channel_id=1, source_target_pairs={{0,1},{1,0},{2,3},{3,2},{4,5},{5,4},{6,7},{7,6},{8,9},{9,8},{10,11... | collective-permute-start | bytes 1572872 | tf_op jit(solution)/shard_map/ppermute | solution.py:305
  26.0 6.8 %collective-permute-start.11 = (f32[288,256]{1,0:T(8,128)S(1)}, f32[288,256]{1,0:T(8,128)S(1)}, u32[]{:S(2)}, u32[]{:S(2)}) collective-permute-start(f32[288,256]{1,0:T(8,128)S(1)} %get-tuple-element.84.refs_2_), channel_id=1, source_target_pairs={{0,2},{1,5},{2,0},{3,7},{4,6},{5,1},{6,4},{7,3},{8,10},{9,13},{10,... | collective-permute-start | bytes 884744 | tf_op jit(solution)/shard_map/ppermute | solution.py:316
  27.6 8.0 %collective-permute-start.14 = (f32[256,256]{1,0:T(8,128)S(1)}, f32[256,256]{1,0:T(8,128)S(1)}, u32[]{:S(2)}, u32[]{:S(2)}) collective-permute-start(f32[256,256]{1,0:T(8,128)S(1)} %get-tuple-element.85.refs_1_), channel_id=1, source_target_pairs={{0,2},{1,5},{2,0},{3,7},{4,6},{5,1},{6,4},{7,3},{8,10},{9,13},{10,... | collective-permute-start | bytes 786440 | tf_op jit(solution)/shard_map/ppermute | solution.py:316
  29.1 8.0 %collective-permute-start.13 = (f32[64,256]{1,0:T(8,128)S(1)}, f32[64,256]{1,0:T(8,128)S(1)}, u32[]{:S(2)}, u32[]{:S(2)}) collective-permute-start(f32[64,256]{1,0:T(8,128)S(1)} %get-tuple-element.86.refs_6_), channel_id=1, source_target_pairs={{0,8},{1,9},{2,10},{3,11},{4,12},{5,13},{6,14},{7,15},{8,0},{9,1},... | collective-permute-start | bytes 196616 | tf_op jit(solution)/shard_map/ppermute | solution.py:316
  32.8 5.4 %collective-permute-start.12 = (f32[160,256]{1,0:T(8,128)S(1)}, f32[160,256]{1,0:T(8,128)S(1)}, u32[]{:S(2)}, u32[]{:S(2)}) collective-permute-start(f32[160,256]{1,0:T(8,128)S(1)} %get-tuple-element.88.refs_2_), channel_id=1, source_target_pairs={{0,4},{1,3},{2,6},{3,1},{4,0},{5,7},{6,2},{7,5},{8,12},{9,11},{10,... | collective-permute-start | bytes 491528 | tf_op jit(solution)/shard_map/ppermute | solution.py:316
  35.7 5.6 %collective-permute-start.16 = (f32[128,256]{1,0:T(8,128)S(1)}, f32[128,256]{1,0:T(8,128)S(1)}, u32[]{:S(2)}, u32[]{:S(2)}) collective-permute-start(f32[128,256]{1,0:T(8,128)S(1)} %get-tuple-element.92.rest_0_), channel_id=1, source_target_pairs={{0,4},{1,9},{2,6},{3,11},{4,0},{5,13},{6,2},{7,15},{8,12},{9,1},{1... | collective-permute-start | bytes 393224 | tf_op jit(solution)/shard_map/ppermute | solution.py:316
  37.0 7.6 %copy-start = (bf16[1024,512]{1,0:T(8,128)(2,1)S(1)}, bf16[1024,512]{1,0:T(8,128)(2,1)}, u32[]{:S(2)}) copy-start(bf16[1024,512]{1,0:T(8,128)(2,1)} %c_ref.3) | copy-start | bytes 3145732
  37.0 7.6 %copy-start.1 = (bf16[512,512]{1,0:T(8,128)(2,1)S(1)}, bf16[512,512]{1,0:T(8,128)(2,1)}, u32[]{:S(2)}) copy-start(bf16[512,512]{1,0:T(8,128)(2,1)} %wq_ref.3) | copy-start | bytes 1572868
  38.3 6.3 %collective-permute-start.15 = (f32[32,256]{1,0:T(8,128)S(1)}, f32[32,256]{1,0:T(8,128)S(1)}, u32[]{:S(2)}, u32[]{:S(2)}) collective-permute-start(f32[32,256]{1,0:T(8,128)S(1)} %sum_state.4.refs_2_.a_ref), channel_id=1, source_target_pairs={{0,8},{1,9},{2,10},{3,11},{4,12},{5,13},{6,14},{7,15},{8,0},{9,1},... | collective-permute-start | bytes 98312 | tf_op jit(solution)/shard_map/ppermute | solution.py:316
  39.5 8.4 %collective-permute-start.18 = (f32[64,256]{1,0:T(8,128)S(1)}, f32[64,256]{1,0:T(8,128)S(1)}, u32[]{:S(2)}, u32[]{:S(2)}) collective-permute-start(f32[64,256]{1,0:T(8,128)S(1)} %get-tuple-element.93.rest_0_), channel_id=1, source_target_pairs={{0,8},{1,9},{2,10},{3,11},{4,12},{5,13},{6,14},{7,15},{8,0},{9,1},... | collective-permute-start | bytes 196616 | tf_op jit(solution)/shard_map/ppermute | solution.py:316
  41.3 6.6 %collective-permute-start.19 = (f32[64,256]{1,0:T(8,128)S(1)}, f32[64,256]{1,0:T(8,128)S(1)}, u32[]{:S(2)}, u32[]{:S(2)}) collective-permute-start(f32[64,256]{1,0:T(8,128)S(1)} %get-tuple-element.95.rest_0_), channel_id=1, source_target_pairs={{0,8},{1,3},{2,10},{3,1},{4,12},{5,7},{6,14},{7,5},{8,0},{9,11},{1... | collective-permute-start | bytes 196616 | tf_op jit(solution)/shard_map/ppermute | solution.py:316
  44.6 1.2 %collective-permute-start.17 = (f32[32,256]{1,0:T(8,128)S(1)}, f32[32,256]{1,0:T(8,128)S(1)}, u32[]{:S(2)}, u32[]{:S(2)}) collective-permute-start(f32[32,256]{1,0:T(8,128)S(1)} %sum_state.5.own_ref), channel_id=1, source_target_pairs={{0,1},{1,0},{2,3},{3,2},{4,5},{5,4},{6,7},{7,6},{8,9},{9,8},{10,11... | collective-permute-start | bytes 98312 | tf_op jit(solution)/shard_map/ppermute | solution.py:305

commit v9 on v8

--- a/solution.py
+++ b/solution.py
@@ -19,7 +19,7 @@
 CHUNKS = 2
 BLOCKS = 4
 EARLY_Z = ("state", "value")
-ORDER = "kVMPkVTKSVS"
+ORDER = "kVMPkVTSKVS"
 US = {"end_query": 2.0, "grad_points": 0.01, "back_own": 0.01, "add_key_0": 5.0, "sum_0": 5.0, "back_key": 5.0, "back_value": 5.0}
 
 PARAMS = pltpu.CompilerParams(vmem_limit_bytes=16 * 1024 * 1024)

time: 48.7 us -> 48.7 us (level)
  no operation moved by 1% of the time
where the time goes in v9:
time: 48.7 us; the launch traced here: 48.6 us
  starting transfers between devices  23.5 us (48%)
  Pallas kernels  15.8 us (32%)
  waiting for transfers between devices  8.43 us (17%)
  between operations  0.85 us (2%)
    ppermute x13, starting transfers between devices, swap(): return lax.ppermute(value, ('points', 'mp', 'sub'), pairs)  21.6 us
    pallas_call x29, Pallas kernels, call(): pl.pallas_call(kernel, out_shape=out_shape, in_specs=specs, out_specs=out...  15.8 us
    ppermute x13, waiting for transfers between devices, swap(): return lax.ppermute(value, ('points', 'mp', 'sub'), pairs)  7.26 us
    ppermute x7, starting transfers between devices, swap_cores(): lax.ppermute(value, 'sub', [(i, i ^ 1) for i in range(lax.axis_size('sub'...  1.85 us
    ppermute x7, waiting for transfers between devices, swap_cores(): lax.ppermute(value, 'sub', [(i, i ^ 1) for i in range(lax.axis_size('sub'...  1.17 us
  transfers between devices with their start and end apart: 20, of which 9 were waited for; matrix products, arithmetic and copies ran while one was open for 0% of the time, Pallas kernels for 25%

profile of v9, /device:TPU:0, one launch (start us, length us, event | category | flops | bytes accessed | tf_op | source)
XLA Modules:
  0.0 48.6 jit_solution(14932431531186141610)
XLA Ops:
  0.6 2.7 %cross.1 = (f32[512,512]{1,0:T(8,128)S(1)}, f32[2,32,256]{2,1,0:T(8,128)S(1)}, bf16[1024,512]{1,0:T(8,128)(2,1)S(1)}, bf16[512,1024]{1,0:T(8,128)(2,1)S(1)}) custom-call(bf16[1024,512]{1,0:T(8,128)(2,1)} %p_hbm.1, bf16[1024,512]{1,0:T(8,128)(2,1)} %c_ref.3, bf16[512,512]{1,0:T(8,128)(2,1)} %wq_ref.3), custom_call_target="tpu_custom_call" | custom-call | flops 3300000000 | bytes 300000 | tf_op jit(solution)/shard_map/cross/pallas_call | solution.py:292
  3.4 0.5 %collective-permute-start = (f32[32,256]{1,0:T(8,128)S(1)}, f32[32,256]{1,0:T(8,128)S(1)}, u32[]{:S(2)}, u32[]{:S(2)}) collective-permute-start(f32[32,256]{1,0:T(8,128)S(1)} %get-tuple-element.102), channel_id=1, source_target_pairs={{0,1},{1,0},{2,3},{3,2},{4,5},{5,4},{6,7},{7,6},{8,9},{9,8},{10,11... | collective-permute-start | bytes 98312 | tf_op jit(solution)/shard_map/ppermute | solution.py:305
  4.1 0.7 %collective-permute-done.b_ref = f32[32,256]{1,0:T(8,128)S(1)} collective-permute-done((f32[32,256]{1,0:T(8,128)S(1)}, f32[32,256]{1,0:T(8,128)S(1)}, u32[]{:S(2)}, u32[]{:S(2)}) %collective-permute-start) | collective-permute-done | bytes 32800 | tf_op jit(solution)/shard_map/ppermute | solution.py:305
  4.8 2.9 %collective-permute-start.1 = (f32[32,256]{1,0:T(8,128)S(1)}, f32[32,256]{1,0:T(8,128)S(1)}, u32[]{:S(2)}, u32[]{:S(2)}) collective-permute-start(f32[32,256]{1,0:T(8,128)S(1)} %sum_0.1.refs_2_.a_ref), channel_id=1, source_target_pairs={{0,2},{1,5},{2,0},{3,7},{4,6},{5,1},{6,4},{7,3},{8,10},{9,13},{10,... | collective-permute-start | bytes 98312 | tf_op jit(solution)/shard_map/ppermute | solution.py:316
  7.8 1.0 %collective-permute-start.5 = (f32[256,256]{1,0:T(8,128)S(1)}, f32[256,256]{1,0:T(8,128)S(1)}, u32[]{:S(2)}, u32[]{:S(2)}) collective-permute-start(f32[256,256]{1,0:T(8,128)S(1)} %get-tuple-element.58.rest_0_.rest_3_), channel_id=1, source_target_pairs={{0,2},{1,5},{2,0},{3,7},{4,6},{5,1},{6,4},{7,3},{8,10},{9,13},{10,... | collective-permute-start | bytes 786440 | tf_op jit(solution)/shard_map/ppermute | solution.py:316
  8.7 0.9 %collective-permute-done.1.b_ref = f32[32,256]{1,0:T(8,128)S(1)} collective-permute-done((f32[32,256]{1,0:T(8,128)S(1)}, f32[32,256]{1,0:T(8,128)S(1)}, u32[]{:S(2)}, u32[]{:S(2)}) %collective-permute-start.1) | collective-permute-done | bytes 32800 | tf_op jit(solution)/shard_map/ppermute | solution.py:316
  9.6 2.1 %collective-permute-start.3 = (f32[32,256]{1,0:T(8,128)S(1)}, f32[32,256]{1,0:T(8,128)S(1)}, u32[]{:S(2)}, u32[]{:S(2)}) collective-permute-start(f32[32,256]{1,0:T(8,128)S(1)} %sum_1.1.rest_2_.a_ref), channel_id=1, source_target_pairs={{0,4},{1,9},{2,6},{3,11},{4,0},{5,13},{6,2},{7,15},{8,12},{9,1},{1... | collective-permute-start | bytes 98312 | tf_op jit(solution)/shard_map/ppermute | solution.py:316
  11.7 2.1 %norm.2 = (f32[1024,256]{1,0:T(8,128)S(1)}, f32[1024,256]{1,0:T(8,128)S(1)}, f32[1024,256]{1,0:T(8,128)S(1)}, f32[1024,256]{1,0:T(8,128)S(1)}, f32[32,256]{1,0:T(8,128)S(1)}, /*index=5*/bf16[4,512,256]{2,1,0:T(8,128)(2,1)S(1)}) custom-call(bf16[1024,512]{1,0:T(8,128)(2,1)S(1)} %get-tuple-element.59.p_ref, bf16[512,512]{1,0:T(8,128)(2,1)S(1)} %copy-done.2, ...), custom_call_target="tpu_custom_call" | custom-call | flops 2529999872 | bytes 229999 | tf_op jit(solution)/shard_map/norm/pallas_call | solution.py:292
  13.9 2.7 %collective-permute-start.4 = (f32[32,256]{1,0:T(8,128)S(1)}, f32[32,256]{1,0:T(8,128)S(1)}, u32[]{:S(2)}, u32[]{:S(2)}) collective-permute-start(f32[32,256]{1,0:T(8,128)S(1)} %sum_2.1.refs_2_.rest_1_.a_ref), channel_id=1, source_target_pairs={{0,8},{1,3},{2,10},{3,1},{4,12},{5,7},{6,14},{7,5},{8,0},{9,11},{1... | collective-permute-start | bytes 98312 | tf_op jit(solution)/shard_map/ppermute | solution.py:316
  16.7 1.6 %collective-permute-start.7 = (f32[128,256]{1,0:T(8,128)S(1)}, f32[128,256]{1,0:T(8,128)S(1)}, u32[]{:S(2)}, u32[]{:S(2)}) collective-permute-start(f32[128,256]{1,0:T(8,128)S(1)} %get-tuple-element.63.rest_2_), channel_id=1, source_target_pairs={{0,4},{1,3},{2,6},{3,1},{4,0},{5,7},{6,2},{7,5},{8,12},{9,11},{10,... | collective-permute-start | bytes 393224 | tf_op jit(solution)/shard_map/ppermute | solution.py:316
  18.3 1.9 %norm.3 = (f32[1024,256]{1,0:T(8,128)S(1)}, f32[1024,256]{1,0:T(8,128)S(1)}, f32[1024,256]{1,0:T(8,128)S(1)}, f32[1024,256]{1,0:T(8,128)S(1)}, f32[32,256]{1,0:T(8,128)S(1)}) custom-call(bf16[1024,512]{1,0:T(8,128)(2,1)S(1)} %get-tuple-element.59.p_ref, bf16[4,512,256]{2,1,0:T(8,128)(2,1)S(1)} %get-tuple-element.61.rest_0_, ...), custom_call_target="tpu_custom_call" | custom-call | flops 2529999872 | bytes 229999 | tf_op jit(solution)/shard_map/norm/pallas_call | solution.py:292
  20.8 1.9 %back_own.1 = (bf16[1024,256]{1,0:T(8,128)(2,1)S(1)}, bf16[1024,256]{1,0:T(8,128)(2,1)S(1)}, f32[512,256]{1,0:T(8,128)S(1)}, f32[512,256]{1,0:T(8,128)S(1)}) custom-call(bf16[512,1024]{1,0:T(8,128)(2,1)S(1)} %get-tuple-element.53.pt_ref, f32[32,256]{1,0:T(8,128)S(1)} %sum_3.1.g_ref, f32[1024,256]{1,0:T(8,128)S(1)} %get-tuple-element.65.kn_ref, ...), custom_call_target="tpu_custom_call" | custom-call | flops 11000000 | bytes 1000 | tf_op jit(solution)/shard_map/back_own/pallas_call | solution.py:292
  22.7 1.2 %back_key.1 = (bf16[1024,256]{1,0:T(8,128)(2,1)S(1)}, f32[8,64,256]{2,1,0:T(8,128)S(1)}, f32[8,64,256]{2,1,0:T(8,128)S(1)}) custom-call(bf16[512,1024]{1,0:T(8,128)(2,1)S(1)} %get-tuple-element.53.pt_ref, f32[512,256]{1,0:T(8,128)S(1)} %get-tuple-element.70.own_ref, f32[32,256]{1,0:T(8,128)S(1)} %collective-permute-done.6.g_ref, ...), custom_call_target="tpu_custom_call" | custom-call | flops 5500000256 | bytes 500000 | tf_op jit(solution)/shard_map/back_key/pallas_call | solution.py:292
  24.1 1.3 %back_value.1 = (bf16[1024,256]{1,0:T(8,128)(2,1)S(1)}, f32[8,64,256]{2,1,0:T(8,128)S(1)}, f32[8,64,256]{2,1,0:T(8,128)S(1)}) custom-call(bf16[512,1024]{1,0:T(8,128)(2,1)S(1)} %get-tuple-element.53.pt_ref, f32[512,256]{1,0:T(8,128)S(1)} %get-tuple-element.77.own_ref, f32[32,256]{1,0:T(8,128)S(1)} %collective-permute-done.6.g_ref, ...), custom_call_target="tpu_custom_call" | custom-call | flops 5500000256 | bytes 500000 | tf_op jit(solution)/shard_map/back_value/pallas_call | solution.py:292
  25.4 0.5 %collective-permute-start.8 = (f32[8,64,256]{2,1,0:T(8,128)S(1)}, f32[8,64,256]{2,1,0:T(8,128)S(1)}, u32[]{:S(2)}, u32[]{:S(2)}) collective-permute-start(f32[8,64,256]{2,1,0:T(8,128)S(1)} %get-tuple-element.81), channel_id=1, source_target_pairs={{0,1},{1,0},{2,3},{3,2},{4,5},{5,4},{6,7},{7,6},{8,9},{9,8},{10,11... | collective-permute-start | bytes 1572872 | tf_op jit(solution)/shard_map/ppermute | solution.py:305
  26.0 1.6 %collective-permute-start.11 = (f32[288,256]{1,0:T(8,128)S(1)}, f32[288,256]{1,0:T(8,128)S(1)}, u32[]{:S(2)}, u32[]{:S(2)}) collective-permute-start(f32[288,256]{1,0:T(8,128)S(1)} %get-tuple-element.84.refs_2_), channel_id=1, source_target_pairs={{0,2},{1,5},{2,0},{3,7},{4,6},{5,1},{6,4},{7,3},{8,10},{9,13},{10,... | collective-permute-start | bytes 884744 | tf_op jit(solution)/shard_map/ppermute | solution.py:316
  27.6 1.4 %collective-permute-start.14 = (f32[256,256]{1,0:T(8,128)S(1)}, f32[256,256]{1,0:T(8,128)S(1)}, u32[]{:S(2)}, u32[]{:S(2)}) collective-permute-start(f32[256,256]{1,0:T(8,128)S(1)} %get-tuple-element.85.refs_1_), channel_id=1, source_target_pairs={{0,2},{1,5},{2,0},{3,7},{4,6},{5,1},{6,4},{7,3},{8,10},{9,13},{10,... | collective-permute-start | bytes 786440 | tf_op jit(solution)/shard_map/ppermute | solution.py:316
  29.1 1.3 %collective-permute-start.13 = (f32[64,256]{1,0:T(8,128)S(1)}, f32[64,256]{1,0:T(8,128)S(1)}, u32[]{:S(2)}, u32[]{:S(2)}) collective-permute-start(f32[64,256]{1,0:T(8,128)S(1)} %get-tuple-element.86.refs_6_), channel_id=1, source_target_pairs={{0,8},{1,9},{2,10},{3,11},{4,12},{5,13},{6,14},{7,15},{8,0},{9,1},... | collective-permute-start | bytes 196616 | tf_op jit(solution)/shard_map/ppermute | solution.py:316
  30.3 1.3 %grad_points_part.1.refs_3_.acc_ref = f32[1024,512]{1,0:T(8,128)S(1)} custom-call(bf16[1024,256]{1,0:T(8,128)(2,1)S(1)} %get-tuple-element.69.refs_0_, bf16[1024,256]{1,0:T(8,128)(2,1)S(1)} %get-tuple-element.75.rest_0_.refs_1_, bf16[1024,256]{1,0:T(8,128)(2,1)S(1)} %get-tuple-element.76.refs_2_, bf16[1024,256]{1,0:T(8,128)(2,1)S(1)} %get-tuple-element.79.refs_3_, ...), custom_call_target="tpu_custom_call" | custom-call | flops 1430000000 | bytes 130000 | tf_op jit(solution)/shard_map/grad_points_part/pallas_call | solution.py:292
  31.6 1.2 %collective-permute-done.11.refs_1_ = f32[288,256]{1,0:T(8,128)S(1)} collective-permute-done((f32[288,256]{1,0:T(8,128)S(1)}, f32[288,256]{1,0:T(8,128)S(1)}, u32[]{:S(2)}, u32[]{:S(2)}) %collective-permute-start.11) | collective-permute-done | bytes 294944 | tf_op jit(solution)/shard_map/ppermute | solution.py:316
  32.8 0.8 %collective-permute-start.12 = (f32[160,256]{1,0:T(8,128)S(1)}, f32[160,256]{1,0:T(8,128)S(1)}, u32[]{:S(2)}, u32[]{:S(2)}) collective-permute-start(f32[160,256]{1,0:T(8,128)S(1)} %get-tuple-element.88.refs_2_), channel_id=1, source_target_pairs={{0,4},{1,3},{2,6},{3,1},{4,0},{5,7},{6,2},{7,5},{8,12},{9,11},{10,... | collective-permute-start | bytes 491528 | tf_op jit(solution)/shard_map/ppermute | solution.py:316
  33.6 2.0 %collective-permute-done.14.refs_1_ = f32[256,256]{1,0:T(8,128)S(1)} collective-permute-done((f32[256,256]{1,0:T(8,128)S(1)}, f32[256,256]{1,0:T(8,128)S(1)}, u32[]{:S(2)}, u32[]{:S(2)}) %collective-permute-start.14) | collective-permute-done | bytes 262176 | tf_op jit(solution)/shard_map/ppermute | solution.py:316
  35.7 1.3 %collective-permute-start.16 = (f32[128,256]{1,0:T(8,128)S(1)}, f32[128,256]{1,0:T(8,128)S(1)}, u32[]{:S(2)}, u32[]{:S(2)}) collective-permute-start(f32[128,256]{1,0:T(8,128)S(1)} %get-tuple-element.91.rest_0_), channel_id=1, source_target_pairs={{0,4},{1,9},{2,6},{3,11},{4,0},{5,13},{6,2},{7,15},{8,12},{9,1},{1... | collective-permute-start | bytes 393224 | tf_op jit(solution)/shard_map/ppermute | solution.py:316
  37.1 1.2 %collective-permute-done.12.refs_1_ = f32[160,256]{1,0:T(8,128)S(1)} collective-permute-done((f32[160,256]{1,0:T(8,128)S(1)}, f32[160,256]{1,0:T(8,128)S(1)}, u32[]{:S(2)}, u32[]{:S(2)}) %collective-permute-start.12) | collective-permute-done | bytes 163872 | tf_op jit(solution)/shard_map/ppermute | solution.py:316
  38.2 1.3 %collective-permute-start.15 = (f32[32,256]{1,0:T(8,128)S(1)}, f32[32,256]{1,0:T(8,128)S(1)}, u32[]{:S(2)}, u32[]{:S(2)}) collective-permute-start(f32[32,256]{1,0:T(8,128)S(1)} %sum_state.4.refs_2_.a_ref), channel_id=1, source_target_pairs={{0,8},{1,9},{2,10},{3,11},{4,12},{5,13},{6,14},{7,15},{8,0},{9,1},... | collective-permute-start | bytes 98312 | tf_op jit(solution)/shard_map/ppermute | solution.py:316
  39.5 1.8 %collective-permute-start.18 = (f32[64,256]{1,0:T(8,128)S(1)}, f32[64,256]{1,0:T(8,128)S(1)}, u32[]{:S(2)}, u32[]{:S(2)}) collective-permute-start(f32[64,256]{1,0:T(8,128)S(1)} %get-tuple-element.94.refs_2_), channel_id=1, source_target_pairs={{0,8},{1,9},{2,10},{3,11},{4,12},{5,13},{6,14},{7,15},{8,0},{9,1},... | collective-permute-start | bytes 196616 | tf_op jit(solution)/shard_map/ppermute | solution.py:316
  41.3 1.8 %collective-permute-start.19 = (f32[64,256]{1,0:T(8,128)S(1)}, f32[64,256]{1,0:T(8,128)S(1)}, u32[]{:S(2)}, u32[]{:S(2)}) collective-permute-start(f32[64,256]{1,0:T(8,128)S(1)} %get-tuple-element.95.rest_0_), channel_id=1, source_target_pairs={{0,8},{1,3},{2,10},{3,1},{4,12},{5,7},{6,14},{7,5},{8,0},{9,11},{1... | collective-permute-start | bytes 196616 | tf_op jit(solution)/shard_map/ppermute | solution.py:316
  43.2 1.4 %collective-permute-done.15.b_ref = f32[32,256]{1,0:T(8,128)S(1)} collective-permute-done((f32[32,256]{1,0:T(8,128)S(1)}, f32[32,256]{1,0:T(8,128)S(1)}, u32[]{:S(2)}, u32[]{:S(2)}) %collective-permute-start.15) | collective-permute-done | bytes 32800 | tf_op jit(solution)/shard_map/ppermute | solution.py:316
  44.6 0.7 %grad_points_own.1.acc_ref = f32[1024,512]{1,0:T(8,128)S(1)} custom-call(f32[1024,512]{1,0:T(8,128)S(1)} %grad_points_part.1.refs_3_.acc_ref, bf16[1024,512]{1,0:T(8,128)(2,1)S(1)} %copy-done, bf16[512,512]{1,0:T(8,128)(2,1)S(1)} %copy-done.1, f32[32,256]{1,0:T(8,128)S(1)} %sum_state.5.own_ref), custom_call_target="tpu_custom_call" | custom-call | flops 1100000000 | bytes 100000 | tf_op jit(solution)/shard_map/grad_points_own/pallas_call | solution.py:292
  45.8 1.6 %outputs.1 = (bf16[1024,512]{1,0:T(8,128)(2,1)}, f32[64,256]{1,0:T(8,128)}) custom-call(f32[1024,512]{1,0:T(8,128)S(1)} %grad_points_own.1.acc_ref, bf16[1024,512]{1,0:T(8,128)(2,1)S(1)} %copy-done, bf16[512,512]{1,0:T(8,128)(2,1)S(1)} %copy-done.1, f32[32,256]{1,0:T(8,128)S(1)} %sum_state.5.own_ref, f32[32,256]{1,0:T(8,128)S(1)} %collective-permute-done.17.got_ref, ...), custom_call_target="tpu_custom_call" | custom-call | flops 11000000 | bytes 1000 | tf_op jit(solution)/shard_map/outputs/pallas_call | solution.py:292
  47.4 0.5 %collective-permute-done.19.refs_3_ = f32[64,256]{1,0:T(8,128)S(1)} collective-permute-done((f32[64,256]{1,0:T(8,128)S(1)}, f32[64,256]{1,0:T(8,128)S(1)}, u32[]{:S(2)}, u32[]{:S(2)}) %collective-permute-start.19) | collective-permute-done | bytes 65568 | tf_op jit(solution)/shard_map/ppermute | solution.py:316
  47.9 0.7 %sums_out.1 = (f32[64,256]{1,0:T(8,128)}, f32[64,256]{1,0:T(8,128)}) custom-call(f32[64,256]{1,0:T(8,128)S(1)} %bitcast.14, f32[64,256]{1,0:T(8,128)S(1)} %collective-permute-done.18.refs_1_, f32[64,256]{1,0:T(8,128)S(1)} %bitcast.15, f32[64,256]{1,0:T(8,128)S(1)} %collective-permute-done.19.refs_3_, f32[64,256]{1,0:T(8,128)} %get-tuple-element.50.refs_4_), custom_call_target="tpu_custom_call" | custom-call | flops 11000000 | bytes 1000 | tf_op jit(solution)/shard_map/sums_out/pallas_call | solution.py:292
  (49 shorter events, 1.9 us)
Async XLA Ops:
  3.4 1.4 %collective-permute-start = (f32[32,256]{1,0:T(8,128)S(1)}, f32[32,256]{1,0:T(8,128)S(1)}, u32[]{:S(2)}, u32[]{:S(2)}) collective-permute-start(f32[32,256]{1,0:T(8,128)S(1)} %get-tuple-element.102), channel_id=1, source_target_pairs={{0,1},{1,0},{2,3},{3,2},{4,5},{5,4},{6,7},{7,6},{8,9},{9,8},{10,11... | collective-permute-start | bytes 98312 | tf_op jit(solution)/shard_map/ppermute | solution.py:305
  4.0 3.7 %collective-permute-start.2 = (f32[8,64,256]{2,1,0:T(8,128)S(1)}, f32[8,64,256]{2,1,0:T(8,128)S(1)}, u32[]{:S(2)}, u32[]{:S(2)}) collective-permute-start(f32[8,64,256]{2,1,0:T(8,128)S(1)} %get-tuple-element.57), channel_id=1, source_target_pairs={{0,1},{1,0},{2,3},{3,2},{4,5},{5,4},{6,7},{7,6},{8,9},{9,8},{10,11... | collective-permute-start | bytes 1572872 | tf_op jit(solution)/shard_map/ppermute | solution.py:305
  4.8 6.9 %copy-start.2 = (bf16[512,512]{1,0:T(8,128)(2,1)S(1)}, bf16[512,512]{1,0:T(8,128)(2,1)}, u32[]{:S(2)}) copy-start(bf16[512,512]{1,0:T(8,128)(2,1)} %refs_4_.1) | copy-start | bytes 1572868
  4.8 6.9 %copy-start.3 = (bf16[512,512]{1,0:T(8,128)(2,1)S(1)}, bf16[512,512]{1,0:T(8,128)(2,1)}, u32[]{:S(2)}) copy-start(bf16[512,512]{1,0:T(8,128)(2,1)} %refs_5_.1) | copy-start | bytes 1572868
  4.8 4.8 %collective-permute-start.1 = (f32[32,256]{1,0:T(8,128)S(1)}, f32[32,256]{1,0:T(8,128)S(1)}, u32[]{:S(2)}, u32[]{:S(2)}) collective-permute-start(f32[32,256]{1,0:T(8,128)S(1)} %sum_0.1.refs_2_.a_ref), channel_id=1, source_target_pairs={{0,2},{1,5},{2,0},{3,7},{4,6},{5,1},{6,4},{7,3},{8,10},{9,13},{10,... | collective-permute-start | bytes 98312 | tf_op jit(solution)/shard_map/ppermute | solution.py:316
  7.8 8.9 %collective-permute-start.5 = (f32[256,256]{1,0:T(8,128)S(1)}, f32[256,256]{1,0:T(8,128)S(1)}, u32[]{:S(2)}, u32[]{:S(2)}) collective-permute-start(f32[256,256]{1,0:T(8,128)S(1)} %get-tuple-element.58.rest_0_.rest_3_), channel_id=1, source_target_pairs={{0,2},{1,5},{2,0},{3,7},{4,6},{5,1},{6,4},{7,3},{8,10},{9,13},{10,... | collective-permute-start | bytes 786440 | tf_op jit(solution)/shard_map/ppermute | solution.py:316
  9.6 4.3 %collective-permute-start.3 = (f32[32,256]{1,0:T(8,128)S(1)}, f32[32,256]{1,0:T(8,128)S(1)}, u32[]{:S(2)}, u32[]{:S(2)}) collective-permute-start(f32[32,256]{1,0:T(8,128)S(1)} %sum_1.1.rest_2_.a_ref), channel_id=1, source_target_pairs={{0,4},{1,9},{2,6},{3,11},{4,0},{5,13},{6,2},{7,15},{8,12},{9,1},{1... | collective-permute-start | bytes 98312 | tf_op jit(solution)/shard_map/ppermute | solution.py:316
  13.9 6.3 %collective-permute-start.4 = (f32[32,256]{1,0:T(8,128)S(1)}, f32[32,256]{1,0:T(8,128)S(1)}, u32[]{:S(2)}, u32[]{:S(2)}) collective-permute-start(f32[32,256]{1,0:T(8,128)S(1)} %sum_2.1.refs_2_.rest_1_.a_ref), channel_id=1, source_target_pairs={{0,8},{1,3},{2,10},{3,1},{4,12},{5,7},{6,14},{7,5},{8,0},{9,11},{1... | collective-permute-start | bytes 98312 | tf_op jit(solution)/shard_map/ppermute | solution.py:316
  16.7 6.0 %collective-permute-start.7 = (f32[128,256]{1,0:T(8,128)S(1)}, f32[128,256]{1,0:T(8,128)S(1)}, u32[]{:S(2)}, u32[]{:S(2)}) collective-permute-start(f32[128,256]{1,0:T(8,128)S(1)} %get-tuple-element.63.rest_2_), channel_id=1, source_target_pairs={{0,4},{1,3},{2,6},{3,1},{4,0},{5,7},{6,2},{7,5},{8,12},{9,11},{10,... | collective-permute-start | bytes 393224 | tf_op jit(solution)/shard_map/ppermute | solution.py:316
  20.2 2.5 %collective-permute-start.6 = (f32[32,256]{1,0:T(8,128)S(1)}, f32[32,256]{1,0:T(8,128)S(1)}, u32[]{:S(2)}, u32[]{:S(2)}) collective-permute-start(f32[32,256]{1,0:T(8,128)S(1)} %sum_3.1.g_ref), channel_id=1, source_target_pairs={{0,1},{1,0},{2,3},{3,2},{4,5},{5,4},{6,7},{7,6},{8,9},{9,8},{10,11... | collective-permute-start | bytes 98312 | tf_op jit(solution)/shard_map/ppermute | solution.py:305
  20.3 3.8 %collective-permute-start.10 = (f32[32,256]{1,0:T(8,128)S(1)}, f32[32,256]{1,0:T(8,128)S(1)}, u32[]{:S(2)}, u32[]{:S(2)}) collective-permute-start(f32[32,256]{1,0:T(8,128)S(1)} %get-tuple-element.64.rest_0_), channel_id=1, source_target_pairs={{0,1},{1,0},{2,3},{3,2},{4,5},{5,4},{6,7},{7,6},{8,9},{9,8},{10,11... | collective-permute-start | bytes 98312 | tf_op jit(solution)/shard_map/ppermute | solution.py:305
  24.0 2.0 %collective-permute-start.9 = (f32[8,64,256]{2,1,0:T(8,128)S(1)}, f32[8,64,256]{2,1,0:T(8,128)S(1)}, u32[]{:S(2)}, u32[]{:S(2)}) collective-permute-start(f32[8,64,256]{2,1,0:T(8,128)S(1)} %get-tuple-element.83), channel_id=1, source_target_pairs={{0,1},{1,0},{2,3},{3,2},{4,5},{5,4},{6,7},{7,6},{8,9},{9,8},{10,11... | collective-permute-start | bytes 1572872 | tf_op jit(solution)/shard_map/ppermute | solution.py:305
  25.4 2.2 %collective-permute-start.8 = (f32[8,64,256]{2,1,0:T(8,128)S(1)}, f32[8,64,256]{2,1,0:T(8,128)S(1)}, u32[]{:S(2)}, u32[]{:S(2)}) collective-permute-start(f32[8,64,256]{2,1,0:T(8,128)S(1)} %get-tuple-element.81), channel_id=1, source_target_pairs={{0,1},{1,0},{2,3},{3,2},{4,5},{5,4},{6,7},{7,6},{8,9},{9,8},{10,11... | collective-permute-start | bytes 1572872 | tf_op jit(solution)/shard_map/ppermute | solution.py:305
  26.0 6.8 %collective-permute-start.11 = (f32[288,256]{1,0:T(8,128)S(1)}, f32[288,256]{1,0:T(8,128)S(1)}, u32[]{:S(2)}, u32[]{:S(2)}) collective-permute-start(f32[288,256]{1,0:T(8,128)S(1)} %get-tuple-element.84.refs_2_), channel_id=1, source_target_pairs={{0,2},{1,5},{2,0},{3,7},{4,6},{5,1},{6,4},{7,3},{8,10},{9,13},{10,... | collective-permute-start | bytes 884744 | tf_op jit(solution)/shard_map/ppermute | solution.py:316
  27.6 8.0 %collective-permute-start.14 = (f32[256,256]{1,0:T(8,128)S(1)}, f32[256,256]{1,0:T(8,128)S(1)}, u32[]{:S(2)}, u32[]{:S(2)}) collective-permute-start(f32[256,256]{1,0:T(8,128)S(1)} %get-tuple-element.85.refs_1_), channel_id=1, source_target_pairs={{0,2},{1,5},{2,0},{3,7},{4,6},{5,1},{6,4},{7,3},{8,10},{9,13},{10,... | collective-permute-start | bytes 786440 | tf_op jit(solution)/shard_map/ppermute | solution.py:316
  29.1 8.0 %collective-permute-start.13 = (f32[64,256]{1,0:T(8,128)S(1)}, f32[64,256]{1,0:T(8,128)S(1)}, u32[]{:S(2)}, u32[]{:S(2)}) collective-permute-start(f32[64,256]{1,0:T(8,128)S(1)} %get-tuple-element.86.refs_6_), channel_id=1, source_target_pairs={{0,8},{1,9},{2,10},{3,11},{4,12},{5,13},{6,14},{7,15},{8,0},{9,1},... | collective-permute-start | bytes 196616 | tf_op jit(solution)/shard_map/ppermute | solution.py:316
  32.8 5.4 %collective-permute-start.12 = (f32[160,256]{1,0:T(8,128)S(1)}, f32[160,256]{1,0:T(8,128)S(1)}, u32[]{:S(2)}, u32[]{:S(2)}) collective-permute-start(f32[160,256]{1,0:T(8,128)S(1)} %get-tuple-element.88.refs_2_), channel_id=1, source_target_pairs={{0,4},{1,3},{2,6},{3,1},{4,0},{5,7},{6,2},{7,5},{8,12},{9,11},{10,... | collective-permute-start | bytes 491528 | tf_op jit(solution)/shard_map/ppermute | solution.py:316
  35.7 5.7 %collective-permute-start.16 = (f32[128,256]{1,0:T(8,128)S(1)}, f32[128,256]{1,0:T(8,128)S(1)}, u32[]{:S(2)}, u32[]{:S(2)}) collective-permute-start(f32[128,256]{1,0:T(8,128)S(1)} %get-tuple-element.91.rest_0_), channel_id=1, source_target_pairs={{0,4},{1,9},{2,6},{3,11},{4,0},{5,13},{6,2},{7,15},{8,12},{9,1},{1... | collective-permute-start | bytes 393224 | tf_op jit(solution)/shard_map/ppermute | solution.py:316
  37.0 7.6 %copy-start = (bf16[1024,512]{1,0:T(8,128)(2,1)S(1)}, bf16[1024,512]{1,0:T(8,128)(2,1)}, u32[]{:S(2)}) copy-start(bf16[1024,512]{1,0:T(8,128)(2,1)} %c_ref.3) | copy-start | bytes 3145732
  37.0 7.6 %copy-start.1 = (bf16[512,512]{1,0:T(8,128)(2,1)S(1)}, bf16[512,512]{1,0:T(8,128)(2,1)}, u32[]{:S(2)}) copy-start(bf16[512,512]{1,0:T(8,128)(2,1)} %wq_ref.3) | copy-start | bytes 1572868
  38.2 6.4 %collective-permute-start.15 = (f32[32,256]{1,0:T(8,128)S(1)}, f32[32,256]{1,0:T(8,128)S(1)}, u32[]{:S(2)}, u32[]{:S(2)}) collective-permute-start(f32[32,256]{1,0:T(8,128)S(1)} %sum_state.4.refs_2_.a_ref), channel_id=1, source_target_pairs={{0,8},{1,9},{2,10},{3,11},{4,12},{5,13},{6,14},{7,15},{8,0},{9,1},... | collective-permute-start | bytes 98312 | tf_op jit(solution)/shard_map/ppermute | solution.py:316
  39.5 8.4 %collective-permute-start.18 = (f32[64,256]{1,0:T(8,128)S(1)}, f32[64,256]{1,0:T(8,128)S(1)}, u32[]{:S(2)}, u32[]{:S(2)}) collective-permute-start(f32[64,256]{1,0:T(8,128)S(1)} %get-tuple-element.94.refs_2_), channel_id=1, source_target_pairs={{0,8},{1,9},{2,10},{3,11},{4,12},{5,13},{6,14},{7,15},{8,0},{9,1},... | collective-permute-start | bytes 196616 | tf_op jit(solution)/shard_map/ppermute | solution.py:316
  41.3 6.6 %collective-permute-start.19 = (f32[64,256]{1,0:T(8,128)S(1)}, f32[64,256]{1,0:T(8,128)S(1)}, u32[]{:S(2)}, u32[]{:S(2)}) collective-permute-start(f32[64,256]{1,0:T(8,128)S(1)} %get-tuple-element.95.rest_0_), channel_id=1, source_target_pairs={{0,8},{1,3},{2,10},{3,1},{4,12},{5,7},{6,14},{7,5},{8,0},{9,11},{1... | collective-permute-start | bytes 196616 | tf_op jit(solution)/shard_map/ppermute | solution.py:316
  44.6 1.2 %collective-permute-start.17 = (f32[32,256]{1,0:T(8,128)S(1)}, f32[32,256]{1,0:T(8,128)S(1)}, u32[]{:S(2)}, u32[]{:S(2)}) collective-permute-start(f32[32,256]{1,0:T(8,128)S(1)} %sum_state.5.own_ref), channel_id=1, source_target_pairs={{0,1},{1,0},{2,3},{3,2},{4,5},{5,4},{6,7},{7,6},{8,9},{9,8},{10,11... | collective-permute-start | bytes 98312 | tf_op jit(solution)/shard_map/ppermute | solution.py:305
